TPU v7x, 256 devices: a whole 4x4x8 slice. The times are simulated.
256 devices in a mesh: dp: 4 (over x), seq: 64 (over z, y, core).
Axes of the slice: x: 4, y: 4, z: 8, core: 2. Of those that a mesh axis runs over, the one named last changes fastest.
Arguments:
- queries: bfloat16 [32768, 4096], P('seq', 'dp'), may hold values from -6 to 6
- keys: bfloat16 [32768, 4096], P('seq', 'dp'), may hold values from -6 to 6
- values: bfloat16 [32768, 4096], P('seq', 'dp'), may hold values from -6 to 6
- out_grad: bfloat16 [32768, 4096], P('seq', 'dp'), may hold values from -16 to 16
- gain: float32 [4096], P('dp'), may hold values from 0.5 to 1.5
- decay_index: int32 [32], P('dp'), may hold values from 0 to 15
- bounds: int32 [3], replicated, may hold values from 7168 to 25600, as said below
Outputs:
- query_grad: bfloat16 [32768, 4096], P('seq', 'dp')
- key_grad: bfloat16 [32768, 4096], P('seq', 'dp')
- value_grad: bfloat16 [32768, 4096], P('seq', 'dp')
- gain_grad: float32 [4096], P(('dp', 'seq'))
Inputs may be any that keep to these rules, and one draw needn't show every extreme that they name: `bounds`: the 3 positions rise strictly and lie inside the stream; token p starts a new episode when p is one of them.
All inputs are finite; a program needn't handle non-finite values.
Results may differ from a plain program's by a relative error of at most 0.0063.
Values sent between devices are 32-bit elements; how exact they have to be, the bound alone decides.
No kernel may reach another device: no remote copies, remote signals or barrier semaphores. Data moves between devices by JAX's collectives and lax.ppermute only.
A program may use at most 128 MiB of HBM per device.

v0:
```python
import jax
import jax.numpy as jnp
from jax import lax
from jax.sharding import PartitionSpec as P


def carried_in(array, axis, combine, identity, reverse):
    size, position = (lax.axis_size(axis), lax.axis_index(axis))
    everything = jax.tree.map(lambda part: lax.all_gather(part, axis), array)
    start = jax.tree.map(
        lambda part, zero: jnp.broadcast_to(jnp.asarray(zero, part.dtype), part.shape),
        array,
        identity,
    )

    def hop(k, before):
        at = size - 1 - k if reverse else k
        reached = at > position if reverse else at < position
        new = combine(before, jax.tree.map(lambda part: part[at], everything))
        return jax.tree.map(lambda a, b: jnp.where(reached, a, b), new, before)

    return lax.fori_loop(0, size, hop, start)


def decay_rates(decay_index, stream_length):
    level = decay_index.astype(jnp.float32)
    slow_rate = -0.25 * jnp.exp(level / 7.0 * jnp.log(8.0)) / stream_length
    lowest = jnp.log(4.0 / stream_length)
    fast_rate = -jnp.exp(lowest + (level - 8.0) / 7.0 * (jnp.log(1.0 / 32.0) - lowest))
    return jnp.where(decay_index < 8, slow_rate, fast_rate)


def shard_masks(rates, bound_row, first_row, tok_rows):
    places = first_row + jnp.arange(tok_rows, dtype=jnp.int32)
    episode = jnp.sum((bound_row[None, :] <= places[:, None]).astype(jnp.int32), axis=1)
    before = jnp.sum((bound_row <= first_row - 1).astype(jnp.int32))
    enter_mask = (episode == before).astype(jnp.float32)
    leave_mask = (episode == episode[tok_rows - 1]).astype(jnp.float32)
    whole_mask = (episode[tok_rows - 1] == before).astype(jnp.float32)
    local_pos = jnp.arange(tok_rows, dtype=jnp.float32)
    enter_decay = jnp.exp(rates[None, :] * (local_pos[:, None] + 1.0)) * enter_mask[:, None]
    leave_decay = (
        jnp.exp(rates[None, :] * (tok_rows - 1.0 - local_pos[:, None])) * leave_mask[:, None]
    )
    passing_decay = jnp.exp(rates * tok_rows) * whole_mask
    spacing = local_pos[:, None] - local_pos[None, :]
    allowed = (spacing >= 0.0) & (episode[:, None] == episode[None, :])
    weights = jnp.where(
        allowed[None], jnp.exp(rates[:, None, None] * jnp.maximum(spacing, 0.0)[None]), 0.0
    )
    return (enter_decay, leave_decay, passing_decay, weights)


def combine_states(earlier, later):
    return (earlier[0] * later[0], later[0][:, None, None] * earlier[1] + later[1])


def shards(queries, keys, values, out_grad, gain, decay_index, bounds):
    tok_rows = queries.shape[0]
    feature_width = queries.shape[1]
    head_count = decay_index.shape[0]
    head_size = feature_width // head_count
    all_features = float(feature_width * lax.axis_size("dp"))
    seq_devices = lax.axis_size("seq")
    first_row = lax.axis_index("seq") * tok_rows
    rates = decay_rates(decay_index, float(tok_rows * seq_devices))
    query_rows = queries.reshape(tok_rows, head_count, head_size)
    key_rows = keys.reshape(tok_rows, head_count, head_size)
    value_rows = values.reshape(tok_rows, head_count, head_size)
    grad_wide_in = out_grad.astype(jnp.float32)
    enter_decay, leave_decay, passing_decay, weights = shard_masks(
        rates, bounds, first_row, tok_rows
    )
    decayed_keys = (leave_decay[:, :, None] * key_rows.astype(jnp.float32)).astype(jnp.bfloat16)
    state_local = jnp.einsum(
        "the,thf->hef", decayed_keys, value_rows, preferred_element_type=jnp.float32
    )
    ones_init = jnp.ones((head_count,), jnp.float32)
    zero_state = jnp.zeros((head_count, head_size, head_size), jnp.float32)
    state_in = carried_in(
        (passing_decay, state_local), "seq", combine_states, (ones_init, zero_state), False
    )[1]
    state_low = state_in.astype(jnp.bfloat16)
    scores = jnp.einsum("the,she->hts", query_rows, key_rows, preferred_element_type=jnp.float32)
    mixing = (scores * weights).astype(jnp.bfloat16)
    attended = jnp.einsum("hts,shf->thf", mixing, value_rows, preferred_element_type=jnp.float32)
    attended = attended + enter_decay[:, :, None] * jnp.einsum(
        "the,hef->thf", query_rows, state_low, preferred_element_type=jnp.float32
    )
    flat = attended.reshape(tok_rows, feature_width)
    gained = grad_wide_in * gain[None, :]
    square_total = lax.psum(jnp.sum(flat * flat, axis=1), "dp")
    inverse_rms = lax.rsqrt(square_total / all_features + 1e-06)[:, None]
    normed = flat * inverse_rms
    cross_total = lax.psum(jnp.sum(gained * normed, axis=1), "dp")
    cross_mean = (cross_total / all_features)[:, None]
    grad_flat = inverse_rms * (gained - normed * cross_mean)
    grad_mixed = grad_flat.astype(jnp.bfloat16).reshape(tok_rows, head_count, head_size)
    decayed_queries = (enter_decay[:, :, None] * query_rows.astype(jnp.float32)).astype(
        jnp.bfloat16
    )
    state_grad_local = jnp.einsum(
        "the,thf->hef", decayed_queries, grad_mixed, preferred_element_type=jnp.float32
    )
    state_grad_end = carried_in(
        (passing_decay, state_grad_local), "seq", combine_states, (ones_init, zero_state), True
    )[1]
    state_grad_low = state_grad_end.astype(jnp.bfloat16)
    gain_term = jnp.sum(grad_wide_in * normed, axis=0)
    gain_part = lax.psum_scatter(gain_term, "seq", scatter_dimension=0, tiled=True)
    grad_scores = jnp.einsum(
        "thf,shf->hts", grad_mixed, value_rows, preferred_element_type=jnp.float32
    )
    grad_mixing = (grad_scores * weights).astype(jnp.bfloat16)
    query_grad = jnp.einsum(
        "hts,she->the", grad_mixing, key_rows, preferred_element_type=jnp.float32
    )
    query_grad = query_grad + enter_decay[:, :, None] * jnp.einsum(
        "thf,hef->the", grad_mixed, state_low, preferred_element_type=jnp.float32
    )
    key_grad = jnp.einsum(
        "hts,the->she", grad_mixing, query_rows, preferred_element_type=jnp.float32
    )
    key_grad = key_grad + leave_decay[:, :, None] * jnp.einsum(
        "thf,hef->the", value_rows, state_grad_low, preferred_element_type=jnp.float32
    )
    value_grad = jnp.einsum("hts,thf->shf", mixing, grad_mixed, preferred_element_type=jnp.float32)
    value_grad = value_grad + leave_decay[:, :, None] * jnp.einsum(
        "the,hef->thf", key_rows, state_grad_low, preferred_element_type=jnp.float32
    )
    out_shape = (tok_rows, feature_width)
    return (
        query_grad.reshape(out_shape).astype(jnp.bfloat16),
        key_grad.reshape(out_shape).astype(jnp.bfloat16),
        value_grad.reshape(out_shape).astype(jnp.bfloat16),
        gain_part,
    )


def solution(mesh):
    return jax.shard_map(
        shards,
        mesh=mesh,
        in_specs=(
            P("seq", "dp"),
            P("seq", "dp"),
            P("seq", "dp"),
            P("seq", "dp"),
            P("dp"),
            P("dp"),
            P(),
        ),
        out_specs=(P("seq", "dp"), P("seq", "dp"), P("seq", "dp"), P(("dp", "seq"))),
        check_vma=False,
    )
```

profile of v0, /device:TPU:1, one launch (start us, length us, event | category | flops | bytes accessed | tf_op | source)
XLA Modules:
  0.0 516.0 jit_solution(8548812948397911630)
XLA Ops:
  7.3 1.4 fusion.36
  11.3 1.3 compare_convert_fusion
  12.6 1.5 copy.72
  15.7 1.3 fusion.15
  17.1 130.3 %all-reduce = f32[512]{0:T(512)S(1)} all-reduce(f32[512]{0:T(512)S(1)} %get-tuple-element.306), channel_id=2, replica_groups=mesh['dp'=4,'seq'=64] {'seq'}, use_global_device_ids=true, to_apply=%add | all-reduce | flops 512 | bytes 4096
  147.5 1.5 copy.71
  149.6 4.1 multiply_convert_fusion.1
  153.7 2.0 copy-done.1
  155.8 2.8 fusion.17
  158.6 6.0 %all-gather.6.cloned.1.call-done = f32[512,128,128]{2,1,0:T(8,128)} async-done(((f32[8,128,128]{2,1,0:T(8,128)}), f32[512,128,128]{2,1,0:T(8,128)}) %all-gather.6.cloned.1.call-update) | async-done | bytes 33554448 | tf_op jit(solution)/shard_map/all_gather | solution.py:9
  164.6 77.9 %while.30 = (s32[]{:T(128)}, f32[8,128,128]{2,1,0:T(8,128)S(1)}, s32[]{:T(128)}, f32[64,8]{1,0:T(8,128)S(1)}, f32[64,8,128,128]{3,2,1,0:T(8,128)}, /*index=5*/s32[]{:T(128)}, s32[]{:T(128)}) while((s32[]{:T(128)}, f32[8,128,128]{2,1,0:T(8,128)S(1)}, s32[]{:T(128)}, f32[64,8]{1,0:T(8,128)S(1)}, f32[64,8,128,128]{3,2,1,0:T(8,128)}, ...), condition=%wide.region_3.4_spmd.clone, body=%wide.region_2.3_spmd.clone.sunk | while | flops 524292 | bytes 1573073 | solution.py:22
  165.9 1.2 fusion.60
  242.6 3.4 multiply_reduce_fusion
  246.0 8.4 %psum.14 = f32[512]{0:T(512)S(1)} all-reduce(f32[512]{0:T(512)S(1)} %get-tuple-element.314), channel_id=1, replica_groups=mesh['dp'=4,'seq'=64] {'dp'}, use_global_device_ids=true, to_apply=%region_5.6 | all-reduce | flops 512 | bytes 4096 | tf_op jit(solution)/shard_map/psum | solution.py:92
  254.4 3.0 copy.79
  257.4 2.3 fusion.7
  259.7 6.0 %psum.15 = f32[512]{0:T(512)S(1)} all-reduce(f32[512]{0:T(512)S(1)} %get-tuple-element.285), channel_id=1, replica_groups=mesh['dp'=4,'seq'=64] {'dp'}, use_global_device_ids=true, to_apply=%region_7.8 | all-reduce | flops 512 | bytes 4096 | tf_op jit(solution)/shard_map/psum | solution.py:95
  265.7 3.0 fusion.6
  268.8 1.5 copy.97
  270.3 2.5 fusion.16
  273.4 3.9 multiply_convert_fusion
  277.3 1.5 fusion.38
  279.3 1.4 fusion.13
  280.7 2.3 copy.88
  283.0 129.7 %all-reduce.1 = f32[1024]{0:T(1024)S(1)} all-reduce(f32[1024]{0:T(1024)S(1)} %get-tuple-element.284), channel_id=5, replica_groups=mesh['dp'=4,'seq'=64] {'seq'}, use_global_device_ids=true, to_apply=%region_11.12.clone | all-reduce | flops 1024 | bytes 8192
  413.3 4.2 fusion.39
  417.5 78.3 %while.31 = (s32[]{:T(128)}, f32[8,128,128]{2,1,0:T(8,128)S(1)}, s32[]{:T(128)}, f32[64,8]{1,0:T(8,128)S(1)}, f32[64,8,128,128]{3,2,1,0:T(8,128)}, /*index=5*/s32[]{:T(128)}, s32[]{:T(128)}, s32[]{:T(128)}, s32[]{:T(128)}) while((s32[]{:T(128)}, f32[8,128,128]{2,1,0:T(8,128)S(1)}, s32[]{:T(128)}, f32[64,8]{1,0:T(8,128)S(1)}, ...), condition=%wide.region_9.10_spmd.clone, body=%wide.region_8.9_spmd.clone.sunk | while | flops 524296 | bytes 1573135 | solution.py:22
  495.8 1.8 fusion.19
  498.5 1.5 fusion.9
  500.0 2.4 copy.90
  502.3 4.6 fusion.11
  506.9 2.3 copy.89
  (303 shorter events, 155.5 us)
Async XLA Ops:
  7.2 8.5 %copy-start = (bf16[512,1024]{1,0:T(8,128)(2,1)S(1)}, bf16[512,1024]{1,0:T(8,128)(2,1)}, u32[]{:S(2)}) copy-start(bf16[512,1024]{1,0:T(8,128)(2,1)} %param.13) | copy-start | bytes 3145732
  7.2 6.9 %copy-start.12 = (u32[256]{0:T(256)S(1)}, u32[256]{0:T(256)}, u32[]{:S(2)}) copy-start(u32[256]{0:T(256)} %constant.114) | copy-start | bytes 3076
  7.2 8.3 %copy-start.13 = (s32[8]{0:T(128)S(1)}, s32[8]{0:T(128)}, u32[]{:S(2)}) copy-start(s32[8]{0:T(128)} %param.16) | copy-start | bytes 100
  7.2 157.4 %all-gather.6.cloned.1.call-start = ((), (), s32[]{:S(2)}) async-start(), calls=%async_computation | async-start | bytes 34078720 | tf_op jit(solution)/shard_map/all_gather | solution.py:9
  14.1 133.3 %copy-start.5 = (bf16[512,1024]{0,1:T(8,128)(2,1)}, bf16[512,1024]{0,1:T(8,128)(2,1)S(1)}, u32[]{:S(2)}) copy-start(bf16[512,1024]{0,1:T(8,128)(2,1)S(1)} %copy.72) | copy-start | bytes 3145732
  17.0 400.5 %all-gather.8.cloned.1.call-start = ((), (), s32[]{:S(2)}) async-start(), calls=%async_computation.1 | async-start | bytes 34078720 | tf_op jit(solution)/shard_map/all_gather | solution.py:9
  149.0 93.5 %copy-start.3 = (bf16[512,1024]{0,1:T(8,128)(2,1)}, bf16[512,1024]{0,1:T(8,128)(2,1)S(1)}, u32[]{:S(2)}) copy-start(bf16[512,1024]{0,1:T(8,128)(2,1)S(1)} %copy.71) | copy-start | bytes 3145732
  149.2 4.5 copy-start.10
  153.7 2.0 copy-start.1
  254.4 3.0 copy-start.9
  254.4 3.0 copy-start.11
  273.4 3.9 copy-start.6
  277.3 1.9 copy-start.2
  495.8 1.8 copy-start.7
  495.8 2.7 copy-start.8
  500.0 2.4 copy-start.4
Sparse Core Ops, SparseCore 0:
  17.1 147.4 all-gather.5
  272.9 142.7 all-gather.7
where the time goes:
time: 523 us; the launch traced here: 516 us
  blocking collectives  274 us (52%)
  other arithmetic  160 us (31%)
  matrix products  33 us (6%)
  local copies, waits for them, and re-layouts  21.1 us (4%)
  between operations  17 us (3%)
  waiting for transfers between devices  6.07 us (1%)
    unnamed x2, blocking collectives  260 us
    select_n x128, other arithmetic, hop(): return jax.tree.map(lambda a, b: jnp.where(reached, a, b), new, before)  150 us
    unnamed x36, local copies, waits for them, and re-layouts  14.6 us
  transfers between devices with their start and end apart: 2, of which 1 were waited for; matrix products, arithmetic and copies ran while one was open for 4% of the time, Pallas kernels for 0%

commit v1 on v0

v1 whole, which is shorter than its diff:
```python
import functools
import math

import jax
import jax.numpy as jnp
from jax import lax
from jax.experimental import pallas as pl
from jax.experimental.pallas import tpu as pltpu
from jax.sharding import PartitionSpec as P

F32, BF16 = jnp.float32, jnp.bfloat16
HEAD, TOK, HEADS_DEV, STREAM, FEATURES = 128, 512, 8, 32768, 4096
BLOCK_Z, BLOCK_Y = 8 * TOK, 2 * TOK
SMEM = pl.BlockSpec(memory_space=pltpu.SMEM)
VMEM = pl.BlockSpec(memory_space=pltpu.VMEM)


def rate_of(level):
    row = jnp.full((1, HEAD), level.astype(F32), F32)
    slow = jnp.exp(row * (math.log(8.0) / 7.0)) * (-0.25 / STREAM)
    lowest = math.log(4.0 / STREAM)
    fast = -jnp.exp(lowest + (row - 8.0) * ((math.log(1.0 / 32.0) - lowest) / 7.0))
    return jnp.where(row < 8.0, slow, fast)


def starts_before(bounds, place):
    return sum((bounds[i] < place).astype(jnp.int32) for i in range(3))


def carry(rate, bounds, left, right):
    same = (starts_before(bounds, left) == starts_before(bounds, right)) & (left <= right)
    span = jnp.maximum(right - left, 0).astype(F32)
    return jnp.exp(rate * span) * jnp.where(same, 1.0, 0.0).astype(F32)


def place():
    at = lax.axis_index("seq")
    return at, at // 8, (at // 2) % 4, at % 2


def tokens_in(bounds, at):
    first = at * TOK
    entering, leaving = TOK, 0
    for i in range(3):
        local = bounds[i] - first
        entering = jnp.where((local >= 0) & (local < entering), local, entering)
        leaving = jnp.where((local < TOK) & (local > leaving), local, leaving)
    return entering, leaving


def enter_decay(rate, entering):
    t = lax.broadcasted_iota(jnp.int32, (TOK, HEAD), 0)
    return jnp.where(t < entering, jnp.exp(rate * (t + 1).astype(F32)), 0.0)


def leave_decay(rate, leaving):
    t = lax.broadcasted_iota(jnp.int32, (TOK, HEAD), 0)
    return jnp.where(t >= leaving, jnp.exp(rate * (TOK - 1 - t).astype(F32)), 0.0)


def pair_weights(rate, bounds, at, rows, columns, flip):
    shape = (rows[1] - rows[0], columns[1] - columns[0])
    r = lax.broadcasted_iota(jnp.int32, shape, 0) + rows[0]
    c = lax.broadcasted_iota(jnp.int32, shape, 1) + columns[0]
    gap = c - r if flip else r - c
    rcol = lax.broadcasted_iota(jnp.int32, (shape[0], 1), 0) + rows[0]
    crow = lax.broadcasted_iota(jnp.int32, (1, shape[1]), 1) + columns[0]
    first = at * TOK
    er = sum((bounds[i] - first <= rcol).astype(jnp.int32) for i in range(3))
    ec = sum((bounds[i] - first <= crow).astype(jnp.int32) for i in range(3))
    weights = jnp.exp(rate[0, 0] * jnp.maximum(gap, 0).astype(F32))
    return jnp.where((gap >= 0) & (er == ec), weights, 0.0)


def mm(a, b):
    return lax.dot_general(a, b, (((1,), (0,)), ((), ())), preferred_element_type=F32)


def mm_bt(a, b):
    return lax.dot_general(a, b, (((1,), (1,)), ((), ())), preferred_element_type=F32)


def mm_at(a, b):
    return lax.dot_general(a, b, (((0,), (0,)), ((), ())), preferred_element_type=F32)


def call(kernel, outs, grid=None, in_specs=None, out_specs=None, scratch=(), flops=0, moved=0, limit=24):
    extra = {} if grid is None else {"grid": grid}
    return pl.pallas_call(
        kernel,
        out_shape=outs,
        in_specs=in_specs,
        out_specs=out_specs,
        scratch_shapes=list(scratch),
        compiler_params=pltpu.CompilerParams(vmem_limit_bytes=limit << 20),
        cost_estimate=pl.CostEstimate(flops=flops, bytes_accessed=moved, transcendentals=0),
        **extra,
    )


def shape(*dims, dtype=F32):
    return jax.ShapeDtypeStruct(dims, dtype)


def store_states(keep_ref, send_ref, low, high, i):
    _, _, y, c = place()
    spot = pl.ds(pl.multiple_of((i ^ y) * HEAD, HEAD), HEAD)
    keep_ref[spot, :] = jnp.where(c == 0, low, high)
    send_ref[spot, :] = jnp.where(c == 0, high, low)


def local_states_kernel(decay, bounds, k0, k1, v0, v1, keep_ref, send_ref):
    i = pl.program_id(0)
    at = place()[0]
    _, leaving = tokens_in(bounds, at)

    def state(head, k, v):
        weights = leave_decay(rate_of(decay[head]), leaving)
        return mm_at((weights * k[...].astype(F32)).astype(BF16), v[...])

    store_states(keep_ref, send_ref, state(i, k0, v0), state(i + 4, k1, v1), i)


def intra_kernel(decay, bounds, q, k, v, out_ref):
    i = pl.program_id(0)
    at = place()[0]
    rate = rate_of(decay[i])
    half = TOK // 2
    for lo in (0, half):
        rows, columns = (lo, lo + half), (0, lo + half)
        scores = mm_bt(q[lo : lo + half, :], k[0 : lo + half, :])
        mixing = (scores * pair_weights(rate, bounds, at, rows, columns, False)).astype(BF16)
        out_ref[lo : lo + half, :] = mm(mixing, v[0 : lo + half, :])


def chip_kernel(decay, bounds, keep, got, *outs, reverse, gains):
    at, z, y, c = place()
    middle = (at - c + 1) * TOK
    for k in range(4):
        rate = rate_of(decay[4 * c + (y ^ k)])
        if reverse:
            far = carry(rate, bounds, middle - TOK, middle)
            own, other = jnp.where(c == 1, far, 1.0), jnp.where(c == 1, 1.0, far)
        else:
            far = carry(rate, bounds, middle, middle + TOK)
            own, other = jnp.where(c == 0, far, 1.0), jnp.where(c == 0, 1.0, far)
        rows = slice(k * HEAD, (k + 1) * HEAD)
        outs[k][0:HEAD, :] = own * keep[rows, :] + other * got[rows, :]
        if gains:
            tail = slice(4 * HEAD, 4 * HEAD + 8)
            outs[k][HEAD : HEAD + 8, :] = keep[tail, :] + got[tail, :]


def row_kernel(decay, bounds, t0, t1, t2, t3, out, *, reverse, gains):
    at, z, y, c = place()
    rate = rate_of(decay[4 * c + y])
    total = 0.0
    for k, t in enumerate((t0, t1, t2, t3)):
        edge = z * BLOCK_Z + (y ^ k) * BLOCK_Y
        if reverse:
            weight = carry(rate, bounds, z * BLOCK_Z, edge)
        else:
            weight = carry(rate, bounds, edge + BLOCK_Y, (z + 1) * BLOCK_Z)
        total += weight * t[0:HEAD, :]
    out[0:HEAD, :] = total
    if gains:
        tail = slice(HEAD, HEAD + 8)
        out[tail, :] = t0[tail, :] + t1[tail, :] + t2[tail, :] + t3[tail, :]


def half_kernel(decay, bounds, r0, r1, r2, r3, out, *, reverse, gains):
    at, z, y, c = place()
    rate = rate_of(decay[4 * c + y])
    total = 0.0
    for k, r in enumerate((r0, r1, r2, r3)):
        edge = (z ^ k) * BLOCK_Z
        if reverse:
            weight = carry(rate, bounds, 4 * BLOCK_Z, edge)
        else:
            weight = carry(rate, bounds, edge + BLOCK_Z, 4 * BLOCK_Z)
        total += weight * r[0:HEAD, :]
    out[0:HEAD, :] = total
    if gains:
        tail = slice(HEAD, HEAD + 8)
        out[tail, :] = r0[tail, :] + r1[tail, :] + r2[tail, :] + r3[tail, :]


def chips_in_kernel(decay, bounds, r0, r1, r2, r3, far, sent, t0, t1, t2, t3, *outs, reverse, gains):
    at, z, y, c = place()
    rate = rate_of(decay[4 * c + y])
    edge = (z + 1) * BLOCK_Z if reverse else z * BLOCK_Z
    if reverse:
        total = carry(rate, bounds, edge, 4 * BLOCK_Z) * far[0:HEAD, :]
    else:
        total = carry(rate, bounds, 4 * BLOCK_Z, edge) * far[0:HEAD, :]
    for k, r in enumerate((r0, r1, r2, r3)):
        if k == 0:
            continue
        other = (z ^ k) * BLOCK_Z
        if reverse:
            weight = carry(rate, bounds, edge, other)
        else:
            weight = carry(rate, bounds, other + BLOCK_Z, edge)
        total += weight * r[0:HEAD, :]
    for k in range(4):
        here = z * BLOCK_Z + (y ^ k) * BLOCK_Y
        if reverse:
            state = carry(rate, bounds, here + BLOCK_Y, edge) * total
        else:
            state = carry(rate, bounds, edge, here) * total
        for m, t in enumerate((t0, t1, t2, t3)):
            if m == k:
                continue
            there = z * BLOCK_Z + (y ^ m) * BLOCK_Y
            if reverse:
                weight = carry(rate, bounds, here + BLOCK_Y, there)
            else:
                weight = carry(rate, bounds, there + BLOCK_Y, here)
            state += weight * t[0:HEAD, :]
        outs[k][...] = state
    if gains:
        tail = slice(HEAD, HEAD + 8)
        outs[4][...] = sent[tail, :] + far[tail, :]


def cores_in_kernel(decay, bounds, v0, v1, v2, v3, keep, got, mine, other, *, reverse):
    at, z, y, c = place()
    middle = (at - c + 1) * TOK
    for k, v in enumerate((v0, v1, v2, v3)):
        rate = rate_of(decay[4 * c + (y ^ k)])
        if reverse:
            step, deep = carry(rate, bounds, middle, middle + TOK), c == 0
        else:
            step, deep = carry(rate, bounds, middle - TOK, middle), c == 1
        rows = slice(k * HEAD, (k + 1) * HEAD)
        state = v[...]
        mine[rows, :] = jnp.where(deep, step * state + got[rows, :], state)
        other[rows, :] = jnp.where(deep, state, step * state + keep[rows, :])


def state_of(mine, other, head):
    _, _, y, c = place()
    spot = pl.ds(pl.multiple_of(((head % 4) ^ y) * HEAD, HEAD), HEAD)
    return jnp.where(head // 4 == c, mine[spot, :], other[spot, :]).astype(BF16)


def attended_kernel(decay, bounds, q, intra, grad, gain, mine, other, out_ref, sums_ref, squares, crosses):
    i = pl.program_id(0)
    at = place()[0]
    entering, _ = tokens_in(bounds, at)
    weights = enter_decay(rate_of(decay[i]), entering)
    out = intra[...] + weights * mm(q[...], state_of(mine, other, i))
    out_ref[...] = out
    gained = grad[...].astype(F32) * gain[pl.ds(i, 1), :]

    @pl.when(i == 0)
    def _():
        squares[...] = out * out
        crosses[...] = out * gained

    @pl.when(i > 0)
    def _():
        squares[...] += out * out
        crosses[...] += out * gained

    @pl.when(i == HEADS_DEV - 1)
    def _():
        sums_ref[0:4, :] = jnp.broadcast_to(jnp.sum(squares[...].T, axis=0, keepdims=True), (4, TOK))
        sums_ref[4:8, :] = jnp.broadcast_to(jnp.sum(crosses[...].T, axis=0, keepdims=True), (4, TOK))


def mixed_kernel(decay, bounds, s0, s1, s2, s3, o0, o1, g0, g1, q0, q1, gain, d0, d1, keep, send, inverse, mean):
    i = pl.program_id(0)
    at = place()[0]
    entering, _ = tokens_in(bounds, at)

    @pl.when(i == 0)
    def _():
        sums = s0[...] + s1[...] + s2[...] + s3[...]
        r = lax.rsqrt(sums[0:1, :] * (1.0 / FEATURES) + 1e-06)
        inverse[...] = jnp.broadcast_to(r, (HEAD, TOK)).T
        mean[...] = jnp.broadcast_to(sums[4:5, :] * r * (1.0 / FEATURES), (HEAD, TOK)).T

    tail = 4 * HEAD

    def state(head, o, g, q, d):
        normed = inverse[...] * o[...]
        wide = g[...].astype(F32)
        low = (inverse[...] * (wide * gain[pl.ds(head, 1), :] - normed * mean[...])).astype(BF16)
        d[...] = low
        term = jnp.sum(wide * normed, axis=0, keepdims=True)
        keep[pl.ds(tail + head, 1), :] = term
        send[pl.ds(tail + head, 1), :] = term
        weights = enter_decay(rate_of(decay[head]), entering)
        return mm_at((weights * q[...].astype(F32)).astype(BF16), low)

    store_states(keep, send, state(i, o0, g0, q0, d0), state(i + 4, o1, g1, q1, d1), i)


def grads_kernel(decay, bounds, q, k, v, d0, d1, mine, other, dq, dk, dv):
    i = pl.program_id(0)
    at = place()[0]
    rate = rate_of(decay[i])
    entering, _ = tokens_in(bounds, at)
    half = TOK // 2
    d = jnp.where(i < 4, d0[...], d1[...])
    state = state_of(mine, other, i)
    weights = enter_decay(rate, entering)
    for lo in (0, half):
        hi = lo + half
        w = pair_weights(rate, bounds, at, (lo, hi), (0, hi), False)
        mixing = (mm_bt(d[lo:hi, :], v[0:hi, :]) * w).astype(BF16)
        grad = mm(mixing, k[0:hi, :]) + weights[lo:hi, :] * mm_bt(d[lo:hi, :], state)
        dq[lo:hi, :] = grad.astype(BF16)
        w = pair_weights(rate, bounds, at, (lo, hi), (lo, TOK), True)
        mixing = (mm_bt(v[lo:hi, :], d[lo:TOK, :]) * w).astype(BF16)
        dk[lo:hi, :] = mm(mixing, q[lo:TOK, :])
        mixing = (mm_bt(k[lo:hi, :], q[lo:TOK, :]) * w).astype(BF16)
        dv[lo:hi, :] = mm(mixing, d[lo:TOK, :])


def last_kernel(decay, bounds, k, v, dk_in, dv_in, mine, other, dk, dv):
    i = pl.program_id(0)
    at = place()[0]
    _, leaving = tokens_in(bounds, at)
    weights = leave_decay(rate_of(decay[i]), leaving)
    state = state_of(mine, other, i)
    dk[...] = (dk_in[...] + weights * mm_bt(v[...], state)).astype(BF16)
    dv[...] = (dv_in[...] + weights * mm(k[...], state)).astype(BF16)


def index(z, y, c):
    return (z * 4 + y) * 2 + c


def exchange(array, dz=0, dy=0, dc=0):
    pairs = [
        (index(z, y, c), index(z ^ dz, y ^ dy, c ^ dc))
        for z in range(8)
        for y in range(4)
        for c in range(2)
    ]
    return lax.ppermute(array, "seq", pairs)


def carried(keep, send, decay, bounds, reverse, gains):
    extra = 8 if gains else 0
    small = shape(HEAD + extra, HEAD)

    def step(kernel, outs, *args, **more):
        return call(
            functools.partial(kernel, reverse=reverse, **more),
            outs,
            in_specs=[SMEM, SMEM] + [VMEM] * len(args),
            out_specs=jax.tree.map(lambda _: VMEM, outs),
            limit=8,
        )(decay, bounds, *args)

    got = exchange(send, dc=1)
    chips = step(chip_kernel, [small] * 4, keep, got, gains=gains)
    chips = [chips[0]] + [exchange(chips[k], dy=k) for k in (1, 2, 3)]
    row = step(row_kernel, small, *chips, gains=gains)
    rows = [row] + [exchange(row, dz=k) for k in (1, 2, 3)]
    sent = step(half_kernel, small, *rows, gains=gains)
    far = exchange(sent, dz=7)
    outs = [shape(HEAD, HEAD)] * 4 + ([shape(8, HEAD)] if gains else [])
    outs = step(chips_in_kernel, outs, *rows, far, sent, *chips, gains=gains)
    states = [outs[0]] + [exchange(outs[k], dy=k) for k in (1, 2, 3)]
    mine, other = step(cores_in_kernel, [shape(4 * HEAD, HEAD)] * 2, *states, keep, got)
    other = exchange(other, dc=1)
    return mine, other, (outs[4] if gains else None)


def shards(queries, keys, values, out_grad, gain, decay, bounds):
    gain = gain.reshape(HEADS_DEV, HEAD)
    low = pl.BlockSpec((TOK, HEAD), lambda i: (0, i))
    high = pl.BlockSpec((TOK, HEAD), lambda i: (0, i + 4))
    either0 = pl.BlockSpec((TOK, HEAD), lambda i: (0, jnp.minimum(i, 3)))
    either1 = pl.BlockSpec((TOK, HEAD), lambda i: (0, jnp.maximum(i - 4, 0)))

    def whole(*dims):
        return pl.BlockSpec(dims, lambda i: (0,) * len(dims))

    states = whole(4 * HEAD, HEAD)
    width = HEADS_DEV * HEAD
    small_mm = 2 * TOK * HEAD * HEAD * HEADS_DEV
    big_mm = 2 * TOK * TOK * HEAD * HEADS_DEV * 3 // 4

    keep, send = call(
        local_states_kernel,
        [shape(4 * HEAD, HEAD)] * 2,
        grid=(4,),
        in_specs=[SMEM, SMEM, low, high, low, high],
        out_specs=[states] * 2,
        flops=small_mm,
        moved=3 << 20,
    )(decay, bounds, keys, keys, values, values)
    intra = call(
        intra_kernel,
        shape(TOK, width),
        grid=(HEADS_DEV,),
        in_specs=[SMEM, SMEM, low, low, low],
        out_specs=low,
        flops=2 * big_mm,
        moved=5 << 20,
    )(decay, bounds, queries, keys, values)
    mine, other, _ = carried(keep, send, decay, bounds, False, False)
    attended, sums = call(
        attended_kernel,
        [shape(TOK, width), shape(8, TOK)],
        grid=(HEADS_DEV,),
        in_specs=[SMEM, SMEM, low, low, low, whole(HEADS_DEV, HEAD), states, states],
        out_specs=[low, whole(8, TOK)],
        scratch=[pltpu.VMEM((TOK, HEAD), F32)] * 2,
        flops=small_mm,
        moved=7 << 20,
    )(decay, bounds, queries, intra, out_grad, gain, mine, other)
    others = [lax.ppermute(sums, "dp", [(i, i ^ k) for i in range(4)]) for k in (1, 2, 3)]
    sums_spec = whole(8, TOK)
    grown = whole(4 * HEAD + 8, HEAD)
    d0, d1, keep, send = call(
        mixed_kernel,
        [shape(TOK, width // 2, dtype=BF16)] * 2 + [shape(4 * HEAD + 8, HEAD)] * 2,
        grid=(4,),
        in_specs=[SMEM, SMEM] + [sums_spec] * 4 + [low, high] * 3 + [whole(HEADS_DEV, HEAD)],
        out_specs=[low, low, grown, grown],
        scratch=[pltpu.VMEM((TOK, HEAD), F32)] * 2,
        flops=small_mm,
        moved=7 << 20,
    )(decay, bounds, sums, *others, attended, attended, out_grad, out_grad, queries, queries, gain)
    dq, dk, dv = call(
        grads_kernel,
        [shape(TOK, width, dtype=BF16), shape(TOK, width), shape(TOK, width)],
        grid=(HEADS_DEV,),
        in_specs=[SMEM, SMEM, low, low, low, either0, either1, states, states],
        out_specs=[low, low, low],
        flops=6 * big_mm,
        moved=9 << 20,
    )(decay, bounds, queries, keys, values, d0, d1, mine, other)
    mine, other, gains = carried(keep, send, decay, bounds, True, True)
    dk, dv = call(
        last_kernel,
        [shape(TOK, width, dtype=BF16)] * 2,
        grid=(HEADS_DEV,),
        in_specs=[SMEM, SMEM, low, low, low, low, states, states],
        out_specs=[low, low],
        flops=2 * small_mm,
        moved=8 << 20,
    )(decay, bounds, keys, values, dk, dv, mine, other)
    part = lax.dynamic_slice(gains.reshape(width), (lax.axis_index("seq") * 16,), (16,))
    return dq, dk, dv, part


def solution(mesh):
    return jax.shard_map(
        shards,
        mesh=mesh,
        in_specs=(
            P("seq", "dp"),
            P("seq", "dp"),
            P("seq", "dp"),
            P("seq", "dp"),
            P("dp"),
            P("dp"),
            P(),
        ),
        out_specs=(P("seq", "dp"), P("seq", "dp"), P("seq", "dp"), P(("dp", "seq"))),
        check_vma=False,
    )
```

time: 523 us -> 131 us (0.25); the launches traced: 516 us -> 131 us
  blocking collectives: 274 us -> 0 us
  other arithmetic: 160 us -> 0 us
  starting transfers between devices: 0.08 us -> 49.3 us
  Pallas kernels: 0 us -> 41 us
  matrix products: 33 us -> 0 us
  waiting for transfers between devices: 6.07 us -> 31.5 us
  between operations: 17 us -> 0.9 us
  local copies, waits for them, and re-layouts: 21.1 us -> 8.14 us
    unnamed x2 -> x0, blocking collectives: 260 us -> none
    select_n x128 -> x0, other arithmetic: 150 us -> none  [hop(): return jax.tree.map(lambda a, b: jnp.where(reached, a, b), new, before)]
    ppermute x0 -> x27, starting transfers between devices: none -> 49.3 us  [the longest x24 46 us: exchange(): return lax.ppermute(array, 'seq', pairs)]
    pallas_call x0 -> x16, Pallas kernels: none -> 41 us  [the longest x1 11.9 us: shards(): call(grads_kernel, [shape(TOK, width, dtype=BF16), shape(TOK, width), sha...]
    dot_general x12 -> x0, matrix products: 33 us -> none  [the longest x1 4.61 us: shards(): jnp.einsum('hts,the->she', grad_mixing, query_rows, preferred_element_typ...]
    ppermute x0 -> x27, waiting for transfers between devices: none -> 31.5 us  [the longest x24 28.2 us: exchange(): return lax.ppermute(array, 'seq', pairs)]
    psum x2 -> x0, blocking collectives: 14.4 us -> none  [the longest x1 8.38 us: shards(): square_total = lax.psum(jnp.sum(flat * flat, axis=1), 'dp')]
    unnamed x36 -> x38, local copies, waits for them, and re-layouts: 14.6 us -> 7.56 us
  transfers between devices with their start and end apart: 2 -> 27, of which waited for: 1 -> 18; matrix products, arithmetic and copies ran while one was open for 4% -> 0% of each run, Pallas kernels for 0% -> 14%
where the time goes in v1:
time: 131 us
  starting transfers between devices  49.3 us (38%)
  Pallas kernels  41 us (31%)
  waiting for transfers between devices  31.5 us (24%)
  local copies, waits for them, and re-layouts  8.14 us (6%)
    ppermute x24, starting transfers between devices, exchange(): return lax.ppermute(array, 'seq', pairs)  46 us
    ppermute x24, waiting for transfers between devices, exchange(): return lax.ppermute(array, 'seq', pairs)  28.2 us
    pallas_call x1, Pallas kernels, shards(): call(grads_kernel, [shape(TOK, width, dtype=BF16), shape(TOK, width), sha...  11.9 us
    unnamed x38, local copies, waits for them, and re-layouts  7.56 us
    pallas_call x10, Pallas kernels, step(): call(functools.partial(kernel, reverse=reverse, **more), outs, in_specs=[...  7.09 us
    pallas_call x1, Pallas kernels, shards(): call(intra_kernel, shape(TOK, width), grid=(HEADS_DEV,), in_specs=[SMEM,...  5.9 us
    pallas_call x1, Pallas kernels, shards(): call(last_kernel, [shape(TOK, width, dtype=BF16)] * 2, grid=(HEADS_DEV,),...  5.67 us
    pallas_call x1, Pallas kernels, shards(): call(attended_kernel, [shape(TOK, width), shape(8, TOK)], grid=(HEADS_DEV...  4.05 us
  transfers between devices with their start and end apart: 27, of which 18 were waited for; matrix products, arithmetic and copies ran while one was open for 0% of the time, Pallas kernels for 14%

profile of v1, /device:TPU:1, one launch (start us, length us, event | category | flops | bytes accessed | tf_op | source)
XLA Modules:
  0.0 130.8 jit_solution(5015312128316019454)
XLA Ops:
  4.4 2.7 %shard_map.103 = (f32[512,128]{1,0:T(8,128)S(1)}, f32[512,128]{1,0:T(8,128)S(1)}) custom-call(s32[8]{0:T(128)S(1)} %copy-done.10, s32[3]{0:T(128)S(1)} %copy-done.12, bf16[512,1024]{1,0:T(8,128)(2,1)S(1)} %copy-done, bf16[512,1024]{1,0:T(8,128)(2,1)S(1)} %copy-done, bf16[512,1024]{1,0:T(8,128)(2,1)S(1)} %copy-done.2, bf16[512,1024]{1,0:T(8,128)(2,1)S(1)} %copy-done.2), custom_call_target="tpu_custom_call" | custom-call | flops 134217728 | bytes 3145728 | tf_op jit(solution)/shard_map/pallas_call | solution.py:389
  7.1 3.3 %collective-permute-start = (f32[512,128]{1,0:T(8,128)S(1)}, f32[512,128]{1,0:T(8,128)S(1)}, u32[]{:S(2)}, u32[]{:S(2)}) collective-permute-start(f32[512,128]{1,0:T(8,128)S(1)} %get-tuple-element.39), channel_id=1, source_target_pairs={{0,1},{1,0},{2,3},{3,2},{4,5},{5,4},{6,7},{7,6},{8,9},{9,8},{10,11... | collective-permute-start | bytes 786440 | tf_op jit(solution)/shard_map/ppermute | solution.py:343
  12.4 2.2 %collective-permute-start.2 = (f32[128,128]{1,0:T(8,128)S(1)}, f32[128,128]{1,0:T(8,128)S(1)}, u32[]{:S(2)}, u32[]{:S(2)}) collective-permute-start(f32[128,128]{1,0:T(8,128)S(1)} %get-tuple-element.42), channel_id=1, source_target_pairs={{0,4},{1,5},{2,6},{3,7},{4,0},{5,1},{6,2},{7,3},{8,12},{9,13},{10,... | collective-permute-start | bytes 196616 | tf_op jit(solution)/shard_map/ppermute | solution.py:343
  14.5 1.7 %collective-permute-start.3 = (f32[128,128]{1,0:T(8,128)S(1)}, f32[128,128]{1,0:T(8,128)S(1)}, u32[]{:S(2)}, u32[]{:S(2)}) collective-permute-start(f32[128,128]{1,0:T(8,128)S(1)} %get-tuple-element.43), channel_id=1, source_target_pairs={{0,6},{1,7},{2,4},{3,5},{4,2},{5,3},{6,0},{7,1},{8,14},{9,15},{10,... | collective-permute-start | bytes 196616 | tf_op jit(solution)/shard_map/ppermute | solution.py:343
  16.2 1.8 %collective-permute-done.2.t2 = f32[128,128]{1,0:T(8,128)S(1)} collective-permute-done((f32[128,128]{1,0:T(8,128)S(1)}, f32[128,128]{1,0:T(8,128)S(1)}, u32[]{:S(2)}, u32[]{:S(2)}) %collective-permute-start.2) | collective-permute-done | bytes 65568 | tf_op jit(solution)/shard_map/ppermute | solution.py:343
  19.7 4.3 %collective-permute-start.6 = (f32[128,128]{1,0:T(8,128)S(1)}, f32[128,128]{1,0:T(8,128)S(1)}, u32[]{:S(2)}, u32[]{:S(2)}) collective-permute-start(f32[128,128]{1,0:T(8,128)S(1)} %shard_map.105.r0), channel_id=1, source_target_pairs={{0,24},{1,25},{2,26},{3,27},{4,28},{5,29},{6,30},{7,31},{8,16},{9,... | collective-permute-start | bytes 196616 | tf_op jit(solution)/shard_map/ppermute | solution.py:343
  25.7 3.0 %collective-permute-done.5.r2 = f32[128,128]{1,0:T(8,128)S(1)} collective-permute-done((f32[128,128]{1,0:T(8,128)S(1)}, f32[128,128]{1,0:T(8,128)S(1)}, u32[]{:S(2)}, u32[]{:S(2)}) %collective-permute-start.5) | collective-permute-done | bytes 65568 | tf_op jit(solution)/shard_map/ppermute | solution.py:343
  29.3 5.1 %collective-permute-start.7 = (f32[128,128]{1,0:T(8,128)S(1)}, f32[128,128]{1,0:T(8,128)S(1)}, u32[]{:S(2)}, u32[]{:S(2)}) collective-permute-start(f32[128,128]{1,0:T(8,128)S(1)} %shard_map.106.sent), channel_id=1, source_target_pairs={{0,56},{1,57},{2,58},{3,59},{4,60},{5,61},{6,62},{7,63},{8,48},{9,... | collective-permute-start | bytes 196616 | tf_op jit(solution)/shard_map/ppermute | solution.py:343
  34.4 1.7 %collective-permute-done.7.far = f32[128,128]{1,0:T(8,128)S(1)} collective-permute-done((f32[128,128]{1,0:T(8,128)S(1)}, f32[128,128]{1,0:T(8,128)S(1)}, u32[]{:S(2)}, u32[]{:S(2)}) %collective-permute-start.7) | collective-permute-done | bytes 65568 | tf_op jit(solution)/shard_map/ppermute | solution.py:343
  37.2 2.6 %collective-permute-start.9 = (f32[128,128]{1,0:T(8,128)S(1)}, f32[128,128]{1,0:T(8,128)S(1)}, u32[]{:S(2)}, u32[]{:S(2)}) collective-permute-start(f32[128,128]{1,0:T(8,128)S(1)} %get-tuple-element.46), channel_id=1, source_target_pairs={{0,4},{1,5},{2,6},{3,7},{4,0},{5,1},{6,2},{7,3},{8,12},{9,13},{10,... | collective-permute-start | bytes 196616 | tf_op jit(solution)/shard_map/ppermute | solution.py:343
  40.7 1.4 %collective-permute-done.9.v2 = f32[128,128]{1,0:T(8,128)S(1)} collective-permute-done((f32[128,128]{1,0:T(8,128)S(1)}, f32[128,128]{1,0:T(8,128)S(1)}, u32[]{:S(2)}, u32[]{:S(2)}) %collective-permute-start.9) | collective-permute-done | bytes 65568 | tf_op jit(solution)/shard_map/ppermute | solution.py:343
  42.1 2.0 %collective-permute-done.10.v3 = f32[128,128]{1,0:T(8,128)S(1)} collective-permute-done((f32[128,128]{1,0:T(8,128)S(1)}, f32[128,128]{1,0:T(8,128)S(1)}, u32[]{:S(2)}, u32[]{:S(2)}) %collective-permute-start.10) | collective-permute-done | bytes 65568 | tf_op jit(solution)/shard_map/ppermute | solution.py:343
  44.7 4.3 %collective-permute-start.11 = (f32[512,128]{1,0:T(8,128)S(1)}, f32[512,128]{1,0:T(8,128)S(1)}, u32[]{:S(2)}, u32[]{:S(2)}) collective-permute-start(f32[512,128]{1,0:T(8,128)S(1)} %get-tuple-element.49), channel_id=1, source_target_pairs={{0,1},{1,0},{2,3},{3,2},{4,5},{5,4},{6,7},{7,6},{8,9},{9,8},{10,11... | collective-permute-start | bytes 786440 | tf_op jit(solution)/shard_map/ppermute | solution.py:343
  49.0 5.9 %shard_map.102.intra = f32[512,1024]{1,0:T(8,128)S(1)} custom-call(s32[8]{0:T(128)S(1)} %copy-done.10, s32[3]{0:T(128)S(1)} %copy-done.12, bf16[512,1024]{1,0:T(8,128)(2,1)S(1)} %copy-done.4, bf16[512,1024]{1,0:T(8,128)(2,1)S(1)} %copy-done.1, bf16[512,1024]{1,0:T(8,128)(2,1)S(1)} %copy-done.2), custom_call_target="tpu_custom_call" | custom-call | flops 805306368 | bytes 5242880 | tf_op jit(solution)/shard_map/pallas_call | solution.py:398
  55.0 4.0 %shard_map.109 = (f32[512,1024]{1,0:T(8,128)S(1)}, f32[8,512]{1,0:T(8,128)S(1)}) custom-call(s32[8]{0:T(128)S(1)} %copy-done.10, s32[3]{0:T(128)S(1)} %copy-done.12, bf16[512,1024]{1,0:T(8,128)(2,1)S(1)} %copy-done.4, f32[512,1024]{1,0:T(8,128)S(1)} %shard_map.102.intra, bf16[512,1024]{1,0:T(8,128)(2,1)S(1)} %copy-done.5, f32[8,128]{1,0:T(8,128)S(1)} %bitcast.2, ...), custom_call_target="tpu_custom_call" | custom-call | flops 134217728 | bytes 7340032 | tf_op jit(solution)/shard_map/pallas_call | solution.py:408
  59.0 2.6 %collective-permute-start.14 = (f32[8,512]{1,0:T(8,128)S(1)}, f32[8,512]{1,0:T(8,128)S(1)}, u32[]{:S(2)}, u32[]{:S(2)}) collective-permute-start(f32[8,512]{1,0:T(8,128)S(1)} %get-tuple-element.50.s0), channel_id=1, source_target_pairs={{0,192},{64,128},{128,64},{192,0},{1,193},{65,129},{129,65},{193,1... | collective-permute-start | bytes 49160 | tf_op jit(solution)/shard_map/ppermute | solution.py:418
  62.9 2.8 %collective-permute-done.13.s2 = f32[8,512]{1,0:T(8,128)S(1)} collective-permute-done((f32[8,512]{1,0:T(8,128)S(1)}, f32[8,512]{1,0:T(8,128)S(1)}, u32[]{:S(2)}, u32[]{:S(2)}) %collective-permute-start.13) | collective-permute-done | bytes 16416 | tf_op jit(solution)/shard_map/ppermute | solution.py:418
  65.7 3.8 %shard_map.110 = (bf16[512,512]{1,0:T(8,128)(2,1)S(1)}, bf16[512,512]{1,0:T(8,128)(2,1)S(1)}, f32[520,128]{1,0:T(8,128)S(1)}, f32[520,128]{1,0:T(8,128)S(1)}) custom-call(s32[8]{0:T(128)S(1)} %copy-done.10, s32[3]{0:T(128)S(1)} %copy-done.12, f32[8,512]{1,0:T(8,128)S(1)} %get-tuple-element.50.s0, f32[8,512]{1,0:T(8,128)S(1)} %collective-permute-done.12.s1, ...), custom_call_target="tpu_custom_call" | custom-call | flops 134217728 | bytes 7340032 | tf_op jit(solution)/shard_map/pallas_call | solution.py:421
  69.5 1.7 %collective-permute-start.15 = (f32[520,128]{1,0:T(8,128)S(1)}, f32[520,128]{1,0:T(8,128)S(1)}, u32[]{:S(2)}, u32[]{:S(2)}) collective-permute-start(f32[520,128]{1,0:T(8,128)S(1)} %get-tuple-element.58), channel_id=1, source_target_pairs={{0,1},{1,0},{2,3},{3,2},{4,5},{5,4},{6,7},{7,6},{8,9},{9,8},{10,11... | collective-permute-start | bytes 798728 | tf_op jit(solution)/shard_map/ppermute | solution.py:343
  73.2 2.7 %collective-permute-start.17 = (f32[136,128]{1,0:T(8,128)S(1)}, f32[136,128]{1,0:T(8,128)S(1)}, u32[]{:S(2)}, u32[]{:S(2)}) collective-permute-start(f32[136,128]{1,0:T(8,128)S(1)} %get-tuple-element.61), channel_id=1, source_target_pairs={{0,4},{1,5},{2,6},{3,7},{4,0},{5,1},{6,2},{7,3},{8,12},{9,13},{10,... | collective-permute-start | bytes 208904 | tf_op jit(solution)/shard_map/ppermute | solution.py:343
  77.0 1.9 %collective-permute-done.17.t2 = f32[136,128]{1,0:T(8,128)S(1)} collective-permute-done((f32[136,128]{1,0:T(8,128)S(1)}, f32[136,128]{1,0:T(8,128)S(1)}, u32[]{:S(2)}, u32[]{:S(2)}) %collective-permute-start.17) | collective-permute-done | bytes 69664 | tf_op jit(solution)/shard_map/ppermute | solution.py:343
  78.9 1.6 %collective-permute-done.18.t3 = f32[136,128]{1,0:T(8,128)S(1)} collective-permute-done((f32[136,128]{1,0:T(8,128)S(1)}, f32[136,128]{1,0:T(8,128)S(1)}, u32[]{:S(2)}, u32[]{:S(2)}) %collective-permute-start.18) | collective-permute-done | bytes 69664 | tf_op jit(solution)/shard_map/ppermute | solution.py:343
  84.7 1.5 %collective-permute-done.21.r3 = f32[136,128]{1,0:T(8,128)S(1)} collective-permute-done((f32[136,128]{1,0:T(8,128)S(1)}, f32[136,128]{1,0:T(8,128)S(1)}, u32[]{:S(2)}, u32[]{:S(2)}) %collective-permute-start.21) | collective-permute-done | bytes 69664 | tf_op jit(solution)/shard_map/ppermute | solution.py:343
  86.3 2.9 %collective-permute-done.20.r2 = f32[136,128]{1,0:T(8,128)S(1)} collective-permute-done((f32[136,128]{1,0:T(8,128)S(1)}, f32[136,128]{1,0:T(8,128)S(1)}, u32[]{:S(2)}, u32[]{:S(2)}) %collective-permute-start.20) | collective-permute-done | bytes 69664 | tf_op jit(solution)/shard_map/ppermute | solution.py:343
  89.8 2.7 %collective-permute-start.22 = (f32[136,128]{1,0:T(8,128)S(1)}, f32[136,128]{1,0:T(8,128)S(1)}, u32[]{:S(2)}, u32[]{:S(2)}) collective-permute-start(f32[136,128]{1,0:T(8,128)S(1)} %shard_map.114.sent), channel_id=1, source_target_pairs={{0,56},{1,57},{2,58},{3,59},{4,60},{5,61},{6,62},{7,63},{8,48},{9,... | collective-permute-start | bytes 208904 | tf_op jit(solution)/shard_map/ppermute | solution.py:343
  92.5 2.5 %collective-permute-done.22.far = f32[136,128]{1,0:T(8,128)S(1)} collective-permute-done((f32[136,128]{1,0:T(8,128)S(1)}, f32[136,128]{1,0:T(8,128)S(1)}, u32[]{:S(2)}, u32[]{:S(2)}) %collective-permute-start.22) | collective-permute-done | bytes 69664 | tf_op jit(solution)/shard_map/ppermute | solution.py:343
  96.2 2.3 %collective-permute-start.24 = (f32[128,128]{1,0:T(8,128)S(1)}, f32[128,128]{1,0:T(8,128)S(1)}, u32[]{:S(2)}, u32[]{:S(2)}) collective-permute-start(f32[128,128]{1,0:T(8,128)S(1)} %get-tuple-element.65), channel_id=1, source_target_pairs={{0,4},{1,5},{2,6},{3,7},{4,0},{5,1},{6,2},{7,3},{8,12},{9,13},{10,... | collective-permute-start | bytes 196616 | tf_op jit(solution)/shard_map/ppermute | solution.py:343
  100.9 2.0 %collective-permute-done.25.v3 = f32[128,128]{1,0:T(8,128)S(1)} collective-permute-done((f32[128,128]{1,0:T(8,128)S(1)}, f32[128,128]{1,0:T(8,128)S(1)}, u32[]{:S(2)}, u32[]{:S(2)}) %collective-permute-start.25) | collective-permute-done | bytes 65568 | tf_op jit(solution)/shard_map/ppermute | solution.py:343
  102.9 1.3 %shard_map.116 = (f32[512,128]{1,0:T(8,128)S(1)}, f32[512,128]{1,0:T(8,128)}) custom-call(s32[8]{0:T(128)S(1)} %copy-done.10, s32[3]{0:T(128)S(1)} %copy-done.12, f32[128,128]{1,0:T(8,128)S(1)} %get-tuple-element.63.v0, f32[128,128]{1,0:T(8,128)S(1)} %collective-permute-done.23.v1, f32[128,128]{1,0:T(8,128)S(1)} %collective-permute-done.24.v2, ...), custom_call_target="tpu_custom_call" | custom-call | tf_op jit(solution)/shard_map/pallas_call | solution.py:351
  104.9 4.7 %collective-permute-start.26 = (f32[512,128]{1,0:T(8,128)}, f32[512,128]{1,0:T(8,128)}, u32[]{:S(2)}, u32[]{:S(2)}) collective-permute-start(f32[512,128]{1,0:T(8,128)} %get-tuple-element.68), channel_id=1, source_target_pairs={{0,1},{1,0},{2,3},{3,2},{4,5},{5,4},{6,7},{7,6},{8,9},{9,8},{10,11... | collective-permute-start | bytes 786440 | tf_op jit(solution)/shard_map/ppermute | solution.py:343
  112.7 11.9 %shard_map.111 = (bf16[512,1024]{1,0:T(8,128)(2,1)}, f32[512,1024]{1,0:T(8,128)S(1)}, f32[512,1024]{1,0:T(8,128)S(1)}) custom-call(s32[8]{0:T(128)S(1)} %copy-done.11, s32[3]{0:T(128)S(1)} %copy-done.13, bf16[512,1024]{1,0:T(8,128)(2,1)S(1)} %copy-done.4, bf16[512,1024]{1,0:T(8,128)(2,1)S(1)} %copy-done.1, bf16[512,1024]{1,0:T(8,128)(2,1)S(1)} %copy-done.3, ...), custom_call_target="tpu_custom_call" | custom-call | flops 2415919104 | bytes 9437184 | tf_op jit(solution)/shard_map/pallas_call | solution.py:431
  125.2 5.7 %shard_map.117 = (bf16[512,1024]{1,0:T(8,128)(2,1)}, bf16[512,1024]{1,0:T(8,128)(2,1)}) custom-call(s32[8]{0:T(128)S(1)} %copy-done.11, s32[3]{0:T(128)S(1)} %copy-done.13, bf16[512,1024]{1,0:T(8,128)(2,1)S(1)} %copy-done.1, bf16[512,1024]{1,0:T(8,128)(2,1)S(1)} %copy-done.3, f32[512,1024]{1,0:T(8,128)S(1)} %get-tuple-element.55.dk_in, ...), custom_call_target="tpu_custom_call" | custom-call | flops 268435456 | bytes 8388608 | tf_op jit(solution)/shard_map/pallas_call | solution.py:441
  (77 shorter events, 29.5 us)
Async XLA Ops:
  7.1 41.9 %copy-start.1 = (bf16[512,1024]{1,0:T(8,128)(2,1)S(1)}, bf16[512,1024]{1,0:T(8,128)(2,1)}, u32[]{:S(2)}) copy-start(bf16[512,1024]{1,0:T(8,128)(2,1)} %k.5) | copy-start | bytes 3145732
  7.1 41.9 %copy-start.4 = (bf16[512,1024]{1,0:T(8,128)(2,1)S(1)}, bf16[512,1024]{1,0:T(8,128)(2,1)}, u32[]{:S(2)}) copy-start(bf16[512,1024]{1,0:T(8,128)(2,1)} %q.5) | copy-start | bytes 3145732
  7.1 4.5 %collective-permute-start = (f32[512,128]{1,0:T(8,128)S(1)}, f32[512,128]{1,0:T(8,128)S(1)}, u32[]{:S(2)}, u32[]{:S(2)}) collective-permute-start(f32[512,128]{1,0:T(8,128)S(1)} %get-tuple-element.39), channel_id=1, source_target_pairs={{0,1},{1,0},{2,3},{3,2},{4,5},{5,4},{6,7},{7,6},{8,9},{9,8},{10,11... | collective-permute-start | bytes 786440 | tf_op jit(solution)/shard_map/ppermute | solution.py:343
  12.3 3.9 %collective-permute-start.1 = (f32[128,128]{1,0:T(8,128)S(1)}, f32[128,128]{1,0:T(8,128)S(1)}, u32[]{:S(2)}, u32[]{:S(2)}) collective-permute-start(f32[128,128]{1,0:T(8,128)S(1)} %get-tuple-element.41), channel_id=1, source_target_pairs={{0,2},{1,3},{2,0},{3,1},{4,6},{5,7},{6,4},{7,5},{8,10},{9,11},{10,... | collective-permute-start | bytes 196616 | tf_op jit(solution)/shard_map/ppermute | solution.py:343
  12.4 5.7 %collective-permute-start.2 = (f32[128,128]{1,0:T(8,128)S(1)}, f32[128,128]{1,0:T(8,128)S(1)}, u32[]{:S(2)}, u32[]{:S(2)}) collective-permute-start(f32[128,128]{1,0:T(8,128)S(1)} %get-tuple-element.42), channel_id=1, source_target_pairs={{0,4},{1,5},{2,6},{3,7},{4,0},{5,1},{6,2},{7,3},{8,12},{9,13},{10,... | collective-permute-start | bytes 196616 | tf_op jit(solution)/shard_map/ppermute | solution.py:343
  14.5 4.6 %collective-permute-start.3 = (f32[128,128]{1,0:T(8,128)S(1)}, f32[128,128]{1,0:T(8,128)S(1)}, u32[]{:S(2)}, u32[]{:S(2)}) collective-permute-start(f32[128,128]{1,0:T(8,128)S(1)} %get-tuple-element.43), channel_id=1, source_target_pairs={{0,6},{1,7},{2,4},{3,5},{4,2},{5,3},{6,0},{7,1},{8,14},{9,15},{10,... | collective-permute-start | bytes 196616 | tf_op jit(solution)/shard_map/ppermute | solution.py:343
  19.7 6.0 %collective-permute-start.6 = (f32[128,128]{1,0:T(8,128)S(1)}, f32[128,128]{1,0:T(8,128)S(1)}, u32[]{:S(2)}, u32[]{:S(2)}) collective-permute-start(f32[128,128]{1,0:T(8,128)S(1)} %shard_map.105.r0), channel_id=1, source_target_pairs={{0,24},{1,25},{2,26},{3,27},{4,28},{5,29},{6,30},{7,31},{8,16},{9,... | collective-permute-start | bytes 196616 | tf_op jit(solution)/shard_map/ppermute | solution.py:343
  24.0 4.7 %collective-permute-start.5 = (f32[128,128]{1,0:T(8,128)S(1)}, f32[128,128]{1,0:T(8,128)S(1)}, u32[]{:S(2)}, u32[]{:S(2)}) collective-permute-start(f32[128,128]{1,0:T(8,128)S(1)} %shard_map.105.r0), channel_id=1, source_target_pairs={{0,16},{1,17},{2,18},{3,19},{4,20},{5,21},{6,22},{7,23},{8,24},{9,... | collective-permute-start | bytes 196616 | tf_op jit(solution)/shard_map/ppermute | solution.py:343
  24.0 4.7 %collective-permute-start.4 = (f32[128,128]{1,0:T(8,128)S(1)}, f32[128,128]{1,0:T(8,128)S(1)}, u32[]{:S(2)}, u32[]{:S(2)}) collective-permute-start(f32[128,128]{1,0:T(8,128)S(1)} %shard_map.105.r0), channel_id=1, source_target_pairs={{0,8},{1,9},{2,10},{3,11},{4,12},{5,13},{6,14},{7,15},{8,0},{9,1},... | collective-permute-start | bytes 196616 | tf_op jit(solution)/shard_map/ppermute | solution.py:343
  29.3 6.7 %collective-permute-start.7 = (f32[128,128]{1,0:T(8,128)S(1)}, f32[128,128]{1,0:T(8,128)S(1)}, u32[]{:S(2)}, u32[]{:S(2)}) collective-permute-start(f32[128,128]{1,0:T(8,128)S(1)} %shard_map.106.sent), channel_id=1, source_target_pairs={{0,56},{1,57},{2,58},{3,59},{4,60},{5,61},{6,62},{7,63},{8,48},{9,... | collective-permute-start | bytes 196616 | tf_op jit(solution)/shard_map/ppermute | solution.py:343
  36.7 3.9 %collective-permute-start.8 = (f32[128,128]{1,0:T(8,128)S(1)}, f32[128,128]{1,0:T(8,128)S(1)}, u32[]{:S(2)}, u32[]{:S(2)}) collective-permute-start(f32[128,128]{1,0:T(8,128)S(1)} %get-tuple-element.45), channel_id=1, source_target_pairs={{0,2},{1,3},{2,0},{3,1},{4,6},{5,7},{6,4},{7,5},{8,10},{9,11},{10,... | collective-permute-start | bytes 196616 | tf_op jit(solution)/shard_map/ppermute | solution.py:343
  37.2 4.9 %collective-permute-start.9 = (f32[128,128]{1,0:T(8,128)S(1)}, f32[128,128]{1,0:T(8,128)S(1)}, u32[]{:S(2)}, u32[]{:S(2)}) collective-permute-start(f32[128,128]{1,0:T(8,128)S(1)} %get-tuple-element.46), channel_id=1, source_target_pairs={{0,4},{1,5},{2,6},{3,7},{4,0},{5,1},{6,2},{7,3},{8,12},{9,13},{10,... | collective-permute-start | bytes 196616 | tf_op jit(solution)/shard_map/ppermute | solution.py:343
  39.7 4.3 %collective-permute-start.10 = (f32[128,128]{1,0:T(8,128)S(1)}, f32[128,128]{1,0:T(8,128)S(1)}, u32[]{:S(2)}, u32[]{:S(2)}) collective-permute-start(f32[128,128]{1,0:T(8,128)S(1)} %get-tuple-element.47), channel_id=1, source_target_pairs={{0,6},{1,7},{2,4},{3,5},{4,2},{5,3},{6,0},{7,1},{8,14},{9,15},{10,... | collective-permute-start | bytes 196616 | tf_op jit(solution)/shard_map/ppermute | solution.py:343
  44.7 10.2 %collective-permute-start.11 = (f32[512,128]{1,0:T(8,128)S(1)}, f32[512,128]{1,0:T(8,128)S(1)}, u32[]{:S(2)}, u32[]{:S(2)}) collective-permute-start(f32[512,128]{1,0:T(8,128)S(1)} %get-tuple-element.49), channel_id=1, source_target_pairs={{0,1},{1,0},{2,3},{3,2},{4,5},{5,4},{6,7},{7,6},{8,9},{9,8},{10,11... | collective-permute-start | bytes 786440 | tf_op jit(solution)/shard_map/ppermute | solution.py:343
  59.0 3.9 %collective-permute-start.14 = (f32[8,512]{1,0:T(8,128)S(1)}, f32[8,512]{1,0:T(8,128)S(1)}, u32[]{:S(2)}, u32[]{:S(2)}) collective-permute-start(f32[8,512]{1,0:T(8,128)S(1)} %get-tuple-element.50.s0), channel_id=1, source_target_pairs={{0,192},{64,128},{128,64},{192,0},{1,193},{65,129},{129,65},{193,1... | collective-permute-start | bytes 49160 | tf_op jit(solution)/shard_map/ppermute | solution.py:418
  61.6 4.1 %collective-permute-start.13 = (f32[8,512]{1,0:T(8,128)S(1)}, f32[8,512]{1,0:T(8,128)S(1)}, u32[]{:S(2)}, u32[]{:S(2)}) collective-permute-start(f32[8,512]{1,0:T(8,128)S(1)} %get-tuple-element.50.s0), channel_id=1, source_target_pairs={{0,128},{64,192},{128,0},{192,64},{1,129},{65,193},{129,1},{193,65... | collective-permute-start | bytes 49160 | tf_op jit(solution)/shard_map/ppermute | solution.py:418
  62.1 3.6 %collective-permute-start.12 = (f32[8,512]{1,0:T(8,128)S(1)}, f32[8,512]{1,0:T(8,128)S(1)}, u32[]{:S(2)}, u32[]{:S(2)}) collective-permute-start(f32[8,512]{1,0:T(8,128)S(1)} %get-tuple-element.50.s0), channel_id=1, source_target_pairs={{0,64},{64,0},{128,192},{192,128},{1,65},{65,1},{129,193},{193,129... | collective-permute-start | bytes 49160 | tf_op jit(solution)/shard_map/ppermute | solution.py:418
  69.5 40.2 %copy-start.3 = (bf16[512,1024]{1,0:T(8,128)(2,1)S(1)}, bf16[512,1024]{1,0:T(8,128)(2,1)}, u32[]{:S(2)}) copy-start(bf16[512,1024]{1,0:T(8,128)(2,1)} %v.5) | copy-start | bytes 3145732
  69.5 40.2 %copy-start.11 = (s32[8]{0:T(128)S(1)}, s32[8]{0:T(128)}, u32[]{:S(2)}) copy-start(s32[8]{0:T(128)} %decay.31) | copy-start | bytes 100
  69.5 40.2 %copy-start.13 = (s32[3]{0:T(128)S(1)}, s32[3]{0:T(128)}, u32[]{:S(2)}) copy-start(s32[3]{0:T(128)} %bounds.31) | copy-start | bytes 40
  69.5 2.9 %collective-permute-start.15 = (f32[520,128]{1,0:T(8,128)S(1)}, f32[520,128]{1,0:T(8,128)S(1)}, u32[]{:S(2)}, u32[]{:S(2)}) collective-permute-start(f32[520,128]{1,0:T(8,128)S(1)} %get-tuple-element.58), channel_id=1, source_target_pairs={{0,1},{1,0},{2,3},{3,2},{4,5},{5,4},{6,7},{7,6},{8,9},{9,8},{10,11... | collective-permute-start | bytes 798728 | tf_op jit(solution)/shard_map/ppermute | solution.py:343
  73.1 3.9 %collective-permute-start.16 = (f32[136,128]{1,0:T(8,128)S(1)}, f32[136,128]{1,0:T(8,128)S(1)}, u32[]{:S(2)}, u32[]{:S(2)}) collective-permute-start(f32[136,128]{1,0:T(8,128)S(1)} %get-tuple-element.60), channel_id=1, source_target_pairs={{0,2},{1,3},{2,0},{3,1},{4,6},{5,7},{6,4},{7,5},{8,10},{9,11},{10,... | collective-permute-start | bytes 208904 | tf_op jit(solution)/shard_map/ppermute | solution.py:343
  73.2 5.8 %collective-permute-start.17 = (f32[136,128]{1,0:T(8,128)S(1)}, f32[136,128]{1,0:T(8,128)S(1)}, u32[]{:S(2)}, u32[]{:S(2)}) collective-permute-start(f32[136,128]{1,0:T(8,128)S(1)} %get-tuple-element.61), channel_id=1, source_target_pairs={{0,4},{1,5},{2,6},{3,7},{4,0},{5,1},{6,2},{7,3},{8,12},{9,13},{10,... | collective-permute-start | bytes 208904 | tf_op jit(solution)/shard_map/ppermute | solution.py:343
  75.8 4.7 %collective-permute-start.18 = (f32[136,128]{1,0:T(8,128)S(1)}, f32[136,128]{1,0:T(8,128)S(1)}, u32[]{:S(2)}, u32[]{:S(2)}) collective-permute-start(f32[136,128]{1,0:T(8,128)S(1)} %get-tuple-element.62), channel_id=1, source_target_pairs={{0,6},{1,7},{2,4},{3,5},{4,2},{5,3},{6,0},{7,1},{8,14},{9,15},{10,... | collective-permute-start | bytes 208904 | tf_op jit(solution)/shard_map/ppermute | solution.py:343
  81.1 5.2 %collective-permute-start.21 = (f32[136,128]{1,0:T(8,128)S(1)}, f32[136,128]{1,0:T(8,128)S(1)}, u32[]{:S(2)}, u32[]{:S(2)}) collective-permute-start(f32[136,128]{1,0:T(8,128)S(1)} %shard_map.113.r0), channel_id=1, source_target_pairs={{0,24},{1,25},{2,26},{3,27},{4,28},{5,29},{6,30},{7,31},{8,16},{9,... | collective-permute-start | bytes 208904 | tf_op jit(solution)/shard_map/ppermute | solution.py:343
  82.2 7.0 %collective-permute-start.20 = (f32[136,128]{1,0:T(8,128)S(1)}, f32[136,128]{1,0:T(8,128)S(1)}, u32[]{:S(2)}, u32[]{:S(2)}) collective-permute-start(f32[136,128]{1,0:T(8,128)S(1)} %shard_map.113.r0), channel_id=1, source_target_pairs={{0,16},{1,17},{2,18},{3,19},{4,20},{5,21},{6,22},{7,23},{8,24},{9,... | collective-permute-start | bytes 208904 | tf_op jit(solution)/shard_map/ppermute | solution.py:343
  83.4 5.7 %collective-permute-start.19 = (f32[136,128]{1,0:T(8,128)S(1)}, f32[136,128]{1,0:T(8,128)S(1)}, u32[]{:S(2)}, u32[]{:S(2)}) collective-permute-start(f32[136,128]{1,0:T(8,128)S(1)} %shard_map.113.r0), channel_id=1, source_target_pairs={{0,8},{1,9},{2,10},{3,11},{4,12},{5,13},{6,14},{7,15},{8,0},{9,1},... | collective-permute-start | bytes 208904 | tf_op jit(solution)/shard_map/ppermute | solution.py:343
  89.8 5.2 %collective-permute-start.22 = (f32[136,128]{1,0:T(8,128)S(1)}, f32[136,128]{1,0:T(8,128)S(1)}, u32[]{:S(2)}, u32[]{:S(2)}) collective-permute-start(f32[136,128]{1,0:T(8,128)S(1)} %shard_map.114.sent), channel_id=1, source_target_pairs={{0,56},{1,57},{2,58},{3,59},{4,60},{5,61},{6,62},{7,63},{8,48},{9,... | collective-permute-start | bytes 208904 | tf_op jit(solution)/shard_map/ppermute | solution.py:343
  95.7 3.9 %collective-permute-start.23 = (f32[128,128]{1,0:T(8,128)S(1)}, f32[128,128]{1,0:T(8,128)S(1)}, u32[]{:S(2)}, u32[]{:S(2)}) collective-permute-start(f32[128,128]{1,0:T(8,128)S(1)} %get-tuple-element.64), channel_id=1, source_target_pairs={{0,2},{1,3},{2,0},{3,1},{4,6},{5,7},{6,4},{7,5},{8,10},{9,11},{10,... | collective-permute-start | bytes 196616 | tf_op jit(solution)/shard_map/ppermute | solution.py:343
  96.2 4.7 %collective-permute-start.24 = (f32[128,128]{1,0:T(8,128)S(1)}, f32[128,128]{1,0:T(8,128)S(1)}, u32[]{:S(2)}, u32[]{:S(2)}) collective-permute-start(f32[128,128]{1,0:T(8,128)S(1)} %get-tuple-element.65), channel_id=1, source_target_pairs={{0,4},{1,5},{2,6},{3,7},{4,0},{5,1},{6,2},{7,3},{8,12},{9,13},{10,... | collective-permute-start | bytes 196616 | tf_op jit(solution)/shard_map/ppermute | solution.py:343
  98.5 4.3 %collective-permute-start.25 = (f32[128,128]{1,0:T(8,128)S(1)}, f32[128,128]{1,0:T(8,128)S(1)}, u32[]{:S(2)}, u32[]{:S(2)}) collective-permute-start(f32[128,128]{1,0:T(8,128)S(1)} %get-tuple-element.66), channel_id=1, source_target_pairs={{0,6},{1,7},{2,4},{3,5},{4,2},{5,3},{6,0},{7,1},{8,14},{9,15},{10,... | collective-permute-start | bytes 196616 | tf_op jit(solution)/shard_map/ppermute | solution.py:343
  104.9 20.2 %collective-permute-start.26 = (f32[512,128]{1,0:T(8,128)}, f32[512,128]{1,0:T(8,128)}, u32[]{:S(2)}, u32[]{:S(2)}) collective-permute-start(f32[512,128]{1,0:T(8,128)} %get-tuple-element.68), channel_id=1, source_target_pairs={{0,1},{1,0},{2,3},{3,2},{4,5},{5,4},{6,7},{7,6},{8,9},{9,8},{10,11... | collective-permute-start | bytes 786440 | tf_op jit(solution)/shard_map/ppermute | solution.py:343
  (14 other events, 114.8 us)

commit v2 on v1

--- a/solution.py
+++ b/solution.py
@@ -13,6 +13,7 @@
 BLOCK_Z, BLOCK_Y = 8 * TOK, 2 * TOK
 SMEM = pl.BlockSpec(memory_space=pltpu.SMEM)
 VMEM = pl.BlockSpec(memory_space=pltpu.VMEM)
+ANY = pl.BlockSpec(memory_space=pl.ANY)
 
 
 def rate_of(level):
@@ -48,28 +49,43 @@
     return entering, leaving
 
 
+def powers(rate, first, up):
+    t = lax.broadcasted_iota(jnp.int32, (8, HEAD), 0)
+    t = (t if up else 7 - t).astype(F32)
+    rows, size = jnp.exp(rate * (t + first)), 8
+    while size < TOK:
+        more = rows * jnp.exp(rate * float(size))
+        rows = jnp.concatenate([rows, more] if up else [more, rows], axis=0)
+        size *= 2
+    return rows
+
+
+def token_rows():
+    return lax.broadcasted_iota(jnp.int32, (TOK, HEAD), 0)
+
+
 def enter_decay(rate, entering):
-    t = lax.broadcasted_iota(jnp.int32, (TOK, HEAD), 0)
-    return jnp.where(t < entering, jnp.exp(rate * (t + 1).astype(F32)), 0.0)
+    return jnp.where(token_rows() < entering, powers(rate, 1.0, True), 0.0)
 
 
 def leave_decay(rate, leaving):
-    t = lax.broadcasted_iota(jnp.int32, (TOK, HEAD), 0)
-    return jnp.where(t >= leaving, jnp.exp(rate * (TOK - 1 - t).astype(F32)), 0.0)
-
-
-def pair_weights(rate, bounds, at, rows, columns, flip):
-    shape = (rows[1] - rows[0], columns[1] - columns[0])
-    r = lax.broadcasted_iota(jnp.int32, shape, 0) + rows[0]
-    c = lax.broadcasted_iota(jnp.int32, shape, 1) + columns[0]
-    gap = c - r if flip else r - c
-    rcol = lax.broadcasted_iota(jnp.int32, (shape[0], 1), 0) + rows[0]
-    crow = lax.broadcasted_iota(jnp.int32, (1, shape[1]), 1) + columns[0]
-    first = at * TOK
-    er = sum((bounds[i] - first <= rcol).astype(jnp.int32) for i in range(3))
-    ec = sum((bounds[i] - first <= crow).astype(jnp.int32) for i in range(3))
-    weights = jnp.exp(rate[0, 0] * jnp.maximum(gap, 0).astype(F32))
-    return jnp.where((gap >= 0) & (er == ec), weights, 0.0)
+    return jnp.where(token_rows() >= leaving, powers(rate, 0.0, False), 0.0)
+
+
+def masks_kernel(decay, bounds, mask, flipped):
+    first = place()[0] * TOK
+    for lo in range(0, TOK, HEAD):
+        row = lax.broadcasted_iota(jnp.int32, (HEAD, TOK), 0) + lo
+        column = lax.broadcasted_iota(jnp.int32, (HEAD, TOK), 1)
+        since = jnp.zeros((HEAD, TOK), jnp.int32)
+        until = jnp.full((HEAD, TOK), TOK, jnp.int32)
+        for i in range(3):
+            local = bounds[i] - first
+            since = jnp.where(row >= local, jnp.maximum(since, local), since)
+            until = jnp.where(row < local, jnp.minimum(until, local), until)
+        rows = slice(lo, lo + HEAD)
+        mask[rows, :] = jnp.where((column <= row) & (column >= since), 1.0, 0.0).astype(BF16)
+        flipped[rows, :] = jnp.where((column >= row) & (column < until), 1.0, 0.0).astype(BF16)
 
 
 def mm(a, b):
@@ -84,7 +100,7 @@
     return lax.dot_general(a, b, (((0,), (0,)), ((), ())), preferred_element_type=F32)
 
 
-def call(kernel, outs, grid=None, in_specs=None, out_specs=None, scratch=(), flops=0, moved=0, limit=24):
+def call(kernel, outs, grid=None, in_specs=None, out_specs=None, scratch=(), flops=0, moved=0, limit=24, aliases={}):
     extra = {} if grid is None else {"grid": grid}
     return pl.pallas_call(
         kernel,
@@ -92,6 +108,7 @@
         in_specs=in_specs,
         out_specs=out_specs,
         scratch_shapes=list(scratch),
+        input_output_aliases=aliases,
         compiler_params=pltpu.CompilerParams(vmem_limit_bytes=limit << 20),
         cost_estimate=pl.CostEstimate(flops=flops, bytes_accessed=moved, transcendentals=0),
         **extra,
@@ -121,19 +138,18 @@
     store_states(keep_ref, send_ref, state(i, k0, v0), state(i + 4, k1, v1), i)
 
 
-def intra_kernel(decay, bounds, q, k, v, out_ref):
-    i = pl.program_id(0)
-    at = place()[0]
-    rate = rate_of(decay[i])
+def intra_kernel(decay, bounds, q, k, v, mask, after, out_ref, *, start):
+    rate = rate_of(decay[pl.program_id(0) + start])
+    scaled = (powers(-rate, 0.0, True) * k[...].astype(F32)).astype(BF16)
+    down = powers(rate, 0.0, True)
     half = TOK // 2
     for lo in (0, half):
-        rows, columns = (lo, lo + half), (0, lo + half)
-        scores = mm_bt(q[lo : lo + half, :], k[0 : lo + half, :])
-        mixing = (scores * pair_weights(rate, bounds, at, rows, columns, False)).astype(BF16)
-        out_ref[lo : lo + half, :] = mm(mixing, v[0 : lo + half, :])
-
-
-def chip_kernel(decay, bounds, keep, got, *outs, reverse, gains):
+        hi = lo + half
+        mixing = mm_bt(q[lo:hi, :], scaled[0:hi, :]).astype(BF16) * mask[lo:hi, 0:hi]
+        out_ref[lo:hi, :] = down[lo:hi, :] * mm(mixing, v[0:hi, :])
+
+
+def chip_kernel(decay, bounds, keep, got, after, *outs, reverse, gains):
     at, z, y, c = place()
     middle = (at - c + 1) * TOK
     for k in range(4):
@@ -151,7 +167,7 @@
             outs[k][HEAD : HEAD + 8, :] = keep[tail, :] + got[tail, :]
 
 
-def row_kernel(decay, bounds, t0, t1, t2, t3, out, *, reverse, gains):
+def row_kernel(decay, bounds, t0, t1, t2, t3, after, out, *, reverse, gains):
     at, z, y, c = place()
     rate = rate_of(decay[4 * c + y])
     total = 0.0
@@ -168,7 +184,7 @@
         out[tail, :] = t0[tail, :] + t1[tail, :] + t2[tail, :] + t3[tail, :]
 
 
-def half_kernel(decay, bounds, r0, r1, r2, r3, out, *, reverse, gains):
+def half_kernel(decay, bounds, r0, r1, r2, r3, after, out, *, reverse, gains):
     at, z, y, c = place()
     rate = rate_of(decay[4 * c + y])
     total = 0.0
@@ -185,7 +201,7 @@
         out[tail, :] = r0[tail, :] + r1[tail, :] + r2[tail, :] + r3[tail, :]
 
 
-def chips_in_kernel(decay, bounds, r0, r1, r2, r3, far, sent, t0, t1, t2, t3, *outs, reverse, gains):
+def chips_in_kernel(decay, bounds, r0, r1, r2, r3, far, sent, t0, t1, t2, t3, after, *outs, reverse, gains):
     at, z, y, c = place()
     rate = rate_of(decay[4 * c + y])
     edge = (z + 1) * BLOCK_Z if reverse else z * BLOCK_Z
@@ -221,9 +237,12 @@
     if gains:
         tail = slice(HEAD, HEAD + 8)
         outs[4][...] = sent[tail, :] + far[tail, :]
-
-
-def cores_in_kernel(decay, bounds, v0, v1, v2, v3, keep, got, mine, other, *, reverse):
+        row = outs[4][pl.ds(z, 1), :]
+        turned = pltpu.roll(row, (HEAD - 32 * y - 16 * c) % HEAD, axis=1)
+        outs[5][...] = turned[0, 0:16]
+
+
+def cores_in_kernel(decay, bounds, v0, v1, v2, v3, keep, got, after, mine, other, *, reverse):
     at, z, y, c = place()
     middle = (at - c + 1) * TOK
     for k, v in enumerate((v0, v1, v2, v3)):
@@ -244,26 +263,30 @@
     return jnp.where(head // 4 == c, mine[spot, :], other[spot, :]).astype(BF16)
 
 
-def attended_kernel(decay, bounds, q, intra, grad, gain, mine, other, out_ref, sums_ref, squares, crosses):
+def attended_kernel(decay, bounds, q0, q1, i0, i1, g0, g1, gain, mine, other, o0, o1, sums_ref, squares, crosses):
     i = pl.program_id(0)
-    at = place()[0]
-    entering, _ = tokens_in(bounds, at)
-    weights = enter_decay(rate_of(decay[i]), entering)
-    out = intra[...] + weights * mm(q[...], state_of(mine, other, i))
-    out_ref[...] = out
-    gained = grad[...].astype(F32) * gain[pl.ds(i, 1), :]
+    entering, _ = tokens_in(bounds, place()[0])
+
+    def out_of(head, q, intra, grad, out_ref):
+        weights = enter_decay(rate_of(decay[head]), entering)
+        out = intra[...] + weights * mm(q[...], state_of(mine, other, head))
+        out_ref[...] = out
+        return out * out, out * (grad[...].astype(F32) * gain[pl.ds(head, 1), :])
+
+    square, cross = out_of(i, q0, i0, g0, o0)
+    more, also = out_of(i + 4, q1, i1, g1, o1)
 
     @pl.when(i == 0)
     def _():
-        squares[...] = out * out
-        crosses[...] = out * gained
+        squares[...] = square + more
+        crosses[...] = cross + also
 
     @pl.when(i > 0)
     def _():
-        squares[...] += out * out
-        crosses[...] += out * gained
-
-    @pl.when(i == HEADS_DEV - 1)
+        squares[...] += square + more
+        crosses[...] += cross + also
+
+    @pl.when(i == 3)
     def _():
         sums_ref[0:4, :] = jnp.broadcast_to(jnp.sum(squares[...].T, axis=0, keepdims=True), (4, TOK))
         sums_ref[4:8, :] = jnp.broadcast_to(jnp.sum(crosses[...].T, axis=0, keepdims=True), (4, TOK))
@@ -297,26 +320,27 @@
     store_states(keep, send, state(i, o0, g0, q0, d0), state(i + 4, o1, g1, q1, d1), i)
 
 
-def grads_kernel(decay, bounds, q, k, v, d0, d1, mine, other, dq, dk, dv):
-    i = pl.program_id(0)
-    at = place()[0]
-    rate = rate_of(decay[i])
-    entering, _ = tokens_in(bounds, at)
+def grads_kernel(decay, bounds, q, k, v, d, mask, flipped, mine, other, after, *refs, start):
+    dq, dk, dv = refs[-3:]
+    head = pl.program_id(0) + start
+    rate = rate_of(decay[head])
+    entering, _ = tokens_in(bounds, place()[0])
     half = TOK // 2
-    d = jnp.where(i < 4, d0[...], d1[...])
-    state = state_of(mine, other, i)
-    weights = enter_decay(rate, entering)
+    state = state_of(mine, other, head)
+    up, down = powers(-rate, 0.0, True), powers(rate, 0.0, True)
+    inside = jnp.where(token_rows() < entering, jnp.exp(rate), 0.0)
+    v_up = (up * v[...].astype(F32)).astype(BF16)
+    d_down = (down * d[...].astype(F32)).astype(BF16)
+    q_down = (down * q[...].astype(F32)).astype(BF16)
     for lo in (0, half):
         hi = lo + half
-        w = pair_weights(rate, bounds, at, (lo, hi), (0, hi), False)
-        mixing = (mm_bt(d[lo:hi, :], v[0:hi, :]) * w).astype(BF16)
-        grad = mm(mixing, k[0:hi, :]) + weights[lo:hi, :] * mm_bt(d[lo:hi, :], state)
-        dq[lo:hi, :] = grad.astype(BF16)
-        w = pair_weights(rate, bounds, at, (lo, hi), (lo, TOK), True)
-        mixing = (mm_bt(v[lo:hi, :], d[lo:TOK, :]) * w).astype(BF16)
-        dk[lo:hi, :] = mm(mixing, q[lo:TOK, :])
-        mixing = (mm_bt(k[lo:hi, :], q[lo:TOK, :]) * w).astype(BF16)
-        dv[lo:hi, :] = mm(mixing, d[lo:TOK, :])
+        mixing = mm_bt(d[lo:hi, :], v_up[0:hi, :]).astype(BF16) * mask[lo:hi, 0:hi]
+        grad = mm(mixing, k[0:hi, :]) + inside[lo:hi, :] * mm_bt(d[lo:hi, :], state)
+        dq[lo:hi, :] = (down[lo:hi, :] * grad).astype(BF16)
+        mixing = mm_bt(v[lo:hi, :], d_down[lo:TOK, :]).astype(BF16) * flipped[lo:hi, lo:TOK]
+        dk[lo:hi, :] = up[lo:hi, :] * mm(mixing, q[lo:TOK, :])
+        mixing = mm_bt(k[lo:hi, :], q_down[lo:TOK, :]).astype(BF16) * flipped[lo:hi, lo:TOK]
+        dv[lo:hi, :] = up[lo:hi, :] * mm(mixing, d[lo:TOK, :])
 
 
 def last_kernel(decay, bounds, k, v, dk_in, dv_in, mine, other, dk, dv):
@@ -343,40 +367,46 @@
     return lax.ppermute(array, "seq", pairs)
 
 
-def carried(keep, send, decay, bounds, reverse, gains):
+def carried(keep, send, decay, bounds, reverse, gains, work):
     extra = 8 if gains else 0
     small = shape(HEAD + extra, HEAD)
 
-    def step(kernel, outs, *args, **more):
+    def step(kernel, outs, *args, after, **more):
         return call(
             functools.partial(kernel, reverse=reverse, **more),
             outs,
-            in_specs=[SMEM, SMEM] + [VMEM] * len(args),
+            in_specs=[SMEM, SMEM] + [VMEM] * len(args) + [ANY],
             out_specs=jax.tree.map(lambda _: VMEM, outs),
             limit=8,
-        )(decay, bounds, *args)
+        )(decay, bounds, *args, after)
 
     got = exchange(send, dc=1)
-    chips = step(chip_kernel, [small] * 4, keep, got, gains=gains)
+    done = work[0](keep)
+    chips = step(chip_kernel, [small] * 4, keep, got, gains=gains, after=done)
+    done = work[1](chips[0])
     chips = [chips[0]] + [exchange(chips[k], dy=k) for k in (1, 2, 3)]
-    row = step(row_kernel, small, *chips, gains=gains)
+    row = step(row_kernel, small, *chips, gains=gains, after=done)
+    done = work[2](row)
     rows = [row] + [exchange(row, dz=k) for k in (1, 2, 3)]
-    sent = step(half_kernel, small, *rows, gains=gains)
+    sent = step(half_kernel, small, *rows, gains=gains, after=done)
+    done = work[3](sent)
     far = exchange(sent, dz=7)
-    outs = [shape(HEAD, HEAD)] * 4 + ([shape(8, HEAD)] if gains else [])
-    outs = step(chips_in_kernel, outs, *rows, far, sent, *chips, gains=gains)
+    outs = [shape(HEAD, HEAD)] * 4 + ([shape(8, HEAD), shape(16)] if gains else [])
+    outs = step(chips_in_kernel, outs, *rows, far, sent, *chips, gains=gains, after=done)
+    done = work[4](outs[0])
     states = [outs[0]] + [exchange(outs[k], dy=k) for k in (1, 2, 3)]
-    mine, other = step(cores_in_kernel, [shape(4 * HEAD, HEAD)] * 2, *states, keep, got)
+    mine, other = step(cores_in_kernel, [shape(4 * HEAD, HEAD)] * 2, *states, keep, got, after=done)
     other = exchange(other, dc=1)
-    return mine, other, (outs[4] if gains else None)
+    return mine, other, (outs[5] if gains else None)
 
 
 def shards(queries, keys, values, out_grad, gain, decay, bounds):
     gain = gain.reshape(HEADS_DEV, HEAD)
-    low = pl.BlockSpec((TOK, HEAD), lambda i: (0, i))
-    high = pl.BlockSpec((TOK, HEAD), lambda i: (0, i + 4))
-    either0 = pl.BlockSpec((TOK, HEAD), lambda i: (0, jnp.minimum(i, 3)))
-    either1 = pl.BlockSpec((TOK, HEAD), lambda i: (0, jnp.maximum(i - 4, 0)))
+
+    def part(start):
+        return pl.BlockSpec((TOK, HEAD), lambda i: (0, i + start))
+
+    low, high = part(0), part(4)
 
     def whole(*dims):
         return pl.BlockSpec(dims, lambda i: (0,) * len(dims))
@@ -394,27 +424,50 @@
         out_specs=[states] * 2,
         flops=small_mm,
         moved=3 << 20,
-    )(decay, bounds, keys, keys, values, values)
-    intra = call(
-        intra_kernel,
-        shape(TOK, width),
-        grid=(HEADS_DEV,),
-        in_specs=[SMEM, SMEM, low, low, low],
-        out_specs=low,
-        flops=2 * big_mm,
-        moved=5 << 20,
-    )(decay, bounds, queries, keys, values)
-    mine, other, _ = carried(keep, send, decay, bounds, False, False)
-    attended, sums = call(
+    )(*[pltpu.with_memory_space_constraint(x, pltpu.HBM) for x in (decay, bounds, keys, keys, values, values)])
+
+    made = {}
+    pairs = shape(TOK, TOK, dtype=BF16)
+
+    def make_masks(after):
+        made["masks"] = call(masks_kernel, [pairs] * 2, in_specs=[SMEM, SMEM], out_specs=[VMEM] * 2, moved=1 << 20)(
+            decay, bounds
+        )
+        return made["masks"][0]
+
+    def make_intra(start):
+        def run(after):
+            made["intra", start] = call(
+                functools.partial(intra_kernel, start=start),
+                shape(TOK, width // 2),
+                grid=(4,),
+                in_specs=[SMEM, SMEM] + [part(start)] * 3 + [whole(TOK, TOK), ANY],
+                out_specs=low,
+                flops=big_mm,
+                moved=3 << 20,
+            )(decay, bounds, queries, keys, values, made["masks"][0], after)
+            return made["intra", start]
+
+        return run
+
+    def same(after):
+        return after
+
+    mine, other, _ = carried(
+        keep, send, decay, bounds, False, False, [make_masks, make_intra(0), make_intra(4), same, same]
+    )
+    o0, o1, sums = call(
         attended_kernel,
-        [shape(TOK, width), shape(8, TOK)],
-        grid=(HEADS_DEV,),
-        in_specs=[SMEM, SMEM, low, low, low, whole(HEADS_DEV, HEAD), states, states],
-        out_specs=[low, whole(8, TOK)],
+        [shape(TOK, width // 2)] * 2 + [shape(8, TOK)],
+        grid=(4,),
+        in_specs=[SMEM, SMEM, low, high, low, low, low, high, whole(HEADS_DEV, HEAD), states, states],
+        out_specs=[low, low, whole(8, TOK)],
         scratch=[pltpu.VMEM((TOK, HEAD), F32)] * 2,
         flops=small_mm,
         moved=7 << 20,
-    )(decay, bounds, queries, intra, out_grad, gain, mine, other)
+    )(
+        decay, bounds, queries, queries, made["intra", 0], made["intra", 4], out_grad, out_grad, gain, mine, other
+    )
     others = [lax.ppermute(sums, "dp", [(i, i ^ k) for i in range(4)]) for k in (1, 2, 3)]
     sums_spec = whole(8, TOK)
     grown = whole(4 * HEAD + 8, HEAD)
@@ -422,22 +475,57 @@
         mixed_kernel,
         [shape(TOK, width // 2, dtype=BF16)] * 2 + [shape(4 * HEAD + 8, HEAD)] * 2,
         grid=(4,),
-        in_specs=[SMEM, SMEM] + [sums_spec] * 4 + [low, high] * 3 + [whole(HEADS_DEV, HEAD)],
+        in_specs=[SMEM, SMEM] + [sums_spec] * 4 + [low, low, low, high, low, high] + [whole(HEADS_DEV, HEAD)],
         out_specs=[low, low, grown, grown],
         scratch=[pltpu.VMEM((TOK, HEAD), F32)] * 2,
         flops=small_mm,
         moved=7 << 20,
-    )(decay, bounds, sums, *others, attended, attended, out_grad, out_grad, queries, queries, gain)
-    dq, dk, dv = call(
-        grads_kernel,
-        [shape(TOK, width, dtype=BF16), shape(TOK, width), shape(TOK, width)],
-        grid=(HEADS_DEV,),
-        in_specs=[SMEM, SMEM, low, low, low, either0, either1, states, states],
-        out_specs=[low, low, low],
-        flops=6 * big_mm,
-        moved=9 << 20,
-    )(decay, bounds, queries, keys, values, d0, d1, mine, other)
-    mine, other, gains = carried(keep, send, decay, bounds, True, True)
+    )(decay, bounds, sums, *others, o0, o1, out_grad, out_grad, queries, queries, gain)
+
+    grads = [shape(TOK, width, dtype=BF16), shape(TOK, width), shape(TOK, width)]
+    mask, flipped = made["masks"]
+
+    def make_grads(n):
+        start = 2 * n
+
+        def run(after):
+            before = made.get("grads", [])
+            made["grads"] = call(
+                functools.partial(grads_kernel, start=start),
+                grads,
+                grid=(2,),
+                in_specs=[SMEM, SMEM]
+                + [part(start)] * 3
+                + [part(start % 4)]
+                + [whole(TOK, TOK)] * 2
+                + [states] * 2
+                + [ANY] * (1 + len(before)),
+                out_specs=[part(start)] * 3,
+                flops=6 * big_mm // 4,
+                moved=9 << 18,
+                aliases={11 + k: k for k in range(len(before))},
+            )(
+                decay,
+                bounds,
+                queries,
+                keys,
+                values,
+                d0 if start < 4 else d1,
+                mask,
+                flipped,
+                mine,
+                other,
+                after,
+                *before,
+            )
+            return made["grads"][1]
+
+        return run
+
+    last_mine, last_other, gains = carried(
+        keep, send, decay, bounds, True, True, [same] + [make_grads(n) for n in range(4)]
+    )
+    dq, dk, dv = made["grads"]
     dk, dv = call(
         last_kernel,
         [shape(TOK, width, dtype=BF16)] * 2,
@@ -446,9 +534,8 @@
         out_specs=[low, low],
         flops=2 * small_mm,
         moved=8 << 20,
-    )(decay, bounds, keys, values, dk, dv, mine, other)
-    part = lax.dynamic_slice(gains.reshape(width), (lax.axis_index("seq") * 16,), (16,))
-    return dq, dk, dv, part
+    )(decay, bounds, keys, values, dk, dv, last_mine, last_other)
+    return dq, dk, dv, gains
 
 
 def solution(mesh):

time: 131 us -> 108 us (0.82)
  waiting for transfers between devices: 31.5 us -> 15.4 us
  local copies, waits for them, and re-layouts: 8.14 us -> 0.03 us
  Pallas kernels: 41 us -> 44 us
  starting transfers between devices: 49.3 us -> 47.2 us
    ppermute x24, waiting for transfers between devices: 28.2 us -> 12.1 us  [exchange(): return lax.ppermute(array, 'seq', pairs)]
    unnamed x38 -> x14, local copies, waits for them, and re-layouts: 7.56 us -> 0.03 us
    pallas_call x3 -> x8, Pallas kernels: 21.8 us -> 24.7 us  [the longest x4 13.9 us: run(): call(functools.partial(grads_kernel, start=start), grads, grid=(2,), in_s...]
    ppermute x24, starting transfers between devices: 46 us -> 43.8 us  [exchange(): return lax.ppermute(array, 'seq', pairs)]
  transfers between devices with their start and end apart: 27 -> 27, of which waited for: 18 -> 12; matrix products, arithmetic and copies ran while one was open for 0% -> 0% of each run, Pallas kernels for 14% -> 20%
where the time goes in v2:
time: 108 us; the launch traced here: 107 us
  starting transfers between devices  47.2 us (44%)
  Pallas kernels  44 us (41%)
  waiting for transfers between devices  15.4 us (14%)
    ppermute x24, starting transfers between devices, exchange(): return lax.ppermute(array, 'seq', pairs)  43.8 us
    pallas_call x4, Pallas kernels, run(): call(functools.partial(grads_kernel, start=start), grads, grid=(2,), in_s...  13.9 us
    ppermute x24, waiting for transfers between devices, exchange(): return lax.ppermute(array, 'seq', pairs)  12.1 us
    pallas_call x10, Pallas kernels, step(): call(functools.partial(kernel, reverse=reverse, **more), outs, in_specs=[...  6.96 us
    pallas_call x2, Pallas kernels, run(): call(functools.partial(intra_kernel, start=start), shape(TOK, width // 2)...  6.61 us
    pallas_call x1, Pallas kernels, shards(): call(last_kernel, [shape(TOK, width, dtype=BF16)] * 2, grid=(HEADS_DEV,),...  5.2 us
    pallas_call x1, Pallas kernels, shards(): call(mixed_kernel, [shape(TOK, width // 2, dtype=BF16)] * 2 + [shape(4 *...  3.59 us
    pallas_call x1, Pallas kernels, shards(): call(local_states_kernel, [shape(4 * HEAD, HEAD)] * 2, grid=(4,), in_spec...  3.5 us
  transfers between devices with their start and end apart: 27, of which 12 were waited for; matrix products, arithmetic and copies ran while one was open for 0% of the time, Pallas kernels for 20%

profile of v2, /device:TPU:1, one launch (start us, length us, event | category | flops | bytes accessed | tf_op | source)
XLA Modules:
  0.0 107.5 jit_solution(3548096205938278644)
XLA Ops:
  0.7 3.5 %shard_map.103 = (f32[512,128]{1,0:T(8,128)S(1)}, f32[512,128]{1,0:T(8,128)S(1)}) custom-call(s32[8]{0:T(128)} %decay.41, s32[3]{0:T(128)} %bounds.41, bf16[512,1024]{1,0:T(8,128)(2,1)} %k.13, bf16[512,1024]{1,0:T(8,128)(2,1)} %k.13, bf16[512,1024]{1,0:T(8,128)(2,1)} %v.13, bf16[512,1024]{1,0:T(8,128)(2,1)} %v.13), custom_call_target="tpu_custom_call" | custom-call | flops 134217728 | bytes 3145728 | tf_op jit(solution)/shard_map/pallas_call | solution.py:419
  4.2 3.3 %collective-permute-start = (f32[512,128]{1,0:T(8,128)S(1)}, f32[512,128]{1,0:T(8,128)S(1)}, u32[]{:S(2)}, u32[]{:S(2)}) collective-permute-start(f32[512,128]{1,0:T(8,128)S(1)} %get-tuple-element.52), channel_id=1, source_target_pairs={{0,1},{1,0},{2,3},{3,2},{4,5},{5,4},{6,7},{7,6},{8,9},{9,8},{10,11... | collective-permute-start | bytes 786440 | tf_op jit(solution)/shard_map/ppermute | solution.py:367
  9.4 2.2 %collective-permute-start.2 = (f32[128,128]{1,0:T(8,128)S(1)}, f32[128,128]{1,0:T(8,128)S(1)}, u32[]{:S(2)}, u32[]{:S(2)}) collective-permute-start(f32[128,128]{1,0:T(8,128)S(1)} %get-tuple-element.55), channel_id=1, source_target_pairs={{0,4},{1,5},{2,6},{3,7},{4,0},{5,1},{6,2},{7,3},{8,12},{9,13},{10,... | collective-permute-start | bytes 196616 | tf_op jit(solution)/shard_map/ppermute | solution.py:367
  11.6 1.7 %collective-permute-start.3 = (f32[128,128]{1,0:T(8,128)S(1)}, f32[128,128]{1,0:T(8,128)S(1)}, u32[]{:S(2)}, u32[]{:S(2)}) collective-permute-start(f32[128,128]{1,0:T(8,128)S(1)} %get-tuple-element.56), channel_id=1, source_target_pairs={{0,6},{1,7},{2,4},{3,5},{4,2},{5,3},{6,0},{7,1},{8,14},{9,15},{10,... | collective-permute-start | bytes 196616 | tf_op jit(solution)/shard_map/ppermute | solution.py:367
  13.3 3.3 %shard_map.105.after.i0 = f32[512,512]{1,0:T(8,128)S(1)} custom-call(s32[8]{0:T(128)S(1)} %copy-done.4, s32[3]{0:T(128)S(1)} %copy-done.5, bf16[512,1024]{1,0:T(8,128)(2,1)S(1)} %copy-done, bf16[512,1024]{1,0:T(8,128)(2,1)S(1)} %copy-done.1, bf16[512,1024]{1,0:T(8,128)(2,1)S(1)} %copy-done.2, bf16[512,512]{1,0:T(8,128)(2,1)S(1)} %get-tuple-element.50.after.mask, ...), custom_call_target="tpu_custom_call" | custom-call | flops 402653184 | bytes 3145728 | tf_op jit(solution)/shard_map/pallas_call | solution.py:440
  17.2 3.9 %collective-permute-start.6 = (f32[128,128]{1,0:T(8,128)S(1)}, f32[128,128]{1,0:T(8,128)S(1)}, u32[]{:S(2)}, u32[]{:S(2)}) collective-permute-start(f32[128,128]{1,0:T(8,128)S(1)} %shard_map.106.after.r0), channel_id=1, source_target_pairs={{0,24},{1,25},{2,26},{3,27},{4,28},{5,29},{6,30},{7,31},{8,16},{9,... | collective-permute-start | bytes 196616 | tf_op jit(solution)/shard_map/ppermute | solution.py:367
  21.5 3.3 %shard_map.107.after.i1 = f32[512,512]{1,0:T(8,128)S(1)} custom-call(s32[8]{0:T(128)S(1)} %copy-done.4, s32[3]{0:T(128)S(1)} %copy-done.5, bf16[512,1024]{1,0:T(8,128)(2,1)S(1)} %copy-done, bf16[512,1024]{1,0:T(8,128)(2,1)S(1)} %copy-done.1, bf16[512,1024]{1,0:T(8,128)(2,1)S(1)} %copy-done.2, bf16[512,512]{1,0:T(8,128)(2,1)S(1)} %get-tuple-element.50.after.mask, ...), custom_call_target="tpu_custom_call" | custom-call | flops 402653184 | bytes 3145728 | tf_op jit(solution)/shard_map/pallas_call | solution.py:440
  26.3 5.1 %collective-permute-start.7 = (f32[128,128]{1,0:T(8,128)S(1)}, f32[128,128]{1,0:T(8,128)S(1)}, u32[]{:S(2)}, u32[]{:S(2)}) collective-permute-start(f32[128,128]{1,0:T(8,128)S(1)} %shard_map.108.sent.after), channel_id=1, source_target_pairs={{0,56},{1,57},{2,58},{3,59},{4,60},{5,61},{6,62},{7,63},{8,48},{9,... | collective-permute-start | bytes 196616 | tf_op jit(solution)/shard_map/ppermute | solution.py:367
  31.4 1.7 %collective-permute-done.7.far = f32[128,128]{1,0:T(8,128)S(1)} collective-permute-done((f32[128,128]{1,0:T(8,128)S(1)}, f32[128,128]{1,0:T(8,128)S(1)}, u32[]{:S(2)}, u32[]{:S(2)}) %collective-permute-start.7) | collective-permute-done | bytes 65568 | tf_op jit(solution)/shard_map/ppermute | solution.py:367
  34.2 2.8 %collective-permute-start.9 = (f32[128,128]{1,0:T(8,128)S(1)}, f32[128,128]{1,0:T(8,128)S(1)}, u32[]{:S(2)}, u32[]{:S(2)}) collective-permute-start(f32[128,128]{1,0:T(8,128)S(1)} %get-tuple-element.59), channel_id=1, source_target_pairs={{0,4},{1,5},{2,6},{3,7},{4,0},{5,1},{6,2},{7,3},{8,12},{9,13},{10,... | collective-permute-start | bytes 196616 | tf_op jit(solution)/shard_map/ppermute | solution.py:367
  37.7 1.6 %collective-permute-done.9.v2 = f32[128,128]{1,0:T(8,128)S(1)} collective-permute-done((f32[128,128]{1,0:T(8,128)S(1)}, f32[128,128]{1,0:T(8,128)S(1)}, u32[]{:S(2)}, u32[]{:S(2)}) %collective-permute-start.9) | collective-permute-done | bytes 65568 | tf_op jit(solution)/shard_map/ppermute | solution.py:367
  39.3 2.0 %collective-permute-done.10.v3 = f32[128,128]{1,0:T(8,128)S(1)} collective-permute-done((f32[128,128]{1,0:T(8,128)S(1)}, f32[128,128]{1,0:T(8,128)S(1)}, u32[]{:S(2)}, u32[]{:S(2)}) %collective-permute-start.10) | collective-permute-done | bytes 65568 | tf_op jit(solution)/shard_map/ppermute | solution.py:367
  41.9 4.3 %collective-permute-start.11 = (f32[512,128]{1,0:T(8,128)S(1)}, f32[512,128]{1,0:T(8,128)S(1)}, u32[]{:S(2)}, u32[]{:S(2)}) collective-permute-start(f32[512,128]{1,0:T(8,128)S(1)} %get-tuple-element.62), channel_id=1, source_target_pairs={{0,1},{1,0},{2,3},{3,2},{4,5},{5,4},{6,7},{7,6},{8,9},{9,8},{10,11... | collective-permute-start | bytes 786440 | tf_op jit(solution)/shard_map/ppermute | solution.py:367
  47.4 3.3 %shard_map.111 = (f32[512,512]{1,0:T(8,128)S(1)}, f32[512,512]{1,0:T(8,128)S(1)}, f32[8,512]{1,0:T(8,128)S(1)}) custom-call(s32[8]{0:T(128)S(1)} %copy-done.4, s32[3]{0:T(128)S(1)} %copy-done.5, bf16[512,1024]{1,0:T(8,128)(2,1)S(1)} %copy-done, bf16[512,1024]{1,0:T(8,128)(2,1)S(1)} %copy-done, f32[512,512]{1,0:T(8,128)S(1)} %shard_map.105.after.i0, ...), custom_call_target="tpu_custom_call" | custom-call | flops 134217728 | bytes 7340032 | tf_op jit(solution)/shard_map/pallas_call | solution.py:459
  50.7 2.6 %collective-permute-start.14 = (f32[8,512]{1,0:T(8,128)S(1)}, f32[8,512]{1,0:T(8,128)S(1)}, u32[]{:S(2)}, u32[]{:S(2)}) collective-permute-start(f32[8,512]{1,0:T(8,128)S(1)} %get-tuple-element.63.s0), channel_id=1, source_target_pairs={{0,192},{64,128},{128,64},{192,0},{1,193},{65,129},{129,65},{193,1... | collective-permute-start | bytes 49160 | tf_op jit(solution)/shard_map/ppermute | solution.py:471
  54.6 2.8 %collective-permute-done.13.s2 = f32[8,512]{1,0:T(8,128)S(1)} collective-permute-done((f32[8,512]{1,0:T(8,128)S(1)}, f32[8,512]{1,0:T(8,128)S(1)}, u32[]{:S(2)}, u32[]{:S(2)}) %collective-permute-start.13) | collective-permute-done | bytes 16416 | tf_op jit(solution)/shard_map/ppermute | solution.py:471
  57.4 3.6 %shard_map.112 = (bf16[512,512]{1,0:T(8,128)(2,1)S(1)}, bf16[512,512]{1,0:T(8,128)(2,1)S(1)}, f32[520,128]{1,0:T(8,128)S(1)}, f32[520,128]{1,0:T(8,128)S(1)}) custom-call(s32[8]{0:T(128)S(1)} %copy-done.4, s32[3]{0:T(128)S(1)} %copy-done.5, f32[8,512]{1,0:T(8,128)S(1)} %get-tuple-element.63.s0, f32[8,512]{1,0:T(8,128)S(1)} %collective-permute-done.12.s1, ...), custom_call_target="tpu_custom_call" | custom-call | flops 134217728 | bytes 7340032 | tf_op jit(solution)/shard_map/pallas_call | solution.py:474
  61.0 1.9 %collective-permute-start.15 = (f32[520,128]{1,0:T(8,128)S(1)}, f32[520,128]{1,0:T(8,128)S(1)}, u32[]{:S(2)}, u32[]{:S(2)}) collective-permute-start(f32[520,128]{1,0:T(8,128)S(1)} %get-tuple-element.69), channel_id=1, source_target_pairs={{0,1},{1,0},{2,3},{3,2},{4,5},{5,4},{6,7},{7,6},{8,9},{9,8},{10,11... | collective-permute-start | bytes 798728 | tf_op jit(solution)/shard_map/ppermute | solution.py:367
  64.8 2.4 %collective-permute-start.17 = (f32[136,128]{1,0:T(8,128)S(1)}, f32[136,128]{1,0:T(8,128)S(1)}, u32[]{:S(2)}, u32[]{:S(2)}) collective-permute-start(f32[136,128]{1,0:T(8,128)S(1)} %get-tuple-element.72), channel_id=1, source_target_pairs={{0,4},{1,5},{2,6},{3,7},{4,0},{5,1},{6,2},{7,3},{8,12},{9,13},{10,... | collective-permute-start | bytes 208904 | tf_op jit(solution)/shard_map/ppermute | solution.py:367
  67.2 1.4 %collective-permute-start.18 = (f32[136,128]{1,0:T(8,128)S(1)}, f32[136,128]{1,0:T(8,128)S(1)}, u32[]{:S(2)}, u32[]{:S(2)}) collective-permute-start(f32[136,128]{1,0:T(8,128)S(1)} %get-tuple-element.73), channel_id=1, source_target_pairs={{0,6},{1,7},{2,4},{3,5},{4,2},{5,3},{6,0},{7,1},{8,14},{9,15},{10,... | collective-permute-start | bytes 208904 | tf_op jit(solution)/shard_map/ppermute | solution.py:367
  68.6 3.5 %shard_map.114 = (bf16[512,1024]{1,0:T(8,128)(2,1)}, f32[512,1024]{1,0:T(8,128)S(1)}, f32[512,1024]{1,0:T(8,128)S(1)}) custom-call(s32[8]{0:T(128)S(1)} %copy-done.4, s32[3]{0:T(128)S(1)} %copy-done.5, bf16[512,1024]{1,0:T(8,128)(2,1)S(1)} %copy-done, bf16[512,1024]{1,0:T(8,128)(2,1)S(1)} %copy-done.1, bf16[512,1024]{1,0:T(8,128)(2,1)S(1)} %copy-done.2, ...), custom_call_target="tpu_custom_call" | custom-call | flops 603979776 | bytes 2359296 | tf_op jit(solution)/shard_map/pallas_call | solution.py:493
  72.7 1.8 %collective-permute-start.21 = (f32[136,128]{1,0:T(8,128)S(1)}, f32[136,128]{1,0:T(8,128)S(1)}, u32[]{:S(2)}, u32[]{:S(2)}) collective-permute-start(f32[136,128]{1,0:T(8,128)S(1)} %shard_map.115.after.r0), channel_id=1, source_target_pairs={{0,24},{1,25},{2,26},{3,27},{4,28},{5,29},{6,30},{7,31},{8,16},{9,... | collective-permute-start | bytes 208904 | tf_op jit(solution)/shard_map/ppermute | solution.py:367
  74.8 1.6 %collective-permute-start.19 = (f32[136,128]{1,0:T(8,128)S(1)}, f32[136,128]{1,0:T(8,128)S(1)}, u32[]{:S(2)}, u32[]{:S(2)}) collective-permute-start(f32[136,128]{1,0:T(8,128)S(1)} %shard_map.115.after.r0), channel_id=1, source_target_pairs={{0,8},{1,9},{2,10},{3,11},{4,12},{5,13},{6,14},{7,15},{8,0},{9,1},... | collective-permute-start | bytes 208904 | tf_op jit(solution)/shard_map/ppermute | solution.py:367
  76.4 3.5 %shard_map.116 = (bf16[512,1024]{1,0:T(8,128)(2,1)}, f32[512,1024]{1,0:T(8,128)S(1)}, f32[512,1024]{1,0:T(8,128)S(1)}) custom-call(s32[8]{0:T(128)S(1)} %copy-done.4, s32[3]{0:T(128)S(1)} %copy-done.5, bf16[512,1024]{1,0:T(8,128)(2,1)S(1)} %copy-done, bf16[512,1024]{1,0:T(8,128)(2,1)S(1)} %copy-done.1, ...), custom_call_target="tpu_custom_call", output_to_operand_aliasing={{0}: (11, {}), {1}: (12, {}), {2}: (13, {})} | custom-call | flops 603979776 | bytes 2359296 | tf_op jit(solution)/shard_map/pallas_call | solution.py:493
  79.8 2.0 %collective-permute-done.20.r2 = f32[136,128]{1,0:T(8,128)S(1)} collective-permute-done((f32[136,128]{1,0:T(8,128)S(1)}, f32[136,128]{1,0:T(8,128)S(1)}, u32[]{:S(2)}, u32[]{:S(2)}) %collective-permute-start.20) | collective-permute-done | bytes 69664 | tf_op jit(solution)/shard_map/ppermute | solution.py:367
  82.5 2.7 %collective-permute-start.22 = (f32[136,128]{1,0:T(8,128)S(1)}, f32[136,128]{1,0:T(8,128)S(1)}, u32[]{:S(2)}, u32[]{:S(2)}) collective-permute-start(f32[136,128]{1,0:T(8,128)S(1)} %shard_map.117.after.sent), channel_id=1, source_target_pairs={{0,56},{1,57},{2,58},{3,59},{4,60},{5,61},{6,62},{7,63},{8,48},{9,... | collective-permute-start | bytes 208904 | tf_op jit(solution)/shard_map/ppermute | solution.py:367
  85.2 3.5 %shard_map.118 = (bf16[512,1024]{1,0:T(8,128)(2,1)}, f32[512,1024]{1,0:T(8,128)S(1)}, f32[512,1024]{1,0:T(8,128)S(1)}) custom-call(s32[8]{0:T(128)S(1)} %copy-done.4, s32[3]{0:T(128)S(1)} %copy-done.5, bf16[512,1024]{1,0:T(8,128)(2,1)S(1)} %copy-done, bf16[512,1024]{1,0:T(8,128)(2,1)S(1)} %copy-done.1, ...), custom_call_target="tpu_custom_call", output_to_operand_aliasing={{0}: (11, {}), {1}: (12, {}), {2}: (13, {})} | custom-call | flops 603979776 | bytes 2359296 | tf_op jit(solution)/shard_map/pallas_call | solution.py:493
  90.0 2.5 %collective-permute-start.24 = (f32[128,128]{1,0:T(8,128)S(1)}, f32[128,128]{1,0:T(8,128)S(1)}, u32[]{:S(2)}, u32[]{:S(2)}) collective-permute-start(f32[128,128]{1,0:T(8,128)S(1)} %get-tuple-element.89), channel_id=1, source_target_pairs={{0,4},{1,5},{2,6},{3,7},{4,0},{5,1},{6,2},{7,3},{8,12},{9,13},{10,... | collective-permute-start | bytes 196616 | tf_op jit(solution)/shard_map/ppermute | solution.py:367
  92.4 1.4 %collective-permute-start.25 = (f32[128,128]{1,0:T(8,128)S(1)}, f32[128,128]{1,0:T(8,128)S(1)}, u32[]{:S(2)}, u32[]{:S(2)}) collective-permute-start(f32[128,128]{1,0:T(8,128)S(1)} %get-tuple-element.90), channel_id=1, source_target_pairs={{0,6},{1,7},{2,4},{3,5},{4,2},{5,3},{6,0},{7,1},{8,14},{9,15},{10,... | collective-permute-start | bytes 196616 | tf_op jit(solution)/shard_map/ppermute | solution.py:367
  93.8 3.5 %shard_map.120 = (bf16[512,1024]{1,0:T(8,128)(2,1)}, f32[512,1024]{1,0:T(8,128)S(1)}, f32[512,1024]{1,0:T(8,128)S(1)}) custom-call(s32[8]{0:T(128)S(1)} %copy-done.4, s32[3]{0:T(128)S(1)} %copy-done.5, bf16[512,1024]{1,0:T(8,128)(2,1)S(1)} %copy-done, bf16[512,1024]{1,0:T(8,128)(2,1)S(1)} %copy-done.1, ...), custom_call_target="tpu_custom_call", output_to_operand_aliasing={{0}: (11, {}), {1}: (12, {}), {2}: (13, {})} | custom-call | flops 603979776 | bytes 2359296 | tf_op jit(solution)/shard_map/pallas_call | solution.py:493
  98.1 3.0 %collective-permute-start.26 = (f32[512,128]{1,0:T(8,128)S(1)}, f32[512,128]{1,0:T(8,128)S(1)}, u32[]{:S(2)}, u32[]{:S(2)}) collective-permute-start(f32[512,128]{1,0:T(8,128)S(1)} %get-tuple-element.92), channel_id=1, source_target_pairs={{0,1},{1,0},{2,3},{3,2},{4,5},{5,4},{6,7},{7,6},{8,9},{9,8},{10,11... | collective-permute-start | bytes 786440 | tf_op jit(solution)/shard_map/ppermute | solution.py:367
  102.3 5.2 %shard_map.122 = (bf16[512,1024]{1,0:T(8,128)(2,1)}, bf16[512,1024]{1,0:T(8,128)(2,1)}) custom-call(s32[8]{0:T(128)S(1)} %copy-done.4, s32[3]{0:T(128)S(1)} %copy-done.5, bf16[512,1024]{1,0:T(8,128)(2,1)S(1)} %copy-done.1, bf16[512,1024]{1,0:T(8,128)(2,1)S(1)} %copy-done.2, f32[512,1024]{1,0:T(8,128)S(1)} %get-tuple-element.86.after.dk_in, ...), custom_call_target="tpu_custom_call" | custom-call | flops 268435456 | bytes 8388608 | tf_op jit(solution)/shard_map/pallas_call | solution.py:529
  (57 shorter events, 16.0 us)
Async XLA Ops:
  0.7 12.6 %copy-start.2 = (bf16[512,1024]{1,0:T(8,128)(2,1)S(1)}, bf16[512,1024]{1,0:T(8,128)(2,1)}, u32[]{:S(2)}) copy-start(bf16[512,1024]{1,0:T(8,128)(2,1)} %v.13) | copy-start | bytes 3145732
  0.7 12.6 %copy-start.1 = (bf16[512,1024]{1,0:T(8,128)(2,1)S(1)}, bf16[512,1024]{1,0:T(8,128)(2,1)}, u32[]{:S(2)}) copy-start(bf16[512,1024]{1,0:T(8,128)(2,1)} %k.13) | copy-start | bytes 3145732
  0.7 12.6 %copy-start = (bf16[512,1024]{1,0:T(8,128)(2,1)S(1)}, bf16[512,1024]{1,0:T(8,128)(2,1)}, u32[]{:S(2)}) copy-start(bf16[512,1024]{1,0:T(8,128)(2,1)} %q.11) | copy-start | bytes 3145732
  4.2 4.5 %collective-permute-start = (f32[512,128]{1,0:T(8,128)S(1)}, f32[512,128]{1,0:T(8,128)S(1)}, u32[]{:S(2)}, u32[]{:S(2)}) collective-permute-start(f32[512,128]{1,0:T(8,128)S(1)} %get-tuple-element.52), channel_id=1, source_target_pairs={{0,1},{1,0},{2,3},{3,2},{4,5},{5,4},{6,7},{7,6},{8,9},{9,8},{10,11... | collective-permute-start | bytes 786440 | tf_op jit(solution)/shard_map/ppermute | solution.py:367
  9.3 7.3 %collective-permute-start.1 = (f32[128,128]{1,0:T(8,128)S(1)}, f32[128,128]{1,0:T(8,128)S(1)}, u32[]{:S(2)}, u32[]{:S(2)}) collective-permute-start(f32[128,128]{1,0:T(8,128)S(1)} %get-tuple-element.54), channel_id=1, source_target_pairs={{0,2},{1,3},{2,0},{3,1},{4,6},{5,7},{6,4},{7,5},{8,10},{9,11},{10,... | collective-permute-start | bytes 196616 | tf_op jit(solution)/shard_map/ppermute | solution.py:367
  9.4 7.2 %collective-permute-start.2 = (f32[128,128]{1,0:T(8,128)S(1)}, f32[128,128]{1,0:T(8,128)S(1)}, u32[]{:S(2)}, u32[]{:S(2)}) collective-permute-start(f32[128,128]{1,0:T(8,128)S(1)} %get-tuple-element.55), channel_id=1, source_target_pairs={{0,4},{1,5},{2,6},{3,7},{4,0},{5,1},{6,2},{7,3},{8,12},{9,13},{10,... | collective-permute-start | bytes 196616 | tf_op jit(solution)/shard_map/ppermute | solution.py:367
  11.6 5.0 %collective-permute-start.3 = (f32[128,128]{1,0:T(8,128)S(1)}, f32[128,128]{1,0:T(8,128)S(1)}, u32[]{:S(2)}, u32[]{:S(2)}) collective-permute-start(f32[128,128]{1,0:T(8,128)S(1)} %get-tuple-element.56), channel_id=1, source_target_pairs={{0,6},{1,7},{2,4},{3,5},{4,2},{5,3},{6,0},{7,1},{8,14},{9,15},{10,... | collective-permute-start | bytes 196616 | tf_op jit(solution)/shard_map/ppermute | solution.py:367
  17.2 7.6 %collective-permute-start.6 = (f32[128,128]{1,0:T(8,128)S(1)}, f32[128,128]{1,0:T(8,128)S(1)}, u32[]{:S(2)}, u32[]{:S(2)}) collective-permute-start(f32[128,128]{1,0:T(8,128)S(1)} %shard_map.106.after.r0), channel_id=1, source_target_pairs={{0,24},{1,25},{2,26},{3,27},{4,28},{5,29},{6,30},{7,31},{8,16},{9,... | collective-permute-start | bytes 196616 | tf_op jit(solution)/shard_map/ppermute | solution.py:367
  21.1 4.6 %collective-permute-start.5 = (f32[128,128]{1,0:T(8,128)S(1)}, f32[128,128]{1,0:T(8,128)S(1)}, u32[]{:S(2)}, u32[]{:S(2)}) collective-permute-start(f32[128,128]{1,0:T(8,128)S(1)} %shard_map.106.after.r0), channel_id=1, source_target_pairs={{0,16},{1,17},{2,18},{3,19},{4,20},{5,21},{6,22},{7,23},{8,24},{9,... | collective-permute-start | bytes 196616 | tf_op jit(solution)/shard_map/ppermute | solution.py:367
  21.1 4.6 %collective-permute-start.4 = (f32[128,128]{1,0:T(8,128)S(1)}, f32[128,128]{1,0:T(8,128)S(1)}, u32[]{:S(2)}, u32[]{:S(2)}) collective-permute-start(f32[128,128]{1,0:T(8,128)S(1)} %shard_map.106.after.r0), channel_id=1, source_target_pairs={{0,8},{1,9},{2,10},{3,11},{4,12},{5,13},{6,14},{7,15},{8,0},{9,1},... | collective-permute-start | bytes 196616 | tf_op jit(solution)/shard_map/ppermute | solution.py:367
  24.8 22.6 %copy-start.3 = (bf16[512,1024]{1,0:T(8,128)(2,1)S(1)}, bf16[512,1024]{1,0:T(8,128)(2,1)}, u32[]{:S(2)}) copy-start(bf16[512,1024]{1,0:T(8,128)(2,1)} %g1.3) | copy-start | bytes 3145732
  24.8 22.6 %copy-start.6 = (f32[1024]{0:T(1024)S(1)}, f32[1024]{0:T(1024)}, u32[]{:S(2)}) copy-start(f32[1024]{0:T(1024)} %param.11) | copy-start | bytes 12292
  26.3 6.7 %collective-permute-start.7 = (f32[128,128]{1,0:T(8,128)S(1)}, f32[128,128]{1,0:T(8,128)S(1)}, u32[]{:S(2)}, u32[]{:S(2)}) collective-permute-start(f32[128,128]{1,0:T(8,128)S(1)} %shard_map.108.sent.after), channel_id=1, source_target_pairs={{0,56},{1,57},{2,58},{3,59},{4,60},{5,61},{6,62},{7,63},{8,48},{9,... | collective-permute-start | bytes 196616 | tf_op jit(solution)/shard_map/ppermute | solution.py:367
  33.8 3.9 %collective-permute-start.8 = (f32[128,128]{1,0:T(8,128)S(1)}, f32[128,128]{1,0:T(8,128)S(1)}, u32[]{:S(2)}, u32[]{:S(2)}) collective-permute-start(f32[128,128]{1,0:T(8,128)S(1)} %get-tuple-element.58), channel_id=1, source_target_pairs={{0,2},{1,3},{2,0},{3,1},{4,6},{5,7},{6,4},{7,5},{8,10},{9,11},{10,... | collective-permute-start | bytes 196616 | tf_op jit(solution)/shard_map/ppermute | solution.py:367
  34.2 5.1 %collective-permute-start.9 = (f32[128,128]{1,0:T(8,128)S(1)}, f32[128,128]{1,0:T(8,128)S(1)}, u32[]{:S(2)}, u32[]{:S(2)}) collective-permute-start(f32[128,128]{1,0:T(8,128)S(1)} %get-tuple-element.59), channel_id=1, source_target_pairs={{0,4},{1,5},{2,6},{3,7},{4,0},{5,1},{6,2},{7,3},{8,12},{9,13},{10,... | collective-permute-start | bytes 196616 | tf_op jit(solution)/shard_map/ppermute | solution.py:367
  37.0 4.3 %collective-permute-start.10 = (f32[128,128]{1,0:T(8,128)S(1)}, f32[128,128]{1,0:T(8,128)S(1)}, u32[]{:S(2)}, u32[]{:S(2)}) collective-permute-start(f32[128,128]{1,0:T(8,128)S(1)} %get-tuple-element.60), channel_id=1, source_target_pairs={{0,6},{1,7},{2,4},{3,5},{4,2},{5,3},{6,0},{7,1},{8,14},{9,15},{10,... | collective-permute-start | bytes 196616 | tf_op jit(solution)/shard_map/ppermute | solution.py:367
  41.9 5.5 %collective-permute-start.11 = (f32[512,128]{1,0:T(8,128)S(1)}, f32[512,128]{1,0:T(8,128)S(1)}, u32[]{:S(2)}, u32[]{:S(2)}) collective-permute-start(f32[512,128]{1,0:T(8,128)S(1)} %get-tuple-element.62), channel_id=1, source_target_pairs={{0,1},{1,0},{2,3},{3,2},{4,5},{5,4},{6,7},{7,6},{8,9},{9,8},{10,11... | collective-permute-start | bytes 786440 | tf_op jit(solution)/shard_map/ppermute | solution.py:367
  50.7 3.9 %collective-permute-start.14 = (f32[8,512]{1,0:T(8,128)S(1)}, f32[8,512]{1,0:T(8,128)S(1)}, u32[]{:S(2)}, u32[]{:S(2)}) collective-permute-start(f32[8,512]{1,0:T(8,128)S(1)} %get-tuple-element.63.s0), channel_id=1, source_target_pairs={{0,192},{64,128},{128,64},{192,0},{1,193},{65,129},{129,65},{193,1... | collective-permute-start | bytes 49160 | tf_op jit(solution)/shard_map/ppermute | solution.py:471
  53.3 4.1 %collective-permute-start.13 = (f32[8,512]{1,0:T(8,128)S(1)}, f32[8,512]{1,0:T(8,128)S(1)}, u32[]{:S(2)}, u32[]{:S(2)}) collective-permute-start(f32[8,512]{1,0:T(8,128)S(1)} %get-tuple-element.63.s0), channel_id=1, source_target_pairs={{0,128},{64,192},{128,0},{192,64},{1,129},{65,193},{129,1},{193,65... | collective-permute-start | bytes 49160 | tf_op jit(solution)/shard_map/ppermute | solution.py:471
  53.8 3.6 %collective-permute-start.12 = (f32[8,512]{1,0:T(8,128)S(1)}, f32[8,512]{1,0:T(8,128)S(1)}, u32[]{:S(2)}, u32[]{:S(2)}) collective-permute-start(f32[8,512]{1,0:T(8,128)S(1)} %get-tuple-element.63.s0), channel_id=1, source_target_pairs={{0,64},{64,0},{128,192},{192,128},{1,65},{65,1},{129,193},{193,129... | collective-permute-start | bytes 49160 | tf_op jit(solution)/shard_map/ppermute | solution.py:471
  61.0 3.1 %collective-permute-start.15 = (f32[520,128]{1,0:T(8,128)S(1)}, f32[520,128]{1,0:T(8,128)S(1)}, u32[]{:S(2)}, u32[]{:S(2)}) collective-permute-start(f32[520,128]{1,0:T(8,128)S(1)} %get-tuple-element.69), channel_id=1, source_target_pairs={{0,1},{1,0},{2,3},{3,2},{4,5},{5,4},{6,7},{7,6},{8,9},{9,8},{10,11... | collective-permute-start | bytes 798728 | tf_op jit(solution)/shard_map/ppermute | solution.py:367
  64.7 7.4 %collective-permute-start.16 = (f32[136,128]{1,0:T(8,128)S(1)}, f32[136,128]{1,0:T(8,128)S(1)}, u32[]{:S(2)}, u32[]{:S(2)}) collective-permute-start(f32[136,128]{1,0:T(8,128)S(1)} %get-tuple-element.71), channel_id=1, source_target_pairs={{0,2},{1,3},{2,0},{3,1},{4,6},{5,7},{6,4},{7,5},{8,10},{9,11},{10,... | collective-permute-start | bytes 208904 | tf_op jit(solution)/shard_map/ppermute | solution.py:367
  64.8 7.3 %collective-permute-start.17 = (f32[136,128]{1,0:T(8,128)S(1)}, f32[136,128]{1,0:T(8,128)S(1)}, u32[]{:S(2)}, u32[]{:S(2)}) collective-permute-start(f32[136,128]{1,0:T(8,128)S(1)} %get-tuple-element.72), channel_id=1, source_target_pairs={{0,4},{1,5},{2,6},{3,7},{4,0},{5,1},{6,2},{7,3},{8,12},{9,13},{10,... | collective-permute-start | bytes 208904 | tf_op jit(solution)/shard_map/ppermute | solution.py:367
  67.2 4.9 %collective-permute-start.18 = (f32[136,128]{1,0:T(8,128)S(1)}, f32[136,128]{1,0:T(8,128)S(1)}, u32[]{:S(2)}, u32[]{:S(2)}) collective-permute-start(f32[136,128]{1,0:T(8,128)S(1)} %get-tuple-element.73), channel_id=1, source_target_pairs={{0,6},{1,7},{2,4},{3,5},{4,2},{5,3},{6,0},{7,1},{8,14},{9,15},{10,... | collective-permute-start | bytes 208904 | tf_op jit(solution)/shard_map/ppermute | solution.py:367
  72.7 7.1 %collective-permute-start.21 = (f32[136,128]{1,0:T(8,128)S(1)}, f32[136,128]{1,0:T(8,128)S(1)}, u32[]{:S(2)}, u32[]{:S(2)}) collective-permute-start(f32[136,128]{1,0:T(8,128)S(1)} %shard_map.115.after.r0), channel_id=1, source_target_pairs={{0,24},{1,25},{2,26},{3,27},{4,28},{5,29},{6,30},{7,31},{8,16},{9,... | collective-permute-start | bytes 208904 | tf_op jit(solution)/shard_map/ppermute | solution.py:367
  74.6 7.3 %collective-permute-start.20 = (f32[136,128]{1,0:T(8,128)S(1)}, f32[136,128]{1,0:T(8,128)S(1)}, u32[]{:S(2)}, u32[]{:S(2)}) collective-permute-start(f32[136,128]{1,0:T(8,128)S(1)} %shard_map.115.after.r0), channel_id=1, source_target_pairs={{0,16},{1,17},{2,18},{3,19},{4,20},{5,21},{6,22},{7,23},{8,24},{9,... | collective-permute-start | bytes 208904 | tf_op jit(solution)/shard_map/ppermute | solution.py:367
  74.8 7.1 %collective-permute-start.19 = (f32[136,128]{1,0:T(8,128)S(1)}, f32[136,128]{1,0:T(8,128)S(1)}, u32[]{:S(2)}, u32[]{:S(2)}) collective-permute-start(f32[136,128]{1,0:T(8,128)S(1)} %shard_map.115.after.r0), channel_id=1, source_target_pairs={{0,8},{1,9},{2,10},{3,11},{4,12},{5,13},{6,14},{7,15},{8,0},{9,1},... | collective-permute-start | bytes 208904 | tf_op jit(solution)/shard_map/ppermute | solution.py:367
  82.5 6.2 %collective-permute-start.22 = (f32[136,128]{1,0:T(8,128)S(1)}, f32[136,128]{1,0:T(8,128)S(1)}, u32[]{:S(2)}, u32[]{:S(2)}) collective-permute-start(f32[136,128]{1,0:T(8,128)S(1)} %shard_map.117.after.sent), channel_id=1, source_target_pairs={{0,56},{1,57},{2,58},{3,59},{4,60},{5,61},{6,62},{7,63},{8,48},{9,... | collective-permute-start | bytes 208904 | tf_op jit(solution)/shard_map/ppermute | solution.py:367
  90.0 7.4 %collective-permute-start.23 = (f32[128,128]{1,0:T(8,128)S(1)}, f32[128,128]{1,0:T(8,128)S(1)}, u32[]{:S(2)}, u32[]{:S(2)}) collective-permute-start(f32[128,128]{1,0:T(8,128)S(1)} %get-tuple-element.88), channel_id=1, source_target_pairs={{0,2},{1,3},{2,0},{3,1},{4,6},{5,7},{6,4},{7,5},{8,10},{9,11},{10,... | collective-permute-start | bytes 196616 | tf_op jit(solution)/shard_map/ppermute | solution.py:367
  90.0 7.4 %collective-permute-start.24 = (f32[128,128]{1,0:T(8,128)S(1)}, f32[128,128]{1,0:T(8,128)S(1)}, u32[]{:S(2)}, u32[]{:S(2)}) collective-permute-start(f32[128,128]{1,0:T(8,128)S(1)} %get-tuple-element.89), channel_id=1, source_target_pairs={{0,4},{1,5},{2,6},{3,7},{4,0},{5,1},{6,2},{7,3},{8,12},{9,13},{10,... | collective-permute-start | bytes 196616 | tf_op jit(solution)/shard_map/ppermute | solution.py:367
  92.4 5.0 %collective-permute-start.25 = (f32[128,128]{1,0:T(8,128)S(1)}, f32[128,128]{1,0:T(8,128)S(1)}, u32[]{:S(2)}, u32[]{:S(2)}) collective-permute-start(f32[128,128]{1,0:T(8,128)S(1)} %get-tuple-element.90), channel_id=1, source_target_pairs={{0,6},{1,7},{2,4},{3,5},{4,2},{5,3},{6,0},{7,1},{8,14},{9,15},{10,... | collective-permute-start | bytes 196616 | tf_op jit(solution)/shard_map/ppermute | solution.py:367
  98.1 4.2 %collective-permute-start.26 = (f32[512,128]{1,0:T(8,128)S(1)}, f32[512,128]{1,0:T(8,128)S(1)}, u32[]{:S(2)}, u32[]{:S(2)}) collective-permute-start(f32[512,128]{1,0:T(8,128)S(1)} %get-tuple-element.92), channel_id=1, source_target_pairs={{0,1},{1,0},{2,3},{3,2},{4,5},{5,4},{6,7},{7,6},{8,9},{9,8},{10,11... | collective-permute-start | bytes 786440 | tf_op jit(solution)/shard_map/ppermute | solution.py:367
  (2 other events, 13.8 us)

commit v3 on v2

v3 whole, which is shorter than its diff:
```python
import functools
import math

import jax
import jax.numpy as jnp
from jax import lax
from jax.experimental import pallas as pl
from jax.experimental.pallas import tpu as pltpu
from jax.sharding import PartitionSpec as P

F32, BF16 = jnp.float32, jnp.bfloat16
HEAD, TOK, HEADS_DEV, STREAM, FEATURES = 128, 512, 8, 32768, 4096
BLOCK_Z, BLOCK_Y = 8 * TOK, 2 * TOK
SMEM = pl.BlockSpec(memory_space=pltpu.SMEM)
VMEM = pl.BlockSpec(memory_space=pltpu.VMEM)
ANY = pl.BlockSpec(memory_space=pl.ANY)


def rate_of(level):
    row = jnp.full((1, HEAD), level.astype(F32), F32)
    slow = jnp.exp(row * (math.log(8.0) / 7.0)) * (-0.25 / STREAM)
    lowest = math.log(4.0 / STREAM)
    fast = -jnp.exp(lowest + (row - 8.0) * ((math.log(1.0 / 32.0) - lowest) / 7.0))
    return jnp.where(row < 8.0, slow, fast)


def starts_before(bounds, place):
    return sum((bounds[i] < place).astype(jnp.int32) for i in range(3))


def carry(rate, bounds, left, right):
    same = (starts_before(bounds, left) == starts_before(bounds, right)) & (left <= right)
    span = jnp.maximum(right - left, 0).astype(F32)
    return jnp.exp(rate * span) * jnp.where(same, 1.0, 0.0).astype(F32)


def place():
    at = lax.axis_index("seq")
    return at, at // 8, (at // 2) % 4, at % 2


def tokens_in(bounds, at):
    first = at * TOK
    entering, leaving = TOK, 0
    for i in range(3):
        local = bounds[i] - first
        entering = jnp.where((local >= 0) & (local < entering), local, entering)
        leaving = jnp.where((local < TOK) & (local > leaving), local, leaving)
    return entering, leaving


def powers(rate, first, up):
    t = lax.broadcasted_iota(jnp.int32, (8, HEAD), 0)
    t = (t if up else 7 - t).astype(F32)
    rows, size = jnp.exp(rate * (t + first)), 8
    while size < TOK:
        more = rows * jnp.exp(rate * float(size))
        rows = jnp.concatenate([rows, more] if up else [more, rows], axis=0)
        size *= 2
    return rows


def token_rows():
    return lax.broadcasted_iota(jnp.int32, (TOK, HEAD), 0)


def enter_decay(rate, entering):
    return jnp.where(token_rows() < entering, powers(rate, 1.0, True), 0.0)


def leave_decay(rate, leaving):
    return jnp.where(token_rows() >= leaving, powers(rate, 0.0, False), 0.0)


def masks_kernel(decay, bounds, mask, flipped):
    first = place()[0] * TOK
    for lo in range(0, TOK, HEAD):
        row = lax.broadcasted_iota(jnp.int32, (HEAD, TOK), 0) + lo
        column = lax.broadcasted_iota(jnp.int32, (HEAD, TOK), 1)
        since = jnp.zeros((HEAD, TOK), jnp.int32)
        until = jnp.full((HEAD, TOK), TOK, jnp.int32)
        for i in range(3):
            local = bounds[i] - first
            since = jnp.where(row >= local, jnp.maximum(since, local), since)
            until = jnp.where(row < local, jnp.minimum(until, local), until)
        rows = slice(lo, lo + HEAD)
        mask[rows, :] = jnp.where((column <= row) & (column >= since), 1.0, 0.0).astype(BF16)
        flipped[rows, :] = jnp.where((column >= row) & (column < until), 1.0, 0.0).astype(BF16)


def mm(a, b):
    return lax.dot_general(a, b, (((1,), (0,)), ((), ())), preferred_element_type=F32)


def mm_bt(a, b):
    return lax.dot_general(a, b, (((1,), (1,)), ((), ())), preferred_element_type=F32)


def mm_at(a, b):
    return lax.dot_general(a, b, (((0,), (0,)), ((), ())), preferred_element_type=F32)


def call(kernel, outs, grid=None, in_specs=None, out_specs=None, scratch=(), flops=0, moved=0, limit=24, aliases={}):
    extra = {} if grid is None else {"grid": grid}
    return pl.pallas_call(
        kernel,
        out_shape=outs,
        in_specs=in_specs,
        out_specs=out_specs,
        scratch_shapes=list(scratch),
        input_output_aliases=aliases,
        compiler_params=pltpu.CompilerParams(vmem_limit_bytes=limit << 20),
        cost_estimate=pl.CostEstimate(flops=flops, bytes_accessed=moved, transcendentals=0),
        **extra,
    )


def shape(*dims, dtype=F32):
    return jax.ShapeDtypeStruct(dims, dtype)


def columns(index):
    return pl.ds(pl.multiple_of(index * HEAD, HEAD), HEAD)


def first_head(own):
    c = place()[3]
    return 4 * c if own else 4 * (1 - c)


def sent_states_kernel(decay, bounds, k, v, out, k_in, v_in, sems):
    at, _, y, _ = place()
    _, leaving = tokens_in(bounds, at)
    heads = [first_head(False) + (y ^ i) for i in range(4)]
    copies = []
    for i, head in enumerate(heads):
        pair = (
            pltpu.make_async_copy(k.at[:, columns(head)], k_in.at[i], sems.at[0, i]),
            pltpu.make_async_copy(v.at[:, columns(head)], v_in.at[i], sems.at[1, i]),
        )
        for copy in pair:
            copy.start()
        copies.append(pair)
    for i, head in enumerate(heads):
        weights = leave_decay(rate_of(decay[head]), leaving)
        for copy in copies[i]:
            copy.wait()
        decayed = (weights * k_in[i].astype(F32)).astype(BF16)
        out[i * HEAD : (i + 1) * HEAD, :] = mm_at(decayed, v_in[i])


def kept_states_kernel(decay, bounds, k, v, after, out):
    at, _, y, _ = place()
    _, leaving = tokens_in(bounds, at)
    for i in range(4):
        head = first_head(True) + (y ^ i)
        weights = leave_decay(rate_of(decay[head]), leaving)
        decayed = (weights * k[:, columns(head)].astype(F32)).astype(BF16)
        out[i * HEAD : (i + 1) * HEAD, :] = mm_at(decayed, v[:, columns(head)])


def intra_kernel(decay, bounds, q, k, v, mask, after, out_ref, *, own):
    half = TOK // 2
    for j in range(4):
        head = first_head(own) + j
        rate, at = rate_of(decay[head]), columns(head)
        scaled = (powers(-rate, 0.0, True) * k[:, at].astype(F32)).astype(BF16)
        down = powers(rate, 0.0, True)
        for lo in (0, half):
            hi = lo + half
            mixing = mm_bt(q[lo:hi, at], scaled[0:hi, :]).astype(BF16) * mask[lo:hi, 0:hi]
            out_ref[lo:hi, j * HEAD : (j + 1) * HEAD] = down[lo:hi, :] * mm(mixing, v[0:hi, at])


def chip_kernel(decay, bounds, keep, got, send, after, *outs, reverse, gains):
    at, z, y, c = place()
    middle = (at - c + 1) * TOK
    for k in range(4):
        rate = rate_of(decay[4 * c + (y ^ k)])
        if reverse:
            far = carry(rate, bounds, middle - TOK, middle)
            own, other = jnp.where(c == 1, far, 1.0), jnp.where(c == 1, 1.0, far)
        else:
            far = carry(rate, bounds, middle, middle + TOK)
            own, other = jnp.where(c == 0, far, 1.0), jnp.where(c == 0, 1.0, far)
        rows = slice(k * HEAD, (k + 1) * HEAD)
        outs[k][0:HEAD, :] = own * keep[rows, :] + other * got[rows, :]
        if gains:
            tail = slice(4 * HEAD, 4 * HEAD + 8)
            outs[k][HEAD : HEAD + 8, :] = send[tail, :] + got[tail, :]


def row_kernel(decay, bounds, t0, t1, t2, t3, after, out, *, reverse, gains):
    at, z, y, c = place()
    rate = rate_of(decay[4 * c + y])
    total = 0.0
    for k, t in enumerate((t0, t1, t2, t3)):
        edge = z * BLOCK_Z + (y ^ k) * BLOCK_Y
        if reverse:
            weight = carry(rate, bounds, z * BLOCK_Z, edge)
        else:
            weight = carry(rate, bounds, edge + BLOCK_Y, (z + 1) * BLOCK_Z)
        total += weight * t[0:HEAD, :]
    out[0:HEAD, :] = total
    if gains:
        tail = slice(HEAD, HEAD + 8)
        out[tail, :] = t0[tail, :] + t1[tail, :] + t2[tail, :] + t3[tail, :]


def pair_kernel(decay, bounds, r0, r1, after, out, *, reverse, gains):
    at, z, y, c = place()
    rate = rate_of(decay[4 * c + y])
    first = (z - z % 2) * BLOCK_Z
    total = 0.0
    for k, r in enumerate((r0, r1)):
        edge = (z ^ k) * BLOCK_Z
        if reverse:
            weight = carry(rate, bounds, first, edge)
        else:
            weight = carry(rate, bounds, edge + BLOCK_Z, first + 2 * BLOCK_Z)
        total += weight * r[0:HEAD, :]
    out[0:HEAD, :] = total
    if gains:
        tail = slice(HEAD, HEAD + 8)
        out[tail, :] = r0[tail, :] + r1[tail, :]


PAIRS = (2, 5, 6)


def chips_in_kernel(decay, bounds, r1, p0, p1, p2, p3, t0, t1, t2, t3, after, *outs, reverse, gains):
    at, z, y, c = place()
    rate = rate_of(decay[4 * c + y])
    edge = (z + 1) * BLOCK_Z if reverse else z * BLOCK_Z
    other = (z ^ 1) * BLOCK_Z
    if reverse:
        total = carry(rate, bounds, edge, other) * r1[0:HEAD, :]
    else:
        total = carry(rate, bounds, other + BLOCK_Z, edge) * r1[0:HEAD, :]
    for k, p in zip(PAIRS, (p1, p2, p3)):
        there = z ^ k
        first = (there - there % 2) * BLOCK_Z
        if reverse:
            weight = carry(rate, bounds, edge, first)
        else:
            weight = carry(rate, bounds, first + 2 * BLOCK_Z, edge)
        total += weight * p[0:HEAD, :]
    for k in range(4):
        here = z * BLOCK_Z + (y ^ k) * BLOCK_Y
        if reverse:
            state = carry(rate, bounds, here + BLOCK_Y, edge) * total
        else:
            state = carry(rate, bounds, edge, here) * total
        for m, t in enumerate((t0, t1, t2, t3)):
            if m == k:
                continue
            there = z * BLOCK_Z + (y ^ m) * BLOCK_Y
            if reverse:
                weight = carry(rate, bounds, here + BLOCK_Y, there)
            else:
                weight = carry(rate, bounds, there + BLOCK_Y, here)
            state += weight * t[0:HEAD, :]
        outs[k][...] = state
    if gains:
        tail = slice(HEAD, HEAD + 8)
        outs[4][...] = p0[tail, :] + p1[tail, :] + p2[tail, :] + p3[tail, :]
        row = outs[4][pl.ds(z, 1), :]
        turned = pltpu.roll(row, (HEAD - 32 * y - 16 * c) % HEAD, axis=1)
        outs[5][...] = turned[0, 0:16]


def cores_in_kernel(decay, bounds, v0, v1, v2, v3, keep, got, after, mine, other, *, reverse):
    at, z, y, c = place()
    middle = (at - c + 1) * TOK
    for k, v in enumerate((v0, v1, v2, v3)):
        rate = rate_of(decay[4 * c + (y ^ k)])
        if reverse:
            step, deep = carry(rate, bounds, middle, middle + TOK), c == 0
        else:
            step, deep = carry(rate, bounds, middle - TOK, middle), c == 1
        rows = slice(k * HEAD, (k + 1) * HEAD)
        state = v[...]
        mine[rows, :] = jnp.where(deep, step * state + got[rows, :], state)
        other[rows, :] = jnp.where(deep, state, step * state + keep[rows, :])


def state_of(states, j):
    return states[columns(j ^ place()[2]), :].astype(BF16)


def attended_kernel(decay, bounds, q, intra, grad, gain, states, *refs, own):
    out_ref, sums = refs[-2:]
    entering, _ = tokens_in(bounds, place()[0])
    square, cross = 0.0, 0.0
    for j in range(4):
        head = first_head(own) + j
        at, local = columns(head), slice(j * HEAD, (j + 1) * HEAD)
        weights = enter_decay(rate_of(decay[head]), entering)
        out = intra[:, local] + weights * mm(q[:, at], state_of(states, j))
        out_ref[:, local] = out
        square += out * out
        cross += out * (grad[:, at].astype(F32) * gain[pl.ds(head, 1), :])
    square = jnp.sum(square.T, axis=0, keepdims=True)
    cross = jnp.sum(cross.T, axis=0, keepdims=True)
    if not own:
        square += refs[0][0:1, :]
        cross += refs[0][4:5, :]
    sums[0:4, :] = jnp.broadcast_to(square, (4, TOK))
    sums[4:8, :] = jnp.broadcast_to(cross, (4, TOK))


def mixed_kernel(decay, bounds, s0, s1, s2, s3, o, grad, q, gain, *refs, own):
    d, states = refs[-2:]
    at, _, y, _ = place()
    entering, _ = tokens_in(bounds, at)
    sums = s0[...] + s1[...] + s2[...] + s3[...]
    r = lax.rsqrt(sums[0:1, :] * (1.0 / FEATURES) + 1e-06)
    inverse = jnp.broadcast_to(r, (HEAD, TOK)).T
    mean = jnp.broadcast_to(sums[4:5, :] * r * (1.0 / FEATURES), (HEAD, TOK)).T
    tail = 4 * HEAD

    def term(head, wide, normed):
        if not own:
            states[pl.ds(tail + head, 1), :] = jnp.sum(wide * normed, axis=0, keepdims=True)

    for j in range(4):
        head = first_head(own) + j
        local = slice(j * HEAD, (j + 1) * HEAD)
        normed = inverse * o[:, local]
        wide = grad[:, columns(head)].astype(F32)
        low = (inverse * (wide * gain[pl.ds(head, 1), :] - normed * mean)).astype(BF16)
        d[:, local] = low
        term(head, wide, normed)
        weights = enter_decay(rate_of(decay[head]), entering)
        states[columns(j ^ y), :] = mm_at((weights * q[:, columns(head)].astype(F32)).astype(BF16), low)
    if not own:
        for j in range(4):
            head = first_head(True) + j
            term(head, grad[:, columns(head)].astype(F32), inverse * refs[0][:, j * HEAD : (j + 1) * HEAD])


def grads_kernel(decay, bounds, q, k, v, d, mask, flipped, states, after, dq, dk, dv, *, own, start):
    entering, _ = tokens_in(bounds, place()[0])
    half = TOK // 2
    for n in range(2):
        j = start + n
        head = first_head(own) + j
        rate, at = rate_of(decay[head]), columns(head)
        out, local = slice(n * HEAD, (n + 1) * HEAD), slice(j * HEAD, (j + 1) * HEAD)
        state = state_of(states, j)
        up, down = powers(-rate, 0.0, True), powers(rate, 0.0, True)
        inside = jnp.where(token_rows() < entering, jnp.exp(rate), 0.0)
        v_up = (up * v[:, at].astype(F32)).astype(BF16)
        d_down = (down * d[:, local].astype(F32)).astype(BF16)
        q_down = (down * q[:, at].astype(F32)).astype(BF16)
        for lo in (0, half):
            hi = lo + half
            mixing = mm_bt(d[lo:hi, local], v_up[0:hi, :]).astype(BF16) * mask[lo:hi, 0:hi]
            grad = mm(mixing, k[0:hi, at]) + inside[lo:hi, :] * mm_bt(d[lo:hi, local], state)
            dq[lo:hi, out] = (down[lo:hi, :] * grad).astype(BF16)
            mixing = mm_bt(v[lo:hi, at], d_down[lo:TOK, :]).astype(BF16) * flipped[lo:hi, lo:TOK]
            dk[lo:hi, out] = up[lo:hi, :] * mm(mixing, q[lo:TOK, at])
            mixing = mm_bt(k[lo:hi, at], q_down[lo:TOK, :]).astype(BF16) * flipped[lo:hi, lo:TOK]
            dv[lo:hi, out] = up[lo:hi, :] * mm(mixing, d[lo:TOK, local])


def last_kernel(decay, bounds, k, v, states, *refs, own):
    parts, buffers = refs[:4], refs[-3:]
    (dk, dv), sems = refs[-5:-3] if not own else refs[-6:-4], buffers[2]
    _, leaving = tokens_in(bounds, place()[0])
    copies = []
    if own:
        dq = refs[-4]
        for n, part in enumerate(refs[4:8]):
            spot = pl.ds(pl.multiple_of((first_head(n < 2) + 2 * (n % 2)) * HEAD, 2 * HEAD), 2 * HEAD)
            copies.append(pltpu.make_async_copy(part, dq.at[:, spot], sems.at[2, n]))
            copies[-1].start()
    for j in range(4):
        head = first_head(own) + j
        at, local = columns(head), slice(j * HEAD, (j + 1) * HEAD)
        inner = slice(j % 2 * HEAD, (j % 2 + 1) * HEAD)
        weights = leave_decay(rate_of(decay[head]), leaving)
        state = state_of(states, j)
        buffers[0][:, local] = (parts[j // 2][:, inner] + weights * mm_bt(v[:, at], state)).astype(BF16)
        copies.append(pltpu.make_async_copy(buffers[0].at[:, local], dk.at[:, at], sems.at[0, j]))
        copies[-1].start()
        buffers[1][:, local] = (parts[2 + j // 2][:, inner] + weights * mm(k[:, at], state)).astype(BF16)
        copies.append(pltpu.make_async_copy(buffers[1].at[:, local], dv.at[:, at], sems.at[1, j]))
        copies[-1].start()
    for copy in copies:
        copy.wait()


def index(z, y, c):
    return (z * 4 + y) * 2 + c


def exchange(array, dz=0, dy=0, dc=0):
    pairs = [
        (index(z, y, c), index(z ^ dz, y ^ dy, c ^ dc))
        for z in range(8)
        for y in range(4)
        for c in range(2)
    ]
    return lax.ppermute(array, "seq", pairs)


def carried(send, make_keep, decay, bounds, reverse, gains, work):
    extra = 8 if gains else 0
    small = shape(HEAD + extra, HEAD)

    def step(kernel, outs, *args, after, **more):
        return call(
            functools.partial(kernel, reverse=reverse, **more),
            outs,
            in_specs=[SMEM, SMEM] + [VMEM] * len(args) + [ANY],
            out_specs=jax.tree.map(lambda _: VMEM, outs),
            limit=8,
        )(decay, bounds, *args, after)

    got = exchange(send, dc=1)
    keep = make_keep(send)
    chips = step(chip_kernel, [small] * 4, keep, got, send, gains=gains, after=keep)
    done = work[0](chips[0])
    chips = [chips[0]] + [exchange(chips[k], dy=k) for k in (1, 2, 3)]
    row = step(row_kernel, small, *chips, gains=gains, after=done)
    done = work[1](row)
    near = exchange(row, dz=1)
    pair = step(pair_kernel, small, row, near, gains=gains, after=done)
    done = work[2](pair)
    pairs = [pair] + [exchange(pair, dz=k) for k in PAIRS]
    outs = [shape(HEAD, HEAD)] * 4 + ([shape(8, HEAD), shape(16)] if gains else [])
    outs = step(chips_in_kernel, outs, near, *pairs, *chips, gains=gains, after=done)
    done = work[3](outs[0])
    states = [outs[0]] + [exchange(outs[k], dy=k) for k in (1, 2, 3)]
    mine, other = step(cores_in_kernel, [shape(4 * HEAD, HEAD)] * 2, *states, keep, got, after=done)
    return mine, other, (outs[5] if gains else None)


def shards(queries, keys, values, out_grad, gain, decay, bounds):
    gain = gain.reshape(HEADS_DEV, HEAD)
    width = HEADS_DEV * HEAD
    half = width // 2
    small_mm = TOK * HEAD * HEAD * HEADS_DEV
    big_mm = 2 * TOK * TOK * HEAD * HEADS_DEV * 3 // 4
    state_shape = shape(4 * HEAD, HEAD)
    scalars = [SMEM, SMEM]

    def local(kernel, outs, args, order=(), flops=0, moved=0, **more):
        return call(
            functools.partial(kernel, **more),
            outs,
            in_specs=scalars + [VMEM] * len(args) + [ANY] * len(order),
            out_specs=jax.tree.map(lambda _: VMEM, outs),
            flops=flops,
            moved=moved,
        )(decay, bounds, *args, *order)

    send = call(
        sent_states_kernel,
        state_shape,
        in_specs=scalars + [ANY] * 2,
        out_specs=VMEM,
        scratch=[pltpu.VMEM((4, TOK, HEAD), BF16)] * 2 + [pltpu.SemaphoreType.DMA((2, 4))],
        flops=small_mm,
        moved=3 << 19,
    )(*[pltpu.with_memory_space_constraint(x, pltpu.HBM) for x in (decay, bounds, keys, values)])

    def keep_states(after):
        return local(kept_states_kernel, state_shape, [keys, values], [after], small_mm, 3 << 19)

    made = {}
    pairs = shape(TOK, TOK, dtype=BF16)

    def make_intra(own):
        def run(after):
            if own:
                made["masks"] = local(masks_kernel, [pairs] * 2, [], moved=1 << 20)
            made[own] = local(
                intra_kernel,
                shape(TOK, half),
                [queries, keys, values, made["masks"][0]],
                [after],
                big_mm,
                3 << 20,
                own=own,
            )
            return made[own]

        return run

    def same(after):
        return after

    mine, other, _ = carried(
        send, keep_states, decay, bounds, False, False, [make_intra(True), same, make_intra(False), same]
    )
    theirs = exchange(other, dc=1)
    sums = shape(8, TOK)
    outs = [shape(TOK, half), sums]
    o_mine, own_sums = local(
        attended_kernel, outs, [queries, made[True], out_grad, gain, mine], [other], small_mm, 3 << 20, own=True
    )
    o_other, sums = local(
        attended_kernel,
        outs,
        [queries, made[False], out_grad, gain, theirs, own_sums],
        [],
        small_mm,
        3 << 20,
        own=False,
    )
    totals = [sums] + [lax.ppermute(sums, "dp", [(i, i ^ k) for i in range(4)]) for k in (1, 2, 3)]
    outs = [shape(TOK, half, dtype=BF16), shape(4 * HEAD + 8, HEAD)]
    d_other, send = local(
        mixed_kernel,
        outs,
        [*totals, o_other, out_grad, queries, gain, o_mine],
        [],
        small_mm,
        3 << 20,
        own=False,
    )

    def keep_grads(after):
        outs = [shape(TOK, half, dtype=BF16), shape(4 * HEAD, HEAD)]
        made["d"], keep = local(
            mixed_kernel, outs, [*totals, o_mine, out_grad, queries, gain], [after], small_mm, 3 << 20, own=True
        )
        return keep

    mask, flipped = made["masks"]

    def make_grads(n):
        def run(after):
            own = n < 2
            made["grads", n] = local(
                grads_kernel,
                [shape(TOK, 2 * HEAD, dtype=BF16), shape(TOK, 2 * HEAD), shape(TOK, 2 * HEAD)],
                [queries, keys, values, made["d"] if own else d_other, mask, flipped, mine if own else theirs],
                [after],
                6 * big_mm // 4,
                2 << 20,
                own=own,
                start=2 * (n % 2),
            )
            return made["grads", n][1]

        return run

    last_mine, last_other, gains = carried(
        send, keep_grads, decay, bounds, True, True, [make_grads(n) for n in range(4)]
    )
    last_theirs = exchange(last_other, dc=1)
    dq, dk, dv = zip(*[made["grads", n] for n in range(4)])
    full = shape(TOK, width, dtype=BF16)
    scratch = [pltpu.VMEM((TOK, half), BF16)] * 2 + [pltpu.SemaphoreType.DMA((3, 4))]
    dk_out, dv_out, dq_out = call(
        functools.partial(last_kernel, own=True),
        [full] * 3,
        in_specs=scalars + [VMEM] * 11 + [ANY],
        out_specs=[ANY] * 3,
        scratch=scratch,
        flops=2 * small_mm,
        moved=6 << 20,
    )(decay, bounds, keys, values, last_mine, *dk[:2], *dv[:2], *dq, last_other)
    dk_out, dv_out = call(
        functools.partial(last_kernel, own=False),
        [full] * 2,
        in_specs=scalars + [VMEM] * 7 + [ANY] * 2,
        out_specs=[ANY] * 2,
        scratch=scratch,
        flops=2 * small_mm,
        moved=4 << 20,
        aliases={9: 0, 10: 1},
    )(decay, bounds, keys, values, last_theirs, *dk[2:], *dv[2:], dk_out, dv_out)
    return dq_out, dk_out, dv_out, gains


def solution(mesh):
    return jax.shard_map(
        shards,
        mesh=mesh,
        in_specs=(
            P("seq", "dp"),
            P("seq", "dp"),
            P("seq", "dp"),
            P("seq", "dp"),
            P("dp"),
            P("dp"),
            P(),
        ),
        out_specs=(P("seq", "dp"), P("seq", "dp"), P("seq", "dp"), P(("dp", "seq"))),
        check_vma=False,
    )
```

time: 108 us -> 104 us (0.963)
  Pallas kernels: 44 us -> 36 us
  starting transfers between devices: 47.2 us -> 51.1 us
    pallas_call x11 -> x15, Pallas kernels: 37 us -> 29.1 us  [the longest x12 22 us: local(): call(functools.partial(kernel, **more), outs, in_specs=scalars + [VMEM] *...]
    ppermute x24, starting transfers between devices: 43.8 us -> 47.8 us  [exchange(): return lax.ppermute(array, 'seq', pairs)]
  transfers between devices with their start and end apart: 27 -> 27, of which waited for: 12 -> 11; matrix products, arithmetic and copies ran while one was open for 0% -> 0% of each run, Pallas kernels for 20% -> 20%
where the time goes in v3:
time: 104 us; the launch traced here: 103 us
  starting transfers between devices  51.1 us (49%)
  Pallas kernels  36 us (35%)
  waiting for transfers between devices  15.1 us (15%)
  between operations  1.15 us (1%)
    ppermute x24, starting transfers between devices, exchange(): return lax.ppermute(array, 'seq', pairs)  47.8 us
    pallas_call x12, Pallas kernels, local(): call(functools.partial(kernel, **more), outs, in_specs=scalars + [VMEM] *...  22 us
    ppermute x24, waiting for transfers between devices, exchange(): return lax.ppermute(array, 'seq', pairs)  11.8 us
    pallas_call x10, Pallas kernels, step(): call(functools.partial(kernel, reverse=reverse, **more), outs, in_specs=[...  6.94 us
    ppermute x3, starting transfers between devices, shards(): lax.ppermute(sums, 'dp', [(i, i ^ k) for i in range(4)])  3.34 us
    ppermute x3, waiting for transfers between devices, shards(): lax.ppermute(sums, 'dp', [(i, i ^ k) for i in range(4)])  3.32 us
    pallas_call x1, Pallas kernels, shards(): call(sent_states_kernel, state_shape, in_specs=scalars + [ANY] * 2, out_s...  2.88 us
    pallas_call x1, Pallas kernels, shards(): call(functools.partial(last_kernel, own=True), [full] * 3, in_specs=scala...  2.15 us
  transfers between devices with their start and end apart: 27, of which 11 were waited for; matrix products, arithmetic and copies ran while one was open for 0% of the time, Pallas kernels for 20%

profile of v3, /device:TPU:1, one launch (start us, length us, event | category | flops | bytes accessed | tf_op | source)
XLA Modules:
  0.0 103.4 jit_solution(3848200185129433487)
XLA Ops:
  0.7 2.9 %shard_map.103.after.send = f32[512,128]{1,0:T(8,128)S(1)} custom-call(s32[8]{0:T(128)} %decay.49, s32[3]{0:T(128)} %bounds.49, bf16[512,1024]{1,0:T(8,128)(2,1)} %k.19, bf16[512,1024]{1,0:T(8,128)(2,1)} %v.19), custom_call_target="tpu_custom_call" | custom-call | flops 67108864 | bytes 1572864 | tf_op jit(solution)/shard_map/pallas_call | solution.py:459
  3.6 3.3 %collective-permute-start = (f32[512,128]{1,0:T(8,128)S(1)}, f32[512,128]{1,0:T(8,128)S(1)}, u32[]{:S(2)}, u32[]{:S(2)}) collective-permute-start(f32[512,128]{1,0:T(8,128)S(1)} %shard_map.103.after.send), channel_id=1, source_target_pairs={{0,1},{1,0},{2,3},{3,2},{4,5},{5,4},{6,7},{7,6},{8,9},{9,8},{10,11... | collective-permute-start | bytes 786440 | tf_op jit(solution)/shard_map/ppermute | solution.py:405
  8.8 2.2 %collective-permute-start.2 = (f32[128,128]{1,0:T(8,128)S(1)}, f32[128,128]{1,0:T(8,128)S(1)}, u32[]{:S(2)}, u32[]{:S(2)}) collective-permute-start(f32[128,128]{1,0:T(8,128)S(1)} %get-tuple-element.55), channel_id=1, source_target_pairs={{0,4},{1,5},{2,6},{3,7},{4,0},{5,1},{6,2},{7,3},{8,12},{9,13},{10,... | collective-permute-start | bytes 196616 | tf_op jit(solution)/shard_map/ppermute | solution.py:405
  11.0 1.7 %collective-permute-start.3 = (f32[128,128]{1,0:T(8,128)S(1)}, f32[128,128]{1,0:T(8,128)S(1)}, u32[]{:S(2)}, u32[]{:S(2)}) collective-permute-start(f32[128,128]{1,0:T(8,128)S(1)} %get-tuple-element.56), channel_id=1, source_target_pairs={{0,6},{1,7},{2,4},{3,5},{4,2},{5,3},{6,0},{7,1},{8,14},{9,15},{10,... | collective-permute-start | bytes 196616 | tf_op jit(solution)/shard_map/ppermute | solution.py:405
  13.6 2.0 %shard_map.106.after.intra = f32[512,512]{1,0:T(8,128)S(1)} custom-call(s32[8]{0:T(128)S(1)} %copy-done.4, s32[3]{0:T(128)S(1)} %copy-done.5, bf16[512,1024]{1,0:T(8,128)(2,1)S(1)} %copy-done, bf16[512,1024]{1,0:T(8,128)(2,1)S(1)} %copy-done.1, bf16[512,1024]{1,0:T(8,128)(2,1)S(1)} %copy-done.2, bf16[512,512]{1,0:T(8,128)(2,1)S(1)} %get-tuple-element.52.mask, ...), custom_call_target="tpu_custom_call" | custom-call | flops 402653184 | bytes 3145728 | tf_op jit(solution)/shard_map/pallas_call | solution.py:450
  16.3 1.5 %collective-permute-start.4 = (f32[128,128]{1,0:T(8,128)S(1)}, f32[128,128]{1,0:T(8,128)S(1)}, u32[]{:S(2)}, u32[]{:S(2)}) collective-permute-start(f32[128,128]{1,0:T(8,128)S(1)} %shard_map.107.r0.after), channel_id=1, source_target_pairs={{0,8},{1,9},{2,10},{3,11},{4,12},{5,13},{6,14},{7,15},{8,0},{9,1},... | collective-permute-start | bytes 196616 | tf_op jit(solution)/shard_map/ppermute | solution.py:405
  17.8 1.7 %collective-permute-done.4.r1 = f32[128,128]{1,0:T(8,128)S(1)} collective-permute-done((f32[128,128]{1,0:T(8,128)S(1)}, f32[128,128]{1,0:T(8,128)S(1)}, u32[]{:S(2)}, u32[]{:S(2)}) %collective-permute-start.4) | collective-permute-done | bytes 65568 | tf_op jit(solution)/shard_map/ppermute | solution.py:405
  20.1 5.9 %collective-permute-start.7 = (f32[128,128]{1,0:T(8,128)S(1)}, f32[128,128]{1,0:T(8,128)S(1)}, u32[]{:S(2)}, u32[]{:S(2)}) collective-permute-start(f32[128,128]{1,0:T(8,128)S(1)} %shard_map.108.after.p0), channel_id=1, source_target_pairs={{0,48},{1,49},{2,50},{3,51},{4,52},{5,53},{6,54},{7,55},{8,56},{9,... | collective-permute-start | bytes 196616 | tf_op jit(solution)/shard_map/ppermute | solution.py:405
  27.7 2.0 %shard_map.109.after.intra = f32[512,512]{1,0:T(8,128)S(1)} custom-call(s32[8]{0:T(128)S(1)} %copy-done.4, s32[3]{0:T(128)S(1)} %copy-done.5, bf16[512,1024]{1,0:T(8,128)(2,1)S(1)} %copy-done, bf16[512,1024]{1,0:T(8,128)(2,1)S(1)} %copy-done.1, bf16[512,1024]{1,0:T(8,128)(2,1)S(1)} %copy-done.2, bf16[512,512]{1,0:T(8,128)(2,1)S(1)} %get-tuple-element.52.mask, ...), custom_call_target="tpu_custom_call" | custom-call | flops 402653184 | bytes 3145728 | tf_op jit(solution)/shard_map/pallas_call | solution.py:450
  29.8 2.3 %collective-permute-done.6.p2 = f32[128,128]{1,0:T(8,128)S(1)} collective-permute-done((f32[128,128]{1,0:T(8,128)S(1)}, f32[128,128]{1,0:T(8,128)S(1)}, u32[]{:S(2)}, u32[]{:S(2)}) %collective-permute-start.6) | collective-permute-done | bytes 65568 | tf_op jit(solution)/shard_map/ppermute | solution.py:405
  33.0 2.6 %collective-permute-start.9 = (f32[128,128]{1,0:T(8,128)S(1)}, f32[128,128]{1,0:T(8,128)S(1)}, u32[]{:S(2)}, u32[]{:S(2)}) collective-permute-start(f32[128,128]{1,0:T(8,128)S(1)} %get-tuple-element.59), channel_id=1, source_target_pairs={{0,4},{1,5},{2,6},{3,7},{4,0},{5,1},{6,2},{7,3},{8,12},{9,13},{10,... | collective-permute-start | bytes 196616 | tf_op jit(solution)/shard_map/ppermute | solution.py:405
  37.9 2.0 %collective-permute-done.10.v3 = f32[128,128]{1,0:T(8,128)S(1)} collective-permute-done((f32[128,128]{1,0:T(8,128)S(1)}, f32[128,128]{1,0:T(8,128)S(1)}, u32[]{:S(2)}, u32[]{:S(2)}) %collective-permute-start.10) | collective-permute-done | bytes 65568 | tf_op jit(solution)/shard_map/ppermute | solution.py:405
  40.5 6.0 %collective-permute-start.11 = (f32[512,128]{1,0:T(8,128)S(1)}, f32[512,128]{1,0:T(8,128)S(1)}, u32[]{:S(2)}, u32[]{:S(2)}) collective-permute-start(f32[512,128]{1,0:T(8,128)S(1)} %get-tuple-element.61.refs_0_), channel_id=1, source_target_pairs={{0,1},{1,0},{2,3},{3,2},{4,5},{5,4},{6,7},{7,6},{8,9},{9,8},{10,11... | collective-permute-start | bytes 786440 | tf_op jit(solution)/shard_map/ppermute | solution.py:405
  46.5 1.3 %shard_map.112 = (f32[512,512]{1,0:T(8,128)S(1)}, f32[8,512]{1,0:T(8,128)S(1)}) custom-call(s32[8]{0:T(128)S(1)} %copy-done.4, s32[3]{0:T(128)S(1)} %copy-done.5, bf16[512,1024]{1,0:T(8,128)(2,1)S(1)} %copy-done, f32[512,512]{1,0:T(8,128)S(1)} %shard_map.106.after.intra, bf16[512,1024]{1,0:T(8,128)(2,1)S(1)} %copy-done.3, f32[8,128]{1,0:T(8,128)S(1)} %bitcast.1, ...), custom_call_target="tpu_custom_call" | custom-call | flops 67108864 | bytes 3145728 | tf_op jit(solution)/shard_map/pallas_call | solution.py:450
  47.8 1.4 %shard_map.113 = (f32[512,512]{1,0:T(8,128)S(1)}, f32[8,512]{1,0:T(8,128)S(1)}) custom-call(s32[8]{0:T(128)S(1)} %copy-done.4, s32[3]{0:T(128)S(1)} %copy-done.5, bf16[512,1024]{1,0:T(8,128)(2,1)S(1)} %copy-done, f32[512,512]{1,0:T(8,128)S(1)} %shard_map.109.after.intra, bf16[512,1024]{1,0:T(8,128)(2,1)S(1)} %copy-done.3, f32[8,128]{1,0:T(8,128)S(1)} %bitcast.2, ...), custom_call_target="tpu_custom_call" | custom-call | flops 67108864 | bytes 3145728 | tf_op jit(solution)/shard_map/pallas_call | solution.py:450
  49.2 2.6 %collective-permute-start.14 = (f32[8,512]{1,0:T(8,128)S(1)}, f32[8,512]{1,0:T(8,128)S(1)}, u32[]{:S(2)}, u32[]{:S(2)}) collective-permute-start(f32[8,512]{1,0:T(8,128)S(1)} %get-tuple-element.64.s0), channel_id=1, source_target_pairs={{0,192},{64,128},{128,64},{192,0},{1,193},{65,129},{129,65},{193,1... | collective-permute-start | bytes 49160 | tf_op jit(solution)/shard_map/ppermute | solution.py:513
  53.1 2.8 %collective-permute-done.13.s2 = f32[8,512]{1,0:T(8,128)S(1)} collective-permute-done((f32[8,512]{1,0:T(8,128)S(1)}, f32[8,512]{1,0:T(8,128)S(1)}, u32[]{:S(2)}, u32[]{:S(2)}) %collective-permute-start.13) | collective-permute-done | bytes 16416 | tf_op jit(solution)/shard_map/ppermute | solution.py:513
  55.8 1.7 %shard_map.114 = (bf16[512,512]{1,0:T(8,128)(2,1)S(1)}, f32[520,128]{1,0:T(8,128)S(1)}) custom-call(s32[8]{0:T(128)S(1)} %copy-done.4, s32[3]{0:T(128)S(1)} %copy-done.5, f32[8,512]{1,0:T(8,128)S(1)} %get-tuple-element.64.s0, f32[8,512]{1,0:T(8,128)S(1)} %collective-permute-done.12.s1, f32[8,512]{1,0:T(8,128)S(1)} %collective-permute-done.13.s2, ...), custom_call_target="tpu_custom_call" | custom-call | flops 67108864 | bytes 3145728 | tf_op jit(solution)/shard_map/pallas_call | solution.py:450
  57.6 1.9 %collective-permute-start.15 = (f32[520,128]{1,0:T(8,128)S(1)}, f32[520,128]{1,0:T(8,128)S(1)}, u32[]{:S(2)}, u32[]{:S(2)}) collective-permute-start(f32[520,128]{1,0:T(8,128)S(1)} %get-tuple-element.67.refs_0_.send), channel_id=1, source_target_pairs={{0,1},{1,0},{2,3},{3,2},{4,5},{5,4},{6,7},{7,6},{8,9},{9,8},{10,11... | collective-permute-start | bytes 798728 | tf_op jit(solution)/shard_map/ppermute | solution.py:405
  59.5 1.4 %shard_map.115 = (bf16[512,512]{1,0:T(8,128)(2,1)S(1)}, f32[512,128]{1,0:T(8,128)S(1)}) custom-call(s32[8]{0:T(128)S(1)} %copy-done.4, s32[3]{0:T(128)S(1)} %copy-done.5, f32[8,512]{1,0:T(8,128)S(1)} %get-tuple-element.64.s0, f32[8,512]{1,0:T(8,128)S(1)} %collective-permute-done.12.s1, f32[8,512]{1,0:T(8,128)S(1)} %collective-permute-done.13.s2, ...), custom_call_target="tpu_custom_call" | custom-call | flops 67108864 | bytes 3145728 | tf_op jit(solution)/shard_map/pallas_call | solution.py:450
  61.7 3.3 %collective-permute-start.17 = (f32[136,128]{1,0:T(8,128)S(1)}, f32[136,128]{1,0:T(8,128)S(1)}, u32[]{:S(2)}, u32[]{:S(2)}) collective-permute-start(f32[136,128]{1,0:T(8,128)S(1)} %get-tuple-element.71), channel_id=1, source_target_pairs={{0,4},{1,5},{2,6},{3,7},{4,0},{5,1},{6,2},{7,3},{8,12},{9,13},{10,... | collective-permute-start | bytes 208904 | tf_op jit(solution)/shard_map/ppermute | solution.py:405
  65.5 2.5 %shard_map.117 = (bf16[512,256]{1,0:T(8,128)(2,1)S(1)}, f32[512,256]{1,0:T(8,128)S(1)}, f32[512,256]{1,0:T(8,128)S(1)}) custom-call(s32[8]{0:T(128)S(1)} %copy-done.4, s32[3]{0:T(128)S(1)} %copy-done.5, bf16[512,1024]{1,0:T(8,128)(2,1)S(1)} %copy-done, bf16[512,1024]{1,0:T(8,128)(2,1)S(1)} %copy-done.1, bf16[512,1024]{1,0:T(8,128)(2,1)S(1)} %copy-done.2, ...), custom_call_target="tpu_custom_call" | custom-call | flops 603979776 | bytes 2097152 | tf_op jit(solution)/shard_map/pallas_call | solution.py:450
  70.7 2.5 %shard_map.119 = (bf16[512,256]{1,0:T(8,128)(2,1)S(1)}, f32[512,256]{1,0:T(8,128)S(1)}, f32[512,256]{1,0:T(8,128)S(1)}) custom-call(s32[8]{0:T(128)S(1)} %copy-done.4, s32[3]{0:T(128)S(1)} %copy-done.5, bf16[512,1024]{1,0:T(8,128)(2,1)S(1)} %copy-done, bf16[512,1024]{1,0:T(8,128)(2,1)S(1)} %copy-done.1, bf16[512,1024]{1,0:T(8,128)(2,1)S(1)} %copy-done.2, ...), custom_call_target="tpu_custom_call" | custom-call | flops 603979776 | bytes 2097152 | tf_op jit(solution)/shard_map/pallas_call | solution.py:450
  74.1 3.1 %collective-permute-start.22 = (f32[136,128]{1,0:T(8,128)S(1)}, f32[136,128]{1,0:T(8,128)S(1)}, u32[]{:S(2)}, u32[]{:S(2)}) collective-permute-start(f32[136,128]{1,0:T(8,128)S(1)} %shard_map.120.after.p0), channel_id=1, source_target_pairs={{0,48},{1,49},{2,50},{3,51},{4,52},{5,53},{6,54},{7,55},{8,56},{9,... | collective-permute-start | bytes 208904 | tf_op jit(solution)/shard_map/ppermute | solution.py:405
  79.5 2.5 %shard_map.121 = (bf16[512,256]{1,0:T(8,128)(2,1)S(1)}, f32[512,256]{1,0:T(8,128)S(1)}, f32[512,256]{1,0:T(8,128)S(1)}) custom-call(s32[8]{0:T(128)S(1)} %copy-done.4, s32[3]{0:T(128)S(1)} %copy-done.5, bf16[512,1024]{1,0:T(8,128)(2,1)S(1)} %copy-done, bf16[512,1024]{1,0:T(8,128)(2,1)S(1)} %copy-done.1, bf16[512,1024]{1,0:T(8,128)(2,1)S(1)} %copy-done.2, ...), custom_call_target="tpu_custom_call" | custom-call | flops 603979776 | bytes 2097152 | tf_op jit(solution)/shard_map/pallas_call | solution.py:450
  82.0 1.4 %collective-permute-done.21.p2 = f32[136,128]{1,0:T(8,128)S(1)} collective-permute-done((f32[136,128]{1,0:T(8,128)S(1)}, f32[136,128]{1,0:T(8,128)S(1)}, u32[]{:S(2)}, u32[]{:S(2)}) %collective-permute-start.21) | collective-permute-done | bytes 69664 | tf_op jit(solution)/shard_map/ppermute | solution.py:405
  84.9 4.7 %collective-permute-start.24 = (f32[128,128]{1,0:T(8,128)S(1)}, f32[128,128]{1,0:T(8,128)S(1)}, u32[]{:S(2)}, u32[]{:S(2)}) collective-permute-start(f32[128,128]{1,0:T(8,128)S(1)} %get-tuple-element.81), channel_id=1, source_target_pairs={{0,4},{1,5},{2,6},{3,7},{4,0},{5,1},{6,2},{7,3},{8,12},{9,13},{10,... | collective-permute-start | bytes 196616 | tf_op jit(solution)/shard_map/ppermute | solution.py:405
  89.8 2.5 %shard_map.123 = (bf16[512,256]{1,0:T(8,128)(2,1)S(1)}, f32[512,256]{1,0:T(8,128)S(1)}, f32[512,256]{1,0:T(8,128)S(1)}) custom-call(s32[8]{0:T(128)S(1)} %copy-done.4, s32[3]{0:T(128)S(1)} %copy-done.5, bf16[512,1024]{1,0:T(8,128)(2,1)S(1)} %copy-done, bf16[512,1024]{1,0:T(8,128)(2,1)S(1)} %copy-done.1, bf16[512,1024]{1,0:T(8,128)(2,1)S(1)} %copy-done.2, ...), custom_call_target="tpu_custom_call" | custom-call | flops 603979776 | bytes 2097152 | tf_op jit(solution)/shard_map/pallas_call | solution.py:450
  92.4 1.5 %collective-permute-done.25.v3 = f32[128,128]{1,0:T(8,128)S(1)} collective-permute-done((f32[128,128]{1,0:T(8,128)S(1)}, f32[128,128]{1,0:T(8,128)S(1)}, u32[]{:S(2)}, u32[]{:S(2)}) %collective-permute-start.25) | collective-permute-done | bytes 65568 | tf_op jit(solution)/shard_map/ppermute | solution.py:405
  94.5 4.5 %collective-permute-start.26 = (f32[512,128]{1,0:T(8,128)S(1)}, f32[512,128]{1,0:T(8,128)S(1)}, u32[]{:S(2)}, u32[]{:S(2)}) collective-permute-start(f32[512,128]{1,0:T(8,128)S(1)} %get-tuple-element.91.refs_8_), channel_id=1, source_target_pairs={{0,1},{1,0},{2,3},{3,2},{4,5},{5,4},{6,7},{7,6},{8,9},{9,8},{10,11... | collective-permute-start | bytes 786440 | tf_op jit(solution)/shard_map/ppermute | solution.py:405
  99.0 2.2 %shard_map.125 = (bf16[512,1024]{1,0:T(8,128)(2,1)}, bf16[512,1024]{1,0:T(8,128)(2,1)}, bf16[512,1024]{1,0:T(8,128)(2,1)}) custom-call(s32[8]{0:T(128)S(1)} %copy-done.4, s32[3]{0:T(128)S(1)} %copy-done.5, bf16[512,1024]{1,0:T(8,128)(2,1)S(1)} %copy-done.1, bf16[512,1024]{1,0:T(8,128)(2,1)S(1)} %copy-done.2, f32[512,128]{1,0:T(8,128)S(1)} %get-tuple-element.84.states, ...), custom_call_target="tpu_custom_call" | custom-call | flops 134217728 | bytes 6291456 | tf_op jit(solution)/shard_map/pallas_call | solution.py:558
  101.2 2.0 %shard_map.126 = (bf16[512,1024]{1,0:T(8,128)(2,1)}, bf16[512,1024]{1,0:T(8,128)(2,1)}) custom-call(s32[8]{0:T(128)S(1)} %copy-done.4, s32[3]{0:T(128)S(1)} %copy-done.5, bf16[512,1024]{1,0:T(8,128)(2,1)S(1)} %copy-done.1, bf16[512,1024]{1,0:T(8,128)(2,1)S(1)} %copy-done.2, ...), custom_call_target="tpu_custom_call", output_to_operand_aliasing={{0}: (9, {}), {1}: (10, {})} | custom-call | flops 134217728 | bytes 4194304 | tf_op jit(solution)/shard_map/pallas_call | solution.py:567
  (61 shorter events, 20.4 us)
Async XLA Ops:
  0.6 6.3 %copy-start.5 = (s32[3]{0:T(128)S(1)}, s32[3]{0:T(128)}, u32[]{:S(2)}) copy-start(s32[3]{0:T(128)} %bounds.49) | copy-start | bytes 40
  0.6 6.3 %copy-start.4 = (s32[8]{0:T(128)S(1)}, s32[8]{0:T(128)}, u32[]{:S(2)}) copy-start(s32[8]{0:T(128)} %decay.49) | copy-start | bytes 100
  0.7 6.2 %copy-start.2 = (bf16[512,1024]{1,0:T(8,128)(2,1)S(1)}, bf16[512,1024]{1,0:T(8,128)(2,1)}, u32[]{:S(2)}) copy-start(bf16[512,1024]{1,0:T(8,128)(2,1)} %v.19) | copy-start | bytes 3145732
  0.7 6.2 %copy-start.1 = (bf16[512,1024]{1,0:T(8,128)(2,1)S(1)}, bf16[512,1024]{1,0:T(8,128)(2,1)}, u32[]{:S(2)}) copy-start(bf16[512,1024]{1,0:T(8,128)(2,1)} %k.19) | copy-start | bytes 3145732
  3.6 4.5 %collective-permute-start = (f32[512,128]{1,0:T(8,128)S(1)}, f32[512,128]{1,0:T(8,128)S(1)}, u32[]{:S(2)}, u32[]{:S(2)}) collective-permute-start(f32[512,128]{1,0:T(8,128)S(1)} %shard_map.103.after.send), channel_id=1, source_target_pairs={{0,1},{1,0},{2,3},{3,2},{4,5},{5,4},{6,7},{7,6},{8,9},{9,8},{10,11... | collective-permute-start | bytes 786440 | tf_op jit(solution)/shard_map/ppermute | solution.py:405
  8.7 6.9 %collective-permute-start.1 = (f32[128,128]{1,0:T(8,128)S(1)}, f32[128,128]{1,0:T(8,128)S(1)}, u32[]{:S(2)}, u32[]{:S(2)}) collective-permute-start(f32[128,128]{1,0:T(8,128)S(1)} %get-tuple-element.54), channel_id=1, source_target_pairs={{0,2},{1,3},{2,0},{3,1},{4,6},{5,7},{6,4},{7,5},{8,10},{9,11},{10,... | collective-permute-start | bytes 196616 | tf_op jit(solution)/shard_map/ppermute | solution.py:405
  8.8 6.8 %collective-permute-start.2 = (f32[128,128]{1,0:T(8,128)S(1)}, f32[128,128]{1,0:T(8,128)S(1)}, u32[]{:S(2)}, u32[]{:S(2)}) collective-permute-start(f32[128,128]{1,0:T(8,128)S(1)} %get-tuple-element.55), channel_id=1, source_target_pairs={{0,4},{1,5},{2,6},{3,7},{4,0},{5,1},{6,2},{7,3},{8,12},{9,13},{10,... | collective-permute-start | bytes 196616 | tf_op jit(solution)/shard_map/ppermute | solution.py:405
  11.0 4.6 %collective-permute-start.3 = (f32[128,128]{1,0:T(8,128)S(1)}, f32[128,128]{1,0:T(8,128)S(1)}, u32[]{:S(2)}, u32[]{:S(2)}) collective-permute-start(f32[128,128]{1,0:T(8,128)S(1)} %get-tuple-element.56), channel_id=1, source_target_pairs={{0,6},{1,7},{2,4},{3,5},{4,2},{5,3},{6,0},{7,1},{8,14},{9,15},{10,... | collective-permute-start | bytes 196616 | tf_op jit(solution)/shard_map/ppermute | solution.py:405
  16.3 3.2 %collective-permute-start.4 = (f32[128,128]{1,0:T(8,128)S(1)}, f32[128,128]{1,0:T(8,128)S(1)}, u32[]{:S(2)}, u32[]{:S(2)}) collective-permute-start(f32[128,128]{1,0:T(8,128)S(1)} %shard_map.107.r0.after), channel_id=1, source_target_pairs={{0,8},{1,9},{2,10},{3,11},{4,12},{5,13},{6,14},{7,15},{8,0},{9,1},... | collective-permute-start | bytes 196616 | tf_op jit(solution)/shard_map/ppermute | solution.py:405
  20.1 9.7 %collective-permute-start.7 = (f32[128,128]{1,0:T(8,128)S(1)}, f32[128,128]{1,0:T(8,128)S(1)}, u32[]{:S(2)}, u32[]{:S(2)}) collective-permute-start(f32[128,128]{1,0:T(8,128)S(1)} %shard_map.108.after.p0), channel_id=1, source_target_pairs={{0,48},{1,49},{2,50},{3,51},{4,52},{5,53},{6,54},{7,55},{8,56},{9,... | collective-permute-start | bytes 196616 | tf_op jit(solution)/shard_map/ppermute | solution.py:405
  26.0 6.1 %collective-permute-start.6 = (f32[128,128]{1,0:T(8,128)S(1)}, f32[128,128]{1,0:T(8,128)S(1)}, u32[]{:S(2)}, u32[]{:S(2)}) collective-permute-start(f32[128,128]{1,0:T(8,128)S(1)} %shard_map.108.after.p0), channel_id=1, source_target_pairs={{0,40},{1,41},{2,42},{3,43},{4,44},{5,45},{6,46},{7,47},{8,32},{9,... | collective-permute-start | bytes 196616 | tf_op jit(solution)/shard_map/ppermute | solution.py:405
  26.7 5.4 %collective-permute-start.5 = (f32[128,128]{1,0:T(8,128)S(1)}, f32[128,128]{1,0:T(8,128)S(1)}, u32[]{:S(2)}, u32[]{:S(2)}) collective-permute-start(f32[128,128]{1,0:T(8,128)S(1)} %shard_map.108.after.p0), channel_id=1, source_target_pairs={{0,16},{1,17},{2,18},{3,19},{4,20},{5,21},{6,22},{7,23},{8,24},{9,... | collective-permute-start | bytes 196616 | tf_op jit(solution)/shard_map/ppermute | solution.py:405
  29.8 16.7 %copy-start.3 = (bf16[512,1024]{1,0:T(8,128)(2,1)S(1)}, bf16[512,1024]{1,0:T(8,128)(2,1)}, u32[]{:S(2)}) copy-start(bf16[512,1024]{1,0:T(8,128)(2,1)} %grad.7) | copy-start | bytes 3145732
  32.8 3.9 %collective-permute-start.8 = (f32[128,128]{1,0:T(8,128)S(1)}, f32[128,128]{1,0:T(8,128)S(1)}, u32[]{:S(2)}, u32[]{:S(2)}) collective-permute-start(f32[128,128]{1,0:T(8,128)S(1)} %get-tuple-element.58), channel_id=1, source_target_pairs={{0,2},{1,3},{2,0},{3,1},{4,6},{5,7},{6,4},{7,5},{8,10},{9,11},{10,... | collective-permute-start | bytes 196616 | tf_op jit(solution)/shard_map/ppermute | solution.py:405
  33.0 4.9 %collective-permute-start.9 = (f32[128,128]{1,0:T(8,128)S(1)}, f32[128,128]{1,0:T(8,128)S(1)}, u32[]{:S(2)}, u32[]{:S(2)}) collective-permute-start(f32[128,128]{1,0:T(8,128)S(1)} %get-tuple-element.59), channel_id=1, source_target_pairs={{0,4},{1,5},{2,6},{3,7},{4,0},{5,1},{6,2},{7,3},{8,12},{9,13},{10,... | collective-permute-start | bytes 196616 | tf_op jit(solution)/shard_map/ppermute | solution.py:405
  35.5 4.3 %collective-permute-start.10 = (f32[128,128]{1,0:T(8,128)S(1)}, f32[128,128]{1,0:T(8,128)S(1)}, u32[]{:S(2)}, u32[]{:S(2)}) collective-permute-start(f32[128,128]{1,0:T(8,128)S(1)} %get-tuple-element.60), channel_id=1, source_target_pairs={{0,6},{1,7},{2,4},{3,5},{4,2},{5,3},{6,0},{7,1},{8,14},{9,15},{10,... | collective-permute-start | bytes 196616 | tf_op jit(solution)/shard_map/ppermute | solution.py:405
  40.5 7.3 %collective-permute-start.11 = (f32[512,128]{1,0:T(8,128)S(1)}, f32[512,128]{1,0:T(8,128)S(1)}, u32[]{:S(2)}, u32[]{:S(2)}) collective-permute-start(f32[512,128]{1,0:T(8,128)S(1)} %get-tuple-element.61.refs_0_), channel_id=1, source_target_pairs={{0,1},{1,0},{2,3},{3,2},{4,5},{5,4},{6,7},{7,6},{8,9},{9,8},{10,11... | collective-permute-start | bytes 786440 | tf_op jit(solution)/shard_map/ppermute | solution.py:405
  49.2 3.9 %collective-permute-start.14 = (f32[8,512]{1,0:T(8,128)S(1)}, f32[8,512]{1,0:T(8,128)S(1)}, u32[]{:S(2)}, u32[]{:S(2)}) collective-permute-start(f32[8,512]{1,0:T(8,128)S(1)} %get-tuple-element.64.s0), channel_id=1, source_target_pairs={{0,192},{64,128},{128,64},{192,0},{1,193},{65,129},{129,65},{193,1... | collective-permute-start | bytes 49160 | tf_op jit(solution)/shard_map/ppermute | solution.py:513
  51.7 4.1 %collective-permute-start.13 = (f32[8,512]{1,0:T(8,128)S(1)}, f32[8,512]{1,0:T(8,128)S(1)}, u32[]{:S(2)}, u32[]{:S(2)}) collective-permute-start(f32[8,512]{1,0:T(8,128)S(1)} %get-tuple-element.64.s0), channel_id=1, source_target_pairs={{0,128},{64,192},{128,0},{192,64},{1,129},{65,193},{129,1},{193,65... | collective-permute-start | bytes 49160 | tf_op jit(solution)/shard_map/ppermute | solution.py:513
  52.3 3.6 %collective-permute-start.12 = (f32[8,512]{1,0:T(8,128)S(1)}, f32[8,512]{1,0:T(8,128)S(1)}, u32[]{:S(2)}, u32[]{:S(2)}) collective-permute-start(f32[8,512]{1,0:T(8,128)S(1)} %get-tuple-element.64.s0), channel_id=1, source_target_pairs={{0,64},{64,0},{128,192},{192,128},{1,65},{65,1},{129,193},{193,129... | collective-permute-start | bytes 49160 | tf_op jit(solution)/shard_map/ppermute | solution.py:513
  57.6 3.4 %collective-permute-start.15 = (f32[520,128]{1,0:T(8,128)S(1)}, f32[520,128]{1,0:T(8,128)S(1)}, u32[]{:S(2)}, u32[]{:S(2)}) collective-permute-start(f32[520,128]{1,0:T(8,128)S(1)} %get-tuple-element.67.refs_0_.send), channel_id=1, source_target_pairs={{0,1},{1,0},{2,3},{3,2},{4,5},{5,4},{6,7},{7,6},{8,9},{9,8},{10,11... | collective-permute-start | bytes 798728 | tf_op jit(solution)/shard_map/ppermute | solution.py:405
  61.6 6.5 %collective-permute-start.16 = (f32[136,128]{1,0:T(8,128)S(1)}, f32[136,128]{1,0:T(8,128)S(1)}, u32[]{:S(2)}, u32[]{:S(2)}) collective-permute-start(f32[136,128]{1,0:T(8,128)S(1)} %get-tuple-element.70), channel_id=1, source_target_pairs={{0,2},{1,3},{2,0},{3,1},{4,6},{5,7},{6,4},{7,5},{8,10},{9,11},{10,... | collective-permute-start | bytes 208904 | tf_op jit(solution)/shard_map/ppermute | solution.py:405
  61.7 7.0 %collective-permute-start.17 = (f32[136,128]{1,0:T(8,128)S(1)}, f32[136,128]{1,0:T(8,128)S(1)}, u32[]{:S(2)}, u32[]{:S(2)}) collective-permute-start(f32[136,128]{1,0:T(8,128)S(1)} %get-tuple-element.71), channel_id=1, source_target_pairs={{0,4},{1,5},{2,6},{3,7},{4,0},{5,1},{6,2},{7,3},{8,12},{9,13},{10,... | collective-permute-start | bytes 208904 | tf_op jit(solution)/shard_map/ppermute | solution.py:405
  64.9 4.7 %collective-permute-start.18 = (f32[136,128]{1,0:T(8,128)S(1)}, f32[136,128]{1,0:T(8,128)S(1)}, u32[]{:S(2)}, u32[]{:S(2)}) collective-permute-start(f32[136,128]{1,0:T(8,128)S(1)} %get-tuple-element.72), channel_id=1, source_target_pairs={{0,6},{1,7},{2,4},{3,5},{4,2},{5,3},{6,0},{7,1},{8,14},{9,15},{10,... | collective-permute-start | bytes 208904 | tf_op jit(solution)/shard_map/ppermute | solution.py:405
  70.2 3.2 %collective-permute-start.19 = (f32[136,128]{1,0:T(8,128)S(1)}, f32[136,128]{1,0:T(8,128)S(1)}, u32[]{:S(2)}, u32[]{:S(2)}) collective-permute-start(f32[136,128]{1,0:T(8,128)S(1)} %shard_map.118.after.r0), channel_id=1, source_target_pairs={{0,8},{1,9},{2,10},{3,11},{4,12},{5,13},{6,14},{7,15},{8,0},{9,1},... | collective-permute-start | bytes 208904 | tf_op jit(solution)/shard_map/ppermute | solution.py:405
  74.1 7.9 %collective-permute-start.22 = (f32[136,128]{1,0:T(8,128)S(1)}, f32[136,128]{1,0:T(8,128)S(1)}, u32[]{:S(2)}, u32[]{:S(2)}) collective-permute-start(f32[136,128]{1,0:T(8,128)S(1)} %shard_map.120.after.p0), channel_id=1, source_target_pairs={{0,48},{1,49},{2,50},{3,51},{4,52},{5,53},{6,54},{7,55},{8,56},{9,... | collective-permute-start | bytes 208904 | tf_op jit(solution)/shard_map/ppermute | solution.py:405
  77.1 6.2 %collective-permute-start.21 = (f32[136,128]{1,0:T(8,128)S(1)}, f32[136,128]{1,0:T(8,128)S(1)}, u32[]{:S(2)}, u32[]{:S(2)}) collective-permute-start(f32[136,128]{1,0:T(8,128)S(1)} %shard_map.120.after.p0), channel_id=1, source_target_pairs={{0,40},{1,41},{2,42},{3,43},{4,44},{5,45},{6,46},{7,47},{8,32},{9,... | collective-permute-start | bytes 208904 | tf_op jit(solution)/shard_map/ppermute | solution.py:405
  78.4 5.0 %collective-permute-start.20 = (f32[136,128]{1,0:T(8,128)S(1)}, f32[136,128]{1,0:T(8,128)S(1)}, u32[]{:S(2)}, u32[]{:S(2)}) collective-permute-start(f32[136,128]{1,0:T(8,128)S(1)} %shard_map.120.after.p0), channel_id=1, source_target_pairs={{0,16},{1,17},{2,18},{3,19},{4,20},{5,21},{6,22},{7,23},{8,24},{9,... | collective-permute-start | bytes 208904 | tf_op jit(solution)/shard_map/ppermute | solution.py:405
  84.7 7.7 %collective-permute-start.23 = (f32[128,128]{1,0:T(8,128)S(1)}, f32[128,128]{1,0:T(8,128)S(1)}, u32[]{:S(2)}, u32[]{:S(2)}) collective-permute-start(f32[128,128]{1,0:T(8,128)S(1)} %get-tuple-element.80), channel_id=1, source_target_pairs={{0,2},{1,3},{2,0},{3,1},{4,6},{5,7},{6,4},{7,5},{8,10},{9,11},{10,... | collective-permute-start | bytes 196616 | tf_op jit(solution)/shard_map/ppermute | solution.py:405
  84.9 7.5 %collective-permute-start.24 = (f32[128,128]{1,0:T(8,128)S(1)}, f32[128,128]{1,0:T(8,128)S(1)}, u32[]{:S(2)}, u32[]{:S(2)}) collective-permute-start(f32[128,128]{1,0:T(8,128)S(1)} %get-tuple-element.81), channel_id=1, source_target_pairs={{0,4},{1,5},{2,6},{3,7},{4,0},{5,1},{6,2},{7,3},{8,12},{9,13},{10,... | collective-permute-start | bytes 196616 | tf_op jit(solution)/shard_map/ppermute | solution.py:405
  89.5 4.3 %collective-permute-start.25 = (f32[128,128]{1,0:T(8,128)S(1)}, f32[128,128]{1,0:T(8,128)S(1)}, u32[]{:S(2)}, u32[]{:S(2)}) collective-permute-start(f32[128,128]{1,0:T(8,128)S(1)} %get-tuple-element.82), channel_id=1, source_target_pairs={{0,6},{1,7},{2,4},{3,5},{4,2},{5,3},{6,0},{7,1},{8,14},{9,15},{10,... | collective-permute-start | bytes 196616 | tf_op jit(solution)/shard_map/ppermute | solution.py:405
  94.5 6.7 %collective-permute-start.26 = (f32[512,128]{1,0:T(8,128)S(1)}, f32[512,128]{1,0:T(8,128)S(1)}, u32[]{:S(2)}, u32[]{:S(2)}) collective-permute-start(f32[512,128]{1,0:T(8,128)S(1)} %get-tuple-element.91.refs_8_), channel_id=1, source_target_pairs={{0,1},{1,0},{2,3},{3,2},{4,5},{5,4},{6,7},{7,6},{8,9},{9,8},{10,11... | collective-permute-start | bytes 786440 | tf_op jit(solution)/shard_map/ppermute | solution.py:405
  (2 other events, 11.5 us)

commit v4 on v3

--- a/solution.py
+++ b/solution.py
@@ -60,19 +60,77 @@
     return rows
 
 
+RATES, ENTER, LEAVE, FORWARD, BACKWARD = 0, 8, 9, 16, 0
+CHIP_OWN, CHIP_OTHER, ROW, HALF, FAR, NEAR, INTO, ACROSS, CORE = 0, 4, 8, 12, 16, 16, 20, 24, 40
+CHAIN_ROWS = 48
+FAR_Z = 6
+SLOT = (0, 2, 1, 3)
+
+
 def token_rows():
-    return lax.broadcasted_iota(jnp.int32, (TOK, HEAD), 0)
-
-
-def enter_decay(rate, entering):
-    return jnp.where(token_rows() < entering, powers(rate, 1.0, True), 0.0)
-
-
-def leave_decay(rate, leaving):
-    return jnp.where(token_rows() >= leaving, powers(rate, 0.0, False), 0.0)
-
-
-def masks_kernel(decay, bounds, mask, flipped):
+    return lax.broadcasted_iota(jnp.int32, (TOK, HEAD), 0).astype(F32)
+
+
+def rate_row(table, head):
+    return table[pl.ds(head, 1), :]
+
+
+def enter_decay(table, head):
+    return jnp.where(token_rows() < table[ENTER : ENTER + 1, :], powers(rate_row(table, head), 1.0, True), 0.0)
+
+
+def leave_decay(table, head):
+    return jnp.where(token_rows() >= table[LEAVE : LEAVE + 1, :], powers(rate_row(table, head), 0.0, False), 0.0)
+
+
+def fill_chain(table, base, decay, bounds, reverse):
+    at, z, y, c = place()
+    one = jnp.ones((1, HEAD), F32)
+    middle = (at - c + 1) * TOK
+    row, row_end, centre = z * BLOCK_Z, (z + 1) * BLOCK_Z, 4 * BLOCK_Z
+
+    def put(index, value):
+        table[base + index : base + index + 1, :] = value
+
+    def across(rate, earlier, later):
+        return carry(rate, bounds, earlier, later)
+
+    for k in range(4):
+        rate = rate_of(decay[4 * c + (y ^ k)])
+        first, second = across(rate, middle - TOK, middle), across(rate, middle, middle + TOK)
+        if reverse:
+            put(CHIP_OWN + k, jnp.where(c == 1, first, one))
+            put(CHIP_OTHER + k, jnp.where(c == 1, one, first))
+            put(CORE + k, second)
+        else:
+            put(CHIP_OWN + k, jnp.where(c == 0, second, one))
+            put(CHIP_OTHER + k, jnp.where(c == 0, one, second))
+            put(CORE + k, first)
+    rate = rate_of(decay[4 * c + y])
+    for k in range(4):
+        here, line = row + (y ^ k) * BLOCK_Y, (z ^ k) * BLOCK_Z
+        if reverse:
+            put(ROW + k, across(rate, row, here))
+            put(HALF + k, across(rate, centre, line))
+            put(NEAR + k, across(rate, row_end, line if k else centre))
+            put(INTO + k, across(rate, here + BLOCK_Y, row_end))
+        else:
+            put(ROW + k, across(rate, here + BLOCK_Y, row_end))
+            put(HALF + k, across(rate, line + BLOCK_Z, centre))
+            put(NEAR + k, across(rate, line + BLOCK_Z if k else centre, row))
+            put(INTO + k, across(rate, row, here))
+        for m in range(4):
+            if m != k:
+                there = row + (y ^ m) * BLOCK_Y
+                if reverse:
+                    put(ACROSS + 4 * k + m, across(rate, here + BLOCK_Y, there))
+                else:
+                    put(ACROSS + 4 * k + m, across(rate, there + BLOCK_Y, here))
+
+
+def masks_kernel(decay, bounds, gain, after, mask, flipped, table, gain_out):
+    gain_out[...] = gain[...]
+    fill_chain(table, BACKWARD, decay, bounds, True)
     first = place()[0] * TOK
     for lo in range(0, TOK, HEAD):
         row = lax.broadcasted_iota(jnp.int32, (HEAD, TOK), 0) + lo
@@ -128,10 +186,15 @@
     return 4 * c if own else 4 * (1 - c)
 
 
-def sent_states_kernel(decay, bounds, k, v, out, k_in, v_in, sems):
+def sent_states_kernel(decay_in, bounds_in, k, v, out, table, k_in, v_in, decay, bounds, sems):
     at, _, y, _ = place()
-    _, leaving = tokens_in(bounds, at)
     heads = [first_head(False) + (y ^ i) for i in range(4)]
+    numbers = (
+        pltpu.make_async_copy(decay_in, decay, sems.at[2, 0]),
+        pltpu.make_async_copy(bounds_in, bounds, sems.at[2, 1]),
+    )
+    for copy in numbers:
+        copy.start()
     copies = []
     for i, head in enumerate(heads):
         pair = (
@@ -141,29 +204,35 @@
         for copy in pair:
             copy.start()
         copies.append(pair)
+    for copy in numbers:
+        copy.wait()
+    for head in range(HEADS_DEV):
+        table[RATES + head : RATES + head + 1, :] = rate_of(decay[head])
+    entering, leaving = tokens_in(bounds, at)
+    table[ENTER : ENTER + 1, :] = jnp.full((1, HEAD), entering.astype(F32), F32)
+    table[LEAVE : LEAVE + 1, :] = jnp.full((1, HEAD), leaving.astype(F32), F32)
+    fill_chain(table, FORWARD, decay, bounds, False)
     for i, head in enumerate(heads):
-        weights = leave_decay(rate_of(decay[head]), leaving)
+        weights = leave_decay(table, head)
         for copy in copies[i]:
             copy.wait()
         decayed = (weights * k_in[i].astype(F32)).astype(BF16)
         out[i * HEAD : (i + 1) * HEAD, :] = mm_at(decayed, v_in[i])
 
 
-def kept_states_kernel(decay, bounds, k, v, after, out):
-    at, _, y, _ = place()
-    _, leaving = tokens_in(bounds, at)
+def kept_states_kernel(table, k, v, after, out):
+    y = place()[2]
     for i in range(4):
         head = first_head(True) + (y ^ i)
-        weights = leave_decay(rate_of(decay[head]), leaving)
-        decayed = (weights * k[:, columns(head)].astype(F32)).astype(BF16)
+        decayed = (leave_decay(table, head) * k[:, columns(head)].astype(F32)).astype(BF16)
         out[i * HEAD : (i + 1) * HEAD, :] = mm_at(decayed, v[:, columns(head)])
 
 
-def intra_kernel(decay, bounds, q, k, v, mask, after, out_ref, *, own):
+def intra_kernel(table, q, k, v, mask, after, out_ref, *, own):
     half = TOK // 2
     for j in range(4):
         head = first_head(own) + j
-        rate, at = rate_of(decay[head]), columns(head)
+        rate, at = rate_row(table, head), columns(head)
         scaled = (powers(-rate, 0.0, True) * k[:, at].astype(F32)).astype(BF16)
         down = powers(rate, 0.0, True)
         for lo in (0, half):
@@ -172,130 +241,71 @@
             out_ref[lo:hi, j * HEAD : (j + 1) * HEAD] = down[lo:hi, :] * mm(mixing, v[0:hi, at])
 
 
-def chip_kernel(decay, bounds, keep, got, send, after, *outs, reverse, gains):
-    at, z, y, c = place()
-    middle = (at - c + 1) * TOK
+def chip_kernel(table, keep, got, send, after, *outs, base, reverse, gains):
     for k in range(4):
-        rate = rate_of(decay[4 * c + (y ^ k)])
-        if reverse:
-            far = carry(rate, bounds, middle - TOK, middle)
-            own, other = jnp.where(c == 1, far, 1.0), jnp.where(c == 1, 1.0, far)
-        else:
-            far = carry(rate, bounds, middle, middle + TOK)
-            own, other = jnp.where(c == 0, far, 1.0), jnp.where(c == 0, 1.0, far)
+        own, other = base + CHIP_OWN + k, base + CHIP_OTHER + k
         rows = slice(k * HEAD, (k + 1) * HEAD)
-        outs[k][0:HEAD, :] = own * keep[rows, :] + other * got[rows, :]
+        outs[SLOT[k]][0:HEAD, :] = table[own : own + 1, :] * keep[rows, :] + table[other : other + 1, :] * got[rows, :]
         if gains:
             tail = slice(4 * HEAD, 4 * HEAD + 8)
-            outs[k][HEAD : HEAD + 8, :] = send[tail, :] + got[tail, :]
-
-
-def row_kernel(decay, bounds, t0, t1, t2, t3, after, out, *, reverse, gains):
-    at, z, y, c = place()
-    rate = rate_of(decay[4 * c + y])
+            outs[SLOT[k]][HEAD : HEAD + 8, :] = send[tail, :] + got[tail, :]
+
+
+def sum_kernel(table, p0, p1, p2, p3, after, out, *, base, reverse, gains):
     total = 0.0
-    for k, t in enumerate((t0, t1, t2, t3)):
-        edge = z * BLOCK_Z + (y ^ k) * BLOCK_Y
-        if reverse:
-            weight = carry(rate, bounds, z * BLOCK_Z, edge)
-        else:
-            weight = carry(rate, bounds, edge + BLOCK_Y, (z + 1) * BLOCK_Z)
-        total += weight * t[0:HEAD, :]
+    for k, p in enumerate((p0, p1, p2, p3)):
+        total += table[base + k : base + k + 1, :] * p[0:HEAD, :]
     out[0:HEAD, :] = total
     if gains:
         tail = slice(HEAD, HEAD + 8)
-        out[tail, :] = t0[tail, :] + t1[tail, :] + t2[tail, :] + t3[tail, :]
-
-
-def pair_kernel(decay, bounds, r0, r1, after, out, *, reverse, gains):
-    at, z, y, c = place()
-    rate = rate_of(decay[4 * c + y])
-    first = (z - z % 2) * BLOCK_Z
-    total = 0.0
-    for k, r in enumerate((r0, r1)):
-        edge = (z ^ k) * BLOCK_Z
-        if reverse:
-            weight = carry(rate, bounds, first, edge)
-        else:
-            weight = carry(rate, bounds, edge + BLOCK_Z, first + 2 * BLOCK_Z)
-        total += weight * r[0:HEAD, :]
-    out[0:HEAD, :] = total
+        out[tail, :] = p0[tail, :] + p1[tail, :] + p2[tail, :] + p3[tail, :]
+
+
+def chips_in_kernel(table, r1, r2, r3, far, sent, t0, t1, t2, t3, after, *outs, base, reverse, gains):
+    total = table[base + FAR : base + FAR + 1, :] * far[0:HEAD, :]
+    for k, r in enumerate((r1, r2, r3)):
+        at = base + NEAR + 1 + k
+        total += table[at : at + 1, :] * r[0:HEAD, :]
+    for k in range(4):
+        at = base + INTO + k
+        state = table[at : at + 1, :] * total
+        for m, t in enumerate((t0, t1, t2, t3)):
+            if m != k:
+                at = base + ACROSS + 4 * k + m
+                state += table[at : at + 1, :] * t[0:HEAD, :]
+        outs[SLOT[k]][...] = state
     if gains:
+        _, z, y, c = place()
         tail = slice(HEAD, HEAD + 8)
-        out[tail, :] = r0[tail, :] + r1[tail, :]
-
-
-PAIRS = (2, 5, 6)
-
-
-def chips_in_kernel(decay, bounds, r1, p0, p1, p2, p3, t0, t1, t2, t3, after, *outs, reverse, gains):
-    at, z, y, c = place()
-    rate = rate_of(decay[4 * c + y])
-    edge = (z + 1) * BLOCK_Z if reverse else z * BLOCK_Z
-    other = (z ^ 1) * BLOCK_Z
-    if reverse:
-        total = carry(rate, bounds, edge, other) * r1[0:HEAD, :]
-    else:
-        total = carry(rate, bounds, other + BLOCK_Z, edge) * r1[0:HEAD, :]
-    for k, p in zip(PAIRS, (p1, p2, p3)):
-        there = z ^ k
-        first = (there - there % 2) * BLOCK_Z
-        if reverse:
-            weight = carry(rate, bounds, edge, first)
-        else:
-            weight = carry(rate, bounds, first + 2 * BLOCK_Z, edge)
-        total += weight * p[0:HEAD, :]
-    for k in range(4):
-        here = z * BLOCK_Z + (y ^ k) * BLOCK_Y
-        if reverse:
-            state = carry(rate, bounds, here + BLOCK_Y, edge) * total
-        else:
-            state = carry(rate, bounds, edge, here) * total
-        for m, t in enumerate((t0, t1, t2, t3)):
-            if m == k:
-                continue
-            there = z * BLOCK_Z + (y ^ m) * BLOCK_Y
-            if reverse:
-                weight = carry(rate, bounds, here + BLOCK_Y, there)
-            else:
-                weight = carry(rate, bounds, there + BLOCK_Y, here)
-            state += weight * t[0:HEAD, :]
-        outs[k][...] = state
-    if gains:
-        tail = slice(HEAD, HEAD + 8)
-        outs[4][...] = p0[tail, :] + p1[tail, :] + p2[tail, :] + p3[tail, :]
+        outs[4][...] = sent[tail, :] + far[tail, :]
         row = outs[4][pl.ds(z, 1), :]
         turned = pltpu.roll(row, (HEAD - 32 * y - 16 * c) % HEAD, axis=1)
         outs[5][...] = turned[0, 0:16]
 
 
-def cores_in_kernel(decay, bounds, v0, v1, v2, v3, keep, got, after, mine, other, *, reverse):
-    at, z, y, c = place()
-    middle = (at - c + 1) * TOK
+def cores_in_kernel(table, v0, v1, v2, v3, keep, got, after, mine, other, *, base, reverse):
+    c = place()[3]
+    deep = c == 0 if reverse else c == 1
     for k, v in enumerate((v0, v1, v2, v3)):
-        rate = rate_of(decay[4 * c + (y ^ k)])
-        if reverse:
-            step, deep = carry(rate, bounds, middle, middle + TOK), c == 0
-        else:
-            step, deep = carry(rate, bounds, middle - TOK, middle), c == 1
+        at = base + CORE + k
         rows = slice(k * HEAD, (k + 1) * HEAD)
         state = v[...]
-        mine[rows, :] = jnp.where(deep, step * state + got[rows, :], state)
-        other[rows, :] = jnp.where(deep, state, step * state + keep[rows, :])
+        step = table[at : at + 1, :] * state
+        mine[rows, :] = jnp.where(deep, step + got[rows, :], state)
+        other[rows, :] = jnp.where(deep, state, step + keep[rows, :])
 
 
 def state_of(states, j):
     return states[columns(j ^ place()[2]), :].astype(BF16)
 
 
-def attended_kernel(decay, bounds, q, intra, grad, gain, states, *refs, own):
+def attended_kernel(table, q, intra, grad, gain, states, *refs, own):
     out_ref, sums = refs[-2:]
-    entering, _ = tokens_in(bounds, place()[0])
     square, cross = 0.0, 0.0
     for j in range(4):
         head = first_head(own) + j
         at, local = columns(head), slice(j * HEAD, (j + 1) * HEAD)
-        weights = enter_decay(rate_of(decay[head]), entering)
+        weights = enter_decay(table, head)
         out = intra[:, local] + weights * mm(q[:, at], state_of(states, j))
         out_ref[:, local] = out
         square += out * out
@@ -309,10 +319,9 @@
     sums[4:8, :] = jnp.broadcast_to(cross, (4, TOK))
 
 
-def mixed_kernel(decay, bounds, s0, s1, s2, s3, o, grad, q, gain, *refs, own):
+def mixed_kernel(table, s0, s1, s2, s3, o, grad, q, gain, *refs, own):
     d, states = refs[-2:]
-    at, _, y, _ = place()
-    entering, _ = tokens_in(bounds, at)
+    y = place()[2]
     sums = s0[...] + s1[...] + s2[...] + s3[...]
     r = lax.rsqrt(sums[0:1, :] * (1.0 / FEATURES) + 1e-06)
     inverse = jnp.broadcast_to(r, (HEAD, TOK)).T
@@ -331,7 +340,7 @@
         low = (inverse * (wide * gain[pl.ds(head, 1), :] - normed * mean)).astype(BF16)
         d[:, local] = low
         term(head, wide, normed)
-        weights = enter_decay(rate_of(decay[head]), entering)
+        weights = enter_decay(table, head)
         states[columns(j ^ y), :] = mm_at((weights * q[:, columns(head)].astype(F32)).astype(BF16), low)
     if not own:
         for j in range(4):
@@ -339,17 +348,16 @@
             term(head, grad[:, columns(head)].astype(F32), inverse * refs[0][:, j * HEAD : (j + 1) * HEAD])
 
 
-def grads_kernel(decay, bounds, q, k, v, d, mask, flipped, states, after, dq, dk, dv, *, own, start):
-    entering, _ = tokens_in(bounds, place()[0])
+def grads_kernel(table, q, k, v, d, mask, flipped, states, after, dq, dk, dv, *, own, start):
     half = TOK // 2
     for n in range(2):
         j = start + n
         head = first_head(own) + j
-        rate, at = rate_of(decay[head]), columns(head)
+        rate, at = rate_row(table, head), columns(head)
         out, local = slice(n * HEAD, (n + 1) * HEAD), slice(j * HEAD, (j + 1) * HEAD)
         state = state_of(states, j)
         up, down = powers(-rate, 0.0, True), powers(rate, 0.0, True)
-        inside = jnp.where(token_rows() < entering, jnp.exp(rate), 0.0)
+        inside = jnp.where(token_rows() < table[ENTER : ENTER + 1, :], jnp.exp(rate), 0.0)
         v_up = (up * v[:, at].astype(F32)).astype(BF16)
         d_down = (down * d[:, local].astype(F32)).astype(BF16)
         q_down = (down * q[:, at].astype(F32)).astype(BF16)
@@ -364,10 +372,9 @@
             dv[lo:hi, out] = up[lo:hi, :] * mm(mixing, d[lo:TOK, local])
 
 
-def last_kernel(decay, bounds, k, v, states, *refs, own):
+def last_kernel(table, k, v, states, *refs, own):
     parts, buffers = refs[:4], refs[-3:]
     (dk, dv), sems = refs[-5:-3] if not own else refs[-6:-4], buffers[2]
-    _, leaving = tokens_in(bounds, place()[0])
     copies = []
     if own:
         dq = refs[-4]
@@ -379,7 +386,7 @@
         head = first_head(own) + j
         at, local = columns(head), slice(j * HEAD, (j + 1) * HEAD)
         inner = slice(j % 2 * HEAD, (j % 2 + 1) * HEAD)
-        weights = leave_decay(rate_of(decay[head]), leaving)
+        weights = leave_decay(table, head)
         state = state_of(states, j)
         buffers[0][:, local] = (parts[j // 2][:, inner] + weights * mm_bt(v[:, at], state)).astype(BF16)
         copies.append(pltpu.make_async_copy(buffers[0].at[:, local], dk.at[:, at], sems.at[0, j]))
@@ -405,34 +412,38 @@
     return lax.ppermute(array, "seq", pairs)
 
 
-def carried(send, make_keep, decay, bounds, reverse, gains, work):
+def carried(send, make_keep, table, base, reverse, gains, work):
     extra = 8 if gains else 0
     small = shape(HEAD + extra, HEAD)
 
-    def step(kernel, outs, *args, after, **more):
+    def step(kernel, outs, *args, after, base=base, **more):
         return call(
-            functools.partial(kernel, reverse=reverse, **more),
+            functools.partial(kernel, reverse=reverse, base=base, **more),
             outs,
-            in_specs=[SMEM, SMEM] + [VMEM] * len(args) + [ANY],
+            in_specs=[VMEM] * (1 + len(args)) + [ANY],
             out_specs=jax.tree.map(lambda _: VMEM, outs),
             limit=8,
-        )(decay, bounds, *args, after)
+        )(table, *args, after)
+
+    def around(arrays, ks, **axis):
+        moved = {k: exchange(arrays[k], **{name: k for name in axis}) for k in ks}
+        return [arrays[0]] + [moved[k] for k in (1, 2, 3)]
 
     got = exchange(send, dc=1)
     keep = make_keep(send)
     chips = step(chip_kernel, [small] * 4, keep, got, send, gains=gains, after=keep)
     done = work[0](chips[0])
-    chips = [chips[0]] + [exchange(chips[k], dy=k) for k in (1, 2, 3)]
-    row = step(row_kernel, small, *chips, gains=gains, after=done)
+    chips = around([chips[n] for n in SLOT], (2, 1, 3), dy=1)
+    row = step(sum_kernel, small, *chips, gains=gains, after=done, base=base + ROW)
     done = work[1](row)
-    near = exchange(row, dz=1)
-    pair = step(pair_kernel, small, row, near, gains=gains, after=done)
-    done = work[2](pair)
-    pairs = [pair] + [exchange(pair, dz=k) for k in PAIRS]
+    rows = around([row] * 4, (1, 2, 3), dz=1)
+    sent = step(sum_kernel, small, *rows, gains=gains, after=done, base=base + HALF)
+    done = work[2](sent)
+    far = exchange(sent, dz=FAR_Z)
     outs = [shape(HEAD, HEAD)] * 4 + ([shape(8, HEAD), shape(16)] if gains else [])
-    outs = step(chips_in_kernel, outs, near, *pairs, *chips, gains=gains, after=done)
+    outs = step(chips_in_kernel, outs, *rows[1:], far, sent, *chips, gains=gains, after=done)
     done = work[3](outs[0])
-    states = [outs[0]] + [exchange(outs[k], dy=k) for k in (1, 2, 3)]
+    states = around([outs[n] for n in SLOT], (2, 1, 3), dy=1)
     mine, other = step(cores_in_kernel, [shape(4 * HEAD, HEAD)] * 2, *states, keep, got, after=done)
     return mine, other, (outs[5] if gains else None)
 
@@ -444,24 +455,24 @@
     small_mm = TOK * HEAD * HEAD * HEADS_DEV
     big_mm = 2 * TOK * TOK * HEAD * HEADS_DEV * 3 // 4
     state_shape = shape(4 * HEAD, HEAD)
-    scalars = [SMEM, SMEM]
 
     def local(kernel, outs, args, order=(), flops=0, moved=0, **more):
         return call(
             functools.partial(kernel, **more),
             outs,
-            in_specs=scalars + [VMEM] * len(args) + [ANY] * len(order),
+            in_specs=[VMEM] * (1 + len(args)) + [ANY] * len(order),
             out_specs=jax.tree.map(lambda _: VMEM, outs),
             flops=flops,
             moved=moved,
-        )(decay, bounds, *args, *order)
-
-    send = call(
+        )(table, *args, *order)
+
+    send, table = call(
         sent_states_kernel,
-        state_shape,
-        in_specs=scalars + [ANY] * 2,
-        out_specs=VMEM,
-        scratch=[pltpu.VMEM((4, TOK, HEAD), BF16)] * 2 + [pltpu.SemaphoreType.DMA((2, 4))],
+        [state_shape, shape(FORWARD + CHAIN_ROWS, HEAD)],
+        in_specs=[ANY] * 4,
+        out_specs=[VMEM] * 2,
+        scratch=[pltpu.VMEM((4, TOK, HEAD), BF16)] * 2
+        + [pltpu.SMEM((HEADS_DEV,), jnp.int32), pltpu.SMEM((3,), jnp.int32), pltpu.SemaphoreType.DMA((3, 4))],
         flops=small_mm,
         moved=3 << 19,
     )(*[pltpu.with_memory_space_constraint(x, pltpu.HBM) for x in (decay, bounds, keys, values)])
@@ -475,7 +486,14 @@
     def make_intra(own):
         def run(after):
             if own:
-                made["masks"] = local(masks_kernel, [pairs] * 2, [], moved=1 << 20)
+                outs = [pairs] * 2 + [shape(CHAIN_ROWS, HEAD), shape(HEADS_DEV, HEAD)]
+                made["masks"] = call(
+                    masks_kernel,
+                    outs,
+                    in_specs=[SMEM, SMEM, VMEM, ANY],
+                    out_specs=[VMEM] * 4,
+                    moved=1 << 20,
+                )(*[pltpu.with_memory_space_constraint(x, pltpu.HBM) for x in (decay, bounds)], gain, after)
             made[own] = local(
                 intra_kernel,
                 shape(TOK, half),
@@ -493,9 +511,10 @@
         return after
 
     mine, other, _ = carried(
-        send, keep_states, decay, bounds, False, False, [make_intra(True), same, make_intra(False), same]
+        send, keep_states, table, FORWARD, False, False, [make_intra(True), make_intra(False), same, same]
     )
     theirs = exchange(other, dc=1)
+    mask, flipped, back_table, gain = made["masks"]
     sums = shape(8, TOK)
     outs = [shape(TOK, half), sums]
     o_mine, own_sums = local(
@@ -529,7 +548,6 @@
         )
         return keep
 
-    mask, flipped = made["masks"]
 
     def make_grads(n):
         def run(after):
@@ -549,7 +567,7 @@
         return run
 
     last_mine, last_other, gains = carried(
-        send, keep_grads, decay, bounds, True, True, [make_grads(n) for n in range(4)]
+        send, keep_grads, back_table, BACKWARD, True, True, [make_grads(n) for n in range(4)]
     )
     last_theirs = exchange(last_other, dc=1)
     dq, dk, dv = zip(*[made["grads", n] for n in range(4)])
@@ -558,22 +576,22 @@
     dk_out, dv_out, dq_out = call(
         functools.partial(last_kernel, own=True),
         [full] * 3,
-        in_specs=scalars + [VMEM] * 11 + [ANY],
+        in_specs=[VMEM] * 12 + [ANY],
         out_specs=[ANY] * 3,
         scratch=scratch,
         flops=2 * small_mm,
         moved=6 << 20,
-    )(decay, bounds, keys, values, last_mine, *dk[:2], *dv[:2], *dq, last_other)
+    )(table, keys, values, last_mine, *dk[:2], *dv[:2], *dq, last_other)
     dk_out, dv_out = call(
         functools.partial(last_kernel, own=False),
         [full] * 2,
-        in_specs=scalars + [VMEM] * 7 + [ANY] * 2,
+        in_specs=[VMEM] * 8 + [ANY] * 2,
         out_specs=[ANY] * 2,
         scratch=scratch,
         flops=2 * small_mm,
         moved=4 << 20,
-        aliases={9: 0, 10: 1},
-    )(decay, bounds, keys, values, last_theirs, *dk[2:], *dv[2:], dk_out, dv_out)
+        aliases={8: 0, 9: 1},
+    )(table, keys, values, last_theirs, *dk[2:], *dv[2:], dk_out, dv_out)
     return dq_out, dk_out, dv_out, gains
 
 

time: 104 us -> 91.5 us (0.88)
  Pallas kernels: 36 us -> 22.6 us
  waiting for transfers between devices: 15.1 us -> 18.7 us
  starting transfers between devices: 51.1 us -> 49.1 us
    pallas_call x25, Pallas kernels: 36 us -> 22.6 us  [the longest x11 15 us: local(): call(functools.partial(kernel, **more), outs, in_specs=[VMEM] * (1 + len(...]
    ppermute x24, waiting for transfers between devices: 11.8 us -> 15.4 us  [exchange(): return lax.ppermute(array, 'seq', pairs)]
    ppermute x24, starting transfers between devices: 47.8 us -> 45.7 us  [exchange(): return lax.ppermute(array, 'seq', pairs)]
  transfers between devices with their start and end apart: 27 -> 27, of which waited for: 11 -> 15; matrix products, arithmetic and copies ran while one was open for 0% -> 0% of each run, Pallas kernels for 20% -> 17%
where the time goes in v4:
time: 91.5 us; the launch traced here: 91.4 us
  starting transfers between devices  49.1 us (54%)
  Pallas kernels  22.6 us (25%)
  waiting for transfers between devices  18.7 us (20%)
  between operations  1.06 us (1%)
    ppermute x24, starting transfers between devices, exchange(): return lax.ppermute(array, 'seq', pairs)  45.7 us
    ppermute x24, waiting for transfers between devices, exchange(): return lax.ppermute(array, 'seq', pairs)  15.4 us
    pallas_call x11, Pallas kernels, local(): call(functools.partial(kernel, **more), outs, in_specs=[VMEM] * (1 + len(...  15 us
    ppermute x3, starting transfers between devices, shards(): lax.ppermute(sums, 'dp', [(i, i ^ k) for i in range(4)])  3.34 us
    ppermute x3, waiting for transfers between devices, shards(): lax.ppermute(sums, 'dp', [(i, i ^ k) for i in range(4)])  3.32 us
    pallas_call x1, Pallas kernels, shards(): call(sent_states_kernel, [state_shape, shape(FORWARD + CHAIN_ROWS, HEAD)]...  2.28 us
  transfers between devices with their start and end apart: 27, of which 15 were waited for; matrix products, arithmetic and copies ran while one was open for 0% of the time, Pallas kernels for 17%

profile of v4, /device:TPU:1, one launch (start us, length us, event | category | flops | bytes accessed | tf_op | source)
XLA Modules:
  0.0 91.4 jit_solution(1612604684871317300)
XLA Ops:
  0.7 2.3 %shard_map.102 = (f32[512,128]{1,0:T(8,128)S(1)}, f32[64,128]{1,0:T(8,128)S(1)}) custom-call(s32[8]{0:T(128)} %decay.1, s32[3]{0:T(128)} %bounds.1, bf16[512,1024]{1,0:T(8,128)(2,1)} %k.19, bf16[512,1024]{1,0:T(8,128)(2,1)} %v.19), custom_call_target="tpu_custom_call" | custom-call | flops 67108864 | bytes 1572864 | tf_op jit(solution)/shard_map/pallas_call | solution.py:469
  2.9 3.3 %collective-permute-start = (f32[512,128]{1,0:T(8,128)S(1)}, f32[512,128]{1,0:T(8,128)S(1)}, u32[]{:S(2)}, u32[]{:S(2)}) collective-permute-start(f32[512,128]{1,0:T(8,128)S(1)} %get-tuple-element.57.after.send), channel_id=1, source_target_pairs={{0,1},{1,0},{2,3},{3,2},{4,5},{5,4},{6,7},{7,6},{8,9},{9,8},{10,11... | collective-permute-start | bytes 786440 | tf_op jit(solution)/shard_map/ppermute | solution.py:412
  7.6 2.2 %collective-permute-start.2 = (f32[128,128]{1,0:T(8,128)S(1)}, f32[128,128]{1,0:T(8,128)S(1)}, u32[]{:S(2)}, u32[]{:S(2)}) collective-permute-start(f32[128,128]{1,0:T(8,128)S(1)} %get-tuple-element.62), channel_id=1, source_target_pairs={{0,4},{1,5},{2,6},{3,7},{4,0},{5,1},{6,2},{7,3},{8,12},{9,13},{10,... | collective-permute-start | bytes 196616 | tf_op jit(solution)/shard_map/ppermute | solution.py:412
  9.7 1.7 %collective-permute-start.3 = (f32[128,128]{1,0:T(8,128)S(1)}, f32[128,128]{1,0:T(8,128)S(1)}, u32[]{:S(2)}, u32[]{:S(2)}) collective-permute-start(f32[128,128]{1,0:T(8,128)S(1)} %get-tuple-element.63), channel_id=1, source_target_pairs={{0,6},{1,7},{2,4},{3,5},{4,2},{5,3},{6,0},{7,1},{8,14},{9,15},{10,... | collective-permute-start | bytes 196616 | tf_op jit(solution)/shard_map/ppermute | solution.py:412
  12.6 1.5 %shard_map.106.after.intra = f32[512,512]{1,0:T(8,128)S(1)} custom-call(f32[64,128]{1,0:T(8,128)S(1)} %get-tuple-element.56.table, bf16[512,1024]{1,0:T(8,128)(2,1)S(1)} %copy-done, bf16[512,1024]{1,0:T(8,128)(2,1)S(1)} %copy-done.1, bf16[512,1024]{1,0:T(8,128)(2,1)S(1)} %copy-done.2, bf16[512,512]{1,0:T(8,128)(2,1)S(1)} %get-tuple-element.60.mask, ...), custom_call_target="tpu_custom_call" | custom-call | flops 402653184 | bytes 3145728 | tf_op jit(solution)/shard_map/pallas_call | solution.py:460
  14.4 4.3 %collective-permute-start.6 = (f32[128,128]{1,0:T(8,128)S(1)}, f32[128,128]{1,0:T(8,128)S(1)}, u32[]{:S(2)}, u32[]{:S(2)}) collective-permute-start(f32[128,128]{1,0:T(8,128)S(1)} %shard_map.107.after.p0), channel_id=1, source_target_pairs={{0,24},{1,25},{2,26},{3,27},{4,28},{5,29},{6,30},{7,31},{8,16},{9,... | collective-permute-start | bytes 196616 | tf_op jit(solution)/shard_map/ppermute | solution.py:412
  19.0 1.5 %shard_map.108.after.intra = f32[512,512]{1,0:T(8,128)S(1)} custom-call(f32[64,128]{1,0:T(8,128)S(1)} %get-tuple-element.56.table, bf16[512,1024]{1,0:T(8,128)(2,1)S(1)} %copy-done, bf16[512,1024]{1,0:T(8,128)(2,1)S(1)} %copy-done.1, bf16[512,1024]{1,0:T(8,128)(2,1)S(1)} %copy-done.2, bf16[512,512]{1,0:T(8,128)(2,1)S(1)} %get-tuple-element.60.mask, ...), custom_call_target="tpu_custom_call" | custom-call | flops 402653184 | bytes 3145728 | tf_op jit(solution)/shard_map/pallas_call | solution.py:460
  20.5 2.8 %collective-permute-done.5.p2.r2 = f32[128,128]{1,0:T(8,128)S(1)} collective-permute-done((f32[128,128]{1,0:T(8,128)S(1)}, f32[128,128]{1,0:T(8,128)S(1)}, u32[]{:S(2)}, u32[]{:S(2)}) %collective-permute-start.5) | collective-permute-done | bytes 65568 | tf_op jit(solution)/shard_map/ppermute | solution.py:412
  23.3 3.6 %collective-permute-start.7 = (f32[128,128]{1,0:T(8,128)S(1)}, f32[128,128]{1,0:T(8,128)S(1)}, u32[]{:S(2)}, u32[]{:S(2)}) collective-permute-start(f32[128,128]{1,0:T(8,128)S(1)} %shard_map.109.sent.after), channel_id=1, source_target_pairs={{0,48},{1,49},{2,50},{3,51},{4,52},{5,53},{6,54},{7,55},{8,56},{9,... | collective-permute-start | bytes 196616 | tf_op jit(solution)/shard_map/ppermute | solution.py:412
  27.0 2.4 %collective-permute-done.7.far = f32[128,128]{1,0:T(8,128)S(1)} collective-permute-done((f32[128,128]{1,0:T(8,128)S(1)}, f32[128,128]{1,0:T(8,128)S(1)}, u32[]{:S(2)}, u32[]{:S(2)}) %collective-permute-start.7) | collective-permute-done | bytes 65568 | tf_op jit(solution)/shard_map/ppermute | solution.py:412
  29.6 2.6 %collective-permute-start.9 = (f32[128,128]{1,0:T(8,128)S(1)}, f32[128,128]{1,0:T(8,128)S(1)}, u32[]{:S(2)}, u32[]{:S(2)}) collective-permute-start(f32[128,128]{1,0:T(8,128)S(1)} %get-tuple-element.67), channel_id=1, source_target_pairs={{0,4},{1,5},{2,6},{3,7},{4,0},{5,1},{6,2},{7,3},{8,12},{9,13},{10,... | collective-permute-start | bytes 196616 | tf_op jit(solution)/shard_map/ppermute | solution.py:412
  32.1 1.3 %collective-permute-start.10 = (f32[128,128]{1,0:T(8,128)S(1)}, f32[128,128]{1,0:T(8,128)S(1)}, u32[]{:S(2)}, u32[]{:S(2)}) collective-permute-start(f32[128,128]{1,0:T(8,128)S(1)} %get-tuple-element.68), channel_id=1, source_target_pairs={{0,6},{1,7},{2,4},{3,5},{4,2},{5,3},{6,0},{7,1},{8,14},{9,15},{10,... | collective-permute-start | bytes 196616 | tf_op jit(solution)/shard_map/ppermute | solution.py:412
  34.5 2.0 %collective-permute-done.10.v3 = f32[128,128]{1,0:T(8,128)S(1)} collective-permute-done((f32[128,128]{1,0:T(8,128)S(1)}, f32[128,128]{1,0:T(8,128)S(1)}, u32[]{:S(2)}, u32[]{:S(2)}) %collective-permute-start.10) | collective-permute-done | bytes 65568 | tf_op jit(solution)/shard_map/ppermute | solution.py:412
  36.5 4.5 %collective-permute-start.11 = (f32[512,128]{1,0:T(8,128)S(1)}, f32[512,128]{1,0:T(8,128)S(1)}, u32[]{:S(2)}, u32[]{:S(2)}) collective-permute-start(f32[512,128]{1,0:T(8,128)S(1)} %get-tuple-element.69.refs_0_), channel_id=1, source_target_pairs={{0,1},{1,0},{2,3},{3,2},{4,5},{5,4},{6,7},{7,6},{8,9},{9,8},{10,11... | collective-permute-start | bytes 786440 | tf_op jit(solution)/shard_map/ppermute | solution.py:412
  43.0 2.6 %collective-permute-start.14 = (f32[8,512]{1,0:T(8,128)S(1)}, f32[8,512]{1,0:T(8,128)S(1)}, u32[]{:S(2)}, u32[]{:S(2)}) collective-permute-start(f32[8,512]{1,0:T(8,128)S(1)} %get-tuple-element.72.s0), channel_id=1, source_target_pairs={{0,192},{64,128},{128,64},{192,0},{1,193},{65,129},{129,65},{193,1... | collective-permute-start | bytes 49160 | tf_op jit(solution)/shard_map/ppermute | solution.py:532
  46.9 2.8 %collective-permute-done.13.s2 = f32[8,512]{1,0:T(8,128)S(1)} collective-permute-done((f32[8,512]{1,0:T(8,128)S(1)}, f32[8,512]{1,0:T(8,128)S(1)}, u32[]{:S(2)}, u32[]{:S(2)}) %collective-permute-start.13) | collective-permute-done | bytes 16416 | tf_op jit(solution)/shard_map/ppermute | solution.py:532
  50.8 1.9 %collective-permute-start.15 = (f32[520,128]{1,0:T(8,128)S(1)}, f32[520,128]{1,0:T(8,128)S(1)}, u32[]{:S(2)}, u32[]{:S(2)}) collective-permute-start(f32[520,128]{1,0:T(8,128)S(1)} %get-tuple-element.75.refs_0_.send), channel_id=1, source_target_pairs={{0,1},{1,0},{2,3},{3,2},{4,5},{5,4},{6,7},{7,6},{8,9},{9,8},{10,11... | collective-permute-start | bytes 798728 | tf_op jit(solution)/shard_map/ppermute | solution.py:412
  54.0 3.2 %collective-permute-start.17 = (f32[136,128]{1,0:T(8,128)S(1)}, f32[136,128]{1,0:T(8,128)S(1)}, u32[]{:S(2)}, u32[]{:S(2)}) collective-permute-start(f32[136,128]{1,0:T(8,128)S(1)} %get-tuple-element.79), channel_id=1, source_target_pairs={{0,4},{1,5},{2,6},{3,7},{4,0},{5,1},{6,2},{7,3},{8,12},{9,13},{10,... | collective-permute-start | bytes 208904 | tf_op jit(solution)/shard_map/ppermute | solution.py:412
  57.9 2.0 %shard_map.117 = (bf16[512,256]{1,0:T(8,128)(2,1)S(1)}, f32[512,256]{1,0:T(8,128)S(1)}, f32[512,256]{1,0:T(8,128)S(1)}) custom-call(f32[64,128]{1,0:T(8,128)S(1)} %get-tuple-element.56.table, bf16[512,1024]{1,0:T(8,128)(2,1)S(1)} %copy-done, bf16[512,1024]{1,0:T(8,128)(2,1)S(1)} %copy-done.1, bf16[512,1024]{1,0:T(8,128)(2,1)S(1)} %copy-done.2, ...), custom_call_target="tpu_custom_call" | custom-call | flops 603979776 | bytes 2097152 | tf_op jit(solution)/shard_map/pallas_call | solution.py:460
  60.4 1.6 %collective-permute-done.18.p3.t3 = f32[136,128]{1,0:T(8,128)S(1)} collective-permute-done((f32[136,128]{1,0:T(8,128)S(1)}, f32[136,128]{1,0:T(8,128)S(1)}, u32[]{:S(2)}, u32[]{:S(2)}) %collective-permute-start.18) | collective-permute-done | bytes 69664 | tf_op jit(solution)/shard_map/ppermute | solution.py:412
  62.0 1.7 %collective-permute-start.21 = (f32[136,128]{1,0:T(8,128)S(1)}, f32[136,128]{1,0:T(8,128)S(1)}, u32[]{:S(2)}, u32[]{:S(2)}) collective-permute-start(f32[136,128]{1,0:T(8,128)S(1)} %shard_map.118.after.p0), channel_id=1, source_target_pairs={{0,24},{1,25},{2,26},{3,27},{4,28},{5,29},{6,30},{7,31},{8,16},{9,... | collective-permute-start | bytes 208904 | tf_op jit(solution)/shard_map/ppermute | solution.py:412
  63.7 1.2 %collective-permute-start.20 = (f32[136,128]{1,0:T(8,128)S(1)}, f32[136,128]{1,0:T(8,128)S(1)}, u32[]{:S(2)}, u32[]{:S(2)}) collective-permute-start(f32[136,128]{1,0:T(8,128)S(1)} %shard_map.118.after.p0), channel_id=1, source_target_pairs={{0,16},{1,17},{2,18},{3,19},{4,20},{5,21},{6,22},{7,23},{8,24},{9,... | collective-permute-start | bytes 208904 | tf_op jit(solution)/shard_map/ppermute | solution.py:412
  65.6 1.9 %shard_map.119 = (bf16[512,256]{1,0:T(8,128)(2,1)S(1)}, f32[512,256]{1,0:T(8,128)S(1)}, f32[512,256]{1,0:T(8,128)S(1)}) custom-call(f32[64,128]{1,0:T(8,128)S(1)} %get-tuple-element.56.table, bf16[512,1024]{1,0:T(8,128)(2,1)S(1)} %copy-done, bf16[512,1024]{1,0:T(8,128)(2,1)S(1)} %copy-done.1, bf16[512,1024]{1,0:T(8,128)(2,1)S(1)} %copy-done.2, ...), custom_call_target="tpu_custom_call" | custom-call | flops 603979776 | bytes 2097152 | tf_op jit(solution)/shard_map/pallas_call | solution.py:460
  67.5 2.4 %collective-permute-done.20.p2.r2 = f32[136,128]{1,0:T(8,128)S(1)} collective-permute-done((f32[136,128]{1,0:T(8,128)S(1)}, f32[136,128]{1,0:T(8,128)S(1)}, u32[]{:S(2)}, u32[]{:S(2)}) %collective-permute-start.20) | collective-permute-done | bytes 69664 | tf_op jit(solution)/shard_map/ppermute | solution.py:412
  70.0 3.3 %collective-permute-start.22 = (f32[136,128]{1,0:T(8,128)S(1)}, f32[136,128]{1,0:T(8,128)S(1)}, u32[]{:S(2)}, u32[]{:S(2)}) collective-permute-start(f32[136,128]{1,0:T(8,128)S(1)} %shard_map.120.after.sent), channel_id=1, source_target_pairs={{0,48},{1,49},{2,50},{3,51},{4,52},{5,53},{6,54},{7,55},{8,56},{9,... | collective-permute-start | bytes 208904 | tf_op jit(solution)/shard_map/ppermute | solution.py:412
  73.3 2.0 %shard_map.121 = (bf16[512,256]{1,0:T(8,128)(2,1)S(1)}, f32[512,256]{1,0:T(8,128)S(1)}, f32[512,256]{1,0:T(8,128)S(1)}) custom-call(f32[64,128]{1,0:T(8,128)S(1)} %get-tuple-element.56.table, bf16[512,1024]{1,0:T(8,128)(2,1)S(1)} %copy-done, bf16[512,1024]{1,0:T(8,128)(2,1)S(1)} %copy-done.1, bf16[512,1024]{1,0:T(8,128)(2,1)S(1)} %copy-done.2, ...), custom_call_target="tpu_custom_call" | custom-call | flops 603979776 | bytes 2097152 | tf_op jit(solution)/shard_map/pallas_call | solution.py:460
  76.3 1.2 %collective-permute-start.23 = (f32[128,128]{1,0:T(8,128)S(1)}, f32[128,128]{1,0:T(8,128)S(1)}, u32[]{:S(2)}, u32[]{:S(2)}) collective-permute-start(f32[128,128]{1,0:T(8,128)S(1)} %get-tuple-element.88), channel_id=1, source_target_pairs={{0,2},{1,3},{2,0},{3,1},{4,6},{5,7},{6,4},{7,5},{8,10},{9,11},{10,... | collective-permute-start | bytes 196616 | tf_op jit(solution)/shard_map/ppermute | solution.py:412
  78.7 1.4 %collective-permute-start.25 = (f32[128,128]{1,0:T(8,128)S(1)}, f32[128,128]{1,0:T(8,128)S(1)}, u32[]{:S(2)}, u32[]{:S(2)}) collective-permute-start(f32[128,128]{1,0:T(8,128)S(1)} %get-tuple-element.90), channel_id=1, source_target_pairs={{0,6},{1,7},{2,4},{3,5},{4,2},{5,3},{6,0},{7,1},{8,14},{9,15},{10,... | collective-permute-start | bytes 196616 | tf_op jit(solution)/shard_map/ppermute | solution.py:412
  80.1 2.0 %shard_map.123 = (bf16[512,256]{1,0:T(8,128)(2,1)S(1)}, f32[512,256]{1,0:T(8,128)S(1)}, f32[512,256]{1,0:T(8,128)S(1)}) custom-call(f32[64,128]{1,0:T(8,128)S(1)} %get-tuple-element.56.table, bf16[512,1024]{1,0:T(8,128)(2,1)S(1)} %copy-done, bf16[512,1024]{1,0:T(8,128)(2,1)S(1)} %copy-done.1, bf16[512,1024]{1,0:T(8,128)(2,1)S(1)} %copy-done.2, ...), custom_call_target="tpu_custom_call" | custom-call | flops 603979776 | bytes 2097152 | tf_op jit(solution)/shard_map/pallas_call | solution.py:460
  83.1 5.0 %collective-permute-start.26 = (f32[512,128]{1,0:T(8,128)S(1)}, f32[512,128]{1,0:T(8,128)S(1)}, u32[]{:S(2)}, u32[]{:S(2)}) collective-permute-start(f32[512,128]{1,0:T(8,128)S(1)} %get-tuple-element.99.refs_8_), channel_id=1, source_target_pairs={{0,1},{1,0},{2,3},{3,2},{4,5},{5,4},{6,7},{7,6},{8,9},{9,8},{10,11... | collective-permute-start | bytes 786440 | tf_op jit(solution)/shard_map/ppermute | solution.py:412
  88.1 1.6 %shard_map.125 = (bf16[512,1024]{1,0:T(8,128)(2,1)}, bf16[512,1024]{1,0:T(8,128)(2,1)}, bf16[512,1024]{1,0:T(8,128)(2,1)}) custom-call(f32[64,128]{1,0:T(8,128)S(1)} %get-tuple-element.56.table, bf16[512,1024]{1,0:T(8,128)(2,1)S(1)} %copy-done.1, bf16[512,1024]{1,0:T(8,128)(2,1)S(1)} %copy-done.2, f32[512,128]{1,0:T(8,128)S(1)} %get-tuple-element.92.states, ...), custom_call_target="tpu_custom_call" | custom-call | flops 134217728 | bytes 6291456 | tf_op jit(solution)/shard_map/pallas_call | solution.py:576
  89.7 1.5 %shard_map.126 = (bf16[512,1024]{1,0:T(8,128)(2,1)}, bf16[512,1024]{1,0:T(8,128)(2,1)}) custom-call(f32[64,128]{1,0:T(8,128)S(1)} %get-tuple-element.56.table, bf16[512,1024]{1,0:T(8,128)(2,1)S(1)} %copy-done.1, bf16[512,1024]{1,0:T(8,128)(2,1)S(1)} %copy-done.2, ...), custom_call_target="tpu_custom_call", output_to_operand_aliasing={{0}: (8, {}), {1}: (9, {})} | custom-call | flops 134217728 | bytes 4194304 | tf_op jit(solution)/shard_map/pallas_call | solution.py:585
  (57 shorter events, 15.2 us)
Async XLA Ops:
  0.6 5.6 %copy-start.2 = (bf16[512,1024]{1,0:T(8,128)(2,1)S(1)}, bf16[512,1024]{1,0:T(8,128)(2,1)}, u32[]{:S(2)}) copy-start(bf16[512,1024]{1,0:T(8,128)(2,1)} %v.19) | copy-start | bytes 3145732
  0.6 5.6 %copy-start.1 = (bf16[512,1024]{1,0:T(8,128)(2,1)S(1)}, bf16[512,1024]{1,0:T(8,128)(2,1)}, u32[]{:S(2)}) copy-start(bf16[512,1024]{1,0:T(8,128)(2,1)} %k.19) | copy-start | bytes 3145732
  2.9 4.5 %collective-permute-start = (f32[512,128]{1,0:T(8,128)S(1)}, f32[512,128]{1,0:T(8,128)S(1)}, u32[]{:S(2)}, u32[]{:S(2)}) collective-permute-start(f32[512,128]{1,0:T(8,128)S(1)} %get-tuple-element.57.after.send), channel_id=1, source_target_pairs={{0,1},{1,0},{2,3},{3,2},{4,5},{5,4},{6,7},{7,6},{8,9},{9,8},{10,11... | collective-permute-start | bytes 786440 | tf_op jit(solution)/shard_map/ppermute | solution.py:412
  6.9 5.7 %copy-start = (bf16[512,1024]{1,0:T(8,128)(2,1)S(1)}, bf16[512,1024]{1,0:T(8,128)(2,1)}, u32[]{:S(2)}) copy-start(bf16[512,1024]{1,0:T(8,128)(2,1)} %q.19) | copy-start | bytes 3145732
  7.5 4.0 %copy-start.4 = (f32[1024]{0:T(1024)S(1)}, f32[1024]{0:T(1024)}, u32[]{:S(2)}) copy-start(f32[1024]{0:T(1024)} %param.11) | copy-start | bytes 12292
  7.5 6.6 %collective-permute-start.1 = (f32[128,128]{1,0:T(8,128)S(1)}, f32[128,128]{1,0:T(8,128)S(1)}, u32[]{:S(2)}, u32[]{:S(2)}) collective-permute-start(f32[128,128]{1,0:T(8,128)S(1)} %get-tuple-element.61), channel_id=1, source_target_pairs={{0,2},{1,3},{2,0},{3,1},{4,6},{5,7},{6,4},{7,5},{8,10},{9,11},{10,... | collective-permute-start | bytes 196616 | tf_op jit(solution)/shard_map/ppermute | solution.py:412
  7.6 6.5 %collective-permute-start.2 = (f32[128,128]{1,0:T(8,128)S(1)}, f32[128,128]{1,0:T(8,128)S(1)}, u32[]{:S(2)}, u32[]{:S(2)}) collective-permute-start(f32[128,128]{1,0:T(8,128)S(1)} %get-tuple-element.62), channel_id=1, source_target_pairs={{0,4},{1,5},{2,6},{3,7},{4,0},{5,1},{6,2},{7,3},{8,12},{9,13},{10,... | collective-permute-start | bytes 196616 | tf_op jit(solution)/shard_map/ppermute | solution.py:412
  9.7 4.6 %collective-permute-start.3 = (f32[128,128]{1,0:T(8,128)S(1)}, f32[128,128]{1,0:T(8,128)S(1)}, u32[]{:S(2)}, u32[]{:S(2)}) collective-permute-start(f32[128,128]{1,0:T(8,128)S(1)} %get-tuple-element.63), channel_id=1, source_target_pairs={{0,6},{1,7},{2,4},{3,5},{4,2},{5,3},{6,0},{7,1},{8,14},{9,15},{10,... | collective-permute-start | bytes 196616 | tf_op jit(solution)/shard_map/ppermute | solution.py:412
  14.4 6.2 %collective-permute-start.6 = (f32[128,128]{1,0:T(8,128)S(1)}, f32[128,128]{1,0:T(8,128)S(1)}, u32[]{:S(2)}, u32[]{:S(2)}) collective-permute-start(f32[128,128]{1,0:T(8,128)S(1)} %shard_map.107.after.p0), channel_id=1, source_target_pairs={{0,24},{1,25},{2,26},{3,27},{4,28},{5,29},{6,30},{7,31},{8,16},{9,... | collective-permute-start | bytes 196616 | tf_op jit(solution)/shard_map/ppermute | solution.py:412
  18.7 4.6 %collective-permute-start.5 = (f32[128,128]{1,0:T(8,128)S(1)}, f32[128,128]{1,0:T(8,128)S(1)}, u32[]{:S(2)}, u32[]{:S(2)}) collective-permute-start(f32[128,128]{1,0:T(8,128)S(1)} %shard_map.107.after.p0), channel_id=1, source_target_pairs={{0,16},{1,17},{2,18},{3,19},{4,20},{5,21},{6,22},{7,23},{8,24},{9,... | collective-permute-start | bytes 196616 | tf_op jit(solution)/shard_map/ppermute | solution.py:412
  18.7 4.6 %collective-permute-start.4 = (f32[128,128]{1,0:T(8,128)S(1)}, f32[128,128]{1,0:T(8,128)S(1)}, u32[]{:S(2)}, u32[]{:S(2)}) collective-permute-start(f32[128,128]{1,0:T(8,128)S(1)} %shard_map.107.after.p0), channel_id=1, source_target_pairs={{0,8},{1,9},{2,10},{3,11},{4,12},{5,13},{6,14},{7,15},{8,0},{9,1},... | collective-permute-start | bytes 196616 | tf_op jit(solution)/shard_map/ppermute | solution.py:412
  23.3 17.7 %copy-start.3 = (bf16[512,1024]{1,0:T(8,128)(2,1)S(1)}, bf16[512,1024]{1,0:T(8,128)(2,1)}, u32[]{:S(2)}) copy-start(bf16[512,1024]{1,0:T(8,128)(2,1)} %grad.7) | copy-start | bytes 3145732
  23.3 6.0 %collective-permute-start.7 = (f32[128,128]{1,0:T(8,128)S(1)}, f32[128,128]{1,0:T(8,128)S(1)}, u32[]{:S(2)}, u32[]{:S(2)}) collective-permute-start(f32[128,128]{1,0:T(8,128)S(1)} %shard_map.109.sent.after), channel_id=1, source_target_pairs={{0,48},{1,49},{2,50},{3,51},{4,52},{5,53},{6,54},{7,55},{8,56},{9,... | collective-permute-start | bytes 196616 | tf_op jit(solution)/shard_map/ppermute | solution.py:412
  29.5 3.9 %collective-permute-start.8 = (f32[128,128]{1,0:T(8,128)S(1)}, f32[128,128]{1,0:T(8,128)S(1)}, u32[]{:S(2)}, u32[]{:S(2)}) collective-permute-start(f32[128,128]{1,0:T(8,128)S(1)} %get-tuple-element.66), channel_id=1, source_target_pairs={{0,2},{1,3},{2,0},{3,1},{4,6},{5,7},{6,4},{7,5},{8,10},{9,11},{10,... | collective-permute-start | bytes 196616 | tf_op jit(solution)/shard_map/ppermute | solution.py:412
  29.6 4.9 %collective-permute-start.9 = (f32[128,128]{1,0:T(8,128)S(1)}, f32[128,128]{1,0:T(8,128)S(1)}, u32[]{:S(2)}, u32[]{:S(2)}) collective-permute-start(f32[128,128]{1,0:T(8,128)S(1)} %get-tuple-element.67), channel_id=1, source_target_pairs={{0,4},{1,5},{2,6},{3,7},{4,0},{5,1},{6,2},{7,3},{8,12},{9,13},{10,... | collective-permute-start | bytes 196616 | tf_op jit(solution)/shard_map/ppermute | solution.py:412
  32.1 4.3 %collective-permute-start.10 = (f32[128,128]{1,0:T(8,128)S(1)}, f32[128,128]{1,0:T(8,128)S(1)}, u32[]{:S(2)}, u32[]{:S(2)}) collective-permute-start(f32[128,128]{1,0:T(8,128)S(1)} %get-tuple-element.68), channel_id=1, source_target_pairs={{0,6},{1,7},{2,4},{3,5},{4,2},{5,3},{6,0},{7,1},{8,14},{9,15},{10,... | collective-permute-start | bytes 196616 | tf_op jit(solution)/shard_map/ppermute | solution.py:412
  36.5 5.7 %collective-permute-start.11 = (f32[512,128]{1,0:T(8,128)S(1)}, f32[512,128]{1,0:T(8,128)S(1)}, u32[]{:S(2)}, u32[]{:S(2)}) collective-permute-start(f32[512,128]{1,0:T(8,128)S(1)} %get-tuple-element.69.refs_0_), channel_id=1, source_target_pairs={{0,1},{1,0},{2,3},{3,2},{4,5},{5,4},{6,7},{7,6},{8,9},{9,8},{10,11... | collective-permute-start | bytes 786440 | tf_op jit(solution)/shard_map/ppermute | solution.py:412
  43.0 3.9 %collective-permute-start.14 = (f32[8,512]{1,0:T(8,128)S(1)}, f32[8,512]{1,0:T(8,128)S(1)}, u32[]{:S(2)}, u32[]{:S(2)}) collective-permute-start(f32[8,512]{1,0:T(8,128)S(1)} %get-tuple-element.72.s0), channel_id=1, source_target_pairs={{0,192},{64,128},{128,64},{192,0},{1,193},{65,129},{129,65},{193,1... | collective-permute-start | bytes 49160 | tf_op jit(solution)/shard_map/ppermute | solution.py:532
  45.6 4.1 %collective-permute-start.13 = (f32[8,512]{1,0:T(8,128)S(1)}, f32[8,512]{1,0:T(8,128)S(1)}, u32[]{:S(2)}, u32[]{:S(2)}) collective-permute-start(f32[8,512]{1,0:T(8,128)S(1)} %get-tuple-element.72.s0), channel_id=1, source_target_pairs={{0,128},{64,192},{128,0},{192,64},{1,129},{65,193},{129,1},{193,65... | collective-permute-start | bytes 49160 | tf_op jit(solution)/shard_map/ppermute | solution.py:532
  46.1 3.6 %collective-permute-start.12 = (f32[8,512]{1,0:T(8,128)S(1)}, f32[8,512]{1,0:T(8,128)S(1)}, u32[]{:S(2)}, u32[]{:S(2)}) collective-permute-start(f32[8,512]{1,0:T(8,128)S(1)} %get-tuple-element.72.s0), channel_id=1, source_target_pairs={{0,64},{64,0},{128,192},{192,128},{1,65},{65,1},{129,193},{193,129... | collective-permute-start | bytes 49160 | tf_op jit(solution)/shard_map/ppermute | solution.py:532
  50.8 3.0 %collective-permute-start.15 = (f32[520,128]{1,0:T(8,128)S(1)}, f32[520,128]{1,0:T(8,128)S(1)}, u32[]{:S(2)}, u32[]{:S(2)}) collective-permute-start(f32[520,128]{1,0:T(8,128)S(1)} %get-tuple-element.75.refs_0_.send), channel_id=1, source_target_pairs={{0,1},{1,0},{2,3},{3,2},{4,5},{5,4},{6,7},{7,6},{8,9},{9,8},{10,11... | collective-permute-start | bytes 798728 | tf_op jit(solution)/shard_map/ppermute | solution.py:412
  53.9 5.9 %collective-permute-start.16 = (f32[136,128]{1,0:T(8,128)S(1)}, f32[136,128]{1,0:T(8,128)S(1)}, u32[]{:S(2)}, u32[]{:S(2)}) collective-permute-start(f32[136,128]{1,0:T(8,128)S(1)} %get-tuple-element.78), channel_id=1, source_target_pairs={{0,2},{1,3},{2,0},{3,1},{4,6},{5,7},{6,4},{7,5},{8,10},{9,11},{10,... | collective-permute-start | bytes 208904 | tf_op jit(solution)/shard_map/ppermute | solution.py:412
  54.0 6.3 %collective-permute-start.17 = (f32[136,128]{1,0:T(8,128)S(1)}, f32[136,128]{1,0:T(8,128)S(1)}, u32[]{:S(2)}, u32[]{:S(2)}) collective-permute-start(f32[136,128]{1,0:T(8,128)S(1)} %get-tuple-element.79), channel_id=1, source_target_pairs={{0,4},{1,5},{2,6},{3,7},{4,0},{5,1},{6,2},{7,3},{8,12},{9,13},{10,... | collective-permute-start | bytes 208904 | tf_op jit(solution)/shard_map/ppermute | solution.py:412
  57.2 4.7 %collective-permute-start.18 = (f32[136,128]{1,0:T(8,128)S(1)}, f32[136,128]{1,0:T(8,128)S(1)}, u32[]{:S(2)}, u32[]{:S(2)}) collective-permute-start(f32[136,128]{1,0:T(8,128)S(1)} %get-tuple-element.80), channel_id=1, source_target_pairs={{0,6},{1,7},{2,4},{3,5},{4,2},{5,3},{6,0},{7,1},{8,14},{9,15},{10,... | collective-permute-start | bytes 208904 | tf_op jit(solution)/shard_map/ppermute | solution.py:412
  62.0 5.6 %collective-permute-start.21 = (f32[136,128]{1,0:T(8,128)S(1)}, f32[136,128]{1,0:T(8,128)S(1)}, u32[]{:S(2)}, u32[]{:S(2)}) collective-permute-start(f32[136,128]{1,0:T(8,128)S(1)} %shard_map.118.after.p0), channel_id=1, source_target_pairs={{0,24},{1,25},{2,26},{3,27},{4,28},{5,29},{6,30},{7,31},{8,16},{9,... | collective-permute-start | bytes 208904 | tf_op jit(solution)/shard_map/ppermute | solution.py:412
  63.7 6.3 %collective-permute-start.20 = (f32[136,128]{1,0:T(8,128)S(1)}, f32[136,128]{1,0:T(8,128)S(1)}, u32[]{:S(2)}, u32[]{:S(2)}) collective-permute-start(f32[136,128]{1,0:T(8,128)S(1)} %shard_map.118.after.p0), channel_id=1, source_target_pairs={{0,16},{1,17},{2,18},{3,19},{4,20},{5,21},{6,22},{7,23},{8,24},{9,... | collective-permute-start | bytes 208904 | tf_op jit(solution)/shard_map/ppermute | solution.py:412
  64.9 5.1 %collective-permute-start.19 = (f32[136,128]{1,0:T(8,128)S(1)}, f32[136,128]{1,0:T(8,128)S(1)}, u32[]{:S(2)}, u32[]{:S(2)}) collective-permute-start(f32[136,128]{1,0:T(8,128)S(1)} %shard_map.118.after.p0), channel_id=1, source_target_pairs={{0,8},{1,9},{2,10},{3,11},{4,12},{5,13},{6,14},{7,15},{8,0},{9,1},... | collective-permute-start | bytes 208904 | tf_op jit(solution)/shard_map/ppermute | solution.py:412
  70.0 5.6 %collective-permute-start.22 = (f32[136,128]{1,0:T(8,128)S(1)}, f32[136,128]{1,0:T(8,128)S(1)}, u32[]{:S(2)}, u32[]{:S(2)}) collective-permute-start(f32[136,128]{1,0:T(8,128)S(1)} %shard_map.120.after.sent), channel_id=1, source_target_pairs={{0,48},{1,49},{2,50},{3,51},{4,52},{5,53},{6,54},{7,55},{8,56},{9,... | collective-permute-start | bytes 208904 | tf_op jit(solution)/shard_map/ppermute | solution.py:412
  76.3 5.8 %collective-permute-start.23 = (f32[128,128]{1,0:T(8,128)S(1)}, f32[128,128]{1,0:T(8,128)S(1)}, u32[]{:S(2)}, u32[]{:S(2)}) collective-permute-start(f32[128,128]{1,0:T(8,128)S(1)} %get-tuple-element.88), channel_id=1, source_target_pairs={{0,2},{1,3},{2,0},{3,1},{4,6},{5,7},{6,4},{7,5},{8,10},{9,11},{10,... | collective-permute-start | bytes 196616 | tf_op jit(solution)/shard_map/ppermute | solution.py:412
  77.5 4.6 %collective-permute-start.24 = (f32[128,128]{1,0:T(8,128)S(1)}, f32[128,128]{1,0:T(8,128)S(1)}, u32[]{:S(2)}, u32[]{:S(2)}) collective-permute-start(f32[128,128]{1,0:T(8,128)S(1)} %get-tuple-element.89), channel_id=1, source_target_pairs={{0,4},{1,5},{2,6},{3,7},{4,0},{5,1},{6,2},{7,3},{8,12},{9,13},{10,... | collective-permute-start | bytes 196616 | tf_op jit(solution)/shard_map/ppermute | solution.py:412
  78.7 4.3 %collective-permute-start.25 = (f32[128,128]{1,0:T(8,128)S(1)}, f32[128,128]{1,0:T(8,128)S(1)}, u32[]{:S(2)}, u32[]{:S(2)}) collective-permute-start(f32[128,128]{1,0:T(8,128)S(1)} %get-tuple-element.90), channel_id=1, source_target_pairs={{0,6},{1,7},{2,4},{3,5},{4,2},{5,3},{6,0},{7,1},{8,14},{9,15},{10,... | collective-permute-start | bytes 196616 | tf_op jit(solution)/shard_map/ppermute | solution.py:412
  83.1 6.7 %collective-permute-start.26 = (f32[512,128]{1,0:T(8,128)S(1)}, f32[512,128]{1,0:T(8,128)S(1)}, u32[]{:S(2)}, u32[]{:S(2)}) collective-permute-start(f32[512,128]{1,0:T(8,128)S(1)} %get-tuple-element.99.refs_8_), channel_id=1, source_target_pairs={{0,1},{1,0},{2,3},{3,2},{4,5},{5,4},{6,7},{7,6},{8,9},{9,8},{10,11... | collective-permute-start | bytes 786440 | tf_op jit(solution)/shard_map/ppermute | solution.py:412

commit v5 on v4

--- a/solution.py
+++ b/solution.py
@@ -186,24 +186,23 @@
     return 4 * c if own else 4 * (1 - c)
 
 
-def sent_states_kernel(decay_in, bounds_in, k, v, out, table, k_in, v_in, decay, bounds, sems):
+def sent_states_kernel(decay_in, bounds_in, k_in, v_in, out, table, k, v, decay, bounds, sems):
     at, _, y, _ = place()
     heads = [first_head(False) + (y ^ i) for i in range(4)]
-    numbers = (
-        pltpu.make_async_copy(decay_in, decay, sems.at[2, 0]),
-        pltpu.make_async_copy(bounds_in, bounds, sems.at[2, 1]),
-    )
-    for copy in numbers:
+    rest = pl.ds(pl.multiple_of(first_head(True) * HEAD, 4 * HEAD), 4 * HEAD)
+
+    def start(source, target, sem):
+        copy = pltpu.make_async_copy(source, target, sem)
         copy.start()
+        return copy
+
+    numbers = [start(decay_in, decay, sems.at[2, 0]), start(bounds_in, bounds, sems.at[2, 1])]
     copies = []
     for i, head in enumerate(heads):
-        pair = (
-            pltpu.make_async_copy(k.at[:, columns(head)], k_in.at[i], sems.at[0, i]),
-            pltpu.make_async_copy(v.at[:, columns(head)], v_in.at[i], sems.at[1, i]),
-        )
-        for copy in pair:
-            copy.start()
-        copies.append(pair)
+        spot = columns(head)
+        copies.append(start(k_in.at[:, spot], k.at[:, spot], sems.at[0, i]))
+        copies.append(start(v_in.at[:, spot], v.at[:, spot], sems.at[1, i]))
+    halves = [start(k_in.at[:, rest], k.at[:, rest], sems.at[2, 2]), start(v_in.at[:, rest], v.at[:, rest], sems.at[2, 3])]
     for copy in numbers:
         copy.wait()
     for head in range(HEADS_DEV):
@@ -214,10 +213,12 @@
     fill_chain(table, FORWARD, decay, bounds, False)
     for i, head in enumerate(heads):
         weights = leave_decay(table, head)
-        for copy in copies[i]:
-            copy.wait()
-        decayed = (weights * k_in[i].astype(F32)).astype(BF16)
-        out[i * HEAD : (i + 1) * HEAD, :] = mm_at(decayed, v_in[i])
+        copies[2 * i].wait()
+        copies[2 * i + 1].wait()
+        decayed = (weights * k[:, columns(head)].astype(F32)).astype(BF16)
+        out[i * HEAD : (i + 1) * HEAD, :] = mm_at(decayed, v[:, columns(head)])
+    for copy in halves:
+        copy.wait()
 
 
 def kept_states_kernel(table, k, v, after, out):
@@ -275,15 +276,18 @@
                 state += table[at : at + 1, :] * t[0:HEAD, :]
         outs[SLOT[k]][...] = state
     if gains:
-        _, z, y, c = place()
         tail = slice(HEAD, HEAD + 8)
         outs[4][...] = sent[tail, :] + far[tail, :]
-        row = outs[4][pl.ds(z, 1), :]
-        turned = pltpu.roll(row, (HEAD - 32 * y - 16 * c) % HEAD, axis=1)
-        outs[5][...] = turned[0, 0:16]
-
-
-def cores_in_kernel(table, v0, v1, v2, v3, keep, got, after, mine, other, *, base, reverse):
+
+
+def gains_kernel(totals, out):
+    _, z, y, c = place()
+    turned = pltpu.roll(totals[pl.ds(z, 1), :], (HEAD - 32 * y - 16 * c) % HEAD, axis=1)
+    out[...] = turned[0, 0:16]
+
+
+def cores_in_kernel(table, v0, v1, v2, v3, keep, got, *refs, base, reverse):
+    mine, other = refs[-2:]
     c = place()[3]
     deep = c == 0 if reverse else c == 1
     for k, v in enumerate((v0, v1, v2, v3)):
@@ -420,10 +424,10 @@
         return call(
             functools.partial(kernel, reverse=reverse, base=base, **more),
             outs,
-            in_specs=[VMEM] * (1 + len(args)) + [ANY],
+            in_specs=[VMEM] * (1 + len(args)) + [ANY] * len(after),
             out_specs=jax.tree.map(lambda _: VMEM, outs),
             limit=8,
-        )(table, *args, after)
+        )(table, *args, *after)
 
     def around(arrays, ks, **axis):
         moved = {k: exchange(arrays[k], **{name: k for name in axis}) for k in ks}
@@ -431,21 +435,22 @@
 
     got = exchange(send, dc=1)
     keep = make_keep(send)
-    chips = step(chip_kernel, [small] * 4, keep, got, send, gains=gains, after=keep)
+    chips = step(chip_kernel, [small] * 4, keep, got, send, gains=gains, after=[keep])
     done = work[0](chips[0])
     chips = around([chips[n] for n in SLOT], (2, 1, 3), dy=1)
-    row = step(sum_kernel, small, *chips, gains=gains, after=done, base=base + ROW)
+    row = step(sum_kernel, small, *chips, gains=gains, after=[done], base=base + ROW)
     done = work[1](row)
     rows = around([row] * 4, (1, 2, 3), dz=1)
-    sent = step(sum_kernel, small, *rows, gains=gains, after=done, base=base + HALF)
+    sent = step(sum_kernel, small, *rows, gains=gains, after=[done], base=base + HALF)
     done = work[2](sent)
     far = exchange(sent, dz=FAR_Z)
-    outs = [shape(HEAD, HEAD)] * 4 + ([shape(8, HEAD), shape(16)] if gains else [])
-    outs = step(chips_in_kernel, outs, *rows[1:], far, sent, *chips, gains=gains, after=done)
+    outs = [shape(HEAD, HEAD)] * 4 + ([shape(8, HEAD)] if gains else [])
+    outs = step(chips_in_kernel, outs, *rows[1:], far, sent, *chips, gains=gains, after=[done])
     done = work[3](outs[0])
     states = around([outs[n] for n in SLOT], (2, 1, 3), dy=1)
-    mine, other = step(cores_in_kernel, [shape(4 * HEAD, HEAD)] * 2, *states, keep, got, after=done)
-    return mine, other, (outs[5] if gains else None)
+    total = call(gains_kernel, shape(16), in_specs=[VMEM], out_specs=VMEM)(outs[4]) if gains else None
+    mine, other = step(cores_in_kernel, [shape(4 * HEAD, HEAD)] * 2, *states, keep, got, after=[done] + [total] * gains)
+    return mine, other, total
 
 
 def shards(queries, keys, values, out_grad, gain, decay, bounds):
@@ -466,13 +471,13 @@
             moved=moved,
         )(table, *args, *order)
 
-    send, table = call(
+    wide = shape(TOK, width, dtype=BF16)
+    send, table, keys, values = call(
         sent_states_kernel,
-        [state_shape, shape(FORWARD + CHAIN_ROWS, HEAD)],
+        [state_shape, shape(FORWARD + CHAIN_ROWS, HEAD), wide, wide],
         in_specs=[ANY] * 4,
-        out_specs=[VMEM] * 2,
-        scratch=[pltpu.VMEM((4, TOK, HEAD), BF16)] * 2
-        + [pltpu.SMEM((HEADS_DEV,), jnp.int32), pltpu.SMEM((3,), jnp.int32), pltpu.SemaphoreType.DMA((3, 4))],
+        out_specs=[VMEM] * 4,
+        scratch=[pltpu.SMEM((HEADS_DEV,), jnp.int32), pltpu.SMEM((3,), jnp.int32), pltpu.SemaphoreType.DMA((3, 4))],
         flops=small_mm,
         moved=3 << 19,
     )(*[pltpu.with_memory_space_constraint(x, pltpu.HBM) for x in (decay, bounds, keys, values)])

time: 91.5 us -> 91 us (level)
    pallas_call x1 -> x2, Pallas kernels: 2.28 us -> 2.84 us  [the longest x1 2.26 us: shards(): call(sent_states_kernel, [state_shape, shape(FORWARD + CHAIN_ROWS, HEAD),...]
  transfers between devices with their start and end apart: 27 -> 27, of which waited for: 15 -> 15; matrix products, arithmetic and copies ran while one was open for 0% -> 0% of each run, Pallas kernels for 17% -> 18%
where the time goes in v5:
time: 91 us; the launch traced here: 90.9 us
  starting transfers between devices  48.8 us (54%)
  Pallas kernels  22.6 us (25%)
  waiting for transfers between devices  18.1 us (20%)
  between operations  1.05 us (1%)
    ppermute x24, starting transfers between devices, exchange(): return lax.ppermute(array, 'seq', pairs)  45.5 us
    pallas_call x11, Pallas kernels, local(): call(functools.partial(kernel, **more), outs, in_specs=[VMEM] * (1 + len(...  15 us
    ppermute x24, waiting for transfers between devices, exchange(): return lax.ppermute(array, 'seq', pairs)  14.8 us
    ppermute x3, starting transfers between devices, shards(): lax.ppermute(sums, 'dp', [(i, i ^ k) for i in range(4)])  3.34 us
    ppermute x3, waiting for transfers between devices, shards(): lax.ppermute(sums, 'dp', [(i, i ^ k) for i in range(4)])  3.32 us
    pallas_call x1, Pallas kernels, shards(): call(sent_states_kernel, [state_shape, shape(FORWARD + CHAIN_ROWS, HEAD),...  2.26 us
  transfers between devices with their start and end apart: 27, of which 15 were waited for; matrix products, arithmetic and copies ran while one was open for 0% of the time, Pallas kernels for 18%

profile of v5, /device:TPU:1, one launch (start us, length us, event | category | flops | bytes accessed | tf_op | source)
XLA Modules:
  0.0 90.9 jit_solution(10469753344493960135)
XLA Ops:
  0.6 2.3 %shard_map.102 = (f32[512,128]{1,0:T(8,128)S(1)}, f32[64,128]{1,0:T(8,128)S(1)}, bf16[512,1024]{1,0:T(8,128)(2,1)S(1)}, bf16[512,1024]{1,0:T(8,128)(2,1)S(1)}) custom-call(s32[8]{0:T(128)} %decay.1, s32[3]{0:T(128)} %bounds.1, bf16[512,1024]{1,0:T(8,128)(2,1)} %k_in.1, bf16[512,1024]{1,0:T(8,128)(2,1)} %v_in.1), custom_call_target="tpu_custom_call" | custom-call | flops 67108864 | bytes 1572864 | tf_op jit(solution)/shard_map/pallas_call | solution.py:475
  2.9 3.3 %collective-permute-start = (f32[512,128]{1,0:T(8,128)S(1)}, f32[512,128]{1,0:T(8,128)S(1)}, u32[]{:S(2)}, u32[]{:S(2)}) collective-permute-start(f32[512,128]{1,0:T(8,128)S(1)} %get-tuple-element.61.after.send), channel_id=1, source_target_pairs={{0,1},{1,0},{2,3},{3,2},{4,5},{5,4},{6,7},{7,6},{8,9},{9,8},{10,11... | collective-permute-start | bytes 786440 | tf_op jit(solution)/shard_map/ppermute | solution.py:416
  7.5 2.2 %collective-permute-start.2 = (f32[128,128]{1,0:T(8,128)S(1)}, f32[128,128]{1,0:T(8,128)S(1)}, u32[]{:S(2)}, u32[]{:S(2)}) collective-permute-start(f32[128,128]{1,0:T(8,128)S(1)} %get-tuple-element.66), channel_id=1, source_target_pairs={{0,4},{1,5},{2,6},{3,7},{4,0},{5,1},{6,2},{7,3},{8,12},{9,13},{10,... | collective-permute-start | bytes 196616 | tf_op jit(solution)/shard_map/ppermute | solution.py:416
  9.7 1.7 %collective-permute-start.3 = (f32[128,128]{1,0:T(8,128)S(1)}, f32[128,128]{1,0:T(8,128)S(1)}, u32[]{:S(2)}, u32[]{:S(2)}) collective-permute-start(f32[128,128]{1,0:T(8,128)S(1)} %get-tuple-element.67), channel_id=1, source_target_pairs={{0,6},{1,7},{2,4},{3,5},{4,2},{5,3},{6,0},{7,1},{8,14},{9,15},{10,... | collective-permute-start | bytes 196616 | tf_op jit(solution)/shard_map/ppermute | solution.py:416
  12.5 1.5 %shard_map.106.after.intra = f32[512,512]{1,0:T(8,128)S(1)} custom-call(f32[64,128]{1,0:T(8,128)S(1)} %get-tuple-element.58.table, bf16[512,1024]{1,0:T(8,128)(2,1)S(1)} %copy-done, bf16[512,1024]{1,0:T(8,128)(2,1)S(1)} %get-tuple-element.59.k, bf16[512,1024]{1,0:T(8,128)(2,1)S(1)} %get-tuple-element.60.v, bf16[512,512]{1,0:T(8,128)(2,1)S(1)} %get-tuple-element.64.mask, ...), custom_call_target="tpu_custom_call" | custom-call | flops 402653184 | bytes 3145728 | tf_op jit(solution)/shard_map/pallas_call | solution.py:465
  14.3 4.3 %collective-permute-start.6 = (f32[128,128]{1,0:T(8,128)S(1)}, f32[128,128]{1,0:T(8,128)S(1)}, u32[]{:S(2)}, u32[]{:S(2)}) collective-permute-start(f32[128,128]{1,0:T(8,128)S(1)} %shard_map.107.after.p0), channel_id=1, source_target_pairs={{0,24},{1,25},{2,26},{3,27},{4,28},{5,29},{6,30},{7,31},{8,16},{9,... | collective-permute-start | bytes 196616 | tf_op jit(solution)/shard_map/ppermute | solution.py:416
  19.0 1.5 %shard_map.108.after.intra = f32[512,512]{1,0:T(8,128)S(1)} custom-call(f32[64,128]{1,0:T(8,128)S(1)} %get-tuple-element.58.table, bf16[512,1024]{1,0:T(8,128)(2,1)S(1)} %copy-done, bf16[512,1024]{1,0:T(8,128)(2,1)S(1)} %get-tuple-element.59.k, bf16[512,1024]{1,0:T(8,128)(2,1)S(1)} %get-tuple-element.60.v, bf16[512,512]{1,0:T(8,128)(2,1)S(1)} %get-tuple-element.64.mask, ...), custom_call_target="tpu_custom_call" | custom-call | flops 402653184 | bytes 3145728 | tf_op jit(solution)/shard_map/pallas_call | solution.py:465
  20.5 2.8 %collective-permute-done.5.p2.r2 = f32[128,128]{1,0:T(8,128)S(1)} collective-permute-done((f32[128,128]{1,0:T(8,128)S(1)}, f32[128,128]{1,0:T(8,128)S(1)}, u32[]{:S(2)}, u32[]{:S(2)}) %collective-permute-start.5) | collective-permute-done | bytes 65568 | tf_op jit(solution)/shard_map/ppermute | solution.py:416
  23.3 3.6 %collective-permute-start.7 = (f32[128,128]{1,0:T(8,128)S(1)}, f32[128,128]{1,0:T(8,128)S(1)}, u32[]{:S(2)}, u32[]{:S(2)}) collective-permute-start(f32[128,128]{1,0:T(8,128)S(1)} %shard_map.109.sent.after), channel_id=1, source_target_pairs={{0,48},{1,49},{2,50},{3,51},{4,52},{5,53},{6,54},{7,55},{8,56},{9,... | collective-permute-start | bytes 196616 | tf_op jit(solution)/shard_map/ppermute | solution.py:416
  26.9 2.4 %collective-permute-done.7.far = f32[128,128]{1,0:T(8,128)S(1)} collective-permute-done((f32[128,128]{1,0:T(8,128)S(1)}, f32[128,128]{1,0:T(8,128)S(1)}, u32[]{:S(2)}, u32[]{:S(2)}) %collective-permute-start.7) | collective-permute-done | bytes 65568 | tf_op jit(solution)/shard_map/ppermute | solution.py:416
  29.5 2.6 %collective-permute-start.9 = (f32[128,128]{1,0:T(8,128)S(1)}, f32[128,128]{1,0:T(8,128)S(1)}, u32[]{:S(2)}, u32[]{:S(2)}) collective-permute-start(f32[128,128]{1,0:T(8,128)S(1)} %get-tuple-element.71), channel_id=1, source_target_pairs={{0,4},{1,5},{2,6},{3,7},{4,0},{5,1},{6,2},{7,3},{8,12},{9,13},{10,... | collective-permute-start | bytes 196616 | tf_op jit(solution)/shard_map/ppermute | solution.py:416
  32.1 1.3 %collective-permute-start.10 = (f32[128,128]{1,0:T(8,128)S(1)}, f32[128,128]{1,0:T(8,128)S(1)}, u32[]{:S(2)}, u32[]{:S(2)}) collective-permute-start(f32[128,128]{1,0:T(8,128)S(1)} %get-tuple-element.72), channel_id=1, source_target_pairs={{0,6},{1,7},{2,4},{3,5},{4,2},{5,3},{6,0},{7,1},{8,14},{9,15},{10,... | collective-permute-start | bytes 196616 | tf_op jit(solution)/shard_map/ppermute | solution.py:416
  34.4 2.0 %collective-permute-done.10.v3 = f32[128,128]{1,0:T(8,128)S(1)} collective-permute-done((f32[128,128]{1,0:T(8,128)S(1)}, f32[128,128]{1,0:T(8,128)S(1)}, u32[]{:S(2)}, u32[]{:S(2)}) %collective-permute-start.10) | collective-permute-done | bytes 65568 | tf_op jit(solution)/shard_map/ppermute | solution.py:416
  36.5 4.5 %collective-permute-start.11 = (f32[512,128]{1,0:T(8,128)S(1)}, f32[512,128]{1,0:T(8,128)S(1)}, u32[]{:S(2)}, u32[]{:S(2)}) collective-permute-start(f32[512,128]{1,0:T(8,128)S(1)} %get-tuple-element.73.refs_0_), channel_id=1, source_target_pairs={{0,1},{1,0},{2,3},{3,2},{4,5},{5,4},{6,7},{7,6},{8,9},{9,8},{10,11... | collective-permute-start | bytes 786440 | tf_op jit(solution)/shard_map/ppermute | solution.py:416
  43.0 2.6 %collective-permute-start.14 = (f32[8,512]{1,0:T(8,128)S(1)}, f32[8,512]{1,0:T(8,128)S(1)}, u32[]{:S(2)}, u32[]{:S(2)}) collective-permute-start(f32[8,512]{1,0:T(8,128)S(1)} %get-tuple-element.76.s0), channel_id=1, source_target_pairs={{0,192},{64,128},{128,64},{192,0},{1,193},{65,129},{129,65},{193,1... | collective-permute-start | bytes 49160 | tf_op jit(solution)/shard_map/ppermute | solution.py:537
  46.9 2.8 %collective-permute-done.13.s2 = f32[8,512]{1,0:T(8,128)S(1)} collective-permute-done((f32[8,512]{1,0:T(8,128)S(1)}, f32[8,512]{1,0:T(8,128)S(1)}, u32[]{:S(2)}, u32[]{:S(2)}) %collective-permute-start.13) | collective-permute-done | bytes 16416 | tf_op jit(solution)/shard_map/ppermute | solution.py:537
  50.8 1.9 %collective-permute-start.15 = (f32[520,128]{1,0:T(8,128)S(1)}, f32[520,128]{1,0:T(8,128)S(1)}, u32[]{:S(2)}, u32[]{:S(2)}) collective-permute-start(f32[520,128]{1,0:T(8,128)S(1)} %get-tuple-element.79.refs_0_.send), channel_id=1, source_target_pairs={{0,1},{1,0},{2,3},{3,2},{4,5},{5,4},{6,7},{7,6},{8,9},{9,8},{10,11... | collective-permute-start | bytes 798728 | tf_op jit(solution)/shard_map/ppermute | solution.py:416
  54.0 3.2 %collective-permute-start.17 = (f32[136,128]{1,0:T(8,128)S(1)}, f32[136,128]{1,0:T(8,128)S(1)}, u32[]{:S(2)}, u32[]{:S(2)}) collective-permute-start(f32[136,128]{1,0:T(8,128)S(1)} %get-tuple-element.83), channel_id=1, source_target_pairs={{0,4},{1,5},{2,6},{3,7},{4,0},{5,1},{6,2},{7,3},{8,12},{9,13},{10,... | collective-permute-start | bytes 208904 | tf_op jit(solution)/shard_map/ppermute | solution.py:416
  57.8 2.0 %shard_map.117 = (bf16[512,256]{1,0:T(8,128)(2,1)S(1)}, f32[512,256]{1,0:T(8,128)S(1)}, f32[512,256]{1,0:T(8,128)S(1)}) custom-call(f32[64,128]{1,0:T(8,128)S(1)} %get-tuple-element.58.table, bf16[512,1024]{1,0:T(8,128)(2,1)S(1)} %copy-done, bf16[512,1024]{1,0:T(8,128)(2,1)S(1)} %get-tuple-element.59.k, bf16[512,1024]{1,0:T(8,128)(2,1)S(1)} %get-tuple-element.60.v, ...), custom_call_target="tpu_custom_call" | custom-call | flops 603979776 | bytes 2097152 | tf_op jit(solution)/shard_map/pallas_call | solution.py:465
  60.3 1.6 %collective-permute-done.18.p3.t3 = f32[136,128]{1,0:T(8,128)S(1)} collective-permute-done((f32[136,128]{1,0:T(8,128)S(1)}, f32[136,128]{1,0:T(8,128)S(1)}, u32[]{:S(2)}, u32[]{:S(2)}) %collective-permute-start.18) | collective-permute-done | bytes 69664 | tf_op jit(solution)/shard_map/ppermute | solution.py:416
  61.9 1.8 %collective-permute-start.21 = (f32[136,128]{1,0:T(8,128)S(1)}, f32[136,128]{1,0:T(8,128)S(1)}, u32[]{:S(2)}, u32[]{:S(2)}) collective-permute-start(f32[136,128]{1,0:T(8,128)S(1)} %shard_map.118.after.p0), channel_id=1, source_target_pairs={{0,24},{1,25},{2,26},{3,27},{4,28},{5,29},{6,30},{7,31},{8,16},{9,... | collective-permute-start | bytes 208904 | tf_op jit(solution)/shard_map/ppermute | solution.py:416
  63.7 1.2 %collective-permute-start.20 = (f32[136,128]{1,0:T(8,128)S(1)}, f32[136,128]{1,0:T(8,128)S(1)}, u32[]{:S(2)}, u32[]{:S(2)}) collective-permute-start(f32[136,128]{1,0:T(8,128)S(1)} %shard_map.118.after.p0), channel_id=1, source_target_pairs={{0,16},{1,17},{2,18},{3,19},{4,20},{5,21},{6,22},{7,23},{8,24},{9,... | collective-permute-start | bytes 208904 | tf_op jit(solution)/shard_map/ppermute | solution.py:416
  65.6 1.9 %shard_map.119 = (bf16[512,256]{1,0:T(8,128)(2,1)S(1)}, f32[512,256]{1,0:T(8,128)S(1)}, f32[512,256]{1,0:T(8,128)S(1)}) custom-call(f32[64,128]{1,0:T(8,128)S(1)} %get-tuple-element.58.table, bf16[512,1024]{1,0:T(8,128)(2,1)S(1)} %copy-done, bf16[512,1024]{1,0:T(8,128)(2,1)S(1)} %get-tuple-element.59.k, bf16[512,1024]{1,0:T(8,128)(2,1)S(1)} %get-tuple-element.60.v, ...), custom_call_target="tpu_custom_call" | custom-call | flops 603979776 | bytes 2097152 | tf_op jit(solution)/shard_map/pallas_call | solution.py:465
  67.5 2.4 %collective-permute-done.20.p2.r2 = f32[136,128]{1,0:T(8,128)S(1)} collective-permute-done((f32[136,128]{1,0:T(8,128)S(1)}, f32[136,128]{1,0:T(8,128)S(1)}, u32[]{:S(2)}, u32[]{:S(2)}) %collective-permute-start.20) | collective-permute-done | bytes 69664 | tf_op jit(solution)/shard_map/ppermute | solution.py:416
  70.0 3.3 %collective-permute-start.22 = (f32[136,128]{1,0:T(8,128)S(1)}, f32[136,128]{1,0:T(8,128)S(1)}, u32[]{:S(2)}, u32[]{:S(2)}) collective-permute-start(f32[136,128]{1,0:T(8,128)S(1)} %shard_map.120.after.sent), channel_id=1, source_target_pairs={{0,48},{1,49},{2,50},{3,51},{4,52},{5,53},{6,54},{7,55},{8,56},{9,... | collective-permute-start | bytes 208904 | tf_op jit(solution)/shard_map/ppermute | solution.py:416
  73.3 2.0 %shard_map.121 = (bf16[512,256]{1,0:T(8,128)(2,1)S(1)}, f32[512,256]{1,0:T(8,128)S(1)}, f32[512,256]{1,0:T(8,128)S(1)}) custom-call(f32[64,128]{1,0:T(8,128)S(1)} %get-tuple-element.58.table, bf16[512,1024]{1,0:T(8,128)(2,1)S(1)} %copy-done, bf16[512,1024]{1,0:T(8,128)(2,1)S(1)} %get-tuple-element.59.k, bf16[512,1024]{1,0:T(8,128)(2,1)S(1)} %get-tuple-element.60.v, ...), custom_call_target="tpu_custom_call" | custom-call | flops 603979776 | bytes 2097152 | tf_op jit(solution)/shard_map/pallas_call | solution.py:465
  76.6 1.5 %collective-permute-start.24 = (f32[128,128]{1,0:T(8,128)S(1)}, f32[128,128]{1,0:T(8,128)S(1)}, u32[]{:S(2)}, u32[]{:S(2)}) collective-permute-start(f32[128,128]{1,0:T(8,128)S(1)} %get-tuple-element.93), channel_id=1, source_target_pairs={{0,4},{1,5},{2,6},{3,7},{4,0},{5,1},{6,2},{7,3},{8,12},{9,13},{10,... | collective-permute-start | bytes 196616 | tf_op jit(solution)/shard_map/ppermute | solution.py:416
  78.1 1.4 %collective-permute-start.25 = (f32[128,128]{1,0:T(8,128)S(1)}, f32[128,128]{1,0:T(8,128)S(1)}, u32[]{:S(2)}, u32[]{:S(2)}) collective-permute-start(f32[128,128]{1,0:T(8,128)S(1)} %get-tuple-element.94), channel_id=1, source_target_pairs={{0,6},{1,7},{2,4},{3,5},{4,2},{5,3},{6,0},{7,1},{8,14},{9,15},{10,... | collective-permute-start | bytes 196616 | tf_op jit(solution)/shard_map/ppermute | solution.py:416
  80.2 2.0 %shard_map.123 = (bf16[512,256]{1,0:T(8,128)(2,1)S(1)}, f32[512,256]{1,0:T(8,128)S(1)}, f32[512,256]{1,0:T(8,128)S(1)}) custom-call(f32[64,128]{1,0:T(8,128)S(1)} %get-tuple-element.58.table, bf16[512,1024]{1,0:T(8,128)(2,1)S(1)} %copy-done, bf16[512,1024]{1,0:T(8,128)(2,1)S(1)} %get-tuple-element.59.k, bf16[512,1024]{1,0:T(8,128)(2,1)S(1)} %get-tuple-element.60.v, ...), custom_call_target="tpu_custom_call" | custom-call | flops 603979776 | bytes 2097152 | tf_op jit(solution)/shard_map/pallas_call | solution.py:465
  82.9 4.7 %collective-permute-start.26 = (f32[512,128]{1,0:T(8,128)S(1)}, f32[512,128]{1,0:T(8,128)S(1)}, u32[]{:S(2)}, u32[]{:S(2)}) collective-permute-start(f32[512,128]{1,0:T(8,128)S(1)} %get-tuple-element.104.refs_8_), channel_id=1, source_target_pairs={{0,1},{1,0},{2,3},{3,2},{4,5},{5,4},{6,7},{7,6},{8,9},{9,8},{10,11... | collective-permute-start | bytes 786440 | tf_op jit(solution)/shard_map/ppermute | solution.py:416
  87.6 1.6 %shard_map.126 = (bf16[512,1024]{1,0:T(8,128)(2,1)}, bf16[512,1024]{1,0:T(8,128)(2,1)}, bf16[512,1024]{1,0:T(8,128)(2,1)}) custom-call(f32[64,128]{1,0:T(8,128)S(1)} %get-tuple-element.58.table, bf16[512,1024]{1,0:T(8,128)(2,1)S(1)} %get-tuple-element.59.k, bf16[512,1024]{1,0:T(8,128)(2,1)S(1)} %get-tuple-element.60.v, ...), custom_call_target="tpu_custom_call" | custom-call | flops 134217728 | bytes 6291456 | tf_op jit(solution)/shard_map/pallas_call | solution.py:581
  89.2 1.5 %shard_map.127 = (bf16[512,1024]{1,0:T(8,128)(2,1)}, bf16[512,1024]{1,0:T(8,128)(2,1)}) custom-call(f32[64,128]{1,0:T(8,128)S(1)} %get-tuple-element.58.table, bf16[512,1024]{1,0:T(8,128)(2,1)S(1)} %get-tuple-element.59.k, bf16[512,1024]{1,0:T(8,128)(2,1)S(1)} %get-tuple-element.60.v, ...), custom_call_target="tpu_custom_call", output_to_operand_aliasing={{0}: (8, {}), {1}: (9, {})} | custom-call | flops 134217728 | bytes 4194304 | tf_op jit(solution)/shard_map/pallas_call | solution.py:590
  (56 shorter events, 14.7 us)
Async XLA Ops:
  2.9 4.5 %collective-permute-start = (f32[512,128]{1,0:T(8,128)S(1)}, f32[512,128]{1,0:T(8,128)S(1)}, u32[]{:S(2)}, u32[]{:S(2)}) collective-permute-start(f32[512,128]{1,0:T(8,128)S(1)} %get-tuple-element.61.after.send), channel_id=1, source_target_pairs={{0,1},{1,0},{2,3},{3,2},{4,5},{5,4},{6,7},{7,6},{8,9},{9,8},{10,11... | collective-permute-start | bytes 786440 | tf_op jit(solution)/shard_map/ppermute | solution.py:416
  6.8 5.7 %copy-start = (bf16[512,1024]{1,0:T(8,128)(2,1)S(1)}, bf16[512,1024]{1,0:T(8,128)(2,1)}, u32[]{:S(2)}) copy-start(bf16[512,1024]{1,0:T(8,128)(2,1)} %q.19) | copy-start | bytes 3145732
  7.4 4.0 %copy-start.2 = (f32[1024]{0:T(1024)S(1)}, f32[1024]{0:T(1024)}, u32[]{:S(2)}) copy-start(f32[1024]{0:T(1024)} %param.11) | copy-start | bytes 12292
  7.4 6.6 %collective-permute-start.1 = (f32[128,128]{1,0:T(8,128)S(1)}, f32[128,128]{1,0:T(8,128)S(1)}, u32[]{:S(2)}, u32[]{:S(2)}) collective-permute-start(f32[128,128]{1,0:T(8,128)S(1)} %get-tuple-element.65), channel_id=1, source_target_pairs={{0,2},{1,3},{2,0},{3,1},{4,6},{5,7},{6,4},{7,5},{8,10},{9,11},{10,... | collective-permute-start | bytes 196616 | tf_op jit(solution)/shard_map/ppermute | solution.py:416
  7.5 6.5 %collective-permute-start.2 = (f32[128,128]{1,0:T(8,128)S(1)}, f32[128,128]{1,0:T(8,128)S(1)}, u32[]{:S(2)}, u32[]{:S(2)}) collective-permute-start(f32[128,128]{1,0:T(8,128)S(1)} %get-tuple-element.66), channel_id=1, source_target_pairs={{0,4},{1,5},{2,6},{3,7},{4,0},{5,1},{6,2},{7,3},{8,12},{9,13},{10,... | collective-permute-start | bytes 196616 | tf_op jit(solution)/shard_map/ppermute | solution.py:416
  9.7 4.6 %collective-permute-start.3 = (f32[128,128]{1,0:T(8,128)S(1)}, f32[128,128]{1,0:T(8,128)S(1)}, u32[]{:S(2)}, u32[]{:S(2)}) collective-permute-start(f32[128,128]{1,0:T(8,128)S(1)} %get-tuple-element.67), channel_id=1, source_target_pairs={{0,6},{1,7},{2,4},{3,5},{4,2},{5,3},{6,0},{7,1},{8,14},{9,15},{10,... | collective-permute-start | bytes 196616 | tf_op jit(solution)/shard_map/ppermute | solution.py:416
  14.3 6.2 %collective-permute-start.6 = (f32[128,128]{1,0:T(8,128)S(1)}, f32[128,128]{1,0:T(8,128)S(1)}, u32[]{:S(2)}, u32[]{:S(2)}) collective-permute-start(f32[128,128]{1,0:T(8,128)S(1)} %shard_map.107.after.p0), channel_id=1, source_target_pairs={{0,24},{1,25},{2,26},{3,27},{4,28},{5,29},{6,30},{7,31},{8,16},{9,... | collective-permute-start | bytes 196616 | tf_op jit(solution)/shard_map/ppermute | solution.py:416
  18.6 4.6 %collective-permute-start.5 = (f32[128,128]{1,0:T(8,128)S(1)}, f32[128,128]{1,0:T(8,128)S(1)}, u32[]{:S(2)}, u32[]{:S(2)}) collective-permute-start(f32[128,128]{1,0:T(8,128)S(1)} %shard_map.107.after.p0), channel_id=1, source_target_pairs={{0,16},{1,17},{2,18},{3,19},{4,20},{5,21},{6,22},{7,23},{8,24},{9,... | collective-permute-start | bytes 196616 | tf_op jit(solution)/shard_map/ppermute | solution.py:416
  18.6 4.6 %collective-permute-start.4 = (f32[128,128]{1,0:T(8,128)S(1)}, f32[128,128]{1,0:T(8,128)S(1)}, u32[]{:S(2)}, u32[]{:S(2)}) collective-permute-start(f32[128,128]{1,0:T(8,128)S(1)} %shard_map.107.after.p0), channel_id=1, source_target_pairs={{0,8},{1,9},{2,10},{3,11},{4,12},{5,13},{6,14},{7,15},{8,0},{9,1},... | collective-permute-start | bytes 196616 | tf_op jit(solution)/shard_map/ppermute | solution.py:416
  23.3 17.7 %copy-start.1 = (bf16[512,1024]{1,0:T(8,128)(2,1)S(1)}, bf16[512,1024]{1,0:T(8,128)(2,1)}, u32[]{:S(2)}) copy-start(bf16[512,1024]{1,0:T(8,128)(2,1)} %grad.7) | copy-start | bytes 3145732
  23.3 6.0 %collective-permute-start.7 = (f32[128,128]{1,0:T(8,128)S(1)}, f32[128,128]{1,0:T(8,128)S(1)}, u32[]{:S(2)}, u32[]{:S(2)}) collective-permute-start(f32[128,128]{1,0:T(8,128)S(1)} %shard_map.109.sent.after), channel_id=1, source_target_pairs={{0,48},{1,49},{2,50},{3,51},{4,52},{5,53},{6,54},{7,55},{8,56},{9,... | collective-permute-start | bytes 196616 | tf_op jit(solution)/shard_map/ppermute | solution.py:416
  29.4 3.9 %collective-permute-start.8 = (f32[128,128]{1,0:T(8,128)S(1)}, f32[128,128]{1,0:T(8,128)S(1)}, u32[]{:S(2)}, u32[]{:S(2)}) collective-permute-start(f32[128,128]{1,0:T(8,128)S(1)} %get-tuple-element.70), channel_id=1, source_target_pairs={{0,2},{1,3},{2,0},{3,1},{4,6},{5,7},{6,4},{7,5},{8,10},{9,11},{10,... | collective-permute-start | bytes 196616 | tf_op jit(solution)/shard_map/ppermute | solution.py:416
  29.5 4.9 %collective-permute-start.9 = (f32[128,128]{1,0:T(8,128)S(1)}, f32[128,128]{1,0:T(8,128)S(1)}, u32[]{:S(2)}, u32[]{:S(2)}) collective-permute-start(f32[128,128]{1,0:T(8,128)S(1)} %get-tuple-element.71), channel_id=1, source_target_pairs={{0,4},{1,5},{2,6},{3,7},{4,0},{5,1},{6,2},{7,3},{8,12},{9,13},{10,... | collective-permute-start | bytes 196616 | tf_op jit(solution)/shard_map/ppermute | solution.py:416
  32.1 4.3 %collective-permute-start.10 = (f32[128,128]{1,0:T(8,128)S(1)}, f32[128,128]{1,0:T(8,128)S(1)}, u32[]{:S(2)}, u32[]{:S(2)}) collective-permute-start(f32[128,128]{1,0:T(8,128)S(1)} %get-tuple-element.72), channel_id=1, source_target_pairs={{0,6},{1,7},{2,4},{3,5},{4,2},{5,3},{6,0},{7,1},{8,14},{9,15},{10,... | collective-permute-start | bytes 196616 | tf_op jit(solution)/shard_map/ppermute | solution.py:416
  36.5 5.7 %collective-permute-start.11 = (f32[512,128]{1,0:T(8,128)S(1)}, f32[512,128]{1,0:T(8,128)S(1)}, u32[]{:S(2)}, u32[]{:S(2)}) collective-permute-start(f32[512,128]{1,0:T(8,128)S(1)} %get-tuple-element.73.refs_0_), channel_id=1, source_target_pairs={{0,1},{1,0},{2,3},{3,2},{4,5},{5,4},{6,7},{7,6},{8,9},{9,8},{10,11... | collective-permute-start | bytes 786440 | tf_op jit(solution)/shard_map/ppermute | solution.py:416
  43.0 3.9 %collective-permute-start.14 = (f32[8,512]{1,0:T(8,128)S(1)}, f32[8,512]{1,0:T(8,128)S(1)}, u32[]{:S(2)}, u32[]{:S(2)}) collective-permute-start(f32[8,512]{1,0:T(8,128)S(1)} %get-tuple-element.76.s0), channel_id=1, source_target_pairs={{0,192},{64,128},{128,64},{192,0},{1,193},{65,129},{129,65},{193,1... | collective-permute-start | bytes 49160 | tf_op jit(solution)/shard_map/ppermute | solution.py:537
  45.5 4.1 %collective-permute-start.13 = (f32[8,512]{1,0:T(8,128)S(1)}, f32[8,512]{1,0:T(8,128)S(1)}, u32[]{:S(2)}, u32[]{:S(2)}) collective-permute-start(f32[8,512]{1,0:T(8,128)S(1)} %get-tuple-element.76.s0), channel_id=1, source_target_pairs={{0,128},{64,192},{128,0},{192,64},{1,129},{65,193},{129,1},{193,65... | collective-permute-start | bytes 49160 | tf_op jit(solution)/shard_map/ppermute | solution.py:537
  46.1 3.6 %collective-permute-start.12 = (f32[8,512]{1,0:T(8,128)S(1)}, f32[8,512]{1,0:T(8,128)S(1)}, u32[]{:S(2)}, u32[]{:S(2)}) collective-permute-start(f32[8,512]{1,0:T(8,128)S(1)} %get-tuple-element.76.s0), channel_id=1, source_target_pairs={{0,64},{64,0},{128,192},{192,128},{1,65},{65,1},{129,193},{193,129... | collective-permute-start | bytes 49160 | tf_op jit(solution)/shard_map/ppermute | solution.py:537
  50.8 3.0 %collective-permute-start.15 = (f32[520,128]{1,0:T(8,128)S(1)}, f32[520,128]{1,0:T(8,128)S(1)}, u32[]{:S(2)}, u32[]{:S(2)}) collective-permute-start(f32[520,128]{1,0:T(8,128)S(1)} %get-tuple-element.79.refs_0_.send), channel_id=1, source_target_pairs={{0,1},{1,0},{2,3},{3,2},{4,5},{5,4},{6,7},{7,6},{8,9},{9,8},{10,11... | collective-permute-start | bytes 798728 | tf_op jit(solution)/shard_map/ppermute | solution.py:416
  53.9 5.9 %collective-permute-start.16 = (f32[136,128]{1,0:T(8,128)S(1)}, f32[136,128]{1,0:T(8,128)S(1)}, u32[]{:S(2)}, u32[]{:S(2)}) collective-permute-start(f32[136,128]{1,0:T(8,128)S(1)} %get-tuple-element.82), channel_id=1, source_target_pairs={{0,2},{1,3},{2,0},{3,1},{4,6},{5,7},{6,4},{7,5},{8,10},{9,11},{10,... | collective-permute-start | bytes 208904 | tf_op jit(solution)/shard_map/ppermute | solution.py:416
  54.0 6.3 %collective-permute-start.17 = (f32[136,128]{1,0:T(8,128)S(1)}, f32[136,128]{1,0:T(8,128)S(1)}, u32[]{:S(2)}, u32[]{:S(2)}) collective-permute-start(f32[136,128]{1,0:T(8,128)S(1)} %get-tuple-element.83), channel_id=1, source_target_pairs={{0,4},{1,5},{2,6},{3,7},{4,0},{5,1},{6,2},{7,3},{8,12},{9,13},{10,... | collective-permute-start | bytes 208904 | tf_op jit(solution)/shard_map/ppermute | solution.py:416
  57.2 4.7 %collective-permute-start.18 = (f32[136,128]{1,0:T(8,128)S(1)}, f32[136,128]{1,0:T(8,128)S(1)}, u32[]{:S(2)}, u32[]{:S(2)}) collective-permute-start(f32[136,128]{1,0:T(8,128)S(1)} %get-tuple-element.84), channel_id=1, source_target_pairs={{0,6},{1,7},{2,4},{3,5},{4,2},{5,3},{6,0},{7,1},{8,14},{9,15},{10,... | collective-permute-start | bytes 208904 | tf_op jit(solution)/shard_map/ppermute | solution.py:416
  61.9 5.6 %collective-permute-start.21 = (f32[136,128]{1,0:T(8,128)S(1)}, f32[136,128]{1,0:T(8,128)S(1)}, u32[]{:S(2)}, u32[]{:S(2)}) collective-permute-start(f32[136,128]{1,0:T(8,128)S(1)} %shard_map.118.after.p0), channel_id=1, source_target_pairs={{0,24},{1,25},{2,26},{3,27},{4,28},{5,29},{6,30},{7,31},{8,16},{9,... | collective-permute-start | bytes 208904 | tf_op jit(solution)/shard_map/ppermute | solution.py:416
  63.7 6.3 %collective-permute-start.20 = (f32[136,128]{1,0:T(8,128)S(1)}, f32[136,128]{1,0:T(8,128)S(1)}, u32[]{:S(2)}, u32[]{:S(2)}) collective-permute-start(f32[136,128]{1,0:T(8,128)S(1)} %shard_map.118.after.p0), channel_id=1, source_target_pairs={{0,16},{1,17},{2,18},{3,19},{4,20},{5,21},{6,22},{7,23},{8,24},{9,... | collective-permute-start | bytes 208904 | tf_op jit(solution)/shard_map/ppermute | solution.py:416
  64.9 5.1 %collective-permute-start.19 = (f32[136,128]{1,0:T(8,128)S(1)}, f32[136,128]{1,0:T(8,128)S(1)}, u32[]{:S(2)}, u32[]{:S(2)}) collective-permute-start(f32[136,128]{1,0:T(8,128)S(1)} %shard_map.118.after.p0), channel_id=1, source_target_pairs={{0,8},{1,9},{2,10},{3,11},{4,12},{5,13},{6,14},{7,15},{8,0},{9,1},... | collective-permute-start | bytes 208904 | tf_op jit(solution)/shard_map/ppermute | solution.py:416
  70.0 5.6 %collective-permute-start.22 = (f32[136,128]{1,0:T(8,128)S(1)}, f32[136,128]{1,0:T(8,128)S(1)}, u32[]{:S(2)}, u32[]{:S(2)}) collective-permute-start(f32[136,128]{1,0:T(8,128)S(1)} %shard_map.120.after.sent), channel_id=1, source_target_pairs={{0,48},{1,49},{2,50},{3,51},{4,52},{5,53},{6,54},{7,55},{8,56},{9,... | collective-permute-start | bytes 208904 | tf_op jit(solution)/shard_map/ppermute | solution.py:416
  75.6 6.5 %collective-permute-start.23 = (f32[128,128]{1,0:T(8,128)S(1)}, f32[128,128]{1,0:T(8,128)S(1)}, u32[]{:S(2)}, u32[]{:S(2)}) collective-permute-start(f32[128,128]{1,0:T(8,128)S(1)} %get-tuple-element.92), channel_id=1, source_target_pairs={{0,2},{1,3},{2,0},{3,1},{4,6},{5,7},{6,4},{7,5},{8,10},{9,11},{10,... | collective-permute-start | bytes 196616 | tf_op jit(solution)/shard_map/ppermute | solution.py:416
  76.6 5.5 %collective-permute-start.24 = (f32[128,128]{1,0:T(8,128)S(1)}, f32[128,128]{1,0:T(8,128)S(1)}, u32[]{:S(2)}, u32[]{:S(2)}) collective-permute-start(f32[128,128]{1,0:T(8,128)S(1)} %get-tuple-element.93), channel_id=1, source_target_pairs={{0,4},{1,5},{2,6},{3,7},{4,0},{5,1},{6,2},{7,3},{8,12},{9,13},{10,... | collective-permute-start | bytes 196616 | tf_op jit(solution)/shard_map/ppermute | solution.py:416
  78.1 4.3 %collective-permute-start.25 = (f32[128,128]{1,0:T(8,128)S(1)}, f32[128,128]{1,0:T(8,128)S(1)}, u32[]{:S(2)}, u32[]{:S(2)}) collective-permute-start(f32[128,128]{1,0:T(8,128)S(1)} %get-tuple-element.94), channel_id=1, source_target_pairs={{0,6},{1,7},{2,4},{3,5},{4,2},{5,3},{6,0},{7,1},{8,14},{9,15},{10,... | collective-permute-start | bytes 196616 | tf_op jit(solution)/shard_map/ppermute | solution.py:416
  82.1 0.7 copy-start.3
  82.9 6.3 %collective-permute-start.26 = (f32[512,128]{1,0:T(8,128)S(1)}, f32[512,128]{1,0:T(8,128)S(1)}, u32[]{:S(2)}, u32[]{:S(2)}) collective-permute-start(f32[512,128]{1,0:T(8,128)S(1)} %get-tuple-element.104.refs_8_), channel_id=1, source_target_pairs={{0,1},{1,0},{2,3},{3,2},{4,5},{5,4},{6,7},{7,6},{8,9},{9,8},{10,11... | collective-permute-start | bytes 786440 | tf_op jit(solution)/shard_map/ppermute | solution.py:416

commit v6 on v5

--- a/solution.py
+++ b/solution.py
@@ -24,14 +24,14 @@
     return jnp.where(row < 8.0, slow, fast)
 
 
-def starts_before(bounds, place):
-    return sum((bounds[i] < place).astype(jnp.int32) for i in range(3))
-
-
-def carry(rate, bounds, left, right):
-    same = (starts_before(bounds, left) == starts_before(bounds, right)) & (left <= right)
-    span = jnp.maximum(right - left, 0).astype(F32)
-    return jnp.exp(rate * span) * jnp.where(same, 1.0, 0.0).astype(F32)
+def starts_before(edges, place):
+    return sum(jnp.where(edge < place, 1.0, 0.0) for edge in edges)
+
+
+def carry(rate, edges, left, right):
+    left, right = left.astype(F32), right.astype(F32)
+    same = (starts_before(edges, left) == starts_before(edges, right)) & (left <= right)
+    return jnp.where(same, jnp.exp(rate * jnp.maximum(right - left, 0.0)), 0.0)
 
 
 def place():
@@ -60,10 +60,10 @@
     return rows
 
 
-RATES, ENTER, LEAVE, FORWARD, BACKWARD = 0, 8, 9, 16, 0
+RATES, ENTER, LEAVE, EDGES = 0, 8, 9, 10
 CHIP_OWN, CHIP_OTHER, ROW, HALF, FAR, NEAR, INTO, ACROSS, CORE = 0, 4, 8, 12, 16, 16, 20, 24, 40
 CHAIN_ROWS = 48
-FAR_Z = 6
+FAR_Z = 7
 SLOT = (0, 2, 1, 3)
 
 
@@ -83,20 +83,21 @@
     return jnp.where(token_rows() >= table[LEAVE : LEAVE + 1, :], powers(rate_row(table, head), 0.0, False), 0.0)
 
 
-def fill_chain(table, base, decay, bounds, reverse):
+def fill_chain(out, table, reverse):
     at, z, y, c = place()
     one = jnp.ones((1, HEAD), F32)
+    edges = [table[EDGES + i : EDGES + i + 1, :] for i in range(3)]
     middle = (at - c + 1) * TOK
-    row, row_end, centre = z * BLOCK_Z, (z + 1) * BLOCK_Z, 4 * BLOCK_Z
+    row, row_end, centre = z * BLOCK_Z, (z + 1) * BLOCK_Z, jnp.int32(4 * BLOCK_Z)
 
     def put(index, value):
-        table[base + index : base + index + 1, :] = value
+        out[index : index + 1, :] = value
 
     def across(rate, earlier, later):
-        return carry(rate, bounds, earlier, later)
+        return carry(rate, edges, earlier, later)
 
     for k in range(4):
-        rate = rate_of(decay[4 * c + (y ^ k)])
+        rate = rate_row(table, 4 * c + (y ^ k))
         first, second = across(rate, middle - TOK, middle), across(rate, middle, middle + TOK)
         if reverse:
             put(CHIP_OWN + k, jnp.where(c == 1, first, one))
@@ -106,7 +107,7 @@
             put(CHIP_OWN + k, jnp.where(c == 0, second, one))
             put(CHIP_OTHER + k, jnp.where(c == 0, one, second))
             put(CORE + k, first)
-    rate = rate_of(decay[4 * c + y])
+    rate = rate_row(table, 4 * c + y)
     for k in range(4):
         here, line = row + (y ^ k) * BLOCK_Y, (z ^ k) * BLOCK_Z
         if reverse:
@@ -128,9 +129,9 @@
                     put(ACROSS + 4 * k + m, across(rate, there + BLOCK_Y, here))
 
 
-def masks_kernel(decay, bounds, gain, after, mask, flipped, table, gain_out):
+def masks_kernel(bounds, table, gain, after, mask, flipped, chain, gain_out):
     gain_out[...] = gain[...]
-    fill_chain(table, BACKWARD, decay, bounds, True)
+    fill_chain(chain, table, True)
     first = place()[0] * TOK
     for lo in range(0, TOK, HEAD):
         row = lax.broadcasted_iota(jnp.int32, (HEAD, TOK), 0) + lo
@@ -210,7 +211,8 @@
     entering, leaving = tokens_in(bounds, at)
     table[ENTER : ENTER + 1, :] = jnp.full((1, HEAD), entering.astype(F32), F32)
     table[LEAVE : LEAVE + 1, :] = jnp.full((1, HEAD), leaving.astype(F32), F32)
-    fill_chain(table, FORWARD, decay, bounds, False)
+    for i in range(3):
+        table[EDGES + i : EDGES + i + 1, :] = jnp.full((1, HEAD), bounds[i].astype(F32), F32)
     for i, head in enumerate(heads):
         weights = leave_decay(table, head)
         copies[2 * i].wait()
@@ -221,7 +223,8 @@
         copy.wait()
 
 
-def kept_states_kernel(table, k, v, after, out):
+def kept_states_kernel(table, k, v, after, out, chain):
+    fill_chain(chain, table, False)
     y = place()[2]
     for i in range(4):
         head = first_head(True) + (y ^ i)
@@ -252,7 +255,7 @@
             outs[SLOT[k]][HEAD : HEAD + 8, :] = send[tail, :] + got[tail, :]
 
 
-def sum_kernel(table, p0, p1, p2, p3, after, out, *, base, reverse, gains):
+def sum_kernel(table, p0, p1, p2, p3, after, out, *tails, base, reverse, gains):
     total = 0.0
     for k, p in enumerate((p0, p1, p2, p3)):
         total += table[base + k : base + k + 1, :] * p[0:HEAD, :]
@@ -260,9 +263,11 @@
     if gains:
         tail = slice(HEAD, HEAD + 8)
         out[tail, :] = p0[tail, :] + p1[tail, :] + p2[tail, :] + p3[tail, :]
-
-
-def chips_in_kernel(table, r1, r2, r3, far, sent, t0, t1, t2, t3, after, *outs, base, reverse, gains):
+        for copy in tails:
+            copy[...] = out[tail, :]
+
+
+def chips_in_kernel(table, r1, r2, r3, far, t0, t1, t2, t3, after, *outs, base, reverse):
     total = table[base + FAR : base + FAR + 1, :] * far[0:HEAD, :]
     for k, r in enumerate((r1, r2, r3)):
         at = base + NEAR + 1 + k
@@ -275,13 +280,11 @@
                 at = base + ACROSS + 4 * k + m
                 state += table[at : at + 1, :] * t[0:HEAD, :]
         outs[SLOT[k]][...] = state
-    if gains:
-        tail = slice(HEAD, HEAD + 8)
-        outs[4][...] = sent[tail, :] + far[tail, :]
-
-
-def gains_kernel(totals, out):
+
+
+def gains_kernel(own, far, back, after, out, totals):
     _, z, y, c = place()
+    totals[...] = own[...] + far[HEAD : HEAD + 8, :] + back[...]
     turned = pltpu.roll(totals[pl.ds(z, 1), :], (HEAD - 32 * y - 16 * c) % HEAD, axis=1)
     out[...] = turned[0, 0:16]
 
@@ -416,11 +419,22 @@
     return lax.ppermute(array, "seq", pairs)
 
 
-def carried(send, make_keep, table, base, reverse, gains, work):
+def one_way(array, dz, up):
+    pairs = [
+        (index(z, y, c), index(z ^ dz, y, c))
+        for z in range(8)
+        for y in range(4)
+        for c in range(2)
+        if ((z ^ dz) > z) == up
+    ]
+    return lax.ppermute(array, "seq", pairs)
+
+
+def carried(send, make_keep, reverse, gains, work):
     extra = 8 if gains else 0
     small = shape(HEAD + extra, HEAD)
 
-    def step(kernel, outs, *args, after, base=base, **more):
+    def step(kernel, outs, *args, after, base=0, **more):
         return call(
             functools.partial(kernel, reverse=reverse, base=base, **more),
             outs,
@@ -434,21 +448,30 @@
         return [arrays[0]] + [moved[k] for k in (1, 2, 3)]
 
     got = exchange(send, dc=1)
-    keep = make_keep(send)
+    keep, table = make_keep(send)
     chips = step(chip_kernel, [small] * 4, keep, got, send, gains=gains, after=[keep])
     done = work[0](chips[0])
     chips = around([chips[n] for n in SLOT], (2, 1, 3), dy=1)
-    row = step(sum_kernel, small, *chips, gains=gains, after=[done], base=base + ROW)
+    row = step(sum_kernel, [small], *chips, gains=gains, after=[done], base=ROW)[0]
     done = work[1](row)
     rows = around([row] * 4, (1, 2, 3), dz=1)
-    sent = step(sum_kernel, small, *rows, gains=gains, after=[done], base=base + HALF)
-    done = work[2](sent)
-    far = exchange(sent, dz=FAR_Z)
-    outs = [shape(HEAD, HEAD)] * 4 + ([shape(8, HEAD)] if gains else [])
-    outs = step(chips_in_kernel, outs, *rows[1:], far, sent, *chips, gains=gains, after=[done])
+    outs = [small] + ([shape(8, HEAD)] if gains else [])
+    sent = step(sum_kernel, outs, *rows, gains=gains, after=[done], base=HALF)
+    done = work[2](sent[0])
+    far = [one_way(sent[0], FAR_Z, not reverse)] + [one_way(tail, FAR_Z, reverse) for tail in sent[1:]]
+    outs = [shape(HEAD, HEAD)] * 4
+    outs = step(chips_in_kernel, outs, *rows[1:], far[0], *chips, after=[done])
     done = work[3](outs[0])
     states = around([outs[n] for n in SLOT], (2, 1, 3), dy=1)
-    total = call(gains_kernel, shape(16), in_specs=[VMEM], out_specs=VMEM)(outs[4]) if gains else None
+    total = None
+    if gains:
+        total = call(
+            gains_kernel,
+            shape(16),
+            in_specs=[VMEM] * 3 + [ANY],
+            out_specs=VMEM,
+            scratch=[pltpu.VMEM((8, HEAD), F32)],
+        )(sent[1], *far, done)
     mine, other = step(cores_in_kernel, [shape(4 * HEAD, HEAD)] * 2, *states, keep, got, after=[done] + [total] * gains)
     return mine, other, total
 
@@ -474,7 +497,7 @@
     wide = shape(TOK, width, dtype=BF16)
     send, table, keys, values = call(
         sent_states_kernel,
-        [state_shape, shape(FORWARD + CHAIN_ROWS, HEAD), wide, wide],
+        [state_shape, shape(16, HEAD), wide, wide],
         in_specs=[ANY] * 4,
         out_specs=[VMEM] * 4,
         scratch=[pltpu.SMEM((HEADS_DEV,), jnp.int32), pltpu.SMEM((3,), jnp.int32), pltpu.SemaphoreType.DMA((3, 4))],
@@ -483,7 +506,8 @@
     )(*[pltpu.with_memory_space_constraint(x, pltpu.HBM) for x in (decay, bounds, keys, values)])
 
     def keep_states(after):
-        return local(kept_states_kernel, state_shape, [keys, values], [after], small_mm, 3 << 19)
+        outs = [state_shape, shape(CHAIN_ROWS, HEAD)]
+        return local(kept_states_kernel, outs, [keys, values], [after], small_mm, 3 << 19)
 
     made = {}
     pairs = shape(TOK, TOK, dtype=BF16)
@@ -495,10 +519,10 @@
                 made["masks"] = call(
                     masks_kernel,
                     outs,
-                    in_specs=[SMEM, SMEM, VMEM, ANY],
+                    in_specs=[SMEM, VMEM, VMEM, ANY],
                     out_specs=[VMEM] * 4,
                     moved=1 << 20,
-                )(*[pltpu.with_memory_space_constraint(x, pltpu.HBM) for x in (decay, bounds)], gain, after)
+                )(pltpu.with_memory_space_constraint(bounds, pltpu.HBM), table, gain, after)
             made[own] = local(
                 intra_kernel,
                 shape(TOK, half),
@@ -516,7 +540,7 @@
         return after
 
     mine, other, _ = carried(
-        send, keep_states, table, FORWARD, False, False, [make_intra(True), make_intra(False), same, same]
+        send, keep_states, False, False, [make_intra(True), make_intra(False), same, same]
     )
     theirs = exchange(other, dc=1)
     mask, flipped, back_table, gain = made["masks"]
@@ -551,7 +575,7 @@
         made["d"], keep = local(
             mixed_kernel, outs, [*totals, o_mine, out_grad, queries, gain], [after], small_mm, 3 << 20, own=True
         )
-        return keep
+        return keep, back_table
 
 
     def make_grads(n):
@@ -572,7 +596,7 @@
         return run
 
     last_mine, last_other, gains = carried(
-        send, keep_grads, back_table, BACKWARD, True, True, [make_grads(n) for n in range(4)]
+        send, keep_grads, True, True, [make_grads(n) for n in range(4)]
     )
     last_theirs = exchange(last_other, dc=1)
     dq, dk, dv = zip(*[made["grads", n] for n in range(4)])

time: 91 us -> 95.5 us (1.049)
  starting transfers between devices: 48.8 us -> 51.5 us
  waiting for transfers between devices: 18.1 us -> 19.4 us
    ppermute x0 -> x3, starting transfers between devices: none -> 10.2 us  [one_way(): return lax.ppermute(array, 'seq', pairs)]
    ppermute x24 -> x22, starting transfers between devices: 45.5 us -> 37.9 us  [exchange(): return lax.ppermute(array, 'seq', pairs)]
    ppermute x0 -> x3, waiting for transfers between devices: none -> 4.66 us  [one_way(): return lax.ppermute(array, 'seq', pairs)]
    ppermute x24 -> x22, waiting for transfers between devices: 14.8 us -> 11.5 us  [exchange(): return lax.ppermute(array, 'seq', pairs)]
  transfers between devices with their start and end apart: 27 -> 28, of which waited for: 15 -> 13; matrix products, arithmetic and copies ran while one was open for 0% -> 0% of each run, Pallas kernels for 18% -> 17%
where the time goes in v6:
time: 95.5 us; the launch traced here: 95.3 us
  starting transfers between devices  51.5 us (54%)
  Pallas kernels  22.6 us (24%)
  waiting for transfers between devices  19.4 us (20%)
  between operations  1.08 us (1%)
    ppermute x22, starting transfers between devices, exchange(): return lax.ppermute(array, 'seq', pairs)  37.9 us
    pallas_call x11, Pallas kernels, local(): call(functools.partial(kernel, **more), outs, in_specs=[VMEM] * (1 + len(...  15.1 us
    ppermute x22, waiting for transfers between devices, exchange(): return lax.ppermute(array, 'seq', pairs)  11.5 us
    ppermute x3, starting transfers between devices, one_way(): return lax.ppermute(array, 'seq', pairs)  10.2 us
    ppermute x3, waiting for transfers between devices, one_way(): return lax.ppermute(array, 'seq', pairs)  4.66 us
    ppermute x3, starting transfers between devices, shards(): lax.ppermute(sums, 'dp', [(i, i ^ k) for i in range(4)])  3.34 us
    ppermute x3, waiting for transfers between devices, shards(): lax.ppermute(sums, 'dp', [(i, i ^ k) for i in range(4)])  3.32 us
    pallas_call x1, Pallas kernels, shards(): call(sent_states_kernel, [state_shape, shape(16, HEAD), wide, wide], in_s...  2.25 us
  transfers between devices with their start and end apart: 28, of which 13 were waited for; matrix products, arithmetic and copies ran while one was open for 0% of the time, Pallas kernels for 17%

profile of v6, /device:TPU:1, one launch (start us, length us, event | category | flops | bytes accessed | tf_op | source)
XLA Modules:
  0.0 95.3 jit_solution(14107993803035641414)
XLA Ops:
  0.6 2.2 %shard_map.102 = (f32[512,128]{1,0:T(8,128)S(1)}, f32[16,128]{1,0:T(8,128)S(1)}, bf16[512,1024]{1,0:T(8,128)(2,1)S(1)}, bf16[512,1024]{1,0:T(8,128)(2,1)S(1)}) custom-call(s32[8]{0:T(128)} %decay_in.1, s32[3]{0:T(128)} %bounds.1, bf16[512,1024]{1,0:T(8,128)(2,1)} %k_in.1, bf16[512,1024]{1,0:T(8,128)(2,1)} %v_in.1), custom_call_target="tpu_custom_call" | custom-call | flops 67108864 | bytes 1572864 | tf_op jit(solution)/shard_map/pallas_call | solution.py:498
  2.9 3.3 %collective-permute-start = (f32[512,128]{1,0:T(8,128)S(1)}, f32[512,128]{1,0:T(8,128)S(1)}, u32[]{:S(2)}, u32[]{:S(2)}) collective-permute-start(f32[512,128]{1,0:T(8,128)S(1)} %get-tuple-element.64.after.send), channel_id=1, source_target_pairs={{0,1},{1,0},{2,3},{3,2},{4,5},{5,4},{6,7},{7,6},{8,9},{9,8},{10,11... | collective-permute-start | bytes 786440 | tf_op jit(solution)/shard_map/ppermute | solution.py:419
  7.5 2.2 %collective-permute-start.2 = (f32[128,128]{1,0:T(8,128)S(1)}, f32[128,128]{1,0:T(8,128)S(1)}, u32[]{:S(2)}, u32[]{:S(2)}) collective-permute-start(f32[128,128]{1,0:T(8,128)S(1)} %get-tuple-element.71), channel_id=1, source_target_pairs={{0,4},{1,5},{2,6},{3,7},{4,0},{5,1},{6,2},{7,3},{8,12},{9,13},{10,... | collective-permute-start | bytes 196616 | tf_op jit(solution)/shard_map/ppermute | solution.py:419
  9.7 1.7 %collective-permute-start.3 = (f32[128,128]{1,0:T(8,128)S(1)}, f32[128,128]{1,0:T(8,128)S(1)}, u32[]{:S(2)}, u32[]{:S(2)}) collective-permute-start(f32[128,128]{1,0:T(8,128)S(1)} %get-tuple-element.72), channel_id=1, source_target_pairs={{0,6},{1,7},{2,4},{3,5},{4,2},{5,3},{6,0},{7,1},{8,14},{9,15},{10,... | collective-permute-start | bytes 196616 | tf_op jit(solution)/shard_map/ppermute | solution.py:419
  12.5 1.5 %shard_map.106.after.intra = f32[512,512]{1,0:T(8,128)S(1)} custom-call(f32[16,128]{1,0:T(8,128)S(1)} %get-tuple-element.61.table, bf16[512,1024]{1,0:T(8,128)(2,1)S(1)} %copy-done, bf16[512,1024]{1,0:T(8,128)(2,1)S(1)} %get-tuple-element.62.k, bf16[512,1024]{1,0:T(8,128)(2,1)S(1)} %get-tuple-element.63.v, bf16[512,512]{1,0:T(8,128)(2,1)S(1)} %get-tuple-element.69.mask, ...), custom_call_target="tpu_custom_call" | custom-call | flops 402653184 | bytes 3145728 | tf_op jit(solution)/shard_map/pallas_call | solution.py:488
  14.3 4.3 %collective-permute-start.6 = (f32[128,128]{1,0:T(8,128)S(1)}, f32[128,128]{1,0:T(8,128)S(1)}, u32[]{:S(2)}, u32[]{:S(2)}) collective-permute-start(f32[128,128]{1,0:T(8,128)S(1)} %shard_map.107.after.p0), channel_id=1, source_target_pairs={{0,24},{1,25},{2,26},{3,27},{4,28},{5,29},{6,30},{7,31},{8,16},{9,... | collective-permute-start | bytes 196616 | tf_op jit(solution)/shard_map/ppermute | solution.py:419
  19.0 1.5 %shard_map.108.after.intra = f32[512,512]{1,0:T(8,128)S(1)} custom-call(f32[16,128]{1,0:T(8,128)S(1)} %get-tuple-element.61.table, bf16[512,1024]{1,0:T(8,128)(2,1)S(1)} %copy-done, bf16[512,1024]{1,0:T(8,128)(2,1)S(1)} %get-tuple-element.62.k, bf16[512,1024]{1,0:T(8,128)(2,1)S(1)} %get-tuple-element.63.v, bf16[512,512]{1,0:T(8,128)(2,1)S(1)} %get-tuple-element.69.mask, ...), custom_call_target="tpu_custom_call" | custom-call | flops 402653184 | bytes 3145728 | tf_op jit(solution)/shard_map/pallas_call | solution.py:488
  20.5 2.8 %collective-permute-done.5.p2.r2 = f32[128,128]{1,0:T(8,128)S(1)} collective-permute-done((f32[128,128]{1,0:T(8,128)S(1)}, f32[128,128]{1,0:T(8,128)S(1)}, u32[]{:S(2)}, u32[]{:S(2)}) %collective-permute-start.5) | collective-permute-done | bytes 65568 | tf_op jit(solution)/shard_map/ppermute | solution.py:419
  23.3 7.0 %collective-permute-start.7 = (f32[128,128]{1,0:T(8,128)S(1)}, f32[128,128]{1,0:T(8,128)S(1)}, u32[]{:S(2)}, u32[]{:S(2)}) collective-permute-start(f32[128,128]{1,0:T(8,128)S(1)} %shard_map.109.after), channel_id=1, source_target_pairs={{0,56},{1,57},{2,58},{3,59},{4,60},{5,61},{6,62},{7,63},{8,48},{9,... | collective-permute-start | bytes 196616 | tf_op jit(solution)/shard_map/ppermute | solution.py:430
  30.3 1.4 %collective-permute-done.7.far = f32[128,128]{1,0:T(8,128)S(1)} collective-permute-done((f32[128,128]{1,0:T(8,128)S(1)}, f32[128,128]{1,0:T(8,128)S(1)}, u32[]{:S(2)}, u32[]{:S(2)}) %collective-permute-start.7) | collective-permute-done | bytes 65568 | tf_op jit(solution)/shard_map/ppermute | solution.py:430
  32.2 2.6 %collective-permute-start.9 = (f32[128,128]{1,0:T(8,128)S(1)}, f32[128,128]{1,0:T(8,128)S(1)}, u32[]{:S(2)}, u32[]{:S(2)}) collective-permute-start(f32[128,128]{1,0:T(8,128)S(1)} %get-tuple-element.76), channel_id=1, source_target_pairs={{0,4},{1,5},{2,6},{3,7},{4,0},{5,1},{6,2},{7,3},{8,12},{9,13},{10,... | collective-permute-start | bytes 196616 | tf_op jit(solution)/shard_map/ppermute | solution.py:419
  35.7 1.3 %collective-permute-done.9.v2 = f32[128,128]{1,0:T(8,128)S(1)} collective-permute-done((f32[128,128]{1,0:T(8,128)S(1)}, f32[128,128]{1,0:T(8,128)S(1)}, u32[]{:S(2)}, u32[]{:S(2)}) %collective-permute-start.9) | collective-permute-done | bytes 65568 | tf_op jit(solution)/shard_map/ppermute | solution.py:419
  37.1 2.0 %collective-permute-done.10.v3 = f32[128,128]{1,0:T(8,128)S(1)} collective-permute-done((f32[128,128]{1,0:T(8,128)S(1)}, f32[128,128]{1,0:T(8,128)S(1)}, u32[]{:S(2)}, u32[]{:S(2)}) %collective-permute-start.10) | collective-permute-done | bytes 65568 | tf_op jit(solution)/shard_map/ppermute | solution.py:419
  39.1 4.5 %collective-permute-start.11 = (f32[512,128]{1,0:T(8,128)S(1)}, f32[512,128]{1,0:T(8,128)S(1)}, u32[]{:S(2)}, u32[]{:S(2)}) collective-permute-start(f32[512,128]{1,0:T(8,128)S(1)} %get-tuple-element.78.refs_0_), channel_id=1, source_target_pairs={{0,1},{1,0},{2,3},{3,2},{4,5},{5,4},{6,7},{7,6},{8,9},{9,8},{10,11... | collective-permute-start | bytes 786440 | tf_op jit(solution)/shard_map/ppermute | solution.py:419
  45.6 2.6 %collective-permute-start.14 = (f32[8,512]{1,0:T(8,128)S(1)}, f32[8,512]{1,0:T(8,128)S(1)}, u32[]{:S(2)}, u32[]{:S(2)}) collective-permute-start(f32[8,512]{1,0:T(8,128)S(1)} %get-tuple-element.81.s0), channel_id=1, source_target_pairs={{0,192},{64,128},{128,64},{192,0},{1,193},{65,129},{129,65},{193,1... | collective-permute-start | bytes 49160 | tf_op jit(solution)/shard_map/ppermute | solution.py:561
  49.5 2.8 %collective-permute-done.13.s2 = f32[8,512]{1,0:T(8,128)S(1)} collective-permute-done((f32[8,512]{1,0:T(8,128)S(1)}, f32[8,512]{1,0:T(8,128)S(1)}, u32[]{:S(2)}, u32[]{:S(2)}) %collective-permute-start.13) | collective-permute-done | bytes 16416 | tf_op jit(solution)/shard_map/ppermute | solution.py:561
  53.4 1.9 %collective-permute-start.15 = (f32[520,128]{1,0:T(8,128)S(1)}, f32[520,128]{1,0:T(8,128)S(1)}, u32[]{:S(2)}, u32[]{:S(2)}) collective-permute-start(f32[520,128]{1,0:T(8,128)S(1)} %get-tuple-element.84.refs_0_.send), channel_id=1, source_target_pairs={{0,1},{1,0},{2,3},{3,2},{4,5},{5,4},{6,7},{7,6},{8,9},{9,8},{10,11... | collective-permute-start | bytes 798728 | tf_op jit(solution)/shard_map/ppermute | solution.py:419
  56.6 1.9 %collective-permute-start.17 = (f32[136,128]{1,0:T(8,128)S(1)}, f32[136,128]{1,0:T(8,128)S(1)}, u32[]{:S(2)}, u32[]{:S(2)}) collective-permute-start(f32[136,128]{1,0:T(8,128)S(1)} %get-tuple-element.88), channel_id=1, source_target_pairs={{0,4},{1,5},{2,6},{3,7},{4,0},{5,1},{6,2},{7,3},{8,12},{9,13},{10,... | collective-permute-start | bytes 208904 | tf_op jit(solution)/shard_map/ppermute | solution.py:419
  58.5 1.9 %collective-permute-start.18 = (f32[136,128]{1,0:T(8,128)S(1)}, f32[136,128]{1,0:T(8,128)S(1)}, u32[]{:S(2)}, u32[]{:S(2)}) collective-permute-start(f32[136,128]{1,0:T(8,128)S(1)} %get-tuple-element.89), channel_id=1, source_target_pairs={{0,6},{1,7},{2,4},{3,5},{4,2},{5,3},{6,0},{7,1},{8,14},{9,15},{10,... | collective-permute-start | bytes 208904 | tf_op jit(solution)/shard_map/ppermute | solution.py:419
  60.5 2.0 %shard_map.117 = (bf16[512,256]{1,0:T(8,128)(2,1)S(1)}, f32[512,256]{1,0:T(8,128)S(1)}, f32[512,256]{1,0:T(8,128)S(1)}) custom-call(f32[16,128]{1,0:T(8,128)S(1)} %get-tuple-element.61.table, bf16[512,1024]{1,0:T(8,128)(2,1)S(1)} %copy-done, bf16[512,1024]{1,0:T(8,128)(2,1)S(1)} %get-tuple-element.62.k, bf16[512,1024]{1,0:T(8,128)(2,1)S(1)} %get-tuple-element.63.v, ...), custom_call_target="tpu_custom_call" | custom-call | flops 603979776 | bytes 2097152 | tf_op jit(solution)/shard_map/pallas_call | solution.py:488
  63.3 1.7 %collective-permute-start.21 = (f32[136,128]{1,0:T(8,128)S(1)}, f32[136,128]{1,0:T(8,128)S(1)}, u32[]{:S(2)}, u32[]{:S(2)}) collective-permute-start(f32[136,128]{1,0:T(8,128)S(1)} %shard_map.118.after.p0), channel_id=1, source_target_pairs={{0,24},{1,25},{2,26},{3,27},{4,28},{5,29},{6,30},{7,31},{8,16},{9,... | collective-permute-start | bytes 208904 | tf_op jit(solution)/shard_map/ppermute | solution.py:419
  66.9 2.0 %shard_map.119 = (bf16[512,256]{1,0:T(8,128)(2,1)S(1)}, f32[512,256]{1,0:T(8,128)S(1)}, f32[512,256]{1,0:T(8,128)S(1)}) custom-call(f32[16,128]{1,0:T(8,128)S(1)} %get-tuple-element.61.table, bf16[512,1024]{1,0:T(8,128)(2,1)S(1)} %copy-done, bf16[512,1024]{1,0:T(8,128)(2,1)S(1)} %get-tuple-element.62.k, bf16[512,1024]{1,0:T(8,128)(2,1)S(1)} %get-tuple-element.63.v, ...), custom_call_target="tpu_custom_call" | custom-call | flops 603979776 | bytes 2097152 | tf_op jit(solution)/shard_map/pallas_call | solution.py:488
  68.9 3.0 %collective-permute-done.20.p2.r2 = f32[136,128]{1,0:T(8,128)S(1)} collective-permute-done((f32[136,128]{1,0:T(8,128)S(1)}, f32[136,128]{1,0:T(8,128)S(1)}, u32[]{:S(2)}, u32[]{:S(2)}) %collective-permute-start.20) | collective-permute-done | bytes 69664 | tf_op jit(solution)/shard_map/ppermute | solution.py:419
  72.0 1.3 %collective-permute-start.22 = (f32[136,128]{1,0:T(8,128)S(1)}, f32[136,128]{1,0:T(8,128)S(1)}, u32[]{:S(2)}, u32[]{:S(2)}) collective-permute-start(f32[136,128]{1,0:T(8,128)S(1)} %get-tuple-element.94.after), channel_id=1, source_target_pairs={{32,24},{33,25},{34,26},{35,27},{36,28},{37,29},{38,30},{39,31},{4... | collective-permute-start | bytes 208904 | tf_op jit(solution)/shard_map/ppermute | solution.py:430
  73.3 2.0 %shard_map.121 = (bf16[512,256]{1,0:T(8,128)(2,1)S(1)}, f32[512,256]{1,0:T(8,128)S(1)}, f32[512,256]{1,0:T(8,128)S(1)}) custom-call(f32[16,128]{1,0:T(8,128)S(1)} %get-tuple-element.61.table, bf16[512,1024]{1,0:T(8,128)(2,1)S(1)} %copy-done, bf16[512,1024]{1,0:T(8,128)(2,1)S(1)} %get-tuple-element.62.k, bf16[512,1024]{1,0:T(8,128)(2,1)S(1)} %get-tuple-element.63.v, ...), custom_call_target="tpu_custom_call" | custom-call | flops 603979776 | bytes 2097152 | tf_op jit(solution)/shard_map/pallas_call | solution.py:488
  75.3 3.3 %collective-permute-done.22.far = f32[136,128]{1,0:T(8,128)S(1)} collective-permute-done((f32[136,128]{1,0:T(8,128)S(1)}, f32[136,128]{1,0:T(8,128)S(1)}, u32[]{:S(2)}, u32[]{:S(2)}) %collective-permute-start.22) | collective-permute-done | bytes 69664 | tf_op jit(solution)/shard_map/ppermute | solution.py:430
  79.4 2.6 %collective-permute-start.24 = (f32[128,128]{1,0:T(8,128)S(1)}, f32[128,128]{1,0:T(8,128)S(1)}, u32[]{:S(2)}, u32[]{:S(2)}) collective-permute-start(f32[128,128]{1,0:T(8,128)S(1)} %get-tuple-element.99), channel_id=1, source_target_pairs={{0,4},{1,5},{2,6},{3,7},{4,0},{5,1},{6,2},{7,3},{8,12},{9,13},{10,... | collective-permute-start | bytes 196616 | tf_op jit(solution)/shard_map/ppermute | solution.py:419
  82.6 1.9 %collective-permute-start.26 = (f32[8,128]{1,0:T(8,128)S(1)}, f32[8,128]{1,0:T(8,128)S(1)}, u32[]{:S(2)}, u32[]{:S(2)}) collective-permute-start(f32[8,128]{1,0:T(8,128)S(1)} %get-tuple-element.102.own), channel_id=1, source_target_pairs={{0,56},{1,57},{2,58},{3,59},{4,60},{5,61},{6,62},{7,63},{8,48},{9,... | collective-permute-start | bytes 12296 | tf_op jit(solution)/shard_map/ppermute | solution.py:430
  84.5 1.9 %shard_map.123 = (bf16[512,256]{1,0:T(8,128)(2,1)S(1)}, f32[512,256]{1,0:T(8,128)S(1)}, f32[512,256]{1,0:T(8,128)S(1)}) custom-call(f32[16,128]{1,0:T(8,128)S(1)} %get-tuple-element.61.table, bf16[512,1024]{1,0:T(8,128)(2,1)S(1)} %copy-done, bf16[512,1024]{1,0:T(8,128)(2,1)S(1)} %get-tuple-element.62.k, bf16[512,1024]{1,0:T(8,128)(2,1)S(1)} %get-tuple-element.63.v, ...), custom_call_target="tpu_custom_call" | custom-call | flops 603979776 | bytes 2097152 | tf_op jit(solution)/shard_map/pallas_call | solution.py:488
  87.8 4.1 %collective-permute-start.27 = (f32[512,128]{1,0:T(8,128)S(1)}, f32[512,128]{1,0:T(8,128)S(1)}, u32[]{:S(2)}, u32[]{:S(2)}) collective-permute-start(f32[512,128]{1,0:T(8,128)S(1)} %get-tuple-element.110.refs_8_), channel_id=1, source_target_pairs={{0,1},{1,0},{2,3},{3,2},{4,5},{5,4},{6,7},{7,6},{8,9},{9,8},{10,11... | collective-permute-start | bytes 786440 | tf_op jit(solution)/shard_map/ppermute | solution.py:419
  92.0 1.6 %shard_map.126 = (bf16[512,1024]{1,0:T(8,128)(2,1)}, bf16[512,1024]{1,0:T(8,128)(2,1)}, bf16[512,1024]{1,0:T(8,128)(2,1)}) custom-call(f32[16,128]{1,0:T(8,128)S(1)} %get-tuple-element.61.table, bf16[512,1024]{1,0:T(8,128)(2,1)S(1)} %get-tuple-element.62.k, bf16[512,1024]{1,0:T(8,128)(2,1)S(1)} %get-tuple-element.63.v, ...), custom_call_target="tpu_custom_call" | custom-call | flops 134217728 | bytes 6291456 | tf_op jit(solution)/shard_map/pallas_call | solution.py:605
  93.6 1.5 %shard_map.127 = (bf16[512,1024]{1,0:T(8,128)(2,1)}, bf16[512,1024]{1,0:T(8,128)(2,1)}) custom-call(f32[16,128]{1,0:T(8,128)S(1)} %get-tuple-element.61.table, bf16[512,1024]{1,0:T(8,128)(2,1)S(1)} %get-tuple-element.62.k, bf16[512,1024]{1,0:T(8,128)(2,1)S(1)} %get-tuple-element.63.v, ...), custom_call_target="tpu_custom_call", output_to_operand_aliasing={{0}: (8, {}), {1}: (9, {})} | custom-call | flops 134217728 | bytes 4194304 | tf_op jit(solution)/shard_map/pallas_call | solution.py:614
  (58 shorter events, 15.9 us)
Async XLA Ops:
  2.9 4.5 %collective-permute-start = (f32[512,128]{1,0:T(8,128)S(1)}, f32[512,128]{1,0:T(8,128)S(1)}, u32[]{:S(2)}, u32[]{:S(2)}) collective-permute-start(f32[512,128]{1,0:T(8,128)S(1)} %get-tuple-element.64.after.send), channel_id=1, source_target_pairs={{0,1},{1,0},{2,3},{3,2},{4,5},{5,4},{6,7},{7,6},{8,9},{9,8},{10,11... | collective-permute-start | bytes 786440 | tf_op jit(solution)/shard_map/ppermute | solution.py:419
  6.9 5.6 %copy-start = (bf16[512,1024]{1,0:T(8,128)(2,1)S(1)}, bf16[512,1024]{1,0:T(8,128)(2,1)}, u32[]{:S(2)}) copy-start(bf16[512,1024]{1,0:T(8,128)(2,1)} %q.19) | copy-start | bytes 3145732
  7.4 4.0 %copy-start.2 = (f32[1024]{0:T(1024)S(1)}, f32[1024]{0:T(1024)}, u32[]{:S(2)}) copy-start(f32[1024]{0:T(1024)} %param.11) | copy-start | bytes 12292
  7.4 6.5 %collective-permute-start.1 = (f32[128,128]{1,0:T(8,128)S(1)}, f32[128,128]{1,0:T(8,128)S(1)}, u32[]{:S(2)}, u32[]{:S(2)}) collective-permute-start(f32[128,128]{1,0:T(8,128)S(1)} %get-tuple-element.70), channel_id=1, source_target_pairs={{0,2},{1,3},{2,0},{3,1},{4,6},{5,7},{6,4},{7,5},{8,10},{9,11},{10,... | collective-permute-start | bytes 196616 | tf_op jit(solution)/shard_map/ppermute | solution.py:419
  7.5 6.4 %collective-permute-start.2 = (f32[128,128]{1,0:T(8,128)S(1)}, f32[128,128]{1,0:T(8,128)S(1)}, u32[]{:S(2)}, u32[]{:S(2)}) collective-permute-start(f32[128,128]{1,0:T(8,128)S(1)} %get-tuple-element.71), channel_id=1, source_target_pairs={{0,4},{1,5},{2,6},{3,7},{4,0},{5,1},{6,2},{7,3},{8,12},{9,13},{10,... | collective-permute-start | bytes 196616 | tf_op jit(solution)/shard_map/ppermute | solution.py:419
  9.7 4.6 %collective-permute-start.3 = (f32[128,128]{1,0:T(8,128)S(1)}, f32[128,128]{1,0:T(8,128)S(1)}, u32[]{:S(2)}, u32[]{:S(2)}) collective-permute-start(f32[128,128]{1,0:T(8,128)S(1)} %get-tuple-element.72), channel_id=1, source_target_pairs={{0,6},{1,7},{2,4},{3,5},{4,2},{5,3},{6,0},{7,1},{8,14},{9,15},{10,... | collective-permute-start | bytes 196616 | tf_op jit(solution)/shard_map/ppermute | solution.py:419
  14.3 6.2 %collective-permute-start.6 = (f32[128,128]{1,0:T(8,128)S(1)}, f32[128,128]{1,0:T(8,128)S(1)}, u32[]{:S(2)}, u32[]{:S(2)}) collective-permute-start(f32[128,128]{1,0:T(8,128)S(1)} %shard_map.107.after.p0), channel_id=1, source_target_pairs={{0,24},{1,25},{2,26},{3,27},{4,28},{5,29},{6,30},{7,31},{8,16},{9,... | collective-permute-start | bytes 196616 | tf_op jit(solution)/shard_map/ppermute | solution.py:419
  18.6 4.6 %collective-permute-start.5 = (f32[128,128]{1,0:T(8,128)S(1)}, f32[128,128]{1,0:T(8,128)S(1)}, u32[]{:S(2)}, u32[]{:S(2)}) collective-permute-start(f32[128,128]{1,0:T(8,128)S(1)} %shard_map.107.after.p0), channel_id=1, source_target_pairs={{0,16},{1,17},{2,18},{3,19},{4,20},{5,21},{6,22},{7,23},{8,24},{9,... | collective-permute-start | bytes 196616 | tf_op jit(solution)/shard_map/ppermute | solution.py:419
  18.6 4.6 %collective-permute-start.4 = (f32[128,128]{1,0:T(8,128)S(1)}, f32[128,128]{1,0:T(8,128)S(1)}, u32[]{:S(2)}, u32[]{:S(2)}) collective-permute-start(f32[128,128]{1,0:T(8,128)S(1)} %shard_map.107.after.p0), channel_id=1, source_target_pairs={{0,8},{1,9},{2,10},{3,11},{4,12},{5,13},{6,14},{7,15},{8,0},{9,1},... | collective-permute-start | bytes 196616 | tf_op jit(solution)/shard_map/ppermute | solution.py:419
  23.3 20.3 %copy-start.1 = (bf16[512,1024]{1,0:T(8,128)(2,1)S(1)}, bf16[512,1024]{1,0:T(8,128)(2,1)}, u32[]{:S(2)}) copy-start(bf16[512,1024]{1,0:T(8,128)(2,1)} %grad.7) | copy-start | bytes 3145732
  23.3 8.4 %collective-permute-start.7 = (f32[128,128]{1,0:T(8,128)S(1)}, f32[128,128]{1,0:T(8,128)S(1)}, u32[]{:S(2)}, u32[]{:S(2)}) collective-permute-start(f32[128,128]{1,0:T(8,128)S(1)} %shard_map.109.after), channel_id=1, source_target_pairs={{0,56},{1,57},{2,58},{3,59},{4,60},{5,61},{6,62},{7,63},{8,48},{9,... | collective-permute-start | bytes 196616 | tf_op jit(solution)/shard_map/ppermute | solution.py:430
  31.8 3.9 %collective-permute-start.8 = (f32[128,128]{1,0:T(8,128)S(1)}, f32[128,128]{1,0:T(8,128)S(1)}, u32[]{:S(2)}, u32[]{:S(2)}) collective-permute-start(f32[128,128]{1,0:T(8,128)S(1)} %get-tuple-element.75), channel_id=1, source_target_pairs={{0,2},{1,3},{2,0},{3,1},{4,6},{5,7},{6,4},{7,5},{8,10},{9,11},{10,... | collective-permute-start | bytes 196616 | tf_op jit(solution)/shard_map/ppermute | solution.py:419
  32.2 4.9 %collective-permute-start.9 = (f32[128,128]{1,0:T(8,128)S(1)}, f32[128,128]{1,0:T(8,128)S(1)}, u32[]{:S(2)}, u32[]{:S(2)}) collective-permute-start(f32[128,128]{1,0:T(8,128)S(1)} %get-tuple-element.76), channel_id=1, source_target_pairs={{0,4},{1,5},{2,6},{3,7},{4,0},{5,1},{6,2},{7,3},{8,12},{9,13},{10,... | collective-permute-start | bytes 196616 | tf_op jit(solution)/shard_map/ppermute | solution.py:419
  34.7 4.3 %collective-permute-start.10 = (f32[128,128]{1,0:T(8,128)S(1)}, f32[128,128]{1,0:T(8,128)S(1)}, u32[]{:S(2)}, u32[]{:S(2)}) collective-permute-start(f32[128,128]{1,0:T(8,128)S(1)} %get-tuple-element.77), channel_id=1, source_target_pairs={{0,6},{1,7},{2,4},{3,5},{4,2},{5,3},{6,0},{7,1},{8,14},{9,15},{10,... | collective-permute-start | bytes 196616 | tf_op jit(solution)/shard_map/ppermute | solution.py:419
  39.1 5.6 %collective-permute-start.11 = (f32[512,128]{1,0:T(8,128)S(1)}, f32[512,128]{1,0:T(8,128)S(1)}, u32[]{:S(2)}, u32[]{:S(2)}) collective-permute-start(f32[512,128]{1,0:T(8,128)S(1)} %get-tuple-element.78.refs_0_), channel_id=1, source_target_pairs={{0,1},{1,0},{2,3},{3,2},{4,5},{5,4},{6,7},{7,6},{8,9},{9,8},{10,11... | collective-permute-start | bytes 786440 | tf_op jit(solution)/shard_map/ppermute | solution.py:419
  45.6 3.9 %collective-permute-start.14 = (f32[8,512]{1,0:T(8,128)S(1)}, f32[8,512]{1,0:T(8,128)S(1)}, u32[]{:S(2)}, u32[]{:S(2)}) collective-permute-start(f32[8,512]{1,0:T(8,128)S(1)} %get-tuple-element.81.s0), channel_id=1, source_target_pairs={{0,192},{64,128},{128,64},{192,0},{1,193},{65,129},{129,65},{193,1... | collective-permute-start | bytes 49160 | tf_op jit(solution)/shard_map/ppermute | solution.py:561
  48.1 4.1 %collective-permute-start.13 = (f32[8,512]{1,0:T(8,128)S(1)}, f32[8,512]{1,0:T(8,128)S(1)}, u32[]{:S(2)}, u32[]{:S(2)}) collective-permute-start(f32[8,512]{1,0:T(8,128)S(1)} %get-tuple-element.81.s0), channel_id=1, source_target_pairs={{0,128},{64,192},{128,0},{192,64},{1,129},{65,193},{129,1},{193,65... | collective-permute-start | bytes 49160 | tf_op jit(solution)/shard_map/ppermute | solution.py:561
  48.7 3.6 %collective-permute-start.12 = (f32[8,512]{1,0:T(8,128)S(1)}, f32[8,512]{1,0:T(8,128)S(1)}, u32[]{:S(2)}, u32[]{:S(2)}) collective-permute-start(f32[8,512]{1,0:T(8,128)S(1)} %get-tuple-element.81.s0), channel_id=1, source_target_pairs={{0,64},{64,0},{128,192},{192,128},{1,65},{65,1},{129,193},{193,129... | collective-permute-start | bytes 49160 | tf_op jit(solution)/shard_map/ppermute | solution.py:561
  53.4 3.1 %collective-permute-start.15 = (f32[520,128]{1,0:T(8,128)S(1)}, f32[520,128]{1,0:T(8,128)S(1)}, u32[]{:S(2)}, u32[]{:S(2)}) collective-permute-start(f32[520,128]{1,0:T(8,128)S(1)} %get-tuple-element.84.refs_0_.send), channel_id=1, source_target_pairs={{0,1},{1,0},{2,3},{3,2},{4,5},{5,4},{6,7},{7,6},{8,9},{9,8},{10,11... | collective-permute-start | bytes 798728 | tf_op jit(solution)/shard_map/ppermute | solution.py:419
  56.5 5.9 %collective-permute-start.16 = (f32[136,128]{1,0:T(8,128)S(1)}, f32[136,128]{1,0:T(8,128)S(1)}, u32[]{:S(2)}, u32[]{:S(2)}) collective-permute-start(f32[136,128]{1,0:T(8,128)S(1)} %get-tuple-element.87), channel_id=1, source_target_pairs={{0,2},{1,3},{2,0},{3,1},{4,6},{5,7},{6,4},{7,5},{8,10},{9,11},{10,... | collective-permute-start | bytes 208904 | tf_op jit(solution)/shard_map/ppermute | solution.py:419
  56.6 5.9 %collective-permute-start.17 = (f32[136,128]{1,0:T(8,128)S(1)}, f32[136,128]{1,0:T(8,128)S(1)}, u32[]{:S(2)}, u32[]{:S(2)}) collective-permute-start(f32[136,128]{1,0:T(8,128)S(1)} %get-tuple-element.88), channel_id=1, source_target_pairs={{0,4},{1,5},{2,6},{3,7},{4,0},{5,1},{6,2},{7,3},{8,12},{9,13},{10,... | collective-permute-start | bytes 208904 | tf_op jit(solution)/shard_map/ppermute | solution.py:419
  58.5 4.8 %collective-permute-start.18 = (f32[136,128]{1,0:T(8,128)S(1)}, f32[136,128]{1,0:T(8,128)S(1)}, u32[]{:S(2)}, u32[]{:S(2)}) collective-permute-start(f32[136,128]{1,0:T(8,128)S(1)} %get-tuple-element.89), channel_id=1, source_target_pairs={{0,6},{1,7},{2,4},{3,5},{4,2},{5,3},{6,0},{7,1},{8,14},{9,15},{10,... | collective-permute-start | bytes 208904 | tf_op jit(solution)/shard_map/ppermute | solution.py:419
  63.3 5.6 %collective-permute-start.21 = (f32[136,128]{1,0:T(8,128)S(1)}, f32[136,128]{1,0:T(8,128)S(1)}, u32[]{:S(2)}, u32[]{:S(2)}) collective-permute-start(f32[136,128]{1,0:T(8,128)S(1)} %shard_map.118.after.p0), channel_id=1, source_target_pairs={{0,24},{1,25},{2,26},{3,27},{4,28},{5,29},{6,30},{7,31},{8,16},{9,... | collective-permute-start | bytes 208904 | tf_op jit(solution)/shard_map/ppermute | solution.py:419
  65.0 7.0 %collective-permute-start.20 = (f32[136,128]{1,0:T(8,128)S(1)}, f32[136,128]{1,0:T(8,128)S(1)}, u32[]{:S(2)}, u32[]{:S(2)}) collective-permute-start(f32[136,128]{1,0:T(8,128)S(1)} %shard_map.118.after.p0), channel_id=1, source_target_pairs={{0,16},{1,17},{2,18},{3,19},{4,20},{5,21},{6,22},{7,23},{8,24},{9,... | collective-permute-start | bytes 208904 | tf_op jit(solution)/shard_map/ppermute | solution.py:419
  65.9 6.1 %collective-permute-start.19 = (f32[136,128]{1,0:T(8,128)S(1)}, f32[136,128]{1,0:T(8,128)S(1)}, u32[]{:S(2)}, u32[]{:S(2)}) collective-permute-start(f32[136,128]{1,0:T(8,128)S(1)} %shard_map.118.after.p0), channel_id=1, source_target_pairs={{0,8},{1,9},{2,10},{3,11},{4,12},{5,13},{6,14},{7,15},{8,0},{9,1},... | collective-permute-start | bytes 208904 | tf_op jit(solution)/shard_map/ppermute | solution.py:419
  72.0 6.6 %collective-permute-start.22 = (f32[136,128]{1,0:T(8,128)S(1)}, f32[136,128]{1,0:T(8,128)S(1)}, u32[]{:S(2)}, u32[]{:S(2)}) collective-permute-start(f32[136,128]{1,0:T(8,128)S(1)} %get-tuple-element.94.after), channel_id=1, source_target_pairs={{32,24},{33,25},{34,26},{35,27},{36,28},{37,29},{38,30},{39,31},{4... | collective-permute-start | bytes 208904 | tf_op jit(solution)/shard_map/ppermute | solution.py:430
  78.7 8.4 %collective-permute-start.23 = (f32[128,128]{1,0:T(8,128)S(1)}, f32[128,128]{1,0:T(8,128)S(1)}, u32[]{:S(2)}, u32[]{:S(2)}) collective-permute-start(f32[128,128]{1,0:T(8,128)S(1)} %get-tuple-element.98), channel_id=1, source_target_pairs={{0,2},{1,3},{2,0},{3,1},{4,6},{5,7},{6,4},{7,5},{8,10},{9,11},{10,... | collective-permute-start | bytes 196616 | tf_op jit(solution)/shard_map/ppermute | solution.py:419
  79.4 7.7 %collective-permute-start.24 = (f32[128,128]{1,0:T(8,128)S(1)}, f32[128,128]{1,0:T(8,128)S(1)}, u32[]{:S(2)}, u32[]{:S(2)}) collective-permute-start(f32[128,128]{1,0:T(8,128)S(1)} %get-tuple-element.99), channel_id=1, source_target_pairs={{0,4},{1,5},{2,6},{3,7},{4,0},{5,1},{6,2},{7,3},{8,12},{9,13},{10,... | collective-permute-start | bytes 196616 | tf_op jit(solution)/shard_map/ppermute | solution.py:419
  82.0 5.1 %collective-permute-start.25 = (f32[128,128]{1,0:T(8,128)S(1)}, f32[128,128]{1,0:T(8,128)S(1)}, u32[]{:S(2)}, u32[]{:S(2)}) collective-permute-start(f32[128,128]{1,0:T(8,128)S(1)} %get-tuple-element.100), channel_id=1, source_target_pairs={{0,6},{1,7},{2,4},{3,5},{4,2},{5,3},{6,0},{7,1},{8,14},{9,15},{10,... | collective-permute-start | bytes 196616 | tf_op jit(solution)/shard_map/ppermute | solution.py:419
  82.6 3.9 %collective-permute-start.26 = (f32[8,128]{1,0:T(8,128)S(1)}, f32[8,128]{1,0:T(8,128)S(1)}, u32[]{:S(2)}, u32[]{:S(2)}) collective-permute-start(f32[8,128]{1,0:T(8,128)S(1)} %get-tuple-element.102.own), channel_id=1, source_target_pairs={{0,56},{1,57},{2,58},{3,59},{4,60},{5,61},{6,62},{7,63},{8,48},{9,... | collective-permute-start | bytes 12296 | tf_op jit(solution)/shard_map/ppermute | solution.py:430
  87.1 0.7 copy-start.3
  87.8 5.7 %collective-permute-start.27 = (f32[512,128]{1,0:T(8,128)S(1)}, f32[512,128]{1,0:T(8,128)S(1)}, u32[]{:S(2)}, u32[]{:S(2)}) collective-permute-start(f32[512,128]{1,0:T(8,128)S(1)} %get-tuple-element.110.refs_8_), channel_id=1, source_target_pairs={{0,1},{1,0},{2,3},{3,2},{4,5},{5,4},{6,7},{7,6},{8,9},{9,8},{10,11... | collective-permute-start | bytes 786440 | tf_op jit(solution)/shard_map/ppermute | solution.py:419

commit v7 on v5

--- a/solution.py
+++ b/solution.py
@@ -197,11 +197,8 @@
         return copy
 
     numbers = [start(decay_in, decay, sems.at[2, 0]), start(bounds_in, bounds, sems.at[2, 1])]
-    copies = []
-    for i, head in enumerate(heads):
-        spot = columns(head)
-        copies.append(start(k_in.at[:, spot], k.at[:, spot], sems.at[0, i]))
-        copies.append(start(v_in.at[:, spot], v.at[:, spot], sems.at[1, i]))
+    sent = pl.ds(pl.multiple_of(first_head(False) * HEAD, 4 * HEAD), 4 * HEAD)
+    copies = [start(k_in.at[:, sent], k.at[:, sent], sems.at[0, 0]), start(v_in.at[:, sent], v.at[:, sent], sems.at[1, 0])]
     halves = [start(k_in.at[:, rest], k.at[:, rest], sems.at[2, 2]), start(v_in.at[:, rest], v.at[:, rest], sems.at[2, 3])]
     for copy in numbers:
         copy.wait()
@@ -211,10 +208,10 @@
     table[ENTER : ENTER + 1, :] = jnp.full((1, HEAD), entering.astype(F32), F32)
     table[LEAVE : LEAVE + 1, :] = jnp.full((1, HEAD), leaving.astype(F32), F32)
     fill_chain(table, FORWARD, decay, bounds, False)
+    for copy in copies:
+        copy.wait()
     for i, head in enumerate(heads):
         weights = leave_decay(table, head)
-        copies[2 * i].wait()
-        copies[2 * i + 1].wait()
         decayed = (weights * k[:, columns(head)].astype(F32)).astype(BF16)
         out[i * HEAD : (i + 1) * HEAD, :] = mm_at(decayed, v[:, columns(head)])
     for copy in halves:

time: 91 us -> 90.7 us (level)
  no operation moved by 1% of the time
where the time goes in v7:
time: 90.7 us; the launch traced here: 90.6 us
  starting transfers between devices  48.8 us (54%)
  Pallas kernels  22.3 us (25%)
  waiting for transfers between devices  18.1 us (20%)
  between operations  1.06 us (1%)
    ppermute x24, starting transfers between devices, exchange(): return lax.ppermute(array, 'seq', pairs)  45.5 us
    pallas_call x11, Pallas kernels, local(): call(functools.partial(kernel, **more), outs, in_specs=[VMEM] * (1 + len(...  15 us
    ppermute x24, waiting for transfers between devices, exchange(): return lax.ppermute(array, 'seq', pairs)  14.8 us
    ppermute x3, starting transfers between devices, shards(): lax.ppermute(sums, 'dp', [(i, i ^ k) for i in range(4)])  3.34 us
    ppermute x3, waiting for transfers between devices, shards(): lax.ppermute(sums, 'dp', [(i, i ^ k) for i in range(4)])  3.33 us
    pallas_call x1, Pallas kernels, shards(): call(sent_states_kernel, [state_shape, shape(FORWARD + CHAIN_ROWS, HEAD),...  1.93 us
  transfers between devices with their start and end apart: 27, of which 15 were waited for; matrix products, arithmetic and copies ran while one was open for 0% of the time, Pallas kernels for 18%

profile of v7, /device:TPU:1, one launch (start us, length us, event | category | flops | bytes accessed | tf_op | source)
XLA Modules:
  0.0 90.6 jit_solution(5821714829877668816)
XLA Ops:
  0.6 1.9 %shard_map.102 = (f32[512,128]{1,0:T(8,128)S(1)}, f32[64,128]{1,0:T(8,128)S(1)}, bf16[512,1024]{1,0:T(8,128)(2,1)S(1)}, bf16[512,1024]{1,0:T(8,128)(2,1)S(1)}) custom-call(s32[8]{0:T(128)} %decay.1, s32[3]{0:T(128)} %bounds.1, bf16[512,1024]{1,0:T(8,128)(2,1)} %k_in.1, bf16[512,1024]{1,0:T(8,128)(2,1)} %v_in.1), custom_call_target="tpu_custom_call" | custom-call | flops 67108864 | bytes 1572864 | tf_op jit(solution)/shard_map/pallas_call | solution.py:472
  2.6 3.3 %collective-permute-start = (f32[512,128]{1,0:T(8,128)S(1)}, f32[512,128]{1,0:T(8,128)S(1)}, u32[]{:S(2)}, u32[]{:S(2)}) collective-permute-start(f32[512,128]{1,0:T(8,128)S(1)} %get-tuple-element.61.after.send), channel_id=1, source_target_pairs={{0,1},{1,0},{2,3},{3,2},{4,5},{5,4},{6,7},{7,6},{8,9},{9,8},{10,11... | collective-permute-start | bytes 786440 | tf_op jit(solution)/shard_map/ppermute | solution.py:413
  7.2 2.2 %collective-permute-start.2 = (f32[128,128]{1,0:T(8,128)S(1)}, f32[128,128]{1,0:T(8,128)S(1)}, u32[]{:S(2)}, u32[]{:S(2)}) collective-permute-start(f32[128,128]{1,0:T(8,128)S(1)} %get-tuple-element.66), channel_id=1, source_target_pairs={{0,4},{1,5},{2,6},{3,7},{4,0},{5,1},{6,2},{7,3},{8,12},{9,13},{10,... | collective-permute-start | bytes 196616 | tf_op jit(solution)/shard_map/ppermute | solution.py:413
  9.4 1.7 %collective-permute-start.3 = (f32[128,128]{1,0:T(8,128)S(1)}, f32[128,128]{1,0:T(8,128)S(1)}, u32[]{:S(2)}, u32[]{:S(2)}) collective-permute-start(f32[128,128]{1,0:T(8,128)S(1)} %get-tuple-element.67), channel_id=1, source_target_pairs={{0,6},{1,7},{2,4},{3,5},{4,2},{5,3},{6,0},{7,1},{8,14},{9,15},{10,... | collective-permute-start | bytes 196616 | tf_op jit(solution)/shard_map/ppermute | solution.py:413
  12.2 1.5 %shard_map.106.after.intra = f32[512,512]{1,0:T(8,128)S(1)} custom-call(f32[64,128]{1,0:T(8,128)S(1)} %get-tuple-element.58.table, bf16[512,1024]{1,0:T(8,128)(2,1)S(1)} %copy-done, bf16[512,1024]{1,0:T(8,128)(2,1)S(1)} %get-tuple-element.59.k, bf16[512,1024]{1,0:T(8,128)(2,1)S(1)} %get-tuple-element.60.v, bf16[512,512]{1,0:T(8,128)(2,1)S(1)} %get-tuple-element.64.mask, ...), custom_call_target="tpu_custom_call" | custom-call | flops 402653184 | bytes 3145728 | tf_op jit(solution)/shard_map/pallas_call | solution.py:462
  14.0 4.3 %collective-permute-start.6 = (f32[128,128]{1,0:T(8,128)S(1)}, f32[128,128]{1,0:T(8,128)S(1)}, u32[]{:S(2)}, u32[]{:S(2)}) collective-permute-start(f32[128,128]{1,0:T(8,128)S(1)} %shard_map.107.after.p0), channel_id=1, source_target_pairs={{0,24},{1,25},{2,26},{3,27},{4,28},{5,29},{6,30},{7,31},{8,16},{9,... | collective-permute-start | bytes 196616 | tf_op jit(solution)/shard_map/ppermute | solution.py:413
  18.7 1.5 %shard_map.108.after.intra = f32[512,512]{1,0:T(8,128)S(1)} custom-call(f32[64,128]{1,0:T(8,128)S(1)} %get-tuple-element.58.table, bf16[512,1024]{1,0:T(8,128)(2,1)S(1)} %copy-done, bf16[512,1024]{1,0:T(8,128)(2,1)S(1)} %get-tuple-element.59.k, bf16[512,1024]{1,0:T(8,128)(2,1)S(1)} %get-tuple-element.60.v, bf16[512,512]{1,0:T(8,128)(2,1)S(1)} %get-tuple-element.64.mask, ...), custom_call_target="tpu_custom_call" | custom-call | flops 402653184 | bytes 3145728 | tf_op jit(solution)/shard_map/pallas_call | solution.py:462
  20.2 2.8 %collective-permute-done.5.p2.r2 = f32[128,128]{1,0:T(8,128)S(1)} collective-permute-done((f32[128,128]{1,0:T(8,128)S(1)}, f32[128,128]{1,0:T(8,128)S(1)}, u32[]{:S(2)}, u32[]{:S(2)}) %collective-permute-start.5) | collective-permute-done | bytes 65568 | tf_op jit(solution)/shard_map/ppermute | solution.py:413
  23.0 3.6 %collective-permute-start.7 = (f32[128,128]{1,0:T(8,128)S(1)}, f32[128,128]{1,0:T(8,128)S(1)}, u32[]{:S(2)}, u32[]{:S(2)}) collective-permute-start(f32[128,128]{1,0:T(8,128)S(1)} %shard_map.109.sent.after), channel_id=1, source_target_pairs={{0,48},{1,49},{2,50},{3,51},{4,52},{5,53},{6,54},{7,55},{8,56},{9,... | collective-permute-start | bytes 196616 | tf_op jit(solution)/shard_map/ppermute | solution.py:413
  26.6 2.4 %collective-permute-done.7.far = f32[128,128]{1,0:T(8,128)S(1)} collective-permute-done((f32[128,128]{1,0:T(8,128)S(1)}, f32[128,128]{1,0:T(8,128)S(1)}, u32[]{:S(2)}, u32[]{:S(2)}) %collective-permute-start.7) | collective-permute-done | bytes 65568 | tf_op jit(solution)/shard_map/ppermute | solution.py:413
  29.2 2.6 %collective-permute-start.9 = (f32[128,128]{1,0:T(8,128)S(1)}, f32[128,128]{1,0:T(8,128)S(1)}, u32[]{:S(2)}, u32[]{:S(2)}) collective-permute-start(f32[128,128]{1,0:T(8,128)S(1)} %get-tuple-element.71), channel_id=1, source_target_pairs={{0,4},{1,5},{2,6},{3,7},{4,0},{5,1},{6,2},{7,3},{8,12},{9,13},{10,... | collective-permute-start | bytes 196616 | tf_op jit(solution)/shard_map/ppermute | solution.py:413
  31.8 1.3 %collective-permute-start.10 = (f32[128,128]{1,0:T(8,128)S(1)}, f32[128,128]{1,0:T(8,128)S(1)}, u32[]{:S(2)}, u32[]{:S(2)}) collective-permute-start(f32[128,128]{1,0:T(8,128)S(1)} %get-tuple-element.72), channel_id=1, source_target_pairs={{0,6},{1,7},{2,4},{3,5},{4,2},{5,3},{6,0},{7,1},{8,14},{9,15},{10,... | collective-permute-start | bytes 196616 | tf_op jit(solution)/shard_map/ppermute | solution.py:413
  34.1 2.0 %collective-permute-done.10.v3 = f32[128,128]{1,0:T(8,128)S(1)} collective-permute-done((f32[128,128]{1,0:T(8,128)S(1)}, f32[128,128]{1,0:T(8,128)S(1)}, u32[]{:S(2)}, u32[]{:S(2)}) %collective-permute-start.10) | collective-permute-done | bytes 65568 | tf_op jit(solution)/shard_map/ppermute | solution.py:413
  36.2 4.5 %collective-permute-start.11 = (f32[512,128]{1,0:T(8,128)S(1)}, f32[512,128]{1,0:T(8,128)S(1)}, u32[]{:S(2)}, u32[]{:S(2)}) collective-permute-start(f32[512,128]{1,0:T(8,128)S(1)} %get-tuple-element.73.refs_0_), channel_id=1, source_target_pairs={{0,1},{1,0},{2,3},{3,2},{4,5},{5,4},{6,7},{7,6},{8,9},{9,8},{10,11... | collective-permute-start | bytes 786440 | tf_op jit(solution)/shard_map/ppermute | solution.py:413
  42.6 2.6 %collective-permute-start.14 = (f32[8,512]{1,0:T(8,128)S(1)}, f32[8,512]{1,0:T(8,128)S(1)}, u32[]{:S(2)}, u32[]{:S(2)}) collective-permute-start(f32[8,512]{1,0:T(8,128)S(1)} %get-tuple-element.76.s0), channel_id=1, source_target_pairs={{0,192},{64,128},{128,64},{192,0},{1,193},{65,129},{129,65},{193,1... | collective-permute-start | bytes 49160 | tf_op jit(solution)/shard_map/ppermute | solution.py:534
  46.5 2.8 %collective-permute-done.13.s2 = f32[8,512]{1,0:T(8,128)S(1)} collective-permute-done((f32[8,512]{1,0:T(8,128)S(1)}, f32[8,512]{1,0:T(8,128)S(1)}, u32[]{:S(2)}, u32[]{:S(2)}) %collective-permute-start.13) | collective-permute-done | bytes 16416 | tf_op jit(solution)/shard_map/ppermute | solution.py:534
  50.5 1.9 %collective-permute-start.15 = (f32[520,128]{1,0:T(8,128)S(1)}, f32[520,128]{1,0:T(8,128)S(1)}, u32[]{:S(2)}, u32[]{:S(2)}) collective-permute-start(f32[520,128]{1,0:T(8,128)S(1)} %get-tuple-element.79.refs_0_.send), channel_id=1, source_target_pairs={{0,1},{1,0},{2,3},{3,2},{4,5},{5,4},{6,7},{7,6},{8,9},{9,8},{10,11... | collective-permute-start | bytes 798728 | tf_op jit(solution)/shard_map/ppermute | solution.py:413
  53.7 3.2 %collective-permute-start.17 = (f32[136,128]{1,0:T(8,128)S(1)}, f32[136,128]{1,0:T(8,128)S(1)}, u32[]{:S(2)}, u32[]{:S(2)}) collective-permute-start(f32[136,128]{1,0:T(8,128)S(1)} %get-tuple-element.83), channel_id=1, source_target_pairs={{0,4},{1,5},{2,6},{3,7},{4,0},{5,1},{6,2},{7,3},{8,12},{9,13},{10,... | collective-permute-start | bytes 208904 | tf_op jit(solution)/shard_map/ppermute | solution.py:413
  57.5 2.0 %shard_map.117 = (bf16[512,256]{1,0:T(8,128)(2,1)S(1)}, f32[512,256]{1,0:T(8,128)S(1)}, f32[512,256]{1,0:T(8,128)S(1)}) custom-call(f32[64,128]{1,0:T(8,128)S(1)} %get-tuple-element.58.table, bf16[512,1024]{1,0:T(8,128)(2,1)S(1)} %copy-done, bf16[512,1024]{1,0:T(8,128)(2,1)S(1)} %get-tuple-element.59.k, bf16[512,1024]{1,0:T(8,128)(2,1)S(1)} %get-tuple-element.60.v, ...), custom_call_target="tpu_custom_call" | custom-call | flops 603979776 | bytes 2097152 | tf_op jit(solution)/shard_map/pallas_call | solution.py:462
  60.0 1.6 %collective-permute-done.18.p3.t3 = f32[136,128]{1,0:T(8,128)S(1)} collective-permute-done((f32[136,128]{1,0:T(8,128)S(1)}, f32[136,128]{1,0:T(8,128)S(1)}, u32[]{:S(2)}, u32[]{:S(2)}) %collective-permute-start.18) | collective-permute-done | bytes 69664 | tf_op jit(solution)/shard_map/ppermute | solution.py:413
  61.6 1.8 %collective-permute-start.21 = (f32[136,128]{1,0:T(8,128)S(1)}, f32[136,128]{1,0:T(8,128)S(1)}, u32[]{:S(2)}, u32[]{:S(2)}) collective-permute-start(f32[136,128]{1,0:T(8,128)S(1)} %shard_map.118.after.p0), channel_id=1, source_target_pairs={{0,24},{1,25},{2,26},{3,27},{4,28},{5,29},{6,30},{7,31},{8,16},{9,... | collective-permute-start | bytes 208904 | tf_op jit(solution)/shard_map/ppermute | solution.py:413
  63.3 1.2 %collective-permute-start.20 = (f32[136,128]{1,0:T(8,128)S(1)}, f32[136,128]{1,0:T(8,128)S(1)}, u32[]{:S(2)}, u32[]{:S(2)}) collective-permute-start(f32[136,128]{1,0:T(8,128)S(1)} %shard_map.118.after.p0), channel_id=1, source_target_pairs={{0,16},{1,17},{2,18},{3,19},{4,20},{5,21},{6,22},{7,23},{8,24},{9,... | collective-permute-start | bytes 208904 | tf_op jit(solution)/shard_map/ppermute | solution.py:413
  65.2 1.9 %shard_map.119 = (bf16[512,256]{1,0:T(8,128)(2,1)S(1)}, f32[512,256]{1,0:T(8,128)S(1)}, f32[512,256]{1,0:T(8,128)S(1)}) custom-call(f32[64,128]{1,0:T(8,128)S(1)} %get-tuple-element.58.table, bf16[512,1024]{1,0:T(8,128)(2,1)S(1)} %copy-done, bf16[512,1024]{1,0:T(8,128)(2,1)S(1)} %get-tuple-element.59.k, bf16[512,1024]{1,0:T(8,128)(2,1)S(1)} %get-tuple-element.60.v, ...), custom_call_target="tpu_custom_call" | custom-call | flops 603979776 | bytes 2097152 | tf_op jit(solution)/shard_map/pallas_call | solution.py:462
  67.2 2.4 %collective-permute-done.20.p2.r2 = f32[136,128]{1,0:T(8,128)S(1)} collective-permute-done((f32[136,128]{1,0:T(8,128)S(1)}, f32[136,128]{1,0:T(8,128)S(1)}, u32[]{:S(2)}, u32[]{:S(2)}) %collective-permute-start.20) | collective-permute-done | bytes 69664 | tf_op jit(solution)/shard_map/ppermute | solution.py:413
  69.7 3.3 %collective-permute-start.22 = (f32[136,128]{1,0:T(8,128)S(1)}, f32[136,128]{1,0:T(8,128)S(1)}, u32[]{:S(2)}, u32[]{:S(2)}) collective-permute-start(f32[136,128]{1,0:T(8,128)S(1)} %shard_map.120.after.sent), channel_id=1, source_target_pairs={{0,48},{1,49},{2,50},{3,51},{4,52},{5,53},{6,54},{7,55},{8,56},{9,... | collective-permute-start | bytes 208904 | tf_op jit(solution)/shard_map/ppermute | solution.py:413
  73.0 2.0 %shard_map.121 = (bf16[512,256]{1,0:T(8,128)(2,1)S(1)}, f32[512,256]{1,0:T(8,128)S(1)}, f32[512,256]{1,0:T(8,128)S(1)}) custom-call(f32[64,128]{1,0:T(8,128)S(1)} %get-tuple-element.58.table, bf16[512,1024]{1,0:T(8,128)(2,1)S(1)} %copy-done, bf16[512,1024]{1,0:T(8,128)(2,1)S(1)} %get-tuple-element.59.k, bf16[512,1024]{1,0:T(8,128)(2,1)S(1)} %get-tuple-element.60.v, ...), custom_call_target="tpu_custom_call" | custom-call | flops 603979776 | bytes 2097152 | tf_op jit(solution)/shard_map/pallas_call | solution.py:462
  75.3 1.3 %collective-permute-start.23 = (f32[128,128]{1,0:T(8,128)S(1)}, f32[128,128]{1,0:T(8,128)S(1)}, u32[]{:S(2)}, u32[]{:S(2)}) collective-permute-start(f32[128,128]{1,0:T(8,128)S(1)} %get-tuple-element.92), channel_id=1, source_target_pairs={{0,2},{1,3},{2,0},{3,1},{4,6},{5,7},{6,4},{7,5},{8,10},{9,11},{10,... | collective-permute-start | bytes 196616 | tf_op jit(solution)/shard_map/ppermute | solution.py:413
  77.8 1.4 %collective-permute-start.25 = (f32[128,128]{1,0:T(8,128)S(1)}, f32[128,128]{1,0:T(8,128)S(1)}, u32[]{:S(2)}, u32[]{:S(2)}) collective-permute-start(f32[128,128]{1,0:T(8,128)S(1)} %get-tuple-element.94), channel_id=1, source_target_pairs={{0,6},{1,7},{2,4},{3,5},{4,2},{5,3},{6,0},{7,1},{8,14},{9,15},{10,... | collective-permute-start | bytes 196616 | tf_op jit(solution)/shard_map/ppermute | solution.py:413
  79.8 2.0 %shard_map.123 = (bf16[512,256]{1,0:T(8,128)(2,1)S(1)}, f32[512,256]{1,0:T(8,128)S(1)}, f32[512,256]{1,0:T(8,128)S(1)}) custom-call(f32[64,128]{1,0:T(8,128)S(1)} %get-tuple-element.58.table, bf16[512,1024]{1,0:T(8,128)(2,1)S(1)} %copy-done, bf16[512,1024]{1,0:T(8,128)(2,1)S(1)} %get-tuple-element.59.k, bf16[512,1024]{1,0:T(8,128)(2,1)S(1)} %get-tuple-element.60.v, ...), custom_call_target="tpu_custom_call" | custom-call | flops 603979776 | bytes 2097152 | tf_op jit(solution)/shard_map/pallas_call | solution.py:462
  82.5 4.7 %collective-permute-start.26 = (f32[512,128]{1,0:T(8,128)S(1)}, f32[512,128]{1,0:T(8,128)S(1)}, u32[]{:S(2)}, u32[]{:S(2)}) collective-permute-start(f32[512,128]{1,0:T(8,128)S(1)} %get-tuple-element.104.refs_8_), channel_id=1, source_target_pairs={{0,1},{1,0},{2,3},{3,2},{4,5},{5,4},{6,7},{7,6},{8,9},{9,8},{10,11... | collective-permute-start | bytes 786440 | tf_op jit(solution)/shard_map/ppermute | solution.py:413
  87.3 1.6 %shard_map.126 = (bf16[512,1024]{1,0:T(8,128)(2,1)}, bf16[512,1024]{1,0:T(8,128)(2,1)}, bf16[512,1024]{1,0:T(8,128)(2,1)}) custom-call(f32[64,128]{1,0:T(8,128)S(1)} %get-tuple-element.58.table, bf16[512,1024]{1,0:T(8,128)(2,1)S(1)} %get-tuple-element.59.k, bf16[512,1024]{1,0:T(8,128)(2,1)S(1)} %get-tuple-element.60.v, ...), custom_call_target="tpu_custom_call" | custom-call | flops 134217728 | bytes 6291456 | tf_op jit(solution)/shard_map/pallas_call | solution.py:578
  88.9 1.5 %shard_map.127 = (bf16[512,1024]{1,0:T(8,128)(2,1)}, bf16[512,1024]{1,0:T(8,128)(2,1)}) custom-call(f32[64,128]{1,0:T(8,128)S(1)} %get-tuple-element.58.table, bf16[512,1024]{1,0:T(8,128)(2,1)S(1)} %get-tuple-element.59.k, bf16[512,1024]{1,0:T(8,128)(2,1)S(1)} %get-tuple-element.60.v, ...), custom_call_target="tpu_custom_call", output_to_operand_aliasing={{0}: (8, {}), {1}: (9, {})} | custom-call | flops 134217728 | bytes 4194304 | tf_op jit(solution)/shard_map/pallas_call | solution.py:587
  (56 shorter events, 14.9 us)
Async XLA Ops:
  2.6 4.5 %collective-permute-start = (f32[512,128]{1,0:T(8,128)S(1)}, f32[512,128]{1,0:T(8,128)S(1)}, u32[]{:S(2)}, u32[]{:S(2)}) collective-permute-start(f32[512,128]{1,0:T(8,128)S(1)} %get-tuple-element.61.after.send), channel_id=1, source_target_pairs={{0,1},{1,0},{2,3},{3,2},{4,5},{5,4},{6,7},{7,6},{8,9},{9,8},{10,11... | collective-permute-start | bytes 786440 | tf_op jit(solution)/shard_map/ppermute | solution.py:413
  6.5 5.7 %copy-start = (bf16[512,1024]{1,0:T(8,128)(2,1)S(1)}, bf16[512,1024]{1,0:T(8,128)(2,1)}, u32[]{:S(2)}) copy-start(bf16[512,1024]{1,0:T(8,128)(2,1)} %q.19) | copy-start | bytes 3145732
  7.1 4.0 %copy-start.2 = (f32[1024]{0:T(1024)S(1)}, f32[1024]{0:T(1024)}, u32[]{:S(2)}) copy-start(f32[1024]{0:T(1024)} %param.11) | copy-start | bytes 12292
  7.1 6.6 %collective-permute-start.1 = (f32[128,128]{1,0:T(8,128)S(1)}, f32[128,128]{1,0:T(8,128)S(1)}, u32[]{:S(2)}, u32[]{:S(2)}) collective-permute-start(f32[128,128]{1,0:T(8,128)S(1)} %get-tuple-element.65), channel_id=1, source_target_pairs={{0,2},{1,3},{2,0},{3,1},{4,6},{5,7},{6,4},{7,5},{8,10},{9,11},{10,... | collective-permute-start | bytes 196616 | tf_op jit(solution)/shard_map/ppermute | solution.py:413
  7.2 6.5 %collective-permute-start.2 = (f32[128,128]{1,0:T(8,128)S(1)}, f32[128,128]{1,0:T(8,128)S(1)}, u32[]{:S(2)}, u32[]{:S(2)}) collective-permute-start(f32[128,128]{1,0:T(8,128)S(1)} %get-tuple-element.66), channel_id=1, source_target_pairs={{0,4},{1,5},{2,6},{3,7},{4,0},{5,1},{6,2},{7,3},{8,12},{9,13},{10,... | collective-permute-start | bytes 196616 | tf_op jit(solution)/shard_map/ppermute | solution.py:413
  9.4 4.6 %collective-permute-start.3 = (f32[128,128]{1,0:T(8,128)S(1)}, f32[128,128]{1,0:T(8,128)S(1)}, u32[]{:S(2)}, u32[]{:S(2)}) collective-permute-start(f32[128,128]{1,0:T(8,128)S(1)} %get-tuple-element.67), channel_id=1, source_target_pairs={{0,6},{1,7},{2,4},{3,5},{4,2},{5,3},{6,0},{7,1},{8,14},{9,15},{10,... | collective-permute-start | bytes 196616 | tf_op jit(solution)/shard_map/ppermute | solution.py:413
  14.0 6.2 %collective-permute-start.6 = (f32[128,128]{1,0:T(8,128)S(1)}, f32[128,128]{1,0:T(8,128)S(1)}, u32[]{:S(2)}, u32[]{:S(2)}) collective-permute-start(f32[128,128]{1,0:T(8,128)S(1)} %shard_map.107.after.p0), channel_id=1, source_target_pairs={{0,24},{1,25},{2,26},{3,27},{4,28},{5,29},{6,30},{7,31},{8,16},{9,... | collective-permute-start | bytes 196616 | tf_op jit(solution)/shard_map/ppermute | solution.py:413
  18.3 4.6 %collective-permute-start.5 = (f32[128,128]{1,0:T(8,128)S(1)}, f32[128,128]{1,0:T(8,128)S(1)}, u32[]{:S(2)}, u32[]{:S(2)}) collective-permute-start(f32[128,128]{1,0:T(8,128)S(1)} %shard_map.107.after.p0), channel_id=1, source_target_pairs={{0,16},{1,17},{2,18},{3,19},{4,20},{5,21},{6,22},{7,23},{8,24},{9,... | collective-permute-start | bytes 196616 | tf_op jit(solution)/shard_map/ppermute | solution.py:413
  18.3 4.6 %collective-permute-start.4 = (f32[128,128]{1,0:T(8,128)S(1)}, f32[128,128]{1,0:T(8,128)S(1)}, u32[]{:S(2)}, u32[]{:S(2)}) collective-permute-start(f32[128,128]{1,0:T(8,128)S(1)} %shard_map.107.after.p0), channel_id=1, source_target_pairs={{0,8},{1,9},{2,10},{3,11},{4,12},{5,13},{6,14},{7,15},{8,0},{9,1},... | collective-permute-start | bytes 196616 | tf_op jit(solution)/shard_map/ppermute | solution.py:413
  23.0 17.7 %copy-start.1 = (bf16[512,1024]{1,0:T(8,128)(2,1)S(1)}, bf16[512,1024]{1,0:T(8,128)(2,1)}, u32[]{:S(2)}) copy-start(bf16[512,1024]{1,0:T(8,128)(2,1)} %grad.7) | copy-start | bytes 3145732
  23.0 6.0 %collective-permute-start.7 = (f32[128,128]{1,0:T(8,128)S(1)}, f32[128,128]{1,0:T(8,128)S(1)}, u32[]{:S(2)}, u32[]{:S(2)}) collective-permute-start(f32[128,128]{1,0:T(8,128)S(1)} %shard_map.109.sent.after), channel_id=1, source_target_pairs={{0,48},{1,49},{2,50},{3,51},{4,52},{5,53},{6,54},{7,55},{8,56},{9,... | collective-permute-start | bytes 196616 | tf_op jit(solution)/shard_map/ppermute | solution.py:413
  29.1 3.9 %collective-permute-start.8 = (f32[128,128]{1,0:T(8,128)S(1)}, f32[128,128]{1,0:T(8,128)S(1)}, u32[]{:S(2)}, u32[]{:S(2)}) collective-permute-start(f32[128,128]{1,0:T(8,128)S(1)} %get-tuple-element.70), channel_id=1, source_target_pairs={{0,2},{1,3},{2,0},{3,1},{4,6},{5,7},{6,4},{7,5},{8,10},{9,11},{10,... | collective-permute-start | bytes 196616 | tf_op jit(solution)/shard_map/ppermute | solution.py:413
  29.2 4.9 %collective-permute-start.9 = (f32[128,128]{1,0:T(8,128)S(1)}, f32[128,128]{1,0:T(8,128)S(1)}, u32[]{:S(2)}, u32[]{:S(2)}) collective-permute-start(f32[128,128]{1,0:T(8,128)S(1)} %get-tuple-element.71), channel_id=1, source_target_pairs={{0,4},{1,5},{2,6},{3,7},{4,0},{5,1},{6,2},{7,3},{8,12},{9,13},{10,... | collective-permute-start | bytes 196616 | tf_op jit(solution)/shard_map/ppermute | solution.py:413
  31.8 4.3 %collective-permute-start.10 = (f32[128,128]{1,0:T(8,128)S(1)}, f32[128,128]{1,0:T(8,128)S(1)}, u32[]{:S(2)}, u32[]{:S(2)}) collective-permute-start(f32[128,128]{1,0:T(8,128)S(1)} %get-tuple-element.72), channel_id=1, source_target_pairs={{0,6},{1,7},{2,4},{3,5},{4,2},{5,3},{6,0},{7,1},{8,14},{9,15},{10,... | collective-permute-start | bytes 196616 | tf_op jit(solution)/shard_map/ppermute | solution.py:413
  36.2 5.7 %collective-permute-start.11 = (f32[512,128]{1,0:T(8,128)S(1)}, f32[512,128]{1,0:T(8,128)S(1)}, u32[]{:S(2)}, u32[]{:S(2)}) collective-permute-start(f32[512,128]{1,0:T(8,128)S(1)} %get-tuple-element.73.refs_0_), channel_id=1, source_target_pairs={{0,1},{1,0},{2,3},{3,2},{4,5},{5,4},{6,7},{7,6},{8,9},{9,8},{10,11... | collective-permute-start | bytes 786440 | tf_op jit(solution)/shard_map/ppermute | solution.py:413
  42.6 3.9 %collective-permute-start.14 = (f32[8,512]{1,0:T(8,128)S(1)}, f32[8,512]{1,0:T(8,128)S(1)}, u32[]{:S(2)}, u32[]{:S(2)}) collective-permute-start(f32[8,512]{1,0:T(8,128)S(1)} %get-tuple-element.76.s0), channel_id=1, source_target_pairs={{0,192},{64,128},{128,64},{192,0},{1,193},{65,129},{129,65},{193,1... | collective-permute-start | bytes 49160 | tf_op jit(solution)/shard_map/ppermute | solution.py:534
  45.2 4.1 %collective-permute-start.13 = (f32[8,512]{1,0:T(8,128)S(1)}, f32[8,512]{1,0:T(8,128)S(1)}, u32[]{:S(2)}, u32[]{:S(2)}) collective-permute-start(f32[8,512]{1,0:T(8,128)S(1)} %get-tuple-element.76.s0), channel_id=1, source_target_pairs={{0,128},{64,192},{128,0},{192,64},{1,129},{65,193},{129,1},{193,65... | collective-permute-start | bytes 49160 | tf_op jit(solution)/shard_map/ppermute | solution.py:534
  45.7 3.6 %collective-permute-start.12 = (f32[8,512]{1,0:T(8,128)S(1)}, f32[8,512]{1,0:T(8,128)S(1)}, u32[]{:S(2)}, u32[]{:S(2)}) collective-permute-start(f32[8,512]{1,0:T(8,128)S(1)} %get-tuple-element.76.s0), channel_id=1, source_target_pairs={{0,64},{64,0},{128,192},{192,128},{1,65},{65,1},{129,193},{193,129... | collective-permute-start | bytes 49160 | tf_op jit(solution)/shard_map/ppermute | solution.py:534
  50.5 3.0 %collective-permute-start.15 = (f32[520,128]{1,0:T(8,128)S(1)}, f32[520,128]{1,0:T(8,128)S(1)}, u32[]{:S(2)}, u32[]{:S(2)}) collective-permute-start(f32[520,128]{1,0:T(8,128)S(1)} %get-tuple-element.79.refs_0_.send), channel_id=1, source_target_pairs={{0,1},{1,0},{2,3},{3,2},{4,5},{5,4},{6,7},{7,6},{8,9},{9,8},{10,11... | collective-permute-start | bytes 798728 | tf_op jit(solution)/shard_map/ppermute | solution.py:413
  53.6 5.9 %collective-permute-start.16 = (f32[136,128]{1,0:T(8,128)S(1)}, f32[136,128]{1,0:T(8,128)S(1)}, u32[]{:S(2)}, u32[]{:S(2)}) collective-permute-start(f32[136,128]{1,0:T(8,128)S(1)} %get-tuple-element.82), channel_id=1, source_target_pairs={{0,2},{1,3},{2,0},{3,1},{4,6},{5,7},{6,4},{7,5},{8,10},{9,11},{10,... | collective-permute-start | bytes 208904 | tf_op jit(solution)/shard_map/ppermute | solution.py:413
  53.7 6.3 %collective-permute-start.17 = (f32[136,128]{1,0:T(8,128)S(1)}, f32[136,128]{1,0:T(8,128)S(1)}, u32[]{:S(2)}, u32[]{:S(2)}) collective-permute-start(f32[136,128]{1,0:T(8,128)S(1)} %get-tuple-element.83), channel_id=1, source_target_pairs={{0,4},{1,5},{2,6},{3,7},{4,0},{5,1},{6,2},{7,3},{8,12},{9,13},{10,... | collective-permute-start | bytes 208904 | tf_op jit(solution)/shard_map/ppermute | solution.py:413
  56.9 4.7 %collective-permute-start.18 = (f32[136,128]{1,0:T(8,128)S(1)}, f32[136,128]{1,0:T(8,128)S(1)}, u32[]{:S(2)}, u32[]{:S(2)}) collective-permute-start(f32[136,128]{1,0:T(8,128)S(1)} %get-tuple-element.84), channel_id=1, source_target_pairs={{0,6},{1,7},{2,4},{3,5},{4,2},{5,3},{6,0},{7,1},{8,14},{9,15},{10,... | collective-permute-start | bytes 208904 | tf_op jit(solution)/shard_map/ppermute | solution.py:413
  61.6 5.6 %collective-permute-start.21 = (f32[136,128]{1,0:T(8,128)S(1)}, f32[136,128]{1,0:T(8,128)S(1)}, u32[]{:S(2)}, u32[]{:S(2)}) collective-permute-start(f32[136,128]{1,0:T(8,128)S(1)} %shard_map.118.after.p0), channel_id=1, source_target_pairs={{0,24},{1,25},{2,26},{3,27},{4,28},{5,29},{6,30},{7,31},{8,16},{9,... | collective-permute-start | bytes 208904 | tf_op jit(solution)/shard_map/ppermute | solution.py:413
  63.3 6.3 %collective-permute-start.20 = (f32[136,128]{1,0:T(8,128)S(1)}, f32[136,128]{1,0:T(8,128)S(1)}, u32[]{:S(2)}, u32[]{:S(2)}) collective-permute-start(f32[136,128]{1,0:T(8,128)S(1)} %shard_map.118.after.p0), channel_id=1, source_target_pairs={{0,16},{1,17},{2,18},{3,19},{4,20},{5,21},{6,22},{7,23},{8,24},{9,... | collective-permute-start | bytes 208904 | tf_op jit(solution)/shard_map/ppermute | solution.py:413
  64.5 5.1 %collective-permute-start.19 = (f32[136,128]{1,0:T(8,128)S(1)}, f32[136,128]{1,0:T(8,128)S(1)}, u32[]{:S(2)}, u32[]{:S(2)}) collective-permute-start(f32[136,128]{1,0:T(8,128)S(1)} %shard_map.118.after.p0), channel_id=1, source_target_pairs={{0,8},{1,9},{2,10},{3,11},{4,12},{5,13},{6,14},{7,15},{8,0},{9,1},... | collective-permute-start | bytes 208904 | tf_op jit(solution)/shard_map/ppermute | solution.py:413
  69.7 5.6 %collective-permute-start.22 = (f32[136,128]{1,0:T(8,128)S(1)}, f32[136,128]{1,0:T(8,128)S(1)}, u32[]{:S(2)}, u32[]{:S(2)}) collective-permute-start(f32[136,128]{1,0:T(8,128)S(1)} %shard_map.120.after.sent), channel_id=1, source_target_pairs={{0,48},{1,49},{2,50},{3,51},{4,52},{5,53},{6,54},{7,55},{8,56},{9,... | collective-permute-start | bytes 208904 | tf_op jit(solution)/shard_map/ppermute | solution.py:413
  75.3 6.5 %collective-permute-start.23 = (f32[128,128]{1,0:T(8,128)S(1)}, f32[128,128]{1,0:T(8,128)S(1)}, u32[]{:S(2)}, u32[]{:S(2)}) collective-permute-start(f32[128,128]{1,0:T(8,128)S(1)} %get-tuple-element.92), channel_id=1, source_target_pairs={{0,2},{1,3},{2,0},{3,1},{4,6},{5,7},{6,4},{7,5},{8,10},{9,11},{10,... | collective-permute-start | bytes 196616 | tf_op jit(solution)/shard_map/ppermute | solution.py:413
  76.6 5.2 %collective-permute-start.24 = (f32[128,128]{1,0:T(8,128)S(1)}, f32[128,128]{1,0:T(8,128)S(1)}, u32[]{:S(2)}, u32[]{:S(2)}) collective-permute-start(f32[128,128]{1,0:T(8,128)S(1)} %get-tuple-element.93), channel_id=1, source_target_pairs={{0,4},{1,5},{2,6},{3,7},{4,0},{5,1},{6,2},{7,3},{8,12},{9,13},{10,... | collective-permute-start | bytes 196616 | tf_op jit(solution)/shard_map/ppermute | solution.py:413
  77.8 4.3 %collective-permute-start.25 = (f32[128,128]{1,0:T(8,128)S(1)}, f32[128,128]{1,0:T(8,128)S(1)}, u32[]{:S(2)}, u32[]{:S(2)}) collective-permute-start(f32[128,128]{1,0:T(8,128)S(1)} %get-tuple-element.94), channel_id=1, source_target_pairs={{0,6},{1,7},{2,4},{3,5},{4,2},{5,3},{6,0},{7,1},{8,14},{9,15},{10,... | collective-permute-start | bytes 196616 | tf_op jit(solution)/shard_map/ppermute | solution.py:413
  81.8 0.7 copy-start.3
  82.5 6.3 %collective-permute-start.26 = (f32[512,128]{1,0:T(8,128)S(1)}, f32[512,128]{1,0:T(8,128)S(1)}, u32[]{:S(2)}, u32[]{:S(2)}) collective-permute-start(f32[512,128]{1,0:T(8,128)S(1)} %get-tuple-element.104.refs_8_), channel_id=1, source_target_pairs={{0,1},{1,0},{2,3},{3,2},{4,5},{5,4},{6,7},{7,6},{8,9},{9,8},{10,11... | collective-permute-start | bytes 786440 | tf_op jit(solution)/shard_map/ppermute | solution.py:413

commit v8 on v7

--- a/solution.py
+++ b/solution.py
@@ -315,9 +315,9 @@
     cross = jnp.sum(cross.T, axis=0, keepdims=True)
     if not own:
         square += refs[0][0:1, :]
-        cross += refs[0][4:5, :]
-    sums[0:4, :] = jnp.broadcast_to(square, (4, TOK))
-    sums[4:8, :] = jnp.broadcast_to(cross, (4, TOK))
+        cross += refs[0][1:2, :]
+    sums[0:1, :] = square
+    sums[1:2, :] = cross
 
 
 def mixed_kernel(table, s0, s1, s2, s3, o, grad, q, gain, *refs, own):
@@ -326,7 +326,7 @@
     sums = s0[...] + s1[...] + s2[...] + s3[...]
     r = lax.rsqrt(sums[0:1, :] * (1.0 / FEATURES) + 1e-06)
     inverse = jnp.broadcast_to(r, (HEAD, TOK)).T
-    mean = jnp.broadcast_to(sums[4:5, :] * r * (1.0 / FEATURES), (HEAD, TOK)).T
+    mean = jnp.broadcast_to(sums[1:2, :] * r * (1.0 / FEATURES), (HEAD, TOK)).T
     tail = 4 * HEAD
 
     def term(head, wide, normed):
@@ -517,7 +517,7 @@
     )
     theirs = exchange(other, dc=1)
     mask, flipped, back_table, gain = made["masks"]
-    sums = shape(8, TOK)
+    sums = shape(2, TOK)
     outs = [shape(TOK, half), sums]
     o_mine, own_sums = local(
         attended_kernel, outs, [queries, made[True], out_grad, gain, mine], [other], small_mm, 3 << 20, own=True

time: 90.7 us -> 90.5 us (level)
  no operation moved by 1% of the time
where the time goes in v8:
time: 90.5 us; the launch traced here: 90.4 us
  starting transfers between devices  48.8 us (54%)
  Pallas kernels  22.3 us (25%)
  waiting for transfers between devices  17.9 us (20%)
  between operations  1.06 us (1%)
    ppermute x24, starting transfers between devices, exchange(): return lax.ppermute(array, 'seq', pairs)  45.5 us
    pallas_call x11, Pallas kernels, local(): call(functools.partial(kernel, **more), outs, in_specs=[VMEM] * (1 + len(...  15 us
    ppermute x24, waiting for transfers between devices, exchange(): return lax.ppermute(array, 'seq', pairs)  14.8 us
    ppermute x3, starting transfers between devices, shards(): lax.ppermute(sums, 'dp', [(i, i ^ k) for i in range(4)])  3.34 us
    ppermute x3, waiting for transfers between devices, shards(): lax.ppermute(sums, 'dp', [(i, i ^ k) for i in range(4)])  3.19 us
    pallas_call x1, Pallas kernels, shards(): call(sent_states_kernel, [state_shape, shape(FORWARD + CHAIN_ROWS, HEAD),...  1.93 us
  transfers between devices with their start and end apart: 27, of which 15 were waited for; matrix products, arithmetic and copies ran while one was open for 0% of the time, Pallas kernels for 18%

profile of v8, /device:TPU:1, one launch (start us, length us, event | category | flops | bytes accessed | tf_op | source)
XLA Modules:
  0.0 90.4 jit_solution(3981372185127480307)
XLA Ops:
  0.6 1.9 %shard_map.102 = (f32[512,128]{1,0:T(8,128)S(1)}, f32[64,128]{1,0:T(8,128)S(1)}, bf16[512,1024]{1,0:T(8,128)(2,1)S(1)}, bf16[512,1024]{1,0:T(8,128)(2,1)S(1)}) custom-call(s32[8]{0:T(128)} %decay.1, s32[3]{0:T(128)} %bounds.1, bf16[512,1024]{1,0:T(8,128)(2,1)} %k_in.1, bf16[512,1024]{1,0:T(8,128)(2,1)} %v_in.1), custom_call_target="tpu_custom_call" | custom-call | flops 67108864 | bytes 1572864 | tf_op jit(solution)/shard_map/pallas_call | solution.py:472
  2.6 3.3 %collective-permute-start = (f32[512,128]{1,0:T(8,128)S(1)}, f32[512,128]{1,0:T(8,128)S(1)}, u32[]{:S(2)}, u32[]{:S(2)}) collective-permute-start(f32[512,128]{1,0:T(8,128)S(1)} %get-tuple-element.61.after.send), channel_id=1, source_target_pairs={{0,1},{1,0},{2,3},{3,2},{4,5},{5,4},{6,7},{7,6},{8,9},{9,8},{10,11... | collective-permute-start | bytes 786440 | tf_op jit(solution)/shard_map/ppermute | solution.py:413
  7.2 2.2 %collective-permute-start.2 = (f32[128,128]{1,0:T(8,128)S(1)}, f32[128,128]{1,0:T(8,128)S(1)}, u32[]{:S(2)}, u32[]{:S(2)}) collective-permute-start(f32[128,128]{1,0:T(8,128)S(1)} %get-tuple-element.66), channel_id=1, source_target_pairs={{0,4},{1,5},{2,6},{3,7},{4,0},{5,1},{6,2},{7,3},{8,12},{9,13},{10,... | collective-permute-start | bytes 196616 | tf_op jit(solution)/shard_map/ppermute | solution.py:413
  9.4 1.7 %collective-permute-start.3 = (f32[128,128]{1,0:T(8,128)S(1)}, f32[128,128]{1,0:T(8,128)S(1)}, u32[]{:S(2)}, u32[]{:S(2)}) collective-permute-start(f32[128,128]{1,0:T(8,128)S(1)} %get-tuple-element.67), channel_id=1, source_target_pairs={{0,6},{1,7},{2,4},{3,5},{4,2},{5,3},{6,0},{7,1},{8,14},{9,15},{10,... | collective-permute-start | bytes 196616 | tf_op jit(solution)/shard_map/ppermute | solution.py:413
  12.2 1.5 %shard_map.106.after.intra = f32[512,512]{1,0:T(8,128)S(1)} custom-call(f32[64,128]{1,0:T(8,128)S(1)} %get-tuple-element.58.table, bf16[512,1024]{1,0:T(8,128)(2,1)S(1)} %copy-done, bf16[512,1024]{1,0:T(8,128)(2,1)S(1)} %get-tuple-element.59.k, bf16[512,1024]{1,0:T(8,128)(2,1)S(1)} %get-tuple-element.60.v, bf16[512,512]{1,0:T(8,128)(2,1)S(1)} %get-tuple-element.64.mask, ...), custom_call_target="tpu_custom_call" | custom-call | flops 402653184 | bytes 3145728 | tf_op jit(solution)/shard_map/pallas_call | solution.py:462
  14.0 4.3 %collective-permute-start.6 = (f32[128,128]{1,0:T(8,128)S(1)}, f32[128,128]{1,0:T(8,128)S(1)}, u32[]{:S(2)}, u32[]{:S(2)}) collective-permute-start(f32[128,128]{1,0:T(8,128)S(1)} %shard_map.107.after.p0), channel_id=1, source_target_pairs={{0,24},{1,25},{2,26},{3,27},{4,28},{5,29},{6,30},{7,31},{8,16},{9,... | collective-permute-start | bytes 196616 | tf_op jit(solution)/shard_map/ppermute | solution.py:413
  18.7 1.5 %shard_map.108.after.intra = f32[512,512]{1,0:T(8,128)S(1)} custom-call(f32[64,128]{1,0:T(8,128)S(1)} %get-tuple-element.58.table, bf16[512,1024]{1,0:T(8,128)(2,1)S(1)} %copy-done, bf16[512,1024]{1,0:T(8,128)(2,1)S(1)} %get-tuple-element.59.k, bf16[512,1024]{1,0:T(8,128)(2,1)S(1)} %get-tuple-element.60.v, bf16[512,512]{1,0:T(8,128)(2,1)S(1)} %get-tuple-element.64.mask, ...), custom_call_target="tpu_custom_call" | custom-call | flops 402653184 | bytes 3145728 | tf_op jit(solution)/shard_map/pallas_call | solution.py:462
  20.2 2.8 %collective-permute-done.5.p2.r2 = f32[128,128]{1,0:T(8,128)S(1)} collective-permute-done((f32[128,128]{1,0:T(8,128)S(1)}, f32[128,128]{1,0:T(8,128)S(1)}, u32[]{:S(2)}, u32[]{:S(2)}) %collective-permute-start.5) | collective-permute-done | bytes 65568 | tf_op jit(solution)/shard_map/ppermute | solution.py:413
  23.0 3.6 %collective-permute-start.7 = (f32[128,128]{1,0:T(8,128)S(1)}, f32[128,128]{1,0:T(8,128)S(1)}, u32[]{:S(2)}, u32[]{:S(2)}) collective-permute-start(f32[128,128]{1,0:T(8,128)S(1)} %shard_map.109.sent.after), channel_id=1, source_target_pairs={{0,48},{1,49},{2,50},{3,51},{4,52},{5,53},{6,54},{7,55},{8,56},{9,... | collective-permute-start | bytes 196616 | tf_op jit(solution)/shard_map/ppermute | solution.py:413
  26.6 2.4 %collective-permute-done.7.far = f32[128,128]{1,0:T(8,128)S(1)} collective-permute-done((f32[128,128]{1,0:T(8,128)S(1)}, f32[128,128]{1,0:T(8,128)S(1)}, u32[]{:S(2)}, u32[]{:S(2)}) %collective-permute-start.7) | collective-permute-done | bytes 65568 | tf_op jit(solution)/shard_map/ppermute | solution.py:413
  29.2 2.6 %collective-permute-start.9 = (f32[128,128]{1,0:T(8,128)S(1)}, f32[128,128]{1,0:T(8,128)S(1)}, u32[]{:S(2)}, u32[]{:S(2)}) collective-permute-start(f32[128,128]{1,0:T(8,128)S(1)} %get-tuple-element.71), channel_id=1, source_target_pairs={{0,4},{1,5},{2,6},{3,7},{4,0},{5,1},{6,2},{7,3},{8,12},{9,13},{10,... | collective-permute-start | bytes 196616 | tf_op jit(solution)/shard_map/ppermute | solution.py:413
  31.8 1.3 %collective-permute-start.10 = (f32[128,128]{1,0:T(8,128)S(1)}, f32[128,128]{1,0:T(8,128)S(1)}, u32[]{:S(2)}, u32[]{:S(2)}) collective-permute-start(f32[128,128]{1,0:T(8,128)S(1)} %get-tuple-element.72), channel_id=1, source_target_pairs={{0,6},{1,7},{2,4},{3,5},{4,2},{5,3},{6,0},{7,1},{8,14},{9,15},{10,... | collective-permute-start | bytes 196616 | tf_op jit(solution)/shard_map/ppermute | solution.py:413
  34.1 2.0 %collective-permute-done.10.v3 = f32[128,128]{1,0:T(8,128)S(1)} collective-permute-done((f32[128,128]{1,0:T(8,128)S(1)}, f32[128,128]{1,0:T(8,128)S(1)}, u32[]{:S(2)}, u32[]{:S(2)}) %collective-permute-start.10) | collective-permute-done | bytes 65568 | tf_op jit(solution)/shard_map/ppermute | solution.py:413
  36.2 4.5 %collective-permute-start.11 = (f32[512,128]{1,0:T(8,128)S(1)}, f32[512,128]{1,0:T(8,128)S(1)}, u32[]{:S(2)}, u32[]{:S(2)}) collective-permute-start(f32[512,128]{1,0:T(8,128)S(1)} %get-tuple-element.73.refs_0_), channel_id=1, source_target_pairs={{0,1},{1,0},{2,3},{3,2},{4,5},{5,4},{6,7},{7,6},{8,9},{9,8},{10,11... | collective-permute-start | bytes 786440 | tf_op jit(solution)/shard_map/ppermute | solution.py:413
  42.6 2.6 %collective-permute-start.14 = (f32[2,512]{1,0:T(2,128)S(1)}, f32[2,512]{1,0:T(2,128)S(1)}, u32[]{:S(2)}, u32[]{:S(2)}) collective-permute-start(f32[2,512]{1,0:T(2,128)S(1)} %get-tuple-element.76.s0), channel_id=1, source_target_pairs={{0,192},{64,128},{128,64},{192,0},{1,193},{65,129},{129,65},{193,1... | collective-permute-start | bytes 12296 | tf_op jit(solution)/shard_map/ppermute | solution.py:534
  46.4 2.8 %collective-permute-done.13.s2 = f32[2,512]{1,0:T(2,128)S(1)} collective-permute-done((f32[2,512]{1,0:T(2,128)S(1)}, f32[2,512]{1,0:T(2,128)S(1)}, u32[]{:S(2)}, u32[]{:S(2)}) %collective-permute-start.13) | collective-permute-done | bytes 4128 | tf_op jit(solution)/shard_map/ppermute | solution.py:534
  49.2 1.2 %shard_map.114 = (bf16[512,512]{1,0:T(8,128)(2,1)S(1)}, f32[520,128]{1,0:T(8,128)S(1)}) custom-call(f32[64,128]{1,0:T(8,128)S(1)} %get-tuple-element.58.table, f32[2,512]{1,0:T(2,128)S(1)} %get-tuple-element.76.s0, f32[2,512]{1,0:T(2,128)S(1)} %collective-permute-done.12.s1, f32[2,512]{1,0:T(2,128)S(1)} %collective-permute-done.13.s2, ...), custom_call_target="tpu_custom_call" | custom-call | flops 67108864 | bytes 3145728 | tf_op jit(solution)/shard_map/pallas_call | solution.py:462
  50.4 1.9 %collective-permute-start.15 = (f32[520,128]{1,0:T(8,128)S(1)}, f32[520,128]{1,0:T(8,128)S(1)}, u32[]{:S(2)}, u32[]{:S(2)}) collective-permute-start(f32[520,128]{1,0:T(8,128)S(1)} %get-tuple-element.79.refs_0_.send), channel_id=1, source_target_pairs={{0,1},{1,0},{2,3},{3,2},{4,5},{5,4},{6,7},{7,6},{8,9},{9,8},{10,11... | collective-permute-start | bytes 798728 | tf_op jit(solution)/shard_map/ppermute | solution.py:413
  53.5 3.2 %collective-permute-start.17 = (f32[136,128]{1,0:T(8,128)S(1)}, f32[136,128]{1,0:T(8,128)S(1)}, u32[]{:S(2)}, u32[]{:S(2)}) collective-permute-start(f32[136,128]{1,0:T(8,128)S(1)} %get-tuple-element.83), channel_id=1, source_target_pairs={{0,4},{1,5},{2,6},{3,7},{4,0},{5,1},{6,2},{7,3},{8,12},{9,13},{10,... | collective-permute-start | bytes 208904 | tf_op jit(solution)/shard_map/ppermute | solution.py:413
  57.4 2.0 %shard_map.117 = (bf16[512,256]{1,0:T(8,128)(2,1)S(1)}, f32[512,256]{1,0:T(8,128)S(1)}, f32[512,256]{1,0:T(8,128)S(1)}) custom-call(f32[64,128]{1,0:T(8,128)S(1)} %get-tuple-element.58.table, bf16[512,1024]{1,0:T(8,128)(2,1)S(1)} %copy-done, bf16[512,1024]{1,0:T(8,128)(2,1)S(1)} %get-tuple-element.59.k, bf16[512,1024]{1,0:T(8,128)(2,1)S(1)} %get-tuple-element.60.v, ...), custom_call_target="tpu_custom_call" | custom-call | flops 603979776 | bytes 2097152 | tf_op jit(solution)/shard_map/pallas_call | solution.py:462
  59.9 1.6 %collective-permute-done.18.p3.t3 = f32[136,128]{1,0:T(8,128)S(1)} collective-permute-done((f32[136,128]{1,0:T(8,128)S(1)}, f32[136,128]{1,0:T(8,128)S(1)}, u32[]{:S(2)}, u32[]{:S(2)}) %collective-permute-start.18) | collective-permute-done | bytes 69664 | tf_op jit(solution)/shard_map/ppermute | solution.py:413
  61.4 1.8 %collective-permute-start.21 = (f32[136,128]{1,0:T(8,128)S(1)}, f32[136,128]{1,0:T(8,128)S(1)}, u32[]{:S(2)}, u32[]{:S(2)}) collective-permute-start(f32[136,128]{1,0:T(8,128)S(1)} %shard_map.118.after.p0), channel_id=1, source_target_pairs={{0,24},{1,25},{2,26},{3,27},{4,28},{5,29},{6,30},{7,31},{8,16},{9,... | collective-permute-start | bytes 208904 | tf_op jit(solution)/shard_map/ppermute | solution.py:413
  65.1 1.9 %shard_map.119 = (bf16[512,256]{1,0:T(8,128)(2,1)S(1)}, f32[512,256]{1,0:T(8,128)S(1)}, f32[512,256]{1,0:T(8,128)S(1)}) custom-call(f32[64,128]{1,0:T(8,128)S(1)} %get-tuple-element.58.table, bf16[512,1024]{1,0:T(8,128)(2,1)S(1)} %copy-done, bf16[512,1024]{1,0:T(8,128)(2,1)S(1)} %get-tuple-element.59.k, bf16[512,1024]{1,0:T(8,128)(2,1)S(1)} %get-tuple-element.60.v, ...), custom_call_target="tpu_custom_call" | custom-call | flops 603979776 | bytes 2097152 | tf_op jit(solution)/shard_map/pallas_call | solution.py:462
  67.0 2.4 %collective-permute-done.20.p2.r2 = f32[136,128]{1,0:T(8,128)S(1)} collective-permute-done((f32[136,128]{1,0:T(8,128)S(1)}, f32[136,128]{1,0:T(8,128)S(1)}, u32[]{:S(2)}, u32[]{:S(2)}) %collective-permute-start.20) | collective-permute-done | bytes 69664 | tf_op jit(solution)/shard_map/ppermute | solution.py:413
  69.5 3.3 %collective-permute-start.22 = (f32[136,128]{1,0:T(8,128)S(1)}, f32[136,128]{1,0:T(8,128)S(1)}, u32[]{:S(2)}, u32[]{:S(2)}) collective-permute-start(f32[136,128]{1,0:T(8,128)S(1)} %shard_map.120.after.sent), channel_id=1, source_target_pairs={{0,48},{1,49},{2,50},{3,51},{4,52},{5,53},{6,54},{7,55},{8,56},{9,... | collective-permute-start | bytes 208904 | tf_op jit(solution)/shard_map/ppermute | solution.py:413
  72.8 2.0 %shard_map.121 = (bf16[512,256]{1,0:T(8,128)(2,1)S(1)}, f32[512,256]{1,0:T(8,128)S(1)}, f32[512,256]{1,0:T(8,128)S(1)}) custom-call(f32[64,128]{1,0:T(8,128)S(1)} %get-tuple-element.58.table, bf16[512,1024]{1,0:T(8,128)(2,1)S(1)} %copy-done, bf16[512,1024]{1,0:T(8,128)(2,1)S(1)} %get-tuple-element.59.k, bf16[512,1024]{1,0:T(8,128)(2,1)S(1)} %get-tuple-element.60.v, ...), custom_call_target="tpu_custom_call" | custom-call | flops 603979776 | bytes 2097152 | tf_op jit(solution)/shard_map/pallas_call | solution.py:462
  76.1 1.5 %collective-permute-start.24 = (f32[128,128]{1,0:T(8,128)S(1)}, f32[128,128]{1,0:T(8,128)S(1)}, u32[]{:S(2)}, u32[]{:S(2)}) collective-permute-start(f32[128,128]{1,0:T(8,128)S(1)} %get-tuple-element.93), channel_id=1, source_target_pairs={{0,4},{1,5},{2,6},{3,7},{4,0},{5,1},{6,2},{7,3},{8,12},{9,13},{10,... | collective-permute-start | bytes 196616 | tf_op jit(solution)/shard_map/ppermute | solution.py:413
  77.7 1.4 %collective-permute-start.25 = (f32[128,128]{1,0:T(8,128)S(1)}, f32[128,128]{1,0:T(8,128)S(1)}, u32[]{:S(2)}, u32[]{:S(2)}) collective-permute-start(f32[128,128]{1,0:T(8,128)S(1)} %get-tuple-element.94), channel_id=1, source_target_pairs={{0,6},{1,7},{2,4},{3,5},{4,2},{5,3},{6,0},{7,1},{8,14},{9,15},{10,... | collective-permute-start | bytes 196616 | tf_op jit(solution)/shard_map/ppermute | solution.py:413
  79.7 2.0 %shard_map.123 = (bf16[512,256]{1,0:T(8,128)(2,1)S(1)}, f32[512,256]{1,0:T(8,128)S(1)}, f32[512,256]{1,0:T(8,128)S(1)}) custom-call(f32[64,128]{1,0:T(8,128)S(1)} %get-tuple-element.58.table, bf16[512,1024]{1,0:T(8,128)(2,1)S(1)} %copy-done, bf16[512,1024]{1,0:T(8,128)(2,1)S(1)} %get-tuple-element.59.k, bf16[512,1024]{1,0:T(8,128)(2,1)S(1)} %get-tuple-element.60.v, ...), custom_call_target="tpu_custom_call" | custom-call | flops 603979776 | bytes 2097152 | tf_op jit(solution)/shard_map/pallas_call | solution.py:462
  82.4 4.7 %collective-permute-start.26 = (f32[512,128]{1,0:T(8,128)S(1)}, f32[512,128]{1,0:T(8,128)S(1)}, u32[]{:S(2)}, u32[]{:S(2)}) collective-permute-start(f32[512,128]{1,0:T(8,128)S(1)} %get-tuple-element.104.refs_8_), channel_id=1, source_target_pairs={{0,1},{1,0},{2,3},{3,2},{4,5},{5,4},{6,7},{7,6},{8,9},{9,8},{10,11... | collective-permute-start | bytes 786440 | tf_op jit(solution)/shard_map/ppermute | solution.py:413
  87.1 1.6 %shard_map.126 = (bf16[512,1024]{1,0:T(8,128)(2,1)}, bf16[512,1024]{1,0:T(8,128)(2,1)}, bf16[512,1024]{1,0:T(8,128)(2,1)}) custom-call(f32[64,128]{1,0:T(8,128)S(1)} %get-tuple-element.58.table, bf16[512,1024]{1,0:T(8,128)(2,1)S(1)} %get-tuple-element.59.k, bf16[512,1024]{1,0:T(8,128)(2,1)S(1)} %get-tuple-element.60.v, ...), custom_call_target="tpu_custom_call" | custom-call | flops 134217728 | bytes 6291456 | tf_op jit(solution)/shard_map/pallas_call | solution.py:578
  88.7 1.5 %shard_map.127 = (bf16[512,1024]{1,0:T(8,128)(2,1)}, bf16[512,1024]{1,0:T(8,128)(2,1)}) custom-call(f32[64,128]{1,0:T(8,128)S(1)} %get-tuple-element.58.table, bf16[512,1024]{1,0:T(8,128)(2,1)S(1)} %get-tuple-element.59.k, bf16[512,1024]{1,0:T(8,128)(2,1)S(1)} %get-tuple-element.60.v, ...), custom_call_target="tpu_custom_call", output_to_operand_aliasing={{0}: (8, {}), {1}: (9, {})} | custom-call | flops 134217728 | bytes 4194304 | tf_op jit(solution)/shard_map/pallas_call | solution.py:587
  (56 shorter events, 14.6 us)
Async XLA Ops:
  2.6 4.5 %collective-permute-start = (f32[512,128]{1,0:T(8,128)S(1)}, f32[512,128]{1,0:T(8,128)S(1)}, u32[]{:S(2)}, u32[]{:S(2)}) collective-permute-start(f32[512,128]{1,0:T(8,128)S(1)} %get-tuple-element.61.after.send), channel_id=1, source_target_pairs={{0,1},{1,0},{2,3},{3,2},{4,5},{5,4},{6,7},{7,6},{8,9},{9,8},{10,11... | collective-permute-start | bytes 786440 | tf_op jit(solution)/shard_map/ppermute | solution.py:413
  6.5 5.7 %copy-start = (bf16[512,1024]{1,0:T(8,128)(2,1)S(1)}, bf16[512,1024]{1,0:T(8,128)(2,1)}, u32[]{:S(2)}) copy-start(bf16[512,1024]{1,0:T(8,128)(2,1)} %q.19) | copy-start | bytes 3145732
  7.1 4.0 %copy-start.2 = (f32[1024]{0:T(1024)S(1)}, f32[1024]{0:T(1024)}, u32[]{:S(2)}) copy-start(f32[1024]{0:T(1024)} %param.11) | copy-start | bytes 12292
  7.1 6.6 %collective-permute-start.1 = (f32[128,128]{1,0:T(8,128)S(1)}, f32[128,128]{1,0:T(8,128)S(1)}, u32[]{:S(2)}, u32[]{:S(2)}) collective-permute-start(f32[128,128]{1,0:T(8,128)S(1)} %get-tuple-element.65), channel_id=1, source_target_pairs={{0,2},{1,3},{2,0},{3,1},{4,6},{5,7},{6,4},{7,5},{8,10},{9,11},{10,... | collective-permute-start | bytes 196616 | tf_op jit(solution)/shard_map/ppermute | solution.py:413
  7.2 6.5 %collective-permute-start.2 = (f32[128,128]{1,0:T(8,128)S(1)}, f32[128,128]{1,0:T(8,128)S(1)}, u32[]{:S(2)}, u32[]{:S(2)}) collective-permute-start(f32[128,128]{1,0:T(8,128)S(1)} %get-tuple-element.66), channel_id=1, source_target_pairs={{0,4},{1,5},{2,6},{3,7},{4,0},{5,1},{6,2},{7,3},{8,12},{9,13},{10,... | collective-permute-start | bytes 196616 | tf_op jit(solution)/shard_map/ppermute | solution.py:413
  9.4 4.6 %collective-permute-start.3 = (f32[128,128]{1,0:T(8,128)S(1)}, f32[128,128]{1,0:T(8,128)S(1)}, u32[]{:S(2)}, u32[]{:S(2)}) collective-permute-start(f32[128,128]{1,0:T(8,128)S(1)} %get-tuple-element.67), channel_id=1, source_target_pairs={{0,6},{1,7},{2,4},{3,5},{4,2},{5,3},{6,0},{7,1},{8,14},{9,15},{10,... | collective-permute-start | bytes 196616 | tf_op jit(solution)/shard_map/ppermute | solution.py:413
  14.0 6.2 %collective-permute-start.6 = (f32[128,128]{1,0:T(8,128)S(1)}, f32[128,128]{1,0:T(8,128)S(1)}, u32[]{:S(2)}, u32[]{:S(2)}) collective-permute-start(f32[128,128]{1,0:T(8,128)S(1)} %shard_map.107.after.p0), channel_id=1, source_target_pairs={{0,24},{1,25},{2,26},{3,27},{4,28},{5,29},{6,30},{7,31},{8,16},{9,... | collective-permute-start | bytes 196616 | tf_op jit(solution)/shard_map/ppermute | solution.py:413
  18.3 4.6 %collective-permute-start.5 = (f32[128,128]{1,0:T(8,128)S(1)}, f32[128,128]{1,0:T(8,128)S(1)}, u32[]{:S(2)}, u32[]{:S(2)}) collective-permute-start(f32[128,128]{1,0:T(8,128)S(1)} %shard_map.107.after.p0), channel_id=1, source_target_pairs={{0,16},{1,17},{2,18},{3,19},{4,20},{5,21},{6,22},{7,23},{8,24},{9,... | collective-permute-start | bytes 196616 | tf_op jit(solution)/shard_map/ppermute | solution.py:413
  18.3 4.6 %collective-permute-start.4 = (f32[128,128]{1,0:T(8,128)S(1)}, f32[128,128]{1,0:T(8,128)S(1)}, u32[]{:S(2)}, u32[]{:S(2)}) collective-permute-start(f32[128,128]{1,0:T(8,128)S(1)} %shard_map.107.after.p0), channel_id=1, source_target_pairs={{0,8},{1,9},{2,10},{3,11},{4,12},{5,13},{6,14},{7,15},{8,0},{9,1},... | collective-permute-start | bytes 196616 | tf_op jit(solution)/shard_map/ppermute | solution.py:413
  23.0 17.7 %copy-start.1 = (bf16[512,1024]{1,0:T(8,128)(2,1)S(1)}, bf16[512,1024]{1,0:T(8,128)(2,1)}, u32[]{:S(2)}) copy-start(bf16[512,1024]{1,0:T(8,128)(2,1)} %grad.7) | copy-start | bytes 3145732
  23.0 6.0 %collective-permute-start.7 = (f32[128,128]{1,0:T(8,128)S(1)}, f32[128,128]{1,0:T(8,128)S(1)}, u32[]{:S(2)}, u32[]{:S(2)}) collective-permute-start(f32[128,128]{1,0:T(8,128)S(1)} %shard_map.109.sent.after), channel_id=1, source_target_pairs={{0,48},{1,49},{2,50},{3,51},{4,52},{5,53},{6,54},{7,55},{8,56},{9,... | collective-permute-start | bytes 196616 | tf_op jit(solution)/shard_map/ppermute | solution.py:413
  29.1 3.9 %collective-permute-start.8 = (f32[128,128]{1,0:T(8,128)S(1)}, f32[128,128]{1,0:T(8,128)S(1)}, u32[]{:S(2)}, u32[]{:S(2)}) collective-permute-start(f32[128,128]{1,0:T(8,128)S(1)} %get-tuple-element.70), channel_id=1, source_target_pairs={{0,2},{1,3},{2,0},{3,1},{4,6},{5,7},{6,4},{7,5},{8,10},{9,11},{10,... | collective-permute-start | bytes 196616 | tf_op jit(solution)/shard_map/ppermute | solution.py:413
  29.2 4.9 %collective-permute-start.9 = (f32[128,128]{1,0:T(8,128)S(1)}, f32[128,128]{1,0:T(8,128)S(1)}, u32[]{:S(2)}, u32[]{:S(2)}) collective-permute-start(f32[128,128]{1,0:T(8,128)S(1)} %get-tuple-element.71), channel_id=1, source_target_pairs={{0,4},{1,5},{2,6},{3,7},{4,0},{5,1},{6,2},{7,3},{8,12},{9,13},{10,... | collective-permute-start | bytes 196616 | tf_op jit(solution)/shard_map/ppermute | solution.py:413
  31.8 4.3 %collective-permute-start.10 = (f32[128,128]{1,0:T(8,128)S(1)}, f32[128,128]{1,0:T(8,128)S(1)}, u32[]{:S(2)}, u32[]{:S(2)}) collective-permute-start(f32[128,128]{1,0:T(8,128)S(1)} %get-tuple-element.72), channel_id=1, source_target_pairs={{0,6},{1,7},{2,4},{3,5},{4,2},{5,3},{6,0},{7,1},{8,14},{9,15},{10,... | collective-permute-start | bytes 196616 | tf_op jit(solution)/shard_map/ppermute | solution.py:413
  36.2 5.7 %collective-permute-start.11 = (f32[512,128]{1,0:T(8,128)S(1)}, f32[512,128]{1,0:T(8,128)S(1)}, u32[]{:S(2)}, u32[]{:S(2)}) collective-permute-start(f32[512,128]{1,0:T(8,128)S(1)} %get-tuple-element.73.refs_0_), channel_id=1, source_target_pairs={{0,1},{1,0},{2,3},{3,2},{4,5},{5,4},{6,7},{7,6},{8,9},{9,8},{10,11... | collective-permute-start | bytes 786440 | tf_op jit(solution)/shard_map/ppermute | solution.py:413
  42.6 3.8 %collective-permute-start.14 = (f32[2,512]{1,0:T(2,128)S(1)}, f32[2,512]{1,0:T(2,128)S(1)}, u32[]{:S(2)}, u32[]{:S(2)}) collective-permute-start(f32[2,512]{1,0:T(2,128)S(1)} %get-tuple-element.76.s0), channel_id=1, source_target_pairs={{0,192},{64,128},{128,64},{192,0},{1,193},{65,129},{129,65},{193,1... | collective-permute-start | bytes 12296 | tf_op jit(solution)/shard_map/ppermute | solution.py:534
  45.2 4.0 %collective-permute-start.13 = (f32[2,512]{1,0:T(2,128)S(1)}, f32[2,512]{1,0:T(2,128)S(1)}, u32[]{:S(2)}, u32[]{:S(2)}) collective-permute-start(f32[2,512]{1,0:T(2,128)S(1)} %get-tuple-element.76.s0), channel_id=1, source_target_pairs={{0,128},{64,192},{128,0},{192,64},{1,129},{65,193},{129,1},{193,65... | collective-permute-start | bytes 12296 | tf_op jit(solution)/shard_map/ppermute | solution.py:534
  45.7 3.4 %collective-permute-start.12 = (f32[2,512]{1,0:T(2,128)S(1)}, f32[2,512]{1,0:T(2,128)S(1)}, u32[]{:S(2)}, u32[]{:S(2)}) collective-permute-start(f32[2,512]{1,0:T(2,128)S(1)} %get-tuple-element.76.s0), channel_id=1, source_target_pairs={{0,64},{64,0},{128,192},{192,128},{1,65},{65,1},{129,193},{193,129... | collective-permute-start | bytes 12296 | tf_op jit(solution)/shard_map/ppermute | solution.py:534
  50.4 3.0 %collective-permute-start.15 = (f32[520,128]{1,0:T(8,128)S(1)}, f32[520,128]{1,0:T(8,128)S(1)}, u32[]{:S(2)}, u32[]{:S(2)}) collective-permute-start(f32[520,128]{1,0:T(8,128)S(1)} %get-tuple-element.79.refs_0_.send), channel_id=1, source_target_pairs={{0,1},{1,0},{2,3},{3,2},{4,5},{5,4},{6,7},{7,6},{8,9},{9,8},{10,11... | collective-permute-start | bytes 798728 | tf_op jit(solution)/shard_map/ppermute | solution.py:413
  53.4 5.9 %collective-permute-start.16 = (f32[136,128]{1,0:T(8,128)S(1)}, f32[136,128]{1,0:T(8,128)S(1)}, u32[]{:S(2)}, u32[]{:S(2)}) collective-permute-start(f32[136,128]{1,0:T(8,128)S(1)} %get-tuple-element.82), channel_id=1, source_target_pairs={{0,2},{1,3},{2,0},{3,1},{4,6},{5,7},{6,4},{7,5},{8,10},{9,11},{10,... | collective-permute-start | bytes 208904 | tf_op jit(solution)/shard_map/ppermute | solution.py:413
  53.5 6.3 %collective-permute-start.17 = (f32[136,128]{1,0:T(8,128)S(1)}, f32[136,128]{1,0:T(8,128)S(1)}, u32[]{:S(2)}, u32[]{:S(2)}) collective-permute-start(f32[136,128]{1,0:T(8,128)S(1)} %get-tuple-element.83), channel_id=1, source_target_pairs={{0,4},{1,5},{2,6},{3,7},{4,0},{5,1},{6,2},{7,3},{8,12},{9,13},{10,... | collective-permute-start | bytes 208904 | tf_op jit(solution)/shard_map/ppermute | solution.py:413
  56.7 4.7 %collective-permute-start.18 = (f32[136,128]{1,0:T(8,128)S(1)}, f32[136,128]{1,0:T(8,128)S(1)}, u32[]{:S(2)}, u32[]{:S(2)}) collective-permute-start(f32[136,128]{1,0:T(8,128)S(1)} %get-tuple-element.84), channel_id=1, source_target_pairs={{0,6},{1,7},{2,4},{3,5},{4,2},{5,3},{6,0},{7,1},{8,14},{9,15},{10,... | collective-permute-start | bytes 208904 | tf_op jit(solution)/shard_map/ppermute | solution.py:413
  61.4 5.6 %collective-permute-start.21 = (f32[136,128]{1,0:T(8,128)S(1)}, f32[136,128]{1,0:T(8,128)S(1)}, u32[]{:S(2)}, u32[]{:S(2)}) collective-permute-start(f32[136,128]{1,0:T(8,128)S(1)} %shard_map.118.after.p0), channel_id=1, source_target_pairs={{0,24},{1,25},{2,26},{3,27},{4,28},{5,29},{6,30},{7,31},{8,16},{9,... | collective-permute-start | bytes 208904 | tf_op jit(solution)/shard_map/ppermute | solution.py:413
  63.2 6.3 %collective-permute-start.20 = (f32[136,128]{1,0:T(8,128)S(1)}, f32[136,128]{1,0:T(8,128)S(1)}, u32[]{:S(2)}, u32[]{:S(2)}) collective-permute-start(f32[136,128]{1,0:T(8,128)S(1)} %shard_map.118.after.p0), channel_id=1, source_target_pairs={{0,16},{1,17},{2,18},{3,19},{4,20},{5,21},{6,22},{7,23},{8,24},{9,... | collective-permute-start | bytes 208904 | tf_op jit(solution)/shard_map/ppermute | solution.py:413
  64.4 5.1 %collective-permute-start.19 = (f32[136,128]{1,0:T(8,128)S(1)}, f32[136,128]{1,0:T(8,128)S(1)}, u32[]{:S(2)}, u32[]{:S(2)}) collective-permute-start(f32[136,128]{1,0:T(8,128)S(1)} %shard_map.118.after.p0), channel_id=1, source_target_pairs={{0,8},{1,9},{2,10},{3,11},{4,12},{5,13},{6,14},{7,15},{8,0},{9,1},... | collective-permute-start | bytes 208904 | tf_op jit(solution)/shard_map/ppermute | solution.py:413
  69.5 5.6 %collective-permute-start.22 = (f32[136,128]{1,0:T(8,128)S(1)}, f32[136,128]{1,0:T(8,128)S(1)}, u32[]{:S(2)}, u32[]{:S(2)}) collective-permute-start(f32[136,128]{1,0:T(8,128)S(1)} %shard_map.120.after.sent), channel_id=1, source_target_pairs={{0,48},{1,49},{2,50},{3,51},{4,52},{5,53},{6,54},{7,55},{8,56},{9,... | collective-permute-start | bytes 208904 | tf_op jit(solution)/shard_map/ppermute | solution.py:413
  75.2 6.5 %collective-permute-start.23 = (f32[128,128]{1,0:T(8,128)S(1)}, f32[128,128]{1,0:T(8,128)S(1)}, u32[]{:S(2)}, u32[]{:S(2)}) collective-permute-start(f32[128,128]{1,0:T(8,128)S(1)} %get-tuple-element.92), channel_id=1, source_target_pairs={{0,2},{1,3},{2,0},{3,1},{4,6},{5,7},{6,4},{7,5},{8,10},{9,11},{10,... | collective-permute-start | bytes 196616 | tf_op jit(solution)/shard_map/ppermute | solution.py:413
  76.1 5.5 %collective-permute-start.24 = (f32[128,128]{1,0:T(8,128)S(1)}, f32[128,128]{1,0:T(8,128)S(1)}, u32[]{:S(2)}, u32[]{:S(2)}) collective-permute-start(f32[128,128]{1,0:T(8,128)S(1)} %get-tuple-element.93), channel_id=1, source_target_pairs={{0,4},{1,5},{2,6},{3,7},{4,0},{5,1},{6,2},{7,3},{8,12},{9,13},{10,... | collective-permute-start | bytes 196616 | tf_op jit(solution)/shard_map/ppermute | solution.py:413
  77.7 4.3 %collective-permute-start.25 = (f32[128,128]{1,0:T(8,128)S(1)}, f32[128,128]{1,0:T(8,128)S(1)}, u32[]{:S(2)}, u32[]{:S(2)}) collective-permute-start(f32[128,128]{1,0:T(8,128)S(1)} %get-tuple-element.94), channel_id=1, source_target_pairs={{0,6},{1,7},{2,4},{3,5},{4,2},{5,3},{6,0},{7,1},{8,14},{9,15},{10,... | collective-permute-start | bytes 196616 | tf_op jit(solution)/shard_map/ppermute | solution.py:413
  81.7 0.7 copy-start.3
  82.4 6.3 %collective-permute-start.26 = (f32[512,128]{1,0:T(8,128)S(1)}, f32[512,128]{1,0:T(8,128)S(1)}, u32[]{:S(2)}, u32[]{:S(2)}) collective-permute-start(f32[512,128]{1,0:T(8,128)S(1)} %get-tuple-element.104.refs_8_), channel_id=1, source_target_pairs={{0,1},{1,0},{2,3},{3,2},{4,5},{5,4},{6,7},{7,6},{8,9},{9,8},{10,11... | collective-permute-start | bytes 786440 | tf_op jit(solution)/shard_map/ppermute | solution.py:413
